TPU v7x, 32 devices: a whole 2x2x4 slice. The times are simulated.
32 devices in a mesh: replica: 2 (over x), tp: 16 (over z, y, core).
Axes of the slice: x: 2, y: 2, z: 4, core: 2. Of those that a mesh axis runs over, the one named last changes fastest.
Arguments:
- residual: bfloat16 [64, 16384], P(('replica', 'tp')), parts along dimension 0
- queries: bfloat16 [64, 2048], P('replica', 'tp'), parts along dimension 0
- key_rows: bfloat16 [64, 1024], P('replica'), parts along dimension 0
- value_rows: bfloat16 [64, 1024], P('replica'), parts along dimension 0, may hold values from -6 to 6
- out_weight: bfloat16 [2048, 16384], P('tp'), may hold values from -0.125 to 0.125
- norm_gain: float32 [16384], replicated, may hold values from 0.1 to 1.9
- q_weight: bfloat16 [16384, 2048], P(None, 'tp'), may hold values from -0.046875 to 0.046875
Outputs:
- stream_codes: bfloat16 [64, 16384], P(('replica', 'tp')), parts along dimension 0
- stream_scales: float32 [64, 128], P(('replica', 'tp')), parts along dimension 0
- next_queries: bfloat16 [64, 2048], P('replica', 'tp'), parts along dimension 0
There are 2 independent parts, one for each index of `replica`. A program takes and returns all parts, laid end to end along the dimension named above; an argument that names none is the same for every part. Nothing has to cross between parts.
All inputs are finite; a program needn't handle non-finite values. Where the computation divides by a largest or mean magnitude, that divisor is 1e-20 or more.
Results may differ from a plain program's by a relative error of at most 0.013.
Values may be sent and summed in bfloat16 or wider, within the bound.
No kernel may reach another device: no remote copies, remote signals or barrier semaphores. Data moves between devices by JAX's collectives and lax.ppermute only.
A program may use at most 128 MiB of HBM per device.

v0:
```python
import jax
import jax.numpy as jnp
from jax import lax
from jax.sharding import PartitionSpec as P

D = 16384
HD = 128
QB = 128


epsilon = 1e-06


def encode(values_in, block):
    tok_rows, width = values_in.shape
    grouped = values_in.reshape(tok_rows, width // block, block)
    peaks = jnp.max(jnp.abs(grouped), axis=2) + epsilon
    code_vals = (grouped / peaks[:, :, None]).astype(jnp.bfloat16).reshape(tok_rows, width)
    return (code_vals, peaks)


def decode_sum(code_vals, peaks, sources, block):
    tok_rows = code_vals.shape[0] // sources
    width = code_vals.shape[1]
    grouped = code_vals.reshape(sources, tok_rows, width // block, block).astype(jnp.float32)
    scaled = grouped * peaks[:, :, :, None]
    return jnp.sum(scaled, axis=0).reshape(tok_rows, width)


def on_device(residual, queries, key_rows, value_rows, out_weight, norm_gain, q_weight):
    tp_count = lax.axis_size("tp")
    device = lax.axis_index("tp")
    tok_total = queries.shape[0]
    tok_local = residual.shape[0]
    local_heads = queries.shape[1] // HD
    kv_heads = key_rows.shape[1] // HD
    group = local_heads * tp_count // kv_heads
    positions = jnp.arange(tok_total)
    visible = positions[None, :] <= positions[:, None]
    scale_factor = 1.0 / jnp.sqrt(jnp.float32(HD))
    kv_start = (device * local_heads + 0) // group * HD
    key_head = lax.dynamic_slice_in_dim(key_rows, kv_start, HD, 1)
    value_head = lax.dynamic_slice_in_dim(value_rows, kv_start, HD, 1)
    scores = (
        lax.dot_general(
            queries, key_head, (((1,), (1,)), ((), ())), preferred_element_type=jnp.float32
        )
        * scale_factor
    )
    scores = jnp.where(visible, scores, jnp.float32(-1e30))
    probs = jax.nn.softmax(scores, axis=-1).astype(jnp.bfloat16)
    contexts = jnp.dot(probs, value_head, preferred_element_type=jnp.float32).astype(jnp.bfloat16)
    partial_value = jnp.dot(contexts, out_weight, preferred_element_type=jnp.float32)
    code_vals, peaks = encode(partial_value, QB)
    sent_codes = code_vals.reshape(tp_count, tok_local, D)
    sent_peaks = peaks.reshape(tp_count, tok_local, D // QB)
    got_codes, got_peaks = (
        lax.all_to_all(sent_codes, "tp", split_axis=0, concat_axis=0, tiled=True),
        lax.all_to_all(
            sent_peaks.astype(jnp.bfloat16), "tp", split_axis=0, concat_axis=0, tiled=True
        ).astype(sent_peaks.dtype),
    )
    summed = decode_sum(got_codes.reshape(tp_count * tok_local, D), got_peaks, tp_count, QB)
    stream = residual.astype(jnp.float32) + summed
    stream_codes, stream_scales = encode(stream, QB)
    all_codes, all_scales = (
        lax.all_gather(stream_codes, "tp", axis=0, tiled=True),
        lax.all_gather(stream_scales.astype(jnp.bfloat16), "tp", axis=0, tiled=True).astype(
            stream_scales.dtype
        ),
    )
    grouped = all_codes.reshape(tok_total, D // QB, QB).astype(jnp.float32)
    decoded = (grouped * all_scales[:, :, None]).reshape(tok_total, D)
    mean_sq = jnp.mean(decoded * decoded, axis=1, keepdims=True)
    normed = (decoded * lax.rsqrt(mean_sq + 1e-05) * norm_gain[None, :]).astype(jnp.bfloat16)
    next_queries = jnp.dot(normed, q_weight, preferred_element_type=jnp.float32).astype(
        jnp.bfloat16
    )
    return (stream_codes, stream_scales, next_queries)


def solution(mesh):
    in_specs = (
        P(("replica", "tp"), None),
        P("replica", "tp"),
        P("replica", None),
        P("replica", None),
        P("tp", None),
        P(),
        P(None, "tp"),
    )
    out_specs = (P(("replica", "tp"), None), P(("replica", "tp"), None), P("replica", "tp"))
    return jax.shard_map(
        on_device, mesh=mesh, in_specs=in_specs, out_specs=out_specs, check_vma=False
    )
```

profile of v0, /device:TPU:0, one launch (start us, length us, event | category | flops | bytes accessed | tf_op | source)
XLA Modules:
  0.0 116.8 jit_solution(3280683703810540344)
XLA Ops:
  7.2 0.0 copy-start
  7.2 0.9 fusion.18
  8.1 0.0 copy-done
  8.1 3.0 %fusion.2 = f32[32,16384]{1,0:T(8,128)S(1)} fusion(bf16[128,16384]{1,0:T(8,128)(2,1)} %param.11, f32[32,32]{0,1:T(8,128)S(1)} %get-tuple-element.8, bf16[32,1024]{1,0:T(8,128)(2,1)S(1)} %copy-done, s32[]{:T(128)S(6)} %select_n.14, f32[32]{0:T(128)S(1)} %fusion.6, f32[32]{0:T(128)S(1)} %get-tuple-element.7), kind=kOutput, calls=%fused_computation.12 | convolution fusion | flops 134487040 | bytes 6317060 | tf_op jit(solution)/shard_map/dot_general | solution.py:53
  11.1 0.2 abs_bitcast_fusion
  11.3 0.4 copy.10
  11.7 0.6 bitcast_reduce_fusion
  12.3 0.6 broadcast_add_fusion
  12.9 7.4 %all-to-all-start.1 = ((bf16[16,2,128]{2,1,0:T(2,128)(2,1)}), bf16[16,2,128]{2,1,0:T(2,128)(2,1)S(1)}, u32[]{:S(2)}, u32[]{:S(2)}) async-start(bf16[16,2,128]{2,1,0:T(2,128)(2,1)} %bitcast.1), calls=%async_computation.1 | async-start | bytes 16384 | tf_op jit(solution)/shard_map/all_to_all | solution.py:59
  20.3 2.3 %reshape.47 = f32[16,2,16384]{2,1,0:T(2,128)} reshape(f32[32,16384]{1,0:T(8,128)S(1)} %fusion.2) | data formatting | bytes 4194304 | tf_op jit(solution)/shard_map/reshape | solution.py:16
  22.6 1.9 %div.49 = f32[32,128,128]{2,1,0:T(8,128)} broadcast(f32[32,128]{1,0:T(8,128)S(1)} %get-tuple-element.5), dimensions={0,1} | broadcast | bytes 2113536 | tf_op jit(solution)/shard_map/div | solution.py:18
  24.6 0.0 copy-start.1
  24.6 3.6 %div.50 = f32[16,2,16384]{2,1,0:T(2,128)} reshape(f32[32,128,128]{2,1,0:T(8,128)} %div.49) | data formatting | bytes 4194304 | tf_op jit(solution)/shard_map/div | solution.py:18
  28.2 0.0 copy-done.1
  28.2 3.7 %divide_convert_fusion = bf16[16,2,16384]{2,1,0:T(2,128)(2,1)} fusion(f32[16,2,16384]{2,1,0:T(2,128)S(1)} %copy-done.1, f32[16,2,16384]{2,1,0:T(2,128)} %div.50), kind=kLoop, calls=%fused_computation.6 | loop fusion | flops 1048576 | bytes 5242880 | tf_op jit(solution)/shard_map/convert_element_type | solution.py:18
  31.9 0.0 all-to-all-done.1
  31.9 6.0 %all-to-all-start = ((bf16[16,2,16384]{2,1,0:T(2,128)(2,1)}), bf16[16,2,16384]{2,1,0:T(2,128)(2,1)S(1)}, u32[]{:S(2)}, u32[]{:S(2)}) async-start(bf16[16,2,16384]{2,1,0:T(2,128)(2,1)} %divide_convert_fusion), calls=%async_computation | async-start | bytes 2097152 | tf_op jit(solution)/shard_map/all_to_all | solution.py:58
  37.9 0.0 all-gather.4.cloned.1.call-start
  38.0 2.0 %mul.57 = f32[16,2,128,128]{3,2,1,0:T(8,128)} broadcast(bf16[16,2,128]{2,1,0:T(2,128)(2,1)S(1)} %all-to-all-done.1), dimensions={0,1,2} | broadcast | bytes 2105344 | tf_op jit(solution)/shard_map/mul | solution.py:26
  39.9 2.5 %mul.58 = f32[16,2,16384]{2,1,0:T(2,128)S(1)} reshape(f32[16,2,128,128]{3,2,1,0:T(8,128)} %mul.57) | data formatting | bytes 4194304 | tf_op jit(solution)/shard_map/mul | solution.py:26
  42.4 0.0 copy-start.3
  42.5 18.4 %all-to-all-done = bf16[16,2,16384]{2,1,0:T(2,128)(2,1)S(1)} async-done(((bf16[16,2,16384]{2,1,0:T(2,128)(2,1)}), bf16[16,2,16384]{2,1,0:T(2,128)(2,1)S(1)}, u32[]{:S(2)}, u32[]{:S(2)}) %all-to-all-start) | async-done | bytes 1048608 | tf_op jit(solution)/shard_map/all_to_all | solution.py:58
  60.8 1.2 %multiply_reduce_fusion.1 = f32[2,16384]{1,0:T(2,128)S(1)} fusion(f32[16,2,16384]{2,1,0:T(2,128)S(1)} %mul.58, bf16[16,2,16384]{2,1,0:T(2,128)(2,1)S(1)} %all-to-all-done), kind=kLoop, calls=%fused_computation.4 | loop fusion | flops 1540096 | bytes 3276800 | tf_op jit(solution)/shard_map/reduce_sum | solution.py:27
  62.0 0.0 copy-done.3
  62.0 0.1 abs_bitcast_fusion.1
  62.1 0.1 bitcast_reduce_fusion.1
  62.3 0.0 copy-start.5
  62.3 0.1 broadcast_bitcast_fusion
  62.4 0.8 fusion.5
  63.2 0.0 all-gather.4.cloned.1.call-update
  63.2 22.5 %all-gather.1 = bf16[16,2,128]{2,1,0:T(2,128)(2,1)S(1)} all-gather(bf16[1,2,128]{2,1,0:T(2,128)(2,1)S(1)} %get-tuple-element.3), channel_id=1, replica_groups=mesh['replica'=2,'tp'=16] {'tp'}, dimensions={0}, use_global_device_ids=true | all-gather | bytes 8704 | tf_op jit(solution)/shard_map/all_gather | solution.py:68
  85.7 17.8 %all-gather.4.cloned.1.call-done = bf16[16,2,16384]{2,1,0:T(2,128)(2,1)} async-done(((bf16[1,2,16384]{2,1,0:T(2,128)(2,1)}), bf16[16,2,16384]{2,1,0:T(2,128)(2,1)}) %all-gather.4.cloned.1.call-update) | async-done | bytes 1048592 | tf_op jit(solution)/shard_map/all_gather | solution.py:67
  103.5 1.4 %reshape.52 = f32[32,16384]{1,0:T(8,128)S(1)} reshape(bf16[16,2,16384]{2,1,0:T(2,128)(2,1)} %all-gather.4.cloned.1.call-done) | data formatting | bytes 3145728 | tf_op jit(solution)/shard_map/convert_element_type | solution.py:72
  104.8 0.0 copy-start.4
  104.8 0.6 mul.60
  105.4 0.0 copy-done.5
  105.4 0.0 copy-start.2
  105.5 1.4 %multiply_reduce_fusion = f32[32]{0:T(128)S(1)} fusion(f32[32,16384]{1,0:T(8,128)S(1)} %reshape.52, f32[4,8,128,128]{3,2,1,0:T(8,128)S(1)} %bitcast.37), kind=kLoop, calls=%fused_computation.3 | loop fusion | flops 1572832 | bytes 4194432 | tf_op jit(solution)/shard_map/reduce_sum | solution.py:74
  106.9 0.0 copy-done.4
  106.9 0.8 copy-done.2
  107.6 2.3 %convolution_convert_fusion = bf16[32,128]{1,0:T(8,128)(2,1)} fusion(bf16[16384,128]{1,0:T(8,128)(2,1)S(1)} %copy-done.2, f32[16384]{0:T(1024)S(1)} %copy-done.4, f32[32]{0:T(128)S(1)} %add_rsqrt_fusion, f32[32,16384]{1,0:T(8,128)S(1)} %reshape.52, f32[4,8,128,128]{3,2,1,0:T(8,128)S(1)} %bitcast.38), kind=kOutput, calls=%fused_computation.10 | convolution fusion | flops 136318976 | bytes 8462464 | tf_op jit(solution)/shard_map/dot_general | solution.py:76
  (3 shorter events, 0.0 us)
Async XLA Ops:
  7.2 0.9 copy-start
  12.9 19.0 %all-to-all-start.1 = ((bf16[16,2,128]{2,1,0:T(2,128)(2,1)}), bf16[16,2,128]{2,1,0:T(2,128)(2,1)S(1)}, u32[]{:S(2)}, u32[]{:S(2)}) async-start(bf16[16,2,128]{2,1,0:T(2,128)(2,1)} %bitcast.1), calls=%async_computation.1 | async-start | bytes 16384 | tf_op jit(solution)/shard_map/all_to_all | solution.py:59
  24.6 3.6 %copy-start.1 = (f32[16,2,16384]{2,1,0:T(2,128)S(1)}, f32[16,2,16384]{2,1,0:T(2,128)}, u32[]{:S(2)}) copy-start(f32[16,2,16384]{2,1,0:T(2,128)} %reshape.47) | copy-start | bytes 6291460
  31.9 29.0 %all-to-all-start = ((bf16[16,2,16384]{2,1,0:T(2,128)(2,1)}), bf16[16,2,16384]{2,1,0:T(2,128)(2,1)S(1)}, u32[]{:S(2)}, u32[]{:S(2)}) async-start(bf16[16,2,16384]{2,1,0:T(2,128)(2,1)} %divide_convert_fusion), calls=%async_computation | async-start | bytes 2097152 | tf_op jit(solution)/shard_map/all_to_all | solution.py:58
  37.9 65.5 %all-gather.4.cloned.1.call-start = ((), (), s32[]{:S(2)}) async-start(), calls=%async_computation.2 | async-start | bytes 1114112 | tf_op jit(solution)/shard_map/all_gather | solution.py:67
  42.4 19.6 %copy-start.3 = (bf16[2,16384]{1,0:T(2,128)(2,1)S(1)}, bf16[2,16384]{1,0:T(2,128)(2,1)}, u32[]{:S(2)}) copy-start(bf16[2,16384]{1,0:T(2,128)(2,1)} %param.7) | copy-start | bytes 196612
  62.3 43.2 %copy-start.5 = (f32[2,128]{1,0:T(2,128)}, f32[2,128]{1,0:T(2,128)S(1)}, u32[]{:S(2)}) copy-start(f32[2,128]{1,0:T(2,128)S(1)} %get-tuple-element.4) | copy-start | bytes 3076
  104.8 2.0 %copy-start.4 = (f32[16384]{0:T(1024)S(1)}, f32[16384]{0:T(1024)}, u32[]{:S(2)}) copy-start(f32[16384]{0:T(1024)} %param.12) | copy-start | bytes 196612
  105.4 2.2 %copy-start.2 = (bf16[16384,128]{1,0:T(8,128)(2,1)S(1)}, bf16[16384,128]{1,0:T(8,128)(2,1)}, u32[]{:S(2)}) copy-start(bf16[16384,128]{1,0:T(8,128)(2,1)} %param.13) | copy-start | bytes 12582916
Sparse Core Ops, SparseCore 0:
  63.3 40.1 all-gather.3
where the time goes:
time: 117 us
  waiting for transfers between devices  36.2 us (31%)
  blocking collectives  22.5 us (19%)
  local copies, waits for them, and re-layouts  15.6 us (13%)
  between operations  14.2 us (12%)
  starting transfers between devices  13.4 us (11%)
  other arithmetic  8.67 us (7%)
  matrix products  6.18 us (5%)
    all_gather x1, blocking collectives, on_device(): lax.all_gather(stream_scales.astype(jnp.bfloat16), 'tp', axis=0, tiled=True)  22.5 us
    all_to_all x1, waiting for transfers between devices, on_device(): lax.all_to_all(sent_codes, 'tp', split_axis=0, concat_axis=0, tiled=True)  18.4 us
    all_gather x1, waiting for transfers between devices, on_device(): lax.all_gather(stream_codes, 'tp', axis=0, tiled=True)  17.8 us
    all_to_all x1, starting transfers between devices, on_device(): lax.all_to_all(sent_peaks.astype(jnp.bfloat16), 'tp', split_axis=0, conca...  7.38 us
    all_to_all x1, starting transfers between devices, on_device(): lax.all_to_all(sent_codes, 'tp', split_axis=0, concat_axis=0, tiled=True)  6.01 us
    div x2, local copies, waits for them, and re-layouts, encode(): grouped / peaks[:, :, None]  5.58 us
    mul x2, local copies, waits for them, and re-layouts, decode_sum(): scaled = grouped * peaks[:, :, :, None]  4.48 us
    convert_element_type x2, other arithmetic, encode(): (grouped / peaks[:, :, None]).astype(jnp.bfloat16).reshape(tok_rows, width)  4.47 us
  transfers between devices with their start and end apart: 3, of which 2 were waited for; matrix products, arithmetic and copies ran while one was open for 14% of the time, Pallas kernels for 0%

commit v1 on v0

v1 whole, which is shorter than its diff:
```python
import jax
import jax.numpy as jnp
from jax import lax
from jax.sharding import PartitionSpec as P

HD = 128
QB = 128
EPS = 1e-06


def on_device(residual, queries, key_rows, value_rows, out_weight, norm_gain, q_weight):
    n = lax.axis_size("tp")
    device = lax.axis_index("tp")
    core = device % 2
    chips = n // 2
    tokens = queries.shape[0]
    local = residual.shape[0]
    half = tokens // 2
    D = residual.shape[1]
    heads = queries.shape[1] // HD
    group = heads * n // (key_rows.shape[1] // HD)
    swap = [(i, i ^ 1) for i in range(n)]
    same_core = [[2 * i + c for i in range(chips)] for c in range(2)]

    row = jnp.arange(tokens)
    side = jnp.where(row < half, 1 - core, core)
    in_half = row % half
    token = in_half // local * (2 * local) + side * local + in_half % local
    pick = (token[:, None] == row[None, :]).astype(jnp.bfloat16)
    queries = jnp.dot(pick, queries, preferred_element_type=jnp.float32).astype(jnp.bfloat16)
    visible = row[None, :] <= token[:, None]
    contexts = []
    for h in range(heads):
        kv_start = (device * heads + h) // group * HD
        key_head = lax.dynamic_slice_in_dim(key_rows, kv_start, HD, 1)
        value_head = lax.dynamic_slice_in_dim(value_rows, kv_start, HD, 1)
        scores = lax.dot_general(
            queries[:, h * HD : (h + 1) * HD],
            key_head,
            (((1,), (1,)), ((), ())),
            preferred_element_type=jnp.float32,
        ) / jnp.sqrt(jnp.float32(HD))
        scores = jnp.where(visible, scores, jnp.float32(-1e30))
        probs = jax.nn.softmax(scores, axis=-1).astype(jnp.bfloat16)
        contexts.append(
            jnp.dot(probs, value_head, preferred_element_type=jnp.float32).astype(jnp.bfloat16)
        )
    context = jnp.concatenate(contexts, axis=1)
    sent = jnp.dot(context[:half], out_weight, preferred_element_type=jnp.float32)
    got = lax.ppermute(sent.astype(jnp.bfloat16), "tp", swap)
    kept = jnp.dot(context[half:], out_weight, preferred_element_type=jnp.float32)
    chip_sum = (kept + got.astype(jnp.float32)).astype(jnp.bfloat16)
    parts = lax.all_to_all(
        chip_sum.reshape(chips, local, D),
        "tp",
        split_axis=0,
        concat_axis=0,
        axis_index_groups=same_core,
        tiled=True,
    )
    summed = jnp.sum(parts.astype(jnp.float32), axis=0)
    stream = residual.astype(jnp.float32) + summed
    grouped = stream.reshape(local, D // QB, QB)
    scales = jnp.max(jnp.abs(grouped), axis=2) + EPS
    codes = (grouped / scales[:, :, None]).astype(jnp.bfloat16)
    decoded = (codes.astype(jnp.float32) * scales[:, :, None]).reshape(local, D)
    mean_sq = jnp.mean(decoded * decoded, axis=1, keepdims=True)
    normed = (decoded * lax.rsqrt(mean_sq + 1e-05) * norm_gain[None, :]).astype(jnp.bfloat16)
    mine = lax.all_to_all(
        jnp.broadcast_to(normed[None], (chips, local, D)),
        "tp",
        split_axis=0,
        concat_axis=0,
        axis_index_groups=same_core,
        tiled=True,
    ).reshape(half, D)
    other = lax.ppermute(mine, "tp", swap)
    out_mine = jnp.dot(mine, q_weight, preferred_element_type=jnp.float32).astype(jnp.bfloat16)
    out_other = jnp.dot(other, q_weight, preferred_element_type=jnp.float32).astype(jnp.bfloat16)
    out_mine = out_mine.reshape(chips, 1, local, -1)
    out_other = out_other.reshape(chips, 1, local, -1)
    first = jnp.where(core == 0, out_mine, out_other)
    second = jnp.where(core == 0, out_other, out_mine)
    next_queries = jnp.concatenate([first, second], axis=1).reshape(tokens, -1)
    return (codes.reshape(local, D), scales, next_queries)


def solution(mesh):
    in_specs = (
        P(("replica", "tp"), None),
        P("replica", "tp"),
        P("replica", None),
        P("replica", None),
        P("tp", None),
        P(),
        P(None, "tp"),
    )
    out_specs = (P(("replica", "tp"), None), P(("replica", "tp"), None), P("replica", "tp"))
    return jax.shard_map(
        on_device, mesh=mesh, in_specs=in_specs, out_specs=out_specs, check_vma=False
    )
```

time: 117 us -> 54.3 us (0.46)
  waiting for transfers between devices: 36.2 us -> 1.54 us
  blocking collectives: 22.5 us -> 39.4 us
  local copies, waits for them, and re-layouts: 15.6 us -> 1.96 us
  between operations: 14.2 us -> 0.88 us
  starting transfers between devices: 13.4 us -> 0.59 us
  other arithmetic: 8.67 us -> 1.19 us
  matrix products: 6.18 us -> 8.56 us
    all_to_all x0 -> x2, blocking collectives: none -> 39.4 us  [the longest x1 21.8 us: on_device(): lax.all_to_all(chip_sum.reshape(chips, local, D), 'tp', split_axis=0, con...]
    all_gather x1 -> x0, blocking collectives: 22.5 us -> none  [on_device(): lax.all_gather(stream_scales.astype(jnp.bfloat16), 'tp', axis=0, tiled=True)]
    all_to_all x2 -> x0, waiting for transfers between devices: 18.4 us -> none  [the longest x1 18.4 us: on_device(): lax.all_to_all(sent_codes, 'tp', split_axis=0, concat_axis=0, tiled=True)]
    all_gather x1 -> x0, waiting for transfers between devices: 17.8 us -> none  [on_device(): lax.all_gather(stream_codes, 'tp', axis=0, tiled=True)]
    all_to_all x2 -> x0, starting transfers between devices: 13.4 us -> none  [the longest x1 7.38 us: on_device(): lax.all_to_all(sent_peaks.astype(jnp.bfloat16), 'tp', split_axis=0, conca...]
    div x2 -> x0, local copies, waits for them, and re-layouts: 5.58 us -> none  [encode(): grouped / peaks[:, :, None]]
    mul x3 -> x0, local copies, waits for them, and re-layouts: 5.08 us -> none  [the longest x2 4.48 us: decode_sum(): scaled = grouped * peaks[:, :, :, None]]
    convert_element_type x2 -> x1, other arithmetic: 4.47 us -> 0.18 us  [on_device(): (decoded * lax.rsqrt(mean_sq + 1e-05) * norm_gain[None, :]).astype(jnp.bf...]
  transfers between devices with their start and end apart: 3 -> 2, of which waited for: 2 -> 1; matrix products, arithmetic and copies ran while one was open for 14% -> 6% of each run, Pallas kernels for 0% -> 0%
where the time goes in v1:
time: 54.3 us; the launch traced here: 54.1 us
  blocking collectives  39.4 us (73%)
  matrix products  8.56 us (16%)
  local copies, waits for them, and re-layouts  1.96 us (4%)
  waiting for transfers between devices  1.54 us (3%)
  other arithmetic  1.19 us (2%)
  between operations  0.88 us (2%)
  starting transfers between devices  0.59 us (1%)
    all_to_all x1, blocking collectives, on_device(): lax.all_to_all(chip_sum.reshape(chips, local, D), 'tp', split_axis=0, con...  21.8 us
    all_to_all x1, blocking collectives, on_device(): lax.all_to_all(jnp.broadcast_to(normed[None], (chips, local, D)), 'tp', s...  17.6 us
    dot_general x1, matrix products, on_device(): jnp.dot(mine, q_weight, preferred_element_type=jnp.float32)  3.01 us
    dot_general x1, matrix products, on_device(): jnp.dot(context[:half], out_weight, preferred_element_type=jnp.float32)  2.99 us
    ppermute x1, waiting for transfers between devices, on_device(): got = lax.ppermute(sent.astype(jnp.bfloat16), 'tp', swap)  1.54 us
  transfers between devices with their start and end apart: 2, of which 1 were waited for; matrix products, arithmetic and copies ran while one was open for 6% of the time, Pallas kernels for 0%

profile of v1, /device:TPU:0, one launch (start us, length us, event | category | flops | bytes accessed | tf_op | source)
XLA Modules:
  0.0 54.1 jit_solution(14782172439376379920)
XLA Ops:
  0.6 0.0 copy-start
  0.7 1.0 %fusion.20 = (f32[32]{0:T(128)S(1)}, f32[32,32]{0,1:T(8,128)S(1)}) fusion(bf16[32,1024]{1,0:T(8,128)(2,1)} %param.9, s32[]{:T(128)S(6)} %select_n.96, bf16[32,128]{1,0:T(8,128)(2,1)} %param.8, s32[32]{0:T(128)S(1)} %fusion.14), kind=kOutput, calls=%fused_computation.48 | convolution fusion | flops 533472 | bytes 21636 | tf_op jit(solution)/shard_map/dot_general | solution.py:37
  1.7 0.0 copy-start.1
  1.8 0.0 copy-done
  1.8 0.2 convolution_convert_fusion.1
  2.0 3.0 %convolution_convert_fusion = bf16[16,16384]{1,0:T(8,128)(2,1)S(1)} fusion(bf16[128,16384]{1,0:T(8,128)(2,1)} %param.11, bf16[32,128]{1,0:T(8,128)(2,1)S(1)} %convolution_convert_fusion.1), kind=kOutput, calls=%fused_computation | convolution fusion | flops 67371008 | bytes 4722688 | tf_op jit(solution)/shard_map/dot_general | solution.py:49
  5.0 0.0 copy-start.3
  5.0 0.0 copy-start.5
  5.0 0.5 collective-permute-start
  5.5 1.5 %collective-permute-done = bf16[16,16384]{1,0:T(8,128)(2,1)S(1)} collective-permute-done((bf16[16,16384]{1,0:T(8,128)(2,1)S(1)}, bf16[16,16384]{1,0:T(8,128)(2,1)S(1)}, u32[]{:S(2)}, u32[]{:S(2)}) %collective-permute-start) | collective-permute-done | bytes 524320 | tf_op jit(solution)/shard_map/ppermute | solution.py:50
  7.0 0.0 copy-done.1
  7.0 0.7 %add_convert_fusion = bf16[16,16384]{1,0:T(8,128)(2,1)S(1)} fusion(bf16[16,16384]{1,0:T(8,128)(2,1)S(1)} %collective-permute-done, bf16[128,16384]{1,0:T(8,128)(2,1)S(1)} %copy-done.1, bf16[32,128]{1,0:T(8,128)(2,1)S(1)} %convolution_convert_fusion.1), kind=kOutput, calls=%fused_computation.8 | convolution fusion | flops 67895296 | bytes 5246976 | tf_op jit(solution)/shard_map/dot_general | solution.py:51
  7.7 0.3 reshape.125
  8.1 21.8 %all_to_all.10 = bf16[8,2,16384]{2,1,0:T(2,128)(2,1)S(1)} all-to-all(bf16[8,2,16384]{2,1,0:T(2,128)(2,1)S(1)} %reshape.125), channel_id=1, replica_groups={{0,2,4,6,8,10,12,14},{1,3,5,7,9,11,13,15},{16,18,20,22,24,26,28,30},{17..., dimensions={0} | all-to-all | bytes 1048576 | tf_op jit(solution)/shard_map/all_to_all | solution.py:53
  29.8 0.5 convert_reduce_fusion
  30.3 0.0 copy-done.3
  30.3 0.1 abs_bitcast_fusion
  30.4 0.1 bitcast_reduce_fusion
  30.5 0.0 copy-start.6
  30.6 0.1 broadcast_bitcast_fusion
  30.7 0.3 multiply_reduce_fusion
  30.9 0.0 copy-start.4
  31.0 0.0 copy-done.5
  31.0 0.2 multiply_convert_fusion
  31.2 0.3 broadcast_in_dim.17
  31.4 17.6 %all_to_all.11 = bf16[8,2,16384]{2,1,0:T(2,128)(2,1)S(1)} all-to-all(bf16[8,2,16384]{2,1,0:T(2,128)(2,1)S(1)} %broadcast_in_dim.17), channel_id=1, replica_groups={{0,2,4,6,8,10,12,14},{1,3,5,7,9,11,13,15},{16,18,20,22,24,26,28,30},{17..., dimensions={0} | all-to-all | bytes 1048576 | tf_op jit(solution)/shard_map/all_to_all | solution.py:69
  49.0 0.2 reshape.126
  49.2 0.1 collective-permute-start.1
  49.3 0.0 copy-start.2
  49.3 3.0 %convolution_convert_fusion.4 = bf16[16,128]{1,0:T(8,128)(2,1)S(1)} fusion(bf16[16,16384]{1,0:T(8,128)(2,1)S(1)} %reshape.126, bf16[16384,128]{1,0:T(8,128)(2,1)} %param.13), kind=kOutput, calls=%fused_computation.6 | convolution fusion | flops 67110912 | bytes 4722688 | tf_op jit(solution)/shard_map/dot_general | solution.py:78
  52.3 0.0 collective-permute-done.1
  52.3 0.4 copy-done.2
  52.7 0.7 %broadcast_select_fusion.1 = (bf16[16,128]{1,0:T(8,128)(2,1)S(1)}, bf16[16,128]{1,0:T(8,128)(2,1)S(1)}) fusion(bf16[16,128]{1,0:T(8,128)(2,1)S(1)} %convolution_convert_fusion.4, pred[]{:T(512)S(6)} %eq.10, bf16[16,16384]{1,0:T(8,128)(2,1)S(1)} %collective-permute-done.1, bf16[16384,128]{1,0:T(8,128)(2,1)S(1)} %copy-done.2), kind=kOutput, calls=%fused_computation.33 | convolution fusion | flops 67115008 | bytes 4730881 | tf_op jit(solution)/shard_map/dot_general | solution.py:79
  53.4 0.0 copy-done.6
  53.4 0.0 copy-done.4
  53.5 0.6 %copy.10 = bf16[8,2,2,128]{3,2,1,0:T(2,128)(2,1)} copy(bf16[8,2,2,128]{3,2,0,1:T(2,128)(2,1)S(1)} %pad_maximum_fusion) | data formatting | bytes 16384 | tf_op jit(solution)/shard_map/concatenate | solution.py:84
  (5 shorter events, 0.1 us)
Async XLA Ops:
  0.6 1.2 %copy-start = (bf16[32,1024]{1,0:T(8,128)(2,1)S(1)}, bf16[32,1024]{1,0:T(8,128)(2,1)}, u32[]{:S(2)}) copy-start(bf16[32,1024]{1,0:T(8,128)(2,1)} %param.10) | copy-start | bytes 196612
  1.7 5.3 %copy-start.1 = (bf16[128,16384]{1,0:T(8,128)(2,1)S(1)}, bf16[128,16384]{1,0:T(8,128)(2,1)}, u32[]{:S(2)}) copy-start(bf16[128,16384]{1,0:T(8,128)(2,1)} %param.11) | copy-start | bytes 12582916
  5.0 25.3 %copy-start.3 = (bf16[2,16384]{1,0:T(2,128)(2,1)S(1)}, bf16[2,16384]{1,0:T(2,128)(2,1)}, u32[]{:S(2)}) copy-start(bf16[2,16384]{1,0:T(2,128)(2,1)} %param.7) | copy-start | bytes 196612
  5.0 26.0 %copy-start.5 = (f32[16384]{0:T(1024)S(1)}, f32[16384]{0:T(1024)}, u32[]{:S(2)}) copy-start(f32[16384]{0:T(1024)} %param.12) | copy-start | bytes 196612
  5.0 2.1 %collective-permute-start = (bf16[16,16384]{1,0:T(8,128)(2,1)S(1)}, bf16[16,16384]{1,0:T(8,128)(2,1)S(1)}, u32[]{:S(2)}, u32[]{:S(2)}) collective-permute-start(bf16[16,16384]{1,0:T(8,128)(2,1)S(1)} %convolution_convert_fusion), channel_id=1, source_target_pairs={{0,1},{1,0},{2,3},{3,2},{4,5},{5,4},{6,7},{7,6},{8,9},{9,8},{10,11... | collective-permute-start | bytes 1572872 | tf_op jit(solution)/shard_map/ppermute | solution.py:50
  30.5 22.9 %copy-start.6 = (f32[2,128]{1,0:T(2,128)}, f32[2,128]{1,0:T(2,128)S(1)}, u32[]{:S(2)}) copy-start(f32[2,128]{1,0:T(2,128)S(1)} %broadcast_add_fusion) | copy-start | bytes 3076
  30.9 22.5 %copy-start.4 = (bf16[2,16384]{1,0:T(2,128)(2,1)}, bf16[2,16384]{1,0:T(2,128)(2,1)S(1)}, u32[]{:S(2)}) copy-start(bf16[2,16384]{1,0:T(2,128)(2,1)S(1)} %get-tuple-element.4) | copy-start | bytes 196612
  49.2 3.1 %collective-permute-start.1 = (bf16[16,16384]{1,0:T(8,128)(2,1)S(1)}, bf16[16,16384]{1,0:T(8,128)(2,1)S(1)}, u32[]{:S(2)}, u32[]{:S(2)}) collective-permute-start(bf16[16,16384]{1,0:T(8,128)(2,1)S(1)} %reshape.126), channel_id=1, source_target_pairs={{0,1},{1,0},{2,3},{3,2},{4,5},{5,4},{6,7},{7,6},{8,9},{9,8},{10,11... | collective-permute-start | bytes 1572872 | tf_op jit(solution)/shard_map/ppermute | solution.py:77
  49.3 3.5 %copy-start.2 = (bf16[16384,128]{1,0:T(8,128)(2,1)S(1)}, bf16[16384,128]{1,0:T(8,128)(2,1)}, u32[]{:S(2)}) copy-start(bf16[16384,128]{1,0:T(8,128)(2,1)} %param.13) | copy-start | bytes 12582916

commit v2 on v1

v2 whole, which is shorter than its diff:
```python
import jax
import jax.numpy as jnp
from jax import lax
from jax.sharding import PartitionSpec as P

HD = 128
QB = 128
EPS = 1e-06
F32 = jnp.float32
BF16 = jnp.bfloat16


def on_device(residual, queries, key_rows, value_rows, out_weight, norm_gain, q_weight):
    n = lax.axis_size("tp")
    device = lax.axis_index("tp")
    tokens = queries.shape[0]
    local = residual.shape[0]
    D = residual.shape[1]
    far = n // 4
    heads = queries.shape[1] // HD
    group = heads * n // (key_rows.shape[1] // HD)

    def swap(x, distance):
        return lax.ppermute(x, "tp", [(i, i ^ distance) for i in range(n)])

    row = jnp.arange(tokens)
    block = row // local
    distance = block % far * 4 + block // far % 2 * 2 + block // (2 * far)
    token = (device ^ distance) * local + row % local
    pick = (token[:, None] == row[None, :]).astype(BF16)
    queries = jnp.dot(pick, queries, preferred_element_type=F32).astype(BF16)
    visible = row[None, :] <= token[:, None]
    contexts = []
    for h in range(heads):
        kv_start = (device * heads + h) // group * HD
        key_head = lax.dynamic_slice_in_dim(key_rows, kv_start, HD, 1)
        value_head = lax.dynamic_slice_in_dim(value_rows, kv_start, HD, 1)
        scores = lax.dot_general(
            queries[:, h * HD : (h + 1) * HD],
            key_head,
            (((1,), (1,)), ((), ())),
            preferred_element_type=F32,
        ) / jnp.sqrt(F32(HD))
        scores = jnp.where(visible, scores, F32(-1e30))
        probs = jax.nn.softmax(scores, axis=-1).astype(BF16)
        contexts.append(jnp.dot(probs, value_head, preferred_element_type=F32).astype(BF16))
    context = jnp.concatenate(contexts, axis=1)
    half, quarter = tokens // 2, tokens // 4
    sent = jnp.dot(context[half:], out_weight, preferred_element_type=F32)
    got = swap(sent.astype(BF16), 1)
    kept = jnp.dot(context[:half], out_weight, preferred_element_type=F32)
    chip_sum = kept + got.astype(F32)
    got = swap(chip_sum[quarter:].astype(BF16), 2)
    pair_sum = chip_sum[:quarter] + got.astype(F32)
    stream = residual.astype(F32) + pair_sum[:local]
    arrived = [
        swap(pair_sum[f * local : (f + 1) * local].astype(BF16), 4 * f) for f in range(1, far)
    ]
    for piece in arrived:
        stream = stream + piece.astype(F32)
    grouped = stream.reshape(local, D // QB, QB)
    scales = jnp.max(jnp.abs(grouped), axis=2) + EPS
    codes = (grouped / scales[:, :, None]).astype(BF16)
    decoded = (codes.astype(F32) * scales[:, :, None]).reshape(local, D)
    mean_sq = jnp.mean(decoded * decoded, axis=1, keepdims=True)
    normed = (decoded * lax.rsqrt(mean_sq + 1e-05) * norm_gain[None, :]).astype(BF16)
    near = jnp.concatenate([normed] + [swap(normed, 4 * f) for f in range(1, far)], axis=0)
    mine = jnp.concatenate([near, swap(near, 2)], axis=0)
    other = swap(mine, 1)
    out_mine = jnp.dot(mine, q_weight, preferred_element_type=F32).astype(BF16)
    out_other = jnp.dot(other, q_weight, preferred_element_type=F32).astype(BF16)
    found = jnp.concatenate([out_mine, out_other], axis=0)
    next_queries = lax.dot_general(
        pick, found, (((0,), (0,)), ((), ())), preferred_element_type=F32
    ).astype(BF16)
    return (codes.reshape(local, D), scales, next_queries)


def solution(mesh):
    in_specs = (
        P(("replica", "tp"), None),
        P("replica", "tp"),
        P("replica", None),
        P("replica", None),
        P("tp", None),
        P(),
        P(None, "tp"),
    )
    out_specs = (P(("replica", "tp"), None), P(("replica", "tp"), None), P("replica", "tp"))
    return jax.shard_map(
        on_device, mesh=mesh, in_specs=in_specs, out_specs=out_specs, check_vma=False
    )
```

time: 54.3 us -> 49.5 us (0.912)
  blocking collectives: 39.4 us -> 0 us
  waiting for transfers between devices: 1.54 us -> 22.9 us
  starting transfers between devices: 0.59 us -> 14 us
  local copies, waits for them, and re-layouts: 1.96 us -> 1.19 us
  matrix products: 8.56 us -> 9.28 us
    all_to_all x2 -> x0, blocking collectives: 39.4 us -> none  [the longest x1 21.8 us: on_device(): lax.all_to_all(chip_sum.reshape(chips, local, D), 'tp', split_axis=0, con...]
    ppermute x2 -> x10, waiting for transfers between devices: 1.54 us -> 22.9 us  [swap(): return lax.ppermute(x, 'tp', [(i, i ^ distance) for i in range(n)])]
    ppermute x2 -> x10, starting transfers between devices: 0.59 us -> 14 us  [swap(): return lax.ppermute(x, 'tp', [(i, i ^ distance) for i in range(n)])]
    dot_general x5 -> x6, matrix products: 7.52 us -> 8.24 us  [the longest x1 3.01 us: on_device(): out_mine = jnp.dot(mine, q_weight, preferred_element_type=F32).astype(BF16)]
  transfers between devices with their start and end apart: 2 -> 10, of which waited for: 1 -> 7; matrix products, arithmetic and copies ran while one was open for 6% -> 6% of each run, Pallas kernels for 0% -> 0%
where the time goes in v2:
time: 49.5 us; the launch traced here: 49.4 us
  waiting for transfers between devices  22.9 us (46%)
  starting transfers between devices  14 us (28%)
  matrix products  9.28 us (19%)
  local copies, waits for them, and re-layouts  1.19 us (2%)
  other arithmetic  1.15 us (2%)
  between operations  0.84 us (2%)
    ppermute x10, waiting for transfers between devices, swap(): return lax.ppermute(x, 'tp', [(i, i ^ distance) for i in range(n)])  22.9 us
    ppermute x10, starting transfers between devices, swap(): return lax.ppermute(x, 'tp', [(i, i ^ distance) for i in range(n)])  14 us
    dot_general x1, matrix products, on_device(): out_mine = jnp.dot(mine, q_weight, preferred_element_type=F32).astype(BF16)  3.01 us
    dot_general x1, matrix products, on_device(): sent = jnp.dot(context[half:], out_weight, preferred_element_type=F32)  2.99 us
    dot_general x1, matrix products, on_device(): lax.dot_general(queries[:, h * HD:(h + 1) * HD], key_head, (((1,), (1,)),...  1.04 us
  transfers between devices with their start and end apart: 10, of which 7 were waited for; matrix products, arithmetic and copies ran while one was open for 6% of the time, Pallas kernels for 0%

profile of v2, /device:TPU:0, one launch (start us, length us, event | category | flops | bytes accessed | tf_op | source)
XLA Modules:
  0.0 49.4 jit_solution(17044395159375301408)
XLA Ops:
  0.6 0.0 copy-start
  0.7 1.0 %fusion.34 = (f32[32]{0:T(128)S(1)}, f32[32,32]{0,1:T(8,128)S(1)}) fusion(bf16[32,1024]{1,0:T(8,128)(2,1)} %param.9, s32[]{:T(128)S(6)} %select_n.69, bf16[32,128]{1,0:T(8,128)(2,1)} %param.8, s32[32]{0:T(128)S(1)} %fusion.21), kind=kOutput, calls=%fused_computation.70 | convolution fusion | flops 533472 | bytes 21636 | tf_op jit(solution)/shard_map/dot_general | solution.py:38
  1.7 0.0 copy-start.1
  1.8 0.0 copy-done
  1.8 0.2 convolution_convert_fusion.2
  2.0 3.0 %convolution_convert_fusion = bf16[16,16384]{1,0:T(8,128)(2,1)S(1)} fusion(bf16[128,16384]{1,0:T(8,128)(2,1)} %param.11, bf16[32,128]{1,0:T(8,128)(2,1)S(1)} %convolution_convert_fusion.2), kind=kOutput, calls=%fused_computation | convolution fusion | flops 67371008 | bytes 4722688 | tf_op jit(solution)/shard_map/dot_general | solution.py:49
  5.0 0.0 copy-start.4
  5.0 0.0 copy-start.5
  5.0 0.5 %collective-permute-start = (bf16[16,16384]{1,0:T(8,128)(2,1)S(1)}, bf16[16,16384]{1,0:T(8,128)(2,1)S(1)}, u32[]{:S(2)}, u32[]{:S(2)}) collective-permute-start(bf16[16,16384]{1,0:T(8,128)(2,1)S(1)} %convolution_convert_fusion), channel_id=1, source_target_pairs={{0,1},{1,0},{2,3},{3,2},{4,5},{5,4},{6,7},{7,6},{8,9},{9,8},{10,11... | collective-permute-start | bytes 1572872 | tf_op jit(solution)/shard_map/ppermute | solution.py:24
  5.5 1.5 %collective-permute-done = bf16[16,16384]{1,0:T(8,128)(2,1)S(1)} collective-permute-done((bf16[16,16384]{1,0:T(8,128)(2,1)S(1)}, bf16[16,16384]{1,0:T(8,128)(2,1)S(1)}, u32[]{:S(2)}, u32[]{:S(2)}) %collective-permute-start) | collective-permute-done | bytes 524320 | tf_op jit(solution)/shard_map/ppermute | solution.py:24
  7.0 0.0 copy-done.1
  7.0 0.7 %convert_add_fusion = f32[16,16384]{1,0:T(8,128)S(1)} fusion(bf16[16,16384]{1,0:T(8,128)(2,1)S(1)} %collective-permute-done, bf16[128,16384]{1,0:T(8,128)(2,1)S(1)} %copy-done.1, bf16[32,128]{1,0:T(8,128)(2,1)S(1)} %convolution_convert_fusion.2), kind=kOutput, calls=%fused_computation.8 | convolution fusion | flops 67633152 | bytes 5771264 | tf_op jit(solution)/shard_map/dot_general | solution.py:51
  7.7 3.0 %collective-permute-start.1 = (bf16[8,16384]{1,0:T(8,128)(2,1)S(1)}, bf16[8,16384]{1,0:T(8,128)(2,1)S(1)}, u32[]{:S(2)}, u32[]{:S(2)}) collective-permute-start(bf16[8,16384]{1,0:T(8,128)(2,1)S(1)} %slice.59), channel_id=1, source_target_pairs={{0,2},{1,3},{2,0},{3,1},{4,6},{5,7},{6,4},{7,5},{8,10},{9,11},{10,... | collective-permute-start | bytes 786440 | tf_op jit(solution)/shard_map/ppermute | solution.py:24
  10.7 6.6 %collective-permute-done.1 = bf16[8,16384]{1,0:T(8,128)(2,1)S(1)} collective-permute-done((bf16[8,16384]{1,0:T(8,128)(2,1)S(1)}, bf16[8,16384]{1,0:T(8,128)(2,1)S(1)}, u32[]{:S(2)}, u32[]{:S(2)}) %collective-permute-start.1) | collective-permute-done | bytes 262176 | tf_op jit(solution)/shard_map/ppermute | solution.py:24
  17.3 0.1 fusion.32
  17.4 0.2 fusion.33
  17.6 1.9 %collective-permute-start.2 = (bf16[2,16384]{1,0:T(2,128)(2,1)S(1)}, bf16[2,16384]{1,0:T(2,128)(2,1)S(1)}, u32[]{:S(2)}, u32[]{:S(2)}) collective-permute-start(bf16[2,16384]{1,0:T(2,128)(2,1)S(1)} %get-tuple-element.9), channel_id=1, source_target_pairs={{0,4},{1,5},{2,6},{3,7},{4,0},{5,1},{6,2},{7,3},{8,12},{9,13},{10,... | collective-permute-start | bytes 196616 | tf_op jit(solution)/shard_map/ppermute | solution.py:24
  19.4 2.5 %collective-permute-start.4 = (bf16[2,16384]{1,0:T(2,128)(2,1)S(1)}, bf16[2,16384]{1,0:T(2,128)(2,1)S(1)}, u32[]{:S(2)}, u32[]{:S(2)}) collective-permute-start(bf16[2,16384]{1,0:T(2,128)(2,1)S(1)} %get-tuple-element.10), channel_id=1, source_target_pairs={{0,12},{1,13},{2,14},{3,15},{4,8},{5,9},{6,10},{7,11},{8,4},{9,5},... | collective-permute-start | bytes 196616 | tf_op jit(solution)/shard_map/ppermute | solution.py:24
  21.9 0.1 collective-permute-start.3
  22.0 0.0 collective-permute-done.2
  22.0 3.7 %collective-permute-done.4 = bf16[2,16384]{1,0:T(2,128)(2,1)S(1)} collective-permute-done((bf16[2,16384]{1,0:T(2,128)(2,1)S(1)}, bf16[2,16384]{1,0:T(2,128)(2,1)S(1)}, u32[]{:S(2)}, u32[]{:S(2)}) %collective-permute-start.4) | collective-permute-done | bytes 65568 | tf_op jit(solution)/shard_map/ppermute | solution.py:24
  25.8 2.1 %collective-permute-done.3 = bf16[2,16384]{1,0:T(2,128)(2,1)S(1)} collective-permute-done((bf16[2,16384]{1,0:T(2,128)(2,1)S(1)}, bf16[2,16384]{1,0:T(2,128)(2,1)S(1)}, u32[]{:S(2)}, u32[]{:S(2)}) %collective-permute-start.3) | collective-permute-done | bytes 65568 | tf_op jit(solution)/shard_map/ppermute | solution.py:24
  27.8 0.0 copy-done.4
  27.8 0.2 abs_bitcast_fusion
  28.0 0.1 bitcast_reduce_fusion
  28.1 0.0 copy-start.6
  28.1 0.1 broadcast_bitcast_fusion
  28.2 0.3 multiply_reduce_fusion
  28.5 0.0 copy-start.3
  28.5 0.0 copy-done.5
  28.5 0.2 multiply_convert_fusion
  28.7 2.5 %collective-permute-start.7 = (bf16[2,16384]{1,0:T(2,128)(2,1)S(1)}, bf16[2,16384]{1,0:T(2,128)(2,1)S(1)}, u32[]{:S(2)}, u32[]{:S(2)}) collective-permute-start(bf16[2,16384]{1,0:T(2,128)(2,1)S(1)} %multiply_convert_fusion), channel_id=1, source_target_pairs={{0,12},{1,13},{2,14},{3,15},{4,8},{5,9},{6,10},{7,11},{8,4},{9,5},... | collective-permute-start | bytes 196616 | tf_op jit(solution)/shard_map/ppermute | solution.py:24
  31.2 0.0 collective-permute-start.6
  31.2 1.9 %collective-permute-start.5 = (bf16[2,16384]{1,0:T(2,128)(2,1)S(1)}, bf16[2,16384]{1,0:T(2,128)(2,1)S(1)}, u32[]{:S(2)}, u32[]{:S(2)}) collective-permute-start(bf16[2,16384]{1,0:T(2,128)(2,1)S(1)} %multiply_convert_fusion), channel_id=1, source_target_pairs={{0,4},{1,5},{2,6},{3,7},{4,0},{5,1},{6,2},{7,3},{8,12},{9,13},{10,... | collective-permute-start | bytes 196616 | tf_op jit(solution)/shard_map/ppermute | solution.py:24
  33.2 2.2 %collective-permute-done.7 = bf16[2,16384]{1,0:T(2,128)(2,1)S(1)} collective-permute-done((bf16[2,16384]{1,0:T(2,128)(2,1)S(1)}, bf16[2,16384]{1,0:T(2,128)(2,1)S(1)}, u32[]{:S(2)}, u32[]{:S(2)}) %collective-permute-start.7) | collective-permute-done | bytes 65568 | tf_op jit(solution)/shard_map/ppermute | solution.py:24
  35.4 1.5 %collective-permute-done.6 = bf16[2,16384]{1,0:T(2,128)(2,1)S(1)} collective-permute-done((bf16[2,16384]{1,0:T(2,128)(2,1)S(1)}, bf16[2,16384]{1,0:T(2,128)(2,1)S(1)}, u32[]{:S(2)}, u32[]{:S(2)}) %collective-permute-start.6) | collective-permute-done | bytes 65568 | tf_op jit(solution)/shard_map/ppermute | solution.py:24
  36.9 0.0 collective-permute-done.5
  36.9 0.3 pad_maximum_fusion
  37.2 1.6 %collective-permute-start.8 = (bf16[8,16384]{1,0:T(8,128)(2,1)S(1)}, bf16[8,16384]{1,0:T(8,128)(2,1)S(1)}, u32[]{:S(2)}, u32[]{:S(2)}) collective-permute-start(bf16[8,16384]{1,0:T(8,128)(2,1)S(1)} %pad_maximum_fusion), channel_id=1, source_target_pairs={{0,2},{1,3},{2,0},{3,1},{4,6},{5,7},{6,4},{7,5},{8,10},{9,11},{10,... | collective-permute-start | bytes 786440 | tf_op jit(solution)/shard_map/ppermute | solution.py:24
  38.8 5.2 %collective-permute-done.8 = bf16[8,16384]{1,0:T(8,128)(2,1)S(1)} collective-permute-done((bf16[8,16384]{1,0:T(8,128)(2,1)S(1)}, bf16[8,16384]{1,0:T(8,128)(2,1)S(1)}, u32[]{:S(2)}, u32[]{:S(2)}) %collective-permute-start.8) | collective-permute-done | bytes 262176 | tf_op jit(solution)/shard_map/ppermute | solution.py:24
  44.0 0.5 %concatenate.11 = bf16[16,16384]{1,0:T(8,128)(2,1)S(1)} concatenate(bf16[2,16384]{1,0:T(2,128)(2,1)S(1)} %multiply_convert_fusion, bf16[2,16384]{1,0:T(2,128)(2,1)S(1)} %collective-permute-done.5, bf16[2,16384]{1,0:T(2,128)(2,1)S(1)} %collective-permute-done.6, bf16[2,16384]{1,0:T(2,128)(2,1)S(1)} %collective-permute-done.7, bf16[8,16384]{1,0:T(8,128)(2,1)S(1)} %collective-permute-done.8), dimensions={0} | concatenate | bytes 1048576 | tf_op jit(solution)/shard_map/concatenate | solution.py:68
  44.5 0.0 copy-start.2
  44.5 0.1 collective-permute-start.9
  44.6 3.0 %convolution_convert_fusion.5 = bf16[16,128]{1,0:T(8,128)(2,1)S(1)} fusion(bf16[16,16384]{1,0:T(8,128)(2,1)S(1)} %concatenate.11, bf16[16384,128]{1,0:T(8,128)(2,1)} %param.13), kind=kOutput, calls=%fused_computation.7 | convolution fusion | flops 67110912 | bytes 4722688 | tf_op jit(solution)/shard_map/dot_general | solution.py:70
  47.6 0.0 collective-permute-done.9
  47.6 0.3 copy-done.2
  48.0 0.7 %convolution_convert_fusion.4 = bf16[16,128]{1,0:T(8,128)(2,1)S(1)} fusion(bf16[16,16384]{1,0:T(8,128)(2,1)S(1)} %collective-permute-done.9, bf16[16384,128]{1,0:T(8,128)(2,1)S(1)} %copy-done.2), kind=kOutput, calls=%fused_computation.6 | convolution fusion | flops 67110912 | bytes 4722688 | tf_op jit(solution)/shard_map/dot_general | solution.py:71
  48.6 0.0 copy-done.6
  48.6 0.0 copy-done.3
  48.6 0.7 %convolution_convert_fusion.1 = bf16[32,128]{1,0:T(8,128)(2,1)} fusion(bf16[16,128]{1,0:T(8,128)(2,1)S(1)} %convolution_convert_fusion.4, bf16[16,128]{1,0:T(8,128)(2,1)S(1)} %convolution_convert_fusion.5, s32[32]{0:T(128)S(1)} %fusion.21), kind=kOutput, calls=%fused_computation.3 | convolution fusion | flops 283648 | bytes 16512 | tf_op jit(solution)/shard_map/dot_general | solution.py:73
  (5 shorter events, 0.1 us)
Async XLA Ops:
  0.6 1.1 %copy-start = (bf16[32,1024]{1,0:T(8,128)(2,1)S(1)}, bf16[32,1024]{1,0:T(8,128)(2,1)}, u32[]{:S(2)}) copy-start(bf16[32,1024]{1,0:T(8,128)(2,1)} %param.10) | copy-start | bytes 196612
  1.7 5.3 %copy-start.1 = (bf16[128,16384]{1,0:T(8,128)(2,1)S(1)}, bf16[128,16384]{1,0:T(8,128)(2,1)}, u32[]{:S(2)}) copy-start(bf16[128,16384]{1,0:T(8,128)(2,1)} %param.11) | copy-start | bytes 12582916
  5.0 22.9 %copy-start.4 = (bf16[2,16384]{1,0:T(2,128)(2,1)S(1)}, bf16[2,16384]{1,0:T(2,128)(2,1)}, u32[]{:S(2)}) copy-start(bf16[2,16384]{1,0:T(2,128)(2,1)} %param.7) | copy-start | bytes 196612
  5.0 23.6 %copy-start.5 = (f32[16384]{0:T(1024)S(1)}, f32[16384]{0:T(1024)}, u32[]{:S(2)}) copy-start(f32[16384]{0:T(1024)} %param.12) | copy-start | bytes 196612
  5.0 2.1 %collective-permute-start = (bf16[16,16384]{1,0:T(8,128)(2,1)S(1)}, bf16[16,16384]{1,0:T(8,128)(2,1)S(1)}, u32[]{:S(2)}, u32[]{:S(2)}) collective-permute-start(bf16[16,16384]{1,0:T(8,128)(2,1)S(1)} %convolution_convert_fusion), channel_id=1, source_target_pairs={{0,1},{1,0},{2,3},{3,2},{4,5},{5,4},{6,7},{7,6},{8,9},{9,8},{10,11... | collective-permute-start | bytes 1572872 | tf_op jit(solution)/shard_map/ppermute | solution.py:24
  7.7 9.6 %collective-permute-start.1 = (bf16[8,16384]{1,0:T(8,128)(2,1)S(1)}, bf16[8,16384]{1,0:T(8,128)(2,1)S(1)}, u32[]{:S(2)}, u32[]{:S(2)}) collective-permute-start(bf16[8,16384]{1,0:T(8,128)(2,1)S(1)} %slice.59), channel_id=1, source_target_pairs={{0,2},{1,3},{2,0},{3,1},{4,6},{5,7},{6,4},{7,5},{8,10},{9,11},{10,... | collective-permute-start | bytes 786440 | tf_op jit(solution)/shard_map/ppermute | solution.py:24
  17.6 4.4 %collective-permute-start.2 = (bf16[2,16384]{1,0:T(2,128)(2,1)S(1)}, bf16[2,16384]{1,0:T(2,128)(2,1)S(1)}, u32[]{:S(2)}, u32[]{:S(2)}) collective-permute-start(bf16[2,16384]{1,0:T(2,128)(2,1)S(1)} %get-tuple-element.9), channel_id=1, source_target_pairs={{0,4},{1,5},{2,6},{3,7},{4,0},{5,1},{6,2},{7,3},{8,12},{9,13},{10,... | collective-permute-start | bytes 196616 | tf_op jit(solution)/shard_map/ppermute | solution.py:24
  19.4 6.3 %collective-permute-start.4 = (bf16[2,16384]{1,0:T(2,128)(2,1)S(1)}, bf16[2,16384]{1,0:T(2,128)(2,1)S(1)}, u32[]{:S(2)}, u32[]{:S(2)}) collective-permute-start(bf16[2,16384]{1,0:T(2,128)(2,1)S(1)} %get-tuple-element.10), channel_id=1, source_target_pairs={{0,12},{1,13},{2,14},{3,15},{4,8},{5,9},{6,10},{7,11},{8,4},{9,5},... | collective-permute-start | bytes 196616 | tf_op jit(solution)/shard_map/ppermute | solution.py:24
  21.9 5.9 %collective-permute-start.3 = (bf16[2,16384]{1,0:T(2,128)(2,1)S(1)}, bf16[2,16384]{1,0:T(2,128)(2,1)S(1)}, u32[]{:S(2)}, u32[]{:S(2)}) collective-permute-start(bf16[2,16384]{1,0:T(2,128)(2,1)S(1)} %get-tuple-element.11), channel_id=1, source_target_pairs={{0,8},{1,9},{2,10},{3,11},{4,12},{5,13},{6,14},{7,15},{8,0},{9,1},... | collective-permute-start | bytes 196616 | tf_op jit(solution)/shard_map/ppermute | solution.py:24
  28.1 20.5 %copy-start.6 = (f32[2,128]{1,0:T(2,128)}, f32[2,128]{1,0:T(2,128)S(1)}, u32[]{:S(2)}) copy-start(f32[2,128]{1,0:T(2,128)S(1)} %broadcast_add_fusion) | copy-start | bytes 3076
  28.5 20.1 %copy-start.3 = (bf16[2,16384]{1,0:T(2,128)(2,1)}, bf16[2,16384]{1,0:T(2,128)(2,1)S(1)}, u32[]{:S(2)}) copy-start(bf16[2,16384]{1,0:T(2,128)(2,1)S(1)} %get-tuple-element.4) | copy-start | bytes 196612
  28.7 6.6 %collective-permute-start.7 = (bf16[2,16384]{1,0:T(2,128)(2,1)S(1)}, bf16[2,16384]{1,0:T(2,128)(2,1)S(1)}, u32[]{:S(2)}, u32[]{:S(2)}) collective-permute-start(bf16[2,16384]{1,0:T(2,128)(2,1)S(1)} %multiply_convert_fusion), channel_id=1, source_target_pairs={{0,12},{1,13},{2,14},{3,15},{4,8},{5,9},{6,10},{7,11},{8,4},{9,5},... | collective-permute-start | bytes 196616 | tf_op jit(solution)/shard_map/ppermute | solution.py:24
  31.2 5.7 %collective-permute-start.6 = (bf16[2,16384]{1,0:T(2,128)(2,1)S(1)}, bf16[2,16384]{1,0:T(2,128)(2,1)S(1)}, u32[]{:S(2)}, u32[]{:S(2)}) collective-permute-start(bf16[2,16384]{1,0:T(2,128)(2,1)S(1)} %multiply_convert_fusion), channel_id=1, source_target_pairs={{0,8},{1,9},{2,10},{3,11},{4,12},{5,13},{6,14},{7,15},{8,0},{9,1},... | collective-permute-start | bytes 196616 | tf_op jit(solution)/shard_map/ppermute | solution.py:24
  31.2 5.7 %collective-permute-start.5 = (bf16[2,16384]{1,0:T(2,128)(2,1)S(1)}, bf16[2,16384]{1,0:T(2,128)(2,1)S(1)}, u32[]{:S(2)}, u32[]{:S(2)}) collective-permute-start(bf16[2,16384]{1,0:T(2,128)(2,1)S(1)} %multiply_convert_fusion), channel_id=1, source_target_pairs={{0,4},{1,5},{2,6},{3,7},{4,0},{5,1},{6,2},{7,3},{8,12},{9,13},{10,... | collective-permute-start | bytes 196616 | tf_op jit(solution)/shard_map/ppermute | solution.py:24
  37.2 6.8 %collective-permute-start.8 = (bf16[8,16384]{1,0:T(8,128)(2,1)S(1)}, bf16[8,16384]{1,0:T(8,128)(2,1)S(1)}, u32[]{:S(2)}, u32[]{:S(2)}) collective-permute-start(bf16[8,16384]{1,0:T(8,128)(2,1)S(1)} %pad_maximum_fusion), channel_id=1, source_target_pairs={{0,2},{1,3},{2,0},{3,1},{4,6},{5,7},{6,4},{7,5},{8,10},{9,11},{10,... | collective-permute-start | bytes 786440 | tf_op jit(solution)/shard_map/ppermute | solution.py:24
  44.5 3.5 %copy-start.2 = (bf16[16384,128]{1,0:T(8,128)(2,1)S(1)}, bf16[16384,128]{1,0:T(8,128)(2,1)}, u32[]{:S(2)}) copy-start(bf16[16384,128]{1,0:T(8,128)(2,1)} %param.13) | copy-start | bytes 12582916
  44.5 3.1 %collective-permute-start.9 = (bf16[16,16384]{1,0:T(8,128)(2,1)S(1)}, bf16[16,16384]{1,0:T(8,128)(2,1)S(1)}, u32[]{:S(2)}, u32[]{:S(2)}) collective-permute-start(bf16[16,16384]{1,0:T(8,128)(2,1)S(1)} %concatenate.11), channel_id=1, source_target_pairs={{0,1},{1,0},{2,3},{3,2},{4,5},{5,4},{6,7},{7,6},{8,9},{9,8},{10,11... | collective-permute-start | bytes 1572872 | tf_op jit(solution)/shard_map/ppermute | solution.py:24

commit v3 on v2

v3 whole, which is shorter than its diff:
```python
import jax
import jax.numpy as jnp
from jax import lax
from jax.sharding import PartitionSpec as P

HD = 128
QB = 128
EPS = 1e-06
F32 = jnp.float32
BF16 = jnp.bfloat16


def on_device(residual, queries, key_rows, value_rows, out_weight, norm_gain, q_weight):
    n = lax.axis_size("tp")
    device = lax.axis_index("tp")
    tokens = queries.shape[0]
    local = residual.shape[0]
    D = residual.shape[1]
    heads = queries.shape[1] // HD
    group = heads * n // (key_rows.shape[1] // HD)
    late = [1 << b for b in range(3, n.bit_length() - 1)]
    orders = ([2, 4], [4, 2])
    cut = D // 2
    columns = ((0, cut), (cut, D))

    def swap(x, distance):
        return lax.ppermute(x, "tp", [(i, i ^ distance) for i in range(n)])

    row = jnp.arange(tokens)
    block = row // local

    def picker(order):
        bits = [1] + order + late
        distance = 0
        for place, bit in enumerate(bits):
            distance = distance + (block >> (len(bits) - 1 - place)) % 2 * bit
        token = (device ^ distance) * local + row % local
        return (token[:, None] == row[None, :]).astype(BF16)

    visible = row[None, :] <= row[:, None]
    contexts = []
    for h in range(heads):
        kv_start = (device * heads + h) // group * HD
        key_head = lax.dynamic_slice_in_dim(key_rows, kv_start, HD, 1)
        value_head = lax.dynamic_slice_in_dim(value_rows, kv_start, HD, 1)
        scores = lax.dot_general(
            queries[:, h * HD : (h + 1) * HD],
            key_head,
            (((1,), (1,)), ((), ())),
            preferred_element_type=F32,
        ) / jnp.sqrt(F32(HD))
        scores = jnp.where(visible, scores, F32(-1e30))
        probs = jax.nn.softmax(scores, axis=-1).astype(BF16)
        contexts.append(jnp.dot(probs, value_head, preferred_element_type=F32).astype(BF16))
    context = jnp.concatenate(contexts, axis=1)
    half, quarter, eighth = tokens // 2, tokens // 4, tokens // 8
    sums = []
    for order, (lo, hi) in zip(orders, columns):
        ordered = jnp.dot(picker(order), context, preferred_element_type=F32).astype(BF16)
        part = jnp.dot(ordered, out_weight[:, lo:hi], preferred_element_type=F32)
        got = swap(part[half:].astype(BF16), 1)
        chip_sum = part[:half] + got.astype(F32)
        got = swap(chip_sum[quarter:].astype(BF16), order[0])
        pair_sum = chip_sum[:quarter] + got.astype(F32)
        got = swap(pair_sum[eighth:].astype(BF16), order[1])
        sums.append(pair_sum[:eighth] + got.astype(F32))
    total = jnp.concatenate(sums, axis=1)
    for distance in late:
        kept = total.shape[0] // 2
        total = total[:kept] + swap(total[kept:].astype(BF16), distance).astype(F32)
    stream = residual.astype(F32) + total
    grouped = stream.reshape(local, D // QB, QB)
    scales = jnp.max(jnp.abs(grouped), axis=2) + EPS
    codes = (grouped / scales[:, :, None]).astype(BF16)
    decoded = (codes.astype(F32) * scales[:, :, None]).reshape(local, D)
    mean_sq = jnp.mean(decoded * decoded, axis=1, keepdims=True)
    normed = (decoded * lax.rsqrt(mean_sq + 1e-05) * norm_gain[None, :]).astype(BF16)
    for distance in late[::-1]:
        normed = jnp.concatenate([normed, swap(normed, distance)], axis=0)
    next_queries = 0
    for order, (lo, hi) in zip(orders, columns):
        held = normed[:, lo:hi]
        for distance in order[::-1]:
            held = jnp.concatenate([held, swap(held, distance)], axis=0)
        held = jnp.concatenate([held, swap(held, 1)], axis=0)
        found = jnp.dot(held, q_weight[lo:hi], preferred_element_type=F32)
        next_queries = next_queries + lax.dot_general(
            picker(order).astype(F32),
            found,
            (((0,), (0,)), ((), ())),
            precision=lax.Precision.HIGHEST,
        )
    return (codes.reshape(local, D), scales, next_queries.astype(BF16))


def solution(mesh):
    in_specs = (
        P(("replica", "tp"), None),
        P("replica", "tp"),
        P("replica", None),
        P("replica", None),
        P("tp", None),
        P(),
        P(None, "tp"),
    )
    out_specs = (P(("replica", "tp"), None), P(("replica", "tp"), None), P("replica", "tp"))
    return jax.shard_map(
        on_device, mesh=mesh, in_specs=in_specs, out_specs=out_specs, check_vma=False
    )
```

time: 49.5 us -> 46.3 us (0.935)
  waiting for transfers between devices: 22.9 us -> 14.7 us
  starting transfers between devices: 14 us -> 21.1 us
  matrix products: 9.28 us -> 7.48 us
  local copies, waits for them, and re-layouts: 1.19 us -> 0.28 us
    ppermute x10 -> x14, waiting for transfers between devices: 22.9 us -> 14.7 us  [swap(): return lax.ppermute(x, 'tp', [(i, i ^ distance) for i in range(n)])]
    ppermute x10 -> x14, starting transfers between devices: 14 us -> 21.1 us  [swap(): return lax.ppermute(x, 'tp', [(i, i ^ distance) for i in range(n)])]
    dot_general x5 -> x6, matrix products: 8.05 us -> 6.44 us  [the longest x2 4.36 us: on_device(): part = jnp.dot(ordered, out_weight[:, lo:hi], preferred_element_type=F32)]
    concatenate x1 -> x0, local copies, waits for them, and re-layouts: 0.52 us -> none  [on_device(): mine = jnp.concatenate([near, swap(near, 2)], axis=0)]
  transfers between devices with their start and end apart: 10 -> 14, of which waited for: 7 -> 9; matrix products, arithmetic and copies ran while one was open for 6% -> 8% of each run, Pallas kernels for 0% -> 0%
where the time goes in v3:
time: 46.3 us; the launch traced here: 46.1 us
  starting transfers between devices  21.1 us (46%)
  waiting for transfers between devices  14.7 us (32%)
  matrix products  7.48 us (16%)
  other arithmetic  1.57 us (3%)
  between operations  0.92 us (2%)
    ppermute x14, starting transfers between devices, swap(): return lax.ppermute(x, 'tp', [(i, i ^ distance) for i in range(n)])  21.1 us
    ppermute x14, waiting for transfers between devices, swap(): return lax.ppermute(x, 'tp', [(i, i ^ distance) for i in range(n)])  14.7 us
    dot_general x2, matrix products, on_device(): part = jnp.dot(ordered, out_weight[:, lo:hi], preferred_element_type=F32)  4.36 us
    dot_general x2, matrix products, on_device(): lax.dot_general(picker(order).astype(F32), found, (((0,), (0,)), ((), ())...  1.14 us
    dot_general x2, matrix products, on_device(): found = jnp.dot(held, q_weight[lo:hi], preferred_element_type=F32)  0.94 us
  transfers between devices with their start and end apart: 14, of which 9 were waited for; matrix products, arithmetic and copies ran while one was open for 8% of the time, Pallas kernels for 0%

profile of v3, /device:TPU:0, one launch (start us, length us, event | category | flops | bytes accessed | tf_op | source)
XLA Modules:
  0.0 46.1 jit_solution(13481068408274453589)
XLA Ops:
  0.6 0.0 copy-start
  0.7 0.9 %fusion.54 = (f32[32]{0:T(128)S(1)}, f32[32,32]{0,1:T(8,128)S(1)}) fusion(bf16[32,128]{1,0:T(8,128)(2,1)} %param.8, bf16[32,1024]{1,0:T(8,128)(2,1)} %param.9, s32[]{:T(128)S(6)} %select_n.131), kind=kOutput, calls=%fused_computation.110 | convolution fusion | flops 266208 | bytes 20612 | tf_op jit(solution)/shard_map/dot_general | solution.py:46
  1.6 0.0 copy-done
  1.6 0.2 convolution_convert_fusion.2
  1.8 2.2 %fusion.4 = f32[32,8192]{1,0:T(8,128)S(1)} fusion(bf16[128,16384]{1,0:T(8,128)(2,1)} %param.11, bf16[32,128]{1,0:T(8,128)(2,1)S(1)} %convolution_convert_fusion.2, s32[32]{0:T(128)S(1)} %get-tuple-element.11), kind=kOutput, calls=%fused_computation.4 | convolution fusion | flops 67376128 | bytes 3154048 | tf_op jit(solution)/shard_map/dot_general | solution.py:60
  4.0 0.5 %collective-permute-start.3 = (bf16[16,8192]{1,0:T(8,128)(2,1)S(1)}, bf16[16,8192]{1,0:T(8,128)(2,1)S(1)}, u32[]{:S(2)}, u32[]{:S(2)}) collective-permute-start(bf16[16,8192]{1,0:T(8,128)(2,1)S(1)} %slice.139), channel_id=1, source_target_pairs={{0,1},{1,0},{2,3},{3,2},{4,5},{5,4},{6,7},{7,6},{8,9},{9,8},{10,11... | collective-permute-start | bytes 786440 | tf_op jit(solution)/shard_map/ppermute | solution.py:27
  4.5 0.0 copy-start.2
  4.5 2.2 %fusion.6 = f32[32,8192]{1,0:T(8,128)S(1)} fusion(bf16[128,16384]{1,0:T(8,128)(2,1)} %param.11, bf16[32,128]{1,0:T(8,128)(2,1)S(1)} %convolution_convert_fusion.2, s32[32]{0:T(128)S(1)} %get-tuple-element.12), kind=kOutput, calls=%fused_computation.6 | convolution fusion | flops 67376128 | bytes 3154048 | tf_op jit(solution)/shard_map/dot_general | solution.py:60
  6.7 0.0 copy-start.3
  6.7 0.1 collective-permute-start
  6.9 0.0 collective-permute-done.3
  6.9 0.0 copy-start.5
  7.0 3.1 %collective-permute-start.4 = (bf16[8,8192]{1,0:T(8,128)(2,1)S(1)}, bf16[8,8192]{1,0:T(8,128)(2,1)S(1)}, u32[]{:S(2)}, u32[]{:S(2)}) collective-permute-start(bf16[8,8192]{1,0:T(8,128)(2,1)S(1)} %slice.141), channel_id=1, source_target_pairs={{0,4},{1,5},{2,6},{3,7},{4,0},{5,1},{6,2},{7,3},{8,12},{9,13},{10,... | collective-permute-start | bytes 393224 | tf_op jit(solution)/shard_map/ppermute | solution.py:27
  10.0 0.0 collective-permute-done
  10.0 0.1 slice_add_fusion.1
  10.1 1.6 %collective-permute-start.1 = (bf16[8,8192]{1,0:T(8,128)(2,1)S(1)}, bf16[8,8192]{1,0:T(8,128)(2,1)S(1)}, u32[]{:S(2)}, u32[]{:S(2)}) collective-permute-start(bf16[8,8192]{1,0:T(8,128)(2,1)S(1)} %slice.142), channel_id=1, source_target_pairs={{0,2},{1,3},{2,0},{3,1},{4,6},{5,7},{6,4},{7,5},{8,10},{9,11},{10,... | collective-permute-start | bytes 393224 | tf_op jit(solution)/shard_map/ppermute | solution.py:27
  11.7 2.0 %collective-permute-done.4 = bf16[8,8192]{1,0:T(8,128)(2,1)S(1)} collective-permute-done((bf16[8,8192]{1,0:T(8,128)(2,1)S(1)}, bf16[8,8192]{1,0:T(8,128)(2,1)S(1)}, u32[]{:S(2)}, u32[]{:S(2)}) %collective-permute-start.4) | collective-permute-done | bytes 131104 | tf_op jit(solution)/shard_map/ppermute | solution.py:27
  13.8 1.8 %collective-permute-start.5 = (bf16[4,8192]{1,0:T(4,128)(2,1)S(1)}, bf16[4,8192]{1,0:T(4,128)(2,1)S(1)}, u32[]{:S(2)}, u32[]{:S(2)}) collective-permute-start(bf16[4,8192]{1,0:T(4,128)(2,1)S(1)} %slice.143), channel_id=1, source_target_pairs={{0,2},{1,3},{2,0},{3,1},{4,6},{5,7},{6,4},{7,5},{8,10},{9,11},{10,... | collective-permute-start | bytes 196616 | tf_op jit(solution)/shard_map/ppermute | solution.py:27
  15.6 0.0 collective-permute-done.1
  15.6 1.6 %collective-permute-start.2 = (bf16[4,8192]{1,0:T(4,128)(2,1)S(1)}, bf16[4,8192]{1,0:T(4,128)(2,1)S(1)}, u32[]{:S(2)}, u32[]{:S(2)}) collective-permute-start(bf16[4,8192]{1,0:T(4,128)(2,1)S(1)} %slice.144), channel_id=1, source_target_pairs={{0,4},{1,5},{2,6},{3,7},{4,0},{5,1},{6,2},{7,3},{8,12},{9,13},{10,... | collective-permute-start | bytes 196616 | tf_op jit(solution)/shard_map/ppermute | solution.py:27
  17.3 0.9 %collective-permute-done.5 = bf16[4,8192]{1,0:T(4,128)(2,1)S(1)} collective-permute-done((bf16[4,8192]{1,0:T(4,128)(2,1)S(1)}, bf16[4,8192]{1,0:T(4,128)(2,1)S(1)}, u32[]{:S(2)}, u32[]{:S(2)}) %collective-permute-start.5) | collective-permute-done | bytes 65568 | tf_op jit(solution)/shard_map/ppermute | solution.py:27
  18.2 1.8 %collective-permute-done.2 = bf16[4,8192]{1,0:T(4,128)(2,1)S(1)} collective-permute-done((bf16[4,8192]{1,0:T(4,128)(2,1)S(1)}, bf16[4,8192]{1,0:T(4,128)(2,1)S(1)}, u32[]{:S(2)}, u32[]{:S(2)}) %collective-permute-start.2) | collective-permute-done | bytes 65568 | tf_op jit(solution)/shard_map/ppermute | solution.py:27
  20.0 0.1 fusion.28
  20.1 2.6 %collective-permute-start.6 = (bf16[2,16384]{1,0:T(2,128)(2,1)S(1)}, bf16[2,16384]{1,0:T(2,128)(2,1)S(1)}, u32[]{:S(2)}, u32[]{:S(2)}) collective-permute-start(bf16[2,16384]{1,0:T(2,128)(2,1)S(1)} %fusion.28), channel_id=1, source_target_pairs={{0,8},{1,9},{2,10},{3,11},{4,12},{5,13},{6,14},{7,15},{8,0},{9,1},... | collective-permute-start | bytes 196616 | tf_op jit(solution)/shard_map/ppermute | solution.py:27
  22.7 2.6 %collective-permute-done.6 = bf16[2,16384]{1,0:T(2,128)(2,1)S(1)} collective-permute-done((bf16[2,16384]{1,0:T(2,128)(2,1)S(1)}, bf16[2,16384]{1,0:T(2,128)(2,1)S(1)}, u32[]{:S(2)}, u32[]{:S(2)}) %collective-permute-start.6) | collective-permute-done | bytes 65568 | tf_op jit(solution)/shard_map/ppermute | solution.py:27
  25.3 0.0 copy-done.2
  25.3 0.2 abs_bitcast_fusion
  25.5 0.1 bitcast_reduce_fusion
  25.6 0.0 copy-start.4
  25.6 0.1 broadcast_bitcast_fusion
  25.7 0.3 multiply_reduce_fusion
  26.0 0.0 copy-start.1
  26.0 0.0 copy-done.3
  26.0 0.2 multiply_convert_fusion
  26.2 2.7 %collective-permute-start.7 = (bf16[2,16384]{1,0:T(2,128)(2,1)S(1)}, bf16[2,16384]{1,0:T(2,128)(2,1)S(1)}, u32[]{:S(2)}, u32[]{:S(2)}) collective-permute-start(bf16[2,16384]{1,0:T(2,128)(2,1)S(1)} %multiply_convert_fusion), channel_id=1, source_target_pairs={{0,8},{1,9},{2,10},{3,11},{4,12},{5,13},{6,14},{7,15},{8,0},{9,1},... | collective-permute-start | bytes 196616 | tf_op jit(solution)/shard_map/ppermute | solution.py:27
  28.9 2.6 %collective-permute-done.7 = bf16[2,16384]{1,0:T(2,128)(2,1)S(1)} collective-permute-done((bf16[2,16384]{1,0:T(2,128)(2,1)S(1)}, bf16[2,16384]{1,0:T(2,128)(2,1)S(1)}, u32[]{:S(2)}, u32[]{:S(2)}) %collective-permute-start.7) | collective-permute-done | bytes 65568 | tf_op jit(solution)/shard_map/ppermute | solution.py:27
  31.5 0.1 pad_maximum_fusion.5
  31.7 1.8 %collective-permute-start.8 = (bf16[4,8192]{1,0:T(4,128)(2,1)S(1)}, bf16[4,8192]{1,0:T(4,128)(2,1)S(1)}, u32[]{:S(2)}, u32[]{:S(2)}) collective-permute-start(bf16[4,8192]{1,0:T(4,128)(2,1)S(1)} %get-tuple-element.8), channel_id=1, source_target_pairs={{0,4},{1,5},{2,6},{3,7},{4,0},{5,1},{6,2},{7,3},{8,12},{9,13},{10,... | collective-permute-start | bytes 196616 | tf_op jit(solution)/shard_map/ppermute | solution.py:27
  33.5 1.4 %collective-permute-start.11 = (bf16[4,8192]{1,0:T(4,128)(2,1)S(1)}, bf16[4,8192]{1,0:T(4,128)(2,1)S(1)}, u32[]{:S(2)}, u32[]{:S(2)}) collective-permute-start(bf16[4,8192]{1,0:T(4,128)(2,1)S(1)} %get-tuple-element.7), channel_id=1, source_target_pairs={{0,2},{1,3},{2,0},{3,1},{4,6},{5,7},{6,4},{7,5},{8,10},{9,11},{10,... | collective-permute-start | bytes 196616 | tf_op jit(solution)/shard_map/ppermute | solution.py:27
  34.8 1.3 %collective-permute-done.8 = bf16[4,8192]{1,0:T(4,128)(2,1)S(1)} collective-permute-done((bf16[4,8192]{1,0:T(4,128)(2,1)S(1)}, bf16[4,8192]{1,0:T(4,128)(2,1)S(1)}, u32[]{:S(2)}, u32[]{:S(2)}) %collective-permute-start.8) | collective-permute-done | bytes 65568 | tf_op jit(solution)/shard_map/ppermute | solution.py:27
  36.2 0.1 pad_maximum_fusion.3
  36.2 1.7 %collective-permute-start.9 = (bf16[8,8192]{1,0:T(8,128)(2,1)S(1)}, bf16[8,8192]{1,0:T(8,128)(2,1)S(1)}, u32[]{:S(2)}, u32[]{:S(2)}) collective-permute-start(bf16[8,8192]{1,0:T(8,128)(2,1)S(1)} %pad_maximum_fusion.3), channel_id=1, source_target_pairs={{0,2},{1,3},{2,0},{3,1},{4,6},{5,7},{6,4},{7,5},{8,10},{9,11},{10,... | collective-permute-start | bytes 393224 | tf_op jit(solution)/shard_map/ppermute | solution.py:27
  37.9 0.0 collective-permute-done.11
  37.9 0.1 pad_maximum_fusion.4
  38.0 2.1 %collective-permute-start.12 = (bf16[8,8192]{1,0:T(8,128)(2,1)S(1)}, bf16[8,8192]{1,0:T(8,128)(2,1)S(1)}, u32[]{:S(2)}, u32[]{:S(2)}) collective-permute-start(bf16[8,8192]{1,0:T(8,128)(2,1)S(1)} %pad_maximum_fusion.4), channel_id=1, source_target_pairs={{0,4},{1,5},{2,6},{3,7},{4,0},{5,1},{6,2},{7,3},{8,12},{9,13},{10,... | collective-permute-start | bytes 393224 | tf_op jit(solution)/shard_map/ppermute | solution.py:27
  40.1 1.2 %collective-permute-done.9 = bf16[8,8192]{1,0:T(8,128)(2,1)S(1)} collective-permute-done((bf16[8,8192]{1,0:T(8,128)(2,1)S(1)}, bf16[8,8192]{1,0:T(8,128)(2,1)S(1)}, u32[]{:S(2)}, u32[]{:S(2)}) %collective-permute-start.9) | collective-permute-done | bytes 131104 | tf_op jit(solution)/shard_map/ppermute | solution.py:27
  41.3 0.1 pad_maximum_fusion
  41.4 0.1 collective-permute-start.10
  41.5 1.6 %collective-permute-done.12 = bf16[8,8192]{1,0:T(8,128)(2,1)S(1)} collective-permute-done((bf16[8,8192]{1,0:T(8,128)(2,1)S(1)}, bf16[8,8192]{1,0:T(8,128)(2,1)S(1)}, u32[]{:S(2)}, u32[]{:S(2)}) %collective-permute-start.12) | collective-permute-done | bytes 131104 | tf_op jit(solution)/shard_map/ppermute | solution.py:27
  43.0 0.1 pad_maximum_fusion.1
  43.1 0.1 collective-permute-start.13
  43.2 0.0 collective-permute-done.10
  43.2 0.0 copy-done.5
  43.2 0.5 %fusion.2 = f32[32,128]{1,0:T(8,128)S(1)} fusion(bf16[16384,128]{1,0:T(8,128)(2,1)S(1)} %copy-done.5, bf16[16,8192]{1,0:T(8,128)(2,1)S(1)} %collective-permute-done.10, bf16[8,8192]{1,0:T(8,128)(2,1)S(1)} %collective-permute-done.9, bf16[4,8192]{1,0:T(4,128)(2,1)S(1)} %collective-permute-done.8, bf16[4,8192]{1,0:T(4,128)(2,1)S(1)} %get-tuple-element.8), kind=kOutput, calls=%fused_computation.2 | convolution fusion | flops 69206016 | bytes 2637824 | tf_op jit(solution)/shard_map/dot_general | solution.py:86
  43.7 0.3 fusion.31
  44.0 0.8 %collective-permute-done.13 = bf16[16,8192]{1,0:T(8,128)(2,1)S(1)} collective-permute-done((bf16[16,8192]{1,0:T(8,128)(2,1)S(1)}, bf16[16,8192]{1,0:T(8,128)(2,1)S(1)}, u32[]{:S(2)}, u32[]{:S(2)}) %collective-permute-start.13) | collective-permute-done | bytes 262176 | tf_op jit(solution)/shard_map/ppermute | solution.py:27
  44.7 0.5 %fusion = f32[32,128]{1,0:T(8,128)S(1)} fusion(bf16[16384,128]{1,0:T(8,128)(2,1)S(1)} %copy-done.5, bf16[16,8192]{1,0:T(8,128)(2,1)S(1)} %collective-permute-done.13, bf16[8,8192]{1,0:T(8,128)(2,1)S(1)} %collective-permute-done.12, bf16[4,8192]{1,0:T(4,128)(2,1)S(1)} %collective-permute-done.11, bf16[4,8192]{1,0:T(4,128)(2,1)S(1)} %get-tuple-element.7), kind=kOutput, calls=%fused_computation | convolution fusion | flops 69206016 | bytes 2637824 | tf_op jit(solution)/shard_map/dot_general | solution.py:86
  45.2 0.0 copy-done.4
  45.2 0.0 copy-done.1
  45.2 0.9 %fusion.10 = bf16[32,128]{1,0:T(8,128)(2,1)} fusion(f32[32,128]{1,0:T(8,128)S(1)} %fusion.31, f32[32,128]{1,0:T(8,128)S(1)} %fusion, s32[32]{0:T(128)S(1)} %get-tuple-element.11), kind=kOutput, calls=%fused_computation.12 | convolution fusion | flops 1582080 | bytes 41088 | tf_op jit(solution)/shard_map/dot_general | solution.py:87
  (15 shorter events, 0.4 us)
Async XLA Ops:
  0.6 1.0 %copy-start = (bf16[32,1024]{1,0:T(8,128)(2,1)S(1)}, bf16[32,1024]{1,0:T(8,128)(2,1)}, u32[]{:S(2)}) copy-start(bf16[32,1024]{1,0:T(8,128)(2,1)} %param.10) | copy-start | bytes 196612
  4.0 2.9 %collective-permute-start.3 = (bf16[16,8192]{1,0:T(8,128)(2,1)S(1)}, bf16[16,8192]{1,0:T(8,128)(2,1)S(1)}, u32[]{:S(2)}, u32[]{:S(2)}) collective-permute-start(bf16[16,8192]{1,0:T(8,128)(2,1)S(1)} %slice.139), channel_id=1, source_target_pairs={{0,1},{1,0},{2,3},{3,2},{4,5},{5,4},{6,7},{7,6},{8,9},{9,8},{10,11... | collective-permute-start | bytes 786440 | tf_op jit(solution)/shard_map/ppermute | solution.py:27
  4.5 20.8 %copy-start.2 = (bf16[2,16384]{1,0:T(2,128)(2,1)S(1)}, bf16[2,16384]{1,0:T(2,128)(2,1)}, u32[]{:S(2)}) copy-start(bf16[2,16384]{1,0:T(2,128)(2,1)} %param.7) | copy-start | bytes 196612
  6.7 19.3 %copy-start.3 = (f32[16384]{0:T(1024)S(1)}, f32[16384]{0:T(1024)}, u32[]{:S(2)}) copy-start(f32[16384]{0:T(1024)} %param.12) | copy-start | bytes 196612
  6.7 3.3 %collective-permute-start = (bf16[16,8192]{1,0:T(8,128)(2,1)S(1)}, bf16[16,8192]{1,0:T(8,128)(2,1)S(1)}, u32[]{:S(2)}, u32[]{:S(2)}) collective-permute-start(bf16[16,8192]{1,0:T(8,128)(2,1)S(1)} %slice.140), channel_id=1, source_target_pairs={{0,1},{1,0},{2,3},{3,2},{4,5},{5,4},{6,7},{7,6},{8,9},{9,8},{10,11... | collective-permute-start | bytes 786440 | tf_op jit(solution)/shard_map/ppermute | solution.py:27
  6.9 36.3 %copy-start.5 = (bf16[16384,128]{1,0:T(8,128)(2,1)S(1)}, bf16[16384,128]{1,0:T(8,128)(2,1)}, u32[]{:S(2)}) copy-start(bf16[16384,128]{1,0:T(8,128)(2,1)} %param.13) | copy-start | bytes 12582916
  7.0 6.8 %collective-permute-start.4 = (bf16[8,8192]{1,0:T(8,128)(2,1)S(1)}, bf16[8,8192]{1,0:T(8,128)(2,1)S(1)}, u32[]{:S(2)}, u32[]{:S(2)}) collective-permute-start(bf16[8,8192]{1,0:T(8,128)(2,1)S(1)} %slice.141), channel_id=1, source_target_pairs={{0,4},{1,5},{2,6},{3,7},{4,0},{5,1},{6,2},{7,3},{8,12},{9,13},{10,... | collective-permute-start | bytes 393224 | tf_op jit(solution)/shard_map/ppermute | solution.py:27
  10.1 5.4 %collective-permute-start.1 = (bf16[8,8192]{1,0:T(8,128)(2,1)S(1)}, bf16[8,8192]{1,0:T(8,128)(2,1)S(1)}, u32[]{:S(2)}, u32[]{:S(2)}) collective-permute-start(bf16[8,8192]{1,0:T(8,128)(2,1)S(1)} %slice.142), channel_id=1, source_target_pairs={{0,2},{1,3},{2,0},{3,1},{4,6},{5,7},{6,4},{7,5},{8,10},{9,11},{10,... | collective-permute-start | bytes 393224 | tf_op jit(solution)/shard_map/ppermute | solution.py:27
  13.8 4.3 %collective-permute-start.5 = (bf16[4,8192]{1,0:T(4,128)(2,1)S(1)}, bf16[4,8192]{1,0:T(4,128)(2,1)S(1)}, u32[]{:S(2)}, u32[]{:S(2)}) collective-permute-start(bf16[4,8192]{1,0:T(4,128)(2,1)S(1)} %slice.143), channel_id=1, source_target_pairs={{0,2},{1,3},{2,0},{3,1},{4,6},{5,7},{6,4},{7,5},{8,10},{9,11},{10,... | collective-permute-start | bytes 196616 | tf_op jit(solution)/shard_map/ppermute | solution.py:27
  15.6 4.3 %collective-permute-start.2 = (bf16[4,8192]{1,0:T(4,128)(2,1)S(1)}, bf16[4,8192]{1,0:T(4,128)(2,1)S(1)}, u32[]{:S(2)}, u32[]{:S(2)}) collective-permute-start(bf16[4,8192]{1,0:T(4,128)(2,1)S(1)} %slice.144), channel_id=1, source_target_pairs={{0,4},{1,5},{2,6},{3,7},{4,0},{5,1},{6,2},{7,3},{8,12},{9,13},{10,... | collective-permute-start | bytes 196616 | tf_op jit(solution)/shard_map/ppermute | solution.py:27
  20.1 5.2 %collective-permute-start.6 = (bf16[2,16384]{1,0:T(2,128)(2,1)S(1)}, bf16[2,16384]{1,0:T(2,128)(2,1)S(1)}, u32[]{:S(2)}, u32[]{:S(2)}) collective-permute-start(bf16[2,16384]{1,0:T(2,128)(2,1)S(1)} %fusion.28), channel_id=1, source_target_pairs={{0,8},{1,9},{2,10},{3,11},{4,12},{5,13},{6,14},{7,15},{8,0},{9,1},... | collective-permute-start | bytes 196616 | tf_op jit(solution)/shard_map/ppermute | solution.py:27
  25.6 19.6 %copy-start.4 = (f32[2,128]{1,0:T(2,128)}, f32[2,128]{1,0:T(2,128)S(1)}, u32[]{:S(2)}) copy-start(f32[2,128]{1,0:T(2,128)S(1)} %broadcast_add_fusion) | copy-start | bytes 3076
  26.0 19.2 %copy-start.1 = (bf16[2,16384]{1,0:T(2,128)(2,1)}, bf16[2,16384]{1,0:T(2,128)(2,1)S(1)}, u32[]{:S(2)}) copy-start(bf16[2,16384]{1,0:T(2,128)(2,1)S(1)} %get-tuple-element.4) | copy-start | bytes 196612
  26.2 5.3 %collective-permute-start.7 = (bf16[2,16384]{1,0:T(2,128)(2,1)S(1)}, bf16[2,16384]{1,0:T(2,128)(2,1)S(1)}, u32[]{:S(2)}, u32[]{:S(2)}) collective-permute-start(bf16[2,16384]{1,0:T(2,128)(2,1)S(1)} %multiply_convert_fusion), channel_id=1, source_target_pairs={{0,8},{1,9},{2,10},{3,11},{4,12},{5,13},{6,14},{7,15},{8,0},{9,1},... | collective-permute-start | bytes 196616 | tf_op jit(solution)/shard_map/ppermute | solution.py:27
  31.7 4.5 %collective-permute-start.8 = (bf16[4,8192]{1,0:T(4,128)(2,1)S(1)}, bf16[4,8192]{1,0:T(4,128)(2,1)S(1)}, u32[]{:S(2)}, u32[]{:S(2)}) collective-permute-start(bf16[4,8192]{1,0:T(4,128)(2,1)S(1)} %get-tuple-element.8), channel_id=1, source_target_pairs={{0,4},{1,5},{2,6},{3,7},{4,0},{5,1},{6,2},{7,3},{8,12},{9,13},{10,... | collective-permute-start | bytes 196616 | tf_op jit(solution)/shard_map/ppermute | solution.py:27
  33.5 4.4 %collective-permute-start.11 = (bf16[4,8192]{1,0:T(4,128)(2,1)S(1)}, bf16[4,8192]{1,0:T(4,128)(2,1)S(1)}, u32[]{:S(2)}, u32[]{:S(2)}) collective-permute-start(bf16[4,8192]{1,0:T(4,128)(2,1)S(1)} %get-tuple-element.7), channel_id=1, source_target_pairs={{0,2},{1,3},{2,0},{3,1},{4,6},{5,7},{6,4},{7,5},{8,10},{9,11},{10,... | collective-permute-start | bytes 196616 | tf_op jit(solution)/shard_map/ppermute | solution.py:27
  36.2 5.0 %collective-permute-start.9 = (bf16[8,8192]{1,0:T(8,128)(2,1)S(1)}, bf16[8,8192]{1,0:T(8,128)(2,1)S(1)}, u32[]{:S(2)}, u32[]{:S(2)}) collective-permute-start(bf16[8,8192]{1,0:T(8,128)(2,1)S(1)} %pad_maximum_fusion.3), channel_id=1, source_target_pairs={{0,2},{1,3},{2,0},{3,1},{4,6},{5,7},{6,4},{7,5},{8,10},{9,11},{10,... | collective-permute-start | bytes 393224 | tf_op jit(solution)/shard_map/ppermute | solution.py:27
  38.0 5.1 %collective-permute-start.12 = (bf16[8,8192]{1,0:T(8,128)(2,1)S(1)}, bf16[8,8192]{1,0:T(8,128)(2,1)S(1)}, u32[]{:S(2)}, u32[]{:S(2)}) collective-permute-start(bf16[8,8192]{1,0:T(8,128)(2,1)S(1)} %pad_maximum_fusion.4), channel_id=1, source_target_pairs={{0,4},{1,5},{2,6},{3,7},{4,0},{5,1},{6,2},{7,3},{8,12},{9,13},{10,... | collective-permute-start | bytes 393224 | tf_op jit(solution)/shard_map/ppermute | solution.py:27
  41.4 1.8 %collective-permute-start.10 = (bf16[16,8192]{1,0:T(8,128)(2,1)S(1)}, bf16[16,8192]{1,0:T(8,128)(2,1)S(1)}, u32[]{:S(2)}, u32[]{:S(2)}) collective-permute-start(bf16[16,8192]{1,0:T(8,128)(2,1)S(1)} %pad_maximum_fusion), channel_id=1, source_target_pairs={{0,1},{1,0},{2,3},{3,2},{4,5},{5,4},{6,7},{7,6},{8,9},{9,8},{10,11... | collective-permute-start | bytes 786440 | tf_op jit(solution)/shard_map/ppermute | solution.py:27
  43.1 1.6 %collective-permute-start.13 = (bf16[16,8192]{1,0:T(8,128)(2,1)S(1)}, bf16[16,8192]{1,0:T(8,128)(2,1)S(1)}, u32[]{:S(2)}, u32[]{:S(2)}) collective-permute-start(bf16[16,8192]{1,0:T(8,128)(2,1)S(1)} %pad_maximum_fusion.1), channel_id=1, source_target_pairs={{0,1},{1,0},{2,3},{3,2},{4,5},{5,4},{6,7},{7,6},{8,9},{9,8},{10,11... | collective-permute-start | bytes 786440 | tf_op jit(solution)/shard_map/ppermute | solution.py:27

commit v4 on v2

v4 whole, which is shorter than its diff:
```python
import jax
import jax.numpy as jnp
from jax import lax
from jax.sharding import PartitionSpec as P

HD = 128
QB = 128
EPS = 1e-06
F32 = jnp.float32
BF16 = jnp.bfloat16


def on_device(residual, queries, key_rows, value_rows, out_weight, norm_gain, q_weight):
    n = lax.axis_size("tp")
    device = lax.axis_index("tp")
    core = device % 2
    tokens = queries.shape[0]
    local = residual.shape[0]
    D = residual.shape[1]
    heads = queries.shape[1] // HD
    group = heads * n // (key_rows.shape[1] // HD)
    levels = [(2, 4), (4, 2)] + [(1 << b, 1 << b) for b in range(3, n.bit_length() - 1)]
    bits = [(1, 1)] + levels

    def swap(x, level):
        return lax.ppermute(x, "tp", [(i, i ^ level[i % 2]) for i in range(n)])

    row = jnp.arange(tokens)
    block = row // local
    side = (core + block // (n // 2)) % 2
    distance = 0
    for place, (even, odd) in enumerate(bits):
        distance += (block >> (len(bits) - 1 - place)) % 2 * jnp.where(side == 0, even, odd)
    token = (device ^ distance) * local + row % local
    pick = (token[:, None] == row[None, :]).astype(BF16)
    queries = jnp.dot(pick, queries, preferred_element_type=F32).astype(BF16)
    visible = row[None, :] <= token[:, None]
    contexts = []
    for h in range(heads):
        kv_start = (device * heads + h) // group * HD
        key_head = lax.dynamic_slice_in_dim(key_rows, kv_start, HD, 1)
        value_head = lax.dynamic_slice_in_dim(value_rows, kv_start, HD, 1)
        scores = lax.dot_general(
            queries[:, h * HD : (h + 1) * HD],
            key_head,
            (((1,), (1,)), ((), ())),
            preferred_element_type=F32,
        ) / jnp.sqrt(F32(HD))
        scores = jnp.where(visible, scores, F32(-1e30))
        probs = jax.nn.softmax(scores, axis=-1).astype(BF16)
        contexts.append(jnp.dot(probs, value_head, preferred_element_type=F32).astype(BF16))
    context = jnp.concatenate(contexts, axis=1)
    half = tokens // 2
    sent = jnp.dot(context[half:], out_weight, preferred_element_type=F32)
    got = swap(sent.astype(BF16), bits[0])
    total = jnp.dot(context[:half], out_weight, preferred_element_type=F32)
    total = total + got.astype(F32)
    for level in levels[:-1]:
        kept = total.shape[0] // 2
        total = total[:kept] + swap(total[kept:].astype(BF16), level).astype(F32)
    total = jnp.concatenate([total[:local] + residual.astype(F32), total[local:]], axis=0)
    got = swap(total.astype(BF16), levels[-1]).astype(F32)
    stream = total + jnp.concatenate([got[local:], got[:local]], axis=0)
    rows = stream.shape[0]
    grouped = stream.reshape(rows, D // QB, QB)
    scales = jnp.max(jnp.abs(grouped), axis=2) + EPS
    codes = (grouped / scales[:, :, None]).astype(BF16)
    decoded = (codes.astype(F32) * scales[:, :, None]).reshape(rows, D)
    mean_sq = jnp.mean(decoded * decoded, axis=1, keepdims=True)
    held = (decoded * lax.rsqrt(mean_sq + 1e-05) * norm_gain[None, :]).astype(BF16)
    for level in levels[-2::-1]:
        held = jnp.concatenate([held, swap(held, level)], axis=0)
    other = swap(held, bits[0])
    out_mine = jnp.dot(held, q_weight, preferred_element_type=F32).astype(BF16)
    out_other = jnp.dot(other, q_weight, preferred_element_type=F32).astype(BF16)
    found = jnp.concatenate([out_mine, out_other], axis=0)
    next_queries = lax.dot_general(
        pick, found, (((0,), (0,)), ((), ())), preferred_element_type=F32
    ).astype(BF16)
    return (codes.reshape(rows, D)[:local], scales[:local], next_queries)


def solution(mesh):
    in_specs = (
        P(("replica", "tp"), None),
        P("replica", "tp"),
        P("replica", None),
        P("replica", None),
        P("tp", None),
        P(),
        P(None, "tp"),
    )
    out_specs = (P(("replica", "tp"), None), P(("replica", "tp"), None), P("replica", "tp"))
    return jax.shard_map(
        on_device, mesh=mesh, in_specs=in_specs, out_specs=out_specs, check_vma=False
    )
```

time: 49.5 us -> 45.7 us (0.923)
  starting transfers between devices: 14 us -> 11.7 us
  matrix products: 9.28 us -> 7.03 us
    ppermute x10 -> x7, starting transfers between devices: 14 us -> 11.7 us  [swap(): return lax.ppermute(x, 'tp', [(i, i ^ level[i % 2]) for i in range(n)])]
    dot_general x2, matrix products: 3.67 us -> 1.4 us  [the longest x1 0.74 us: on_device(): out_mine = jnp.dot(held, q_weight, preferred_element_type=F32).astype(BF16)]
    slice x2 -> x4, local copies, waits for them, and re-layouts: 0.2 us -> 0.75 us  [the longest x1 0.56 us: on_device(): return (codes.reshape(rows, D)[:local], scales[:local], next_queries)]
    ppermute x10 -> x7, waiting for transfers between devices: 22.9 us -> 22.8 us  [swap(): return lax.ppermute(x, 'tp', [(i, i ^ level[i % 2]) for i in range(n)])]
  transfers between devices with their start and end apart: 10 -> 7, of which waited for: 7 -> 7; matrix products, arithmetic and copies ran while one was open for 6% -> 4% of each run, Pallas kernels for 0% -> 0%
where the time goes in v4:
time: 45.7 us; the launch traced here: 45.6 us
  waiting for transfers between devices  22.8 us (50%)
  starting transfers between devices  11.7 us (26%)
  matrix products  7.03 us (15%)
  local copies, waits for them, and re-layouts  1.62 us (4%)
  other arithmetic  1.61 us (4%)
  between operations  0.82 us (2%)
    ppermute x7, waiting for transfers between devices, swap(): return lax.ppermute(x, 'tp', [(i, i ^ level[i % 2]) for i in range(n)])  22.8 us
    ppermute x7, starting transfers between devices, swap(): return lax.ppermute(x, 'tp', [(i, i ^ level[i % 2]) for i in range(n)])  11.7 us
    dot_general x1, matrix products, on_device(): sent = jnp.dot(context[half:], out_weight, preferred_element_type=F32)  2.99 us
    dot_general x1, matrix products, on_device(): lax.dot_general(queries[:, h * HD:(h + 1) * HD], key_head, (((1,), (1,)),...  1.04 us
  transfers between devices with their start and end apart: 7, of which 7 were waited for; matrix products, arithmetic and copies ran while one was open for 4% of the time, Pallas kernels for 0%

profile of v4, /device:TPU:0, one launch (start us, length us, event | category | flops | bytes accessed | tf_op | source)
XLA Modules:
  0.0 45.6 jit_solution(17031732956345141348)
XLA Ops:
  0.6 0.0 copy-start
  0.7 1.0 %fusion.38 = (f32[32]{0:T(128)S(1)}, f32[32,32]{0,1:T(8,128)S(1)}) fusion(bf16[32,1024]{1,0:T(8,128)(2,1)} %param.9, s32[]{:T(128)S(6)} %select_n.122, bf16[32,128]{1,0:T(8,128)(2,1)} %param.8, s32[32]{0:T(128)S(1)} %fusion.22), kind=kOutput, calls=%fused_computation.100 | convolution fusion | flops 533472 | bytes 21636 | tf_op jit(solution)/shard_map/dot_general | solution.py:43
  1.7 0.0 copy-start.1
  1.8 0.0 copy-done
  1.8 0.2 convolution_convert_fusion.2
  2.0 3.0 %convolution_convert_fusion = bf16[16,16384]{1,0:T(8,128)(2,1)S(1)} fusion(bf16[128,16384]{1,0:T(8,128)(2,1)} %param.11, bf16[32,128]{1,0:T(8,128)(2,1)S(1)} %convolution_convert_fusion.2), kind=kOutput, calls=%fused_computation | convolution fusion | flops 67371008 | bytes 4722688 | tf_op jit(solution)/shard_map/dot_general | solution.py:54
  5.0 0.0 copy-start.4
  5.0 0.5 %collective-permute-start = (bf16[16,16384]{1,0:T(8,128)(2,1)S(1)}, bf16[16,16384]{1,0:T(8,128)(2,1)S(1)}, u32[]{:S(2)}, u32[]{:S(2)}) collective-permute-start(bf16[16,16384]{1,0:T(8,128)(2,1)S(1)} %convolution_convert_fusion), channel_id=1, source_target_pairs={{0,1},{1,0},{2,3},{3,2},{4,5},{5,4},{6,7},{7,6},{8,9},{9,8},{10,11... | collective-permute-start | bytes 1572872 | tf_op jit(solution)/shard_map/ppermute | solution.py:26
  5.5 1.5 %collective-permute-done = bf16[16,16384]{1,0:T(8,128)(2,1)S(1)} collective-permute-done((bf16[16,16384]{1,0:T(8,128)(2,1)S(1)}, bf16[16,16384]{1,0:T(8,128)(2,1)S(1)}, u32[]{:S(2)}, u32[]{:S(2)}) %collective-permute-start) | collective-permute-done | bytes 524320 | tf_op jit(solution)/shard_map/ppermute | solution.py:26
  7.0 0.0 copy-done.1
  7.0 0.7 %convert_add_fusion = f32[16,16384]{1,0:T(8,128)S(1)} fusion(bf16[16,16384]{1,0:T(8,128)(2,1)S(1)} %collective-permute-done, bf16[128,16384]{1,0:T(8,128)(2,1)S(1)} %copy-done.1, bf16[32,128]{1,0:T(8,128)(2,1)S(1)} %convolution_convert_fusion.2), kind=kOutput, calls=%fused_computation.8 | convolution fusion | flops 67633152 | bytes 5771264 | tf_op jit(solution)/shard_map/dot_general | solution.py:56
  7.7 0.0 copy-start.3
  7.7 3.0 %collective-permute-start.1 = (bf16[8,16384]{1,0:T(8,128)(2,1)S(1)}, bf16[8,16384]{1,0:T(8,128)(2,1)S(1)}, u32[]{:S(2)}, u32[]{:S(2)}) collective-permute-start(bf16[8,16384]{1,0:T(8,128)(2,1)S(1)} %slice.80), channel_id=1, source_target_pairs={{0,2},{1,5},{2,0},{3,7},{4,6},{5,1},{6,4},{7,3},{8,10},{9,13},{10,... | collective-permute-start | bytes 786440 | tf_op jit(solution)/shard_map/ppermute | solution.py:26
  10.7 4.4 %collective-permute-done.1 = bf16[8,16384]{1,0:T(8,128)(2,1)S(1)} collective-permute-done((bf16[8,16384]{1,0:T(8,128)(2,1)S(1)}, bf16[8,16384]{1,0:T(8,128)(2,1)S(1)}, u32[]{:S(2)}, u32[]{:S(2)}) %collective-permute-start.1) | collective-permute-done | bytes 262176 | tf_op jit(solution)/shard_map/ppermute | solution.py:26
  15.1 0.1 slice.81
  15.2 0.0 copy-start.2
  15.2 2.1 %collective-permute-start.2 = (bf16[4,16384]{1,0:T(4,128)(2,1)S(1)}, bf16[4,16384]{1,0:T(4,128)(2,1)S(1)}, u32[]{:S(2)}, u32[]{:S(2)}) collective-permute-start(bf16[4,16384]{1,0:T(4,128)(2,1)S(1)} %slice.81), channel_id=1, source_target_pairs={{0,4},{1,3},{2,6},{3,1},{4,0},{5,7},{6,2},{7,5},{8,12},{9,11},{10,... | collective-permute-start | bytes 393224 | tf_op jit(solution)/shard_map/ppermute | solution.py:26
  17.3 2.9 %collective-permute-done.2 = bf16[4,16384]{1,0:T(4,128)(2,1)S(1)} collective-permute-done((bf16[4,16384]{1,0:T(4,128)(2,1)S(1)}, bf16[4,16384]{1,0:T(4,128)(2,1)S(1)}, u32[]{:S(2)}, u32[]{:S(2)}) %collective-permute-start.2) | collective-permute-done | bytes 131104 | tf_op jit(solution)/shard_map/ppermute | solution.py:26
  20.3 0.1 slice_add_fusion.1
  20.3 0.0 copy-done.4
  20.3 0.1 slice_bitcast_fusion.3
  20.5 0.1 fusion.5
  20.6 3.1 %collective-permute-start.3 = (bf16[4,16384]{1,0:T(4,128)(2,1)S(1)}, bf16[4,16384]{1,0:T(4,128)(2,1)S(1)}, u32[]{:S(2)}, u32[]{:S(2)}) collective-permute-start(bf16[4,16384]{1,0:T(4,128)(2,1)S(1)} %fusion.5), channel_id=1, source_target_pairs={{0,8},{1,9},{2,10},{3,11},{4,12},{5,13},{6,14},{7,15},{8,0},{9,1},... | collective-permute-start | bytes 393224 | tf_op jit(solution)/shard_map/ppermute | solution.py:26
  23.7 4.6 %collective-permute-done.3 = bf16[4,16384]{1,0:T(4,128)(2,1)S(1)} collective-permute-done((bf16[4,16384]{1,0:T(4,128)(2,1)S(1)}, bf16[4,16384]{1,0:T(4,128)(2,1)S(1)}, u32[]{:S(2)}, u32[]{:S(2)}) %collective-permute-start.3) | collective-permute-done | bytes 131104 | tf_op jit(solution)/shard_map/ppermute | solution.py:26
  28.4 0.1 slice_bitcast_fusion.2
  28.5 0.1 abs_reduce_fusion
  28.7 0.2 multiply_reduce_fusion
  28.9 0.1 fusion.37
  29.0 0.0 copy-done.3
  29.0 0.4 fusion.3
  29.4 0.8 %collective-permute-start.4 = (bf16[4,16384]{1,0:T(4,128)(2,1)S(1)}, bf16[4,16384]{1,0:T(4,128)(2,1)S(1)}, u32[]{:S(2)}, u32[]{:S(2)}) collective-permute-start(bf16[4,16384]{1,0:T(4,128)(2,1)S(1)} %fusion.3), channel_id=1, source_target_pairs={{0,4},{1,3},{2,6},{3,1},{4,0},{5,7},{6,2},{7,5},{8,12},{9,11},{10,... | collective-permute-start | bytes 393224 | tf_op jit(solution)/shard_map/ppermute | solution.py:26
  30.2 5.2 %collective-permute-done.4 = bf16[4,16384]{1,0:T(4,128)(2,1)S(1)} collective-permute-done((bf16[4,16384]{1,0:T(4,128)(2,1)S(1)}, bf16[4,16384]{1,0:T(4,128)(2,1)S(1)}, u32[]{:S(2)}, u32[]{:S(2)}) %collective-permute-start.4) | collective-permute-done | bytes 131104 | tf_op jit(solution)/shard_map/ppermute | solution.py:26
  35.4 0.1 pad_maximum_fusion.2
  35.5 2.1 %collective-permute-start.5 = (bf16[8,16384]{1,0:T(8,128)(2,1)S(1)}, bf16[8,16384]{1,0:T(8,128)(2,1)S(1)}, u32[]{:S(2)}, u32[]{:S(2)}) collective-permute-start(bf16[8,16384]{1,0:T(8,128)(2,1)S(1)} %pad_maximum_fusion.2), channel_id=1, source_target_pairs={{0,2},{1,5},{2,0},{3,7},{4,6},{5,1},{6,4},{7,3},{8,10},{9,13},{10,... | collective-permute-start | bytes 786440 | tf_op jit(solution)/shard_map/ppermute | solution.py:26
  37.6 0.6 %slice.53 = f32[2,128]{1,0:T(2,128)} slice(f32[4,128]{1,0:T(4,128)S(1)} %broadcast_add_fusion), slice={[0:2], [0:128]} | slice | bytes 2048 | tf_op jit(solution)/shard_map/slice | solution.py:80
  38.2 3.8 %collective-permute-done.5 = bf16[8,16384]{1,0:T(8,128)(2,1)S(1)} collective-permute-done((bf16[8,16384]{1,0:T(8,128)(2,1)S(1)}, bf16[8,16384]{1,0:T(8,128)(2,1)S(1)}, u32[]{:S(2)}, u32[]{:S(2)}) %collective-permute-start.5) | collective-permute-done | bytes 262176 | tf_op jit(solution)/shard_map/ppermute | solution.py:26
  42.0 0.2 pad_maximum_fusion
  42.2 0.1 collective-permute-start.6
  42.3 0.7 %copy.22 = bf16[1,2,128,128]{3,1,2,0:T(2,128)(2,1)} copy(bf16[1,2,128,128]{3,2,1,0:T(8,128)(2,1)S(1)} %slice_bitcast_fusion) | data formatting | bytes 131072
  43.0 0.0 copy-done.2
  43.0 0.7 %convolution_convert_fusion.5 = bf16[16,128]{1,0:T(8,128)(2,1)S(1)} fusion(bf16[16384,128]{1,0:T(8,128)(2,1)S(1)} %copy-done.2, bf16[8,16384]{1,0:T(8,128)(2,1)S(1)} %collective-permute-done.5, bf16[4,16384]{1,0:T(4,128)(2,1)S(1)} %collective-permute-done.4, bf16[4,16384]{1,0:T(4,128)(2,1)S(1)} %fusion.3), kind=kOutput, calls=%fused_computation.7 | convolution fusion | flops 68683776 | bytes 4722688 | tf_op jit(solution)/shard_map/dot_general | solution.py:74
  43.7 0.4 collective-permute-done.6
  44.2 0.7 %convolution_convert_fusion.4 = bf16[16,128]{1,0:T(8,128)(2,1)S(1)} fusion(bf16[16,16384]{1,0:T(8,128)(2,1)S(1)} %collective-permute-done.6, bf16[16384,128]{1,0:T(8,128)(2,1)S(1)} %copy-done.2), kind=kOutput, calls=%fused_computation.6 | convolution fusion | flops 67110912 | bytes 4722688 | tf_op jit(solution)/shard_map/dot_general | solution.py:75
  44.8 0.7 %convolution_convert_fusion.1 = bf16[32,128]{1,0:T(8,128)(2,1)} fusion(bf16[16,128]{1,0:T(8,128)(2,1)S(1)} %convolution_convert_fusion.4, bf16[16,128]{1,0:T(8,128)(2,1)S(1)} %convolution_convert_fusion.5, s32[32]{0:T(128)S(1)} %fusion.22), kind=kOutput, calls=%fused_computation.3 | convolution fusion | flops 283648 | bytes 16512 | tf_op jit(solution)/shard_map/dot_general | solution.py:77
  (10 shorter events, 0.2 us)
Async XLA Ops:
  0.6 1.2 %copy-start = (bf16[32,1024]{1,0:T(8,128)(2,1)S(1)}, bf16[32,1024]{1,0:T(8,128)(2,1)}, u32[]{:S(2)}) copy-start(bf16[32,1024]{1,0:T(8,128)(2,1)} %param.10) | copy-start | bytes 196612
  1.7 5.3 %copy-start.1 = (bf16[128,16384]{1,0:T(8,128)(2,1)S(1)}, bf16[128,16384]{1,0:T(8,128)(2,1)}, u32[]{:S(2)}) copy-start(bf16[128,16384]{1,0:T(8,128)(2,1)} %param.11) | copy-start | bytes 12582916
  5.0 15.4 %copy-start.4 = (bf16[2,16384]{1,0:T(2,128)(2,1)S(1)}, bf16[2,16384]{1,0:T(2,128)(2,1)}, u32[]{:S(2)}) copy-start(bf16[2,16384]{1,0:T(2,128)(2,1)} %param.7) | copy-start | bytes 196612
  5.0 2.1 %collective-permute-start = (bf16[16,16384]{1,0:T(8,128)(2,1)S(1)}, bf16[16,16384]{1,0:T(8,128)(2,1)S(1)}, u32[]{:S(2)}, u32[]{:S(2)}) collective-permute-start(bf16[16,16384]{1,0:T(8,128)(2,1)S(1)} %convolution_convert_fusion), channel_id=1, source_target_pairs={{0,1},{1,0},{2,3},{3,2},{4,5},{5,4},{6,7},{7,6},{8,9},{9,8},{10,11... | collective-permute-start | bytes 1572872 | tf_op jit(solution)/shard_map/ppermute | solution.py:26
  7.7 21.3 %copy-start.3 = (f32[16384]{0:T(1024)S(1)}, f32[16384]{0:T(1024)}, u32[]{:S(2)}) copy-start(f32[16384]{0:T(1024)} %param.12) | copy-start | bytes 196612
  7.7 7.3 %collective-permute-start.1 = (bf16[8,16384]{1,0:T(8,128)(2,1)S(1)}, bf16[8,16384]{1,0:T(8,128)(2,1)S(1)}, u32[]{:S(2)}, u32[]{:S(2)}) collective-permute-start(bf16[8,16384]{1,0:T(8,128)(2,1)S(1)} %slice.80), channel_id=1, source_target_pairs={{0,2},{1,5},{2,0},{3,7},{4,6},{5,1},{6,4},{7,3},{8,10},{9,13},{10,... | collective-permute-start | bytes 786440 | tf_op jit(solution)/shard_map/ppermute | solution.py:26
  15.2 27.8 %copy-start.2 = (bf16[16384,128]{1,0:T(8,128)(2,1)S(1)}, bf16[16384,128]{1,0:T(8,128)(2,1)}, u32[]{:S(2)}) copy-start(bf16[16384,128]{1,0:T(8,128)(2,1)} %param.13) | copy-start | bytes 12582916
  15.2 5.1 %collective-permute-start.2 = (bf16[4,16384]{1,0:T(4,128)(2,1)S(1)}, bf16[4,16384]{1,0:T(4,128)(2,1)S(1)}, u32[]{:S(2)}, u32[]{:S(2)}) collective-permute-start(bf16[4,16384]{1,0:T(4,128)(2,1)S(1)} %slice.81), channel_id=1, source_target_pairs={{0,4},{1,3},{2,6},{3,1},{4,0},{5,7},{6,2},{7,5},{8,12},{9,11},{10,... | collective-permute-start | bytes 393224 | tf_op jit(solution)/shard_map/ppermute | solution.py:26
  20.6 7.7 %collective-permute-start.3 = (bf16[4,16384]{1,0:T(4,128)(2,1)S(1)}, bf16[4,16384]{1,0:T(4,128)(2,1)S(1)}, u32[]{:S(2)}, u32[]{:S(2)}) collective-permute-start(bf16[4,16384]{1,0:T(4,128)(2,1)S(1)} %fusion.5), channel_id=1, source_target_pairs={{0,8},{1,9},{2,10},{3,11},{4,12},{5,13},{6,14},{7,15},{8,0},{9,1},... | collective-permute-start | bytes 393224 | tf_op jit(solution)/shard_map/ppermute | solution.py:26
  29.4 6.0 %collective-permute-start.4 = (bf16[4,16384]{1,0:T(4,128)(2,1)S(1)}, bf16[4,16384]{1,0:T(4,128)(2,1)S(1)}, u32[]{:S(2)}, u32[]{:S(2)}) collective-permute-start(bf16[4,16384]{1,0:T(4,128)(2,1)S(1)} %fusion.3), channel_id=1, source_target_pairs={{0,4},{1,3},{2,6},{3,1},{4,0},{5,7},{6,2},{7,5},{8,12},{9,11},{10,... | collective-permute-start | bytes 393224 | tf_op jit(solution)/shard_map/ppermute | solution.py:26
  35.5 6.5 %collective-permute-start.5 = (bf16[8,16384]{1,0:T(8,128)(2,1)S(1)}, bf16[8,16384]{1,0:T(8,128)(2,1)S(1)}, u32[]{:S(2)}, u32[]{:S(2)}) collective-permute-start(bf16[8,16384]{1,0:T(8,128)(2,1)S(1)} %pad_maximum_fusion.2), channel_id=1, source_target_pairs={{0,2},{1,5},{2,0},{3,7},{4,6},{5,1},{6,4},{7,3},{8,10},{9,13},{10,... | collective-permute-start | bytes 786440 | tf_op jit(solution)/shard_map/ppermute | solution.py:26
  42.2 2.0 %collective-permute-start.6 = (bf16[16,16384]{1,0:T(8,128)(2,1)S(1)}, bf16[16,16384]{1,0:T(8,128)(2,1)S(1)}, u32[]{:S(2)}, u32[]{:S(2)}) collective-permute-start(bf16[16,16384]{1,0:T(8,128)(2,1)S(1)} %pad_maximum_fusion), channel_id=1, source_target_pairs={{0,1},{1,0},{2,3},{3,2},{4,5},{5,4},{6,7},{7,6},{8,9},{9,8},{10,11... | collective-permute-start | bytes 1572872 | tf_op jit(solution)/shard_map/ppermute | solution.py:26

commit v5 on v4

--- a/solution.py
+++ b/solution.py
@@ -13,24 +13,23 @@
 def on_device(residual, queries, key_rows, value_rows, out_weight, norm_gain, q_weight):
     n = lax.axis_size("tp")
     device = lax.axis_index("tp")
-    core = device % 2
     tokens = queries.shape[0]
     local = residual.shape[0]
     D = residual.shape[1]
     heads = queries.shape[1] // HD
     group = heads * n // (key_rows.shape[1] // HD)
-    levels = [(2, 4), (4, 2)] + [(1 << b, 1 << b) for b in range(3, n.bit_length() - 1)]
-    bits = [(1, 1)] + levels
+    square = (4, 2, 6)
+    levels = [1 << b for b in range(3, n.bit_length() - 1)]
+    bits = [1, 2, 4] + levels
 
-    def swap(x, level):
-        return lax.ppermute(x, "tp", [(i, i ^ level[i % 2]) for i in range(n)])
+    def swap(x, distance):
+        return lax.ppermute(x, "tp", [(i, i ^ distance) for i in range(n)])
 
     row = jnp.arange(tokens)
     block = row // local
-    side = (core + block // (n // 2)) % 2
     distance = 0
-    for place, (even, odd) in enumerate(bits):
-        distance += (block >> (len(bits) - 1 - place)) % 2 * jnp.where(side == 0, even, odd)
+    for place, bit in enumerate(bits):
+        distance += (block >> (len(bits) - 1 - place)) % 2 * bit
     token = (device ^ distance) * local + row % local
     pick = (token[:, None] == row[None, :]).astype(BF16)
     queries = jnp.dot(pick, queries, preferred_element_type=F32).astype(BF16)
@@ -52,9 +51,16 @@
     context = jnp.concatenate(contexts, axis=1)
     half = tokens // 2
     sent = jnp.dot(context[half:], out_weight, preferred_element_type=F32)
-    got = swap(sent.astype(BF16), bits[0])
+    got = swap(sent.astype(BF16), 1)
     total = jnp.dot(context[:half], out_weight, preferred_element_type=F32)
     total = total + got.astype(F32)
+    part = half // 4
+    arrived = [
+        swap(total[k * part : (k + 1) * part].astype(BF16), d) for k, d in enumerate(square, 1)
+    ]
+    total = total[:part]
+    for piece in arrived:
+        total = total + piece.astype(F32)
     for level in levels[:-1]:
         kept = total.shape[0] // 2
         total = total[:kept] + swap(total[kept:].astype(BF16), level).astype(F32)
@@ -70,7 +76,8 @@
     held = (decoded * lax.rsqrt(mean_sq + 1e-05) * norm_gain[None, :]).astype(BF16)
     for level in levels[-2::-1]:
         held = jnp.concatenate([held, swap(held, level)], axis=0)
-    other = swap(held, bits[0])
+    held = jnp.concatenate([held] + [swap(held, d) for d in square], axis=0)
+    other = swap(held, 1)
     out_mine = jnp.dot(held, q_weight, preferred_element_type=F32).astype(BF16)
     out_other = jnp.dot(other, q_weight, preferred_element_type=F32).astype(BF16)
     found = jnp.concatenate([out_mine, out_other], axis=0)

time: 45.7 us -> 41.7 us (0.912)
  waiting for transfers between devices: 22.8 us -> 19 us
    ppermute x7 -> x9, waiting for transfers between devices: 22.8 us -> 19 us  [swap(): return lax.ppermute(x, 'tp', [(i, i ^ distance) for i in range(n)])]
    ppermute x7 -> x9, starting transfers between devices: 11.7 us -> 11.3 us  [swap(): return lax.ppermute(x, 'tp', [(i, i ^ distance) for i in range(n)])]
  transfers between devices with their start and end apart: 7 -> 9, of which waited for: 7 -> 8; matrix products, arithmetic and copies ran while one was open for 4% -> 5% of each run, Pallas kernels for 0% -> 0%
where the time goes in v5:
time: 41.7 us; the launch traced here: 41.5 us
  waiting for transfers between devices  19 us (46%)
  starting transfers between devices  11.3 us (27%)
  matrix products  7.08 us (17%)
  local copies, waits for them, and re-layouts  1.69 us (4%)
  other arithmetic  1.57 us (4%)
  between operations  0.81 us (2%)
    ppermute x9, waiting for transfers between devices, swap(): return lax.ppermute(x, 'tp', [(i, i ^ distance) for i in range(n)])  19 us
    ppermute x9, starting transfers between devices, swap(): return lax.ppermute(x, 'tp', [(i, i ^ distance) for i in range(n)])  11.3 us
    dot_general x1, matrix products, on_device(): sent = jnp.dot(context[half:], out_weight, preferred_element_type=F32)  2.99 us
    dot_general x1, matrix products, on_device(): lax.dot_general(queries[:, h * HD:(h + 1) * HD], key_head, (((1,), (1,)),...  1.04 us
    unnamed x13, local copies, waits for them, and re-layouts  0.84 us
  transfers between devices with their start and end apart: 9, of which 8 were waited for; matrix products, arithmetic and copies ran while one was open for 5% of the time, Pallas kernels for 0%

profile of v5, /device:TPU:0, one launch (start us, length us, event | category | flops | bytes accessed | tf_op | source)
XLA Modules:
  0.0 41.5 jit_solution(4279505099488563833)
XLA Ops:
  0.6 0.0 copy-start
  0.7 1.0 %fusion.40 = (f32[32]{0:T(128)S(1)}, f32[32,32]{0,1:T(8,128)S(1)}) fusion(bf16[32,1024]{1,0:T(8,128)(2,1)} %param.9, s32[]{:T(128)S(6)} %select_n.71, bf16[32,128]{1,0:T(8,128)(2,1)} %param.8, s32[32]{0:T(128)S(1)} %fusion.24), kind=kOutput, calls=%fused_computation.89 | convolution fusion | flops 533472 | bytes 21636 | tf_op jit(solution)/shard_map/dot_general | solution.py:42
  1.7 0.0 copy-start.1
  1.8 0.0 copy-done
  1.8 0.2 convolution_convert_fusion.2
  2.0 3.0 %convolution_convert_fusion = bf16[16,16384]{1,0:T(8,128)(2,1)S(1)} fusion(bf16[128,16384]{1,0:T(8,128)(2,1)} %param.11, bf16[32,128]{1,0:T(8,128)(2,1)S(1)} %convolution_convert_fusion.2), kind=kOutput, calls=%fused_computation | convolution fusion | flops 67371008 | bytes 4722688 | tf_op jit(solution)/shard_map/dot_general | solution.py:53
  5.0 0.0 copy-start.4
  5.0 0.5 %collective-permute-start = (bf16[16,16384]{1,0:T(8,128)(2,1)S(1)}, bf16[16,16384]{1,0:T(8,128)(2,1)S(1)}, u32[]{:S(2)}, u32[]{:S(2)}) collective-permute-start(bf16[16,16384]{1,0:T(8,128)(2,1)S(1)} %convolution_convert_fusion), channel_id=1, source_target_pairs={{0,1},{1,0},{2,3},{3,2},{4,5},{5,4},{6,7},{7,6},{8,9},{9,8},{10,11... | collective-permute-start | bytes 1572872 | tf_op jit(solution)/shard_map/ppermute | solution.py:26
  5.5 1.5 %collective-permute-done = bf16[16,16384]{1,0:T(8,128)(2,1)S(1)} collective-permute-done((bf16[16,16384]{1,0:T(8,128)(2,1)S(1)}, bf16[16,16384]{1,0:T(8,128)(2,1)S(1)}, u32[]{:S(2)}, u32[]{:S(2)}) %collective-permute-start) | collective-permute-done | bytes 524320 | tf_op jit(solution)/shard_map/ppermute | solution.py:26
  7.0 0.0 copy-done.1
  7.0 0.7 %fusion.41 = (bf16[16,16384]{1,0:T(8,128)(2,1)S(1)}, f32[16,16384]{1,0:T(8,128)S(1)}) fusion(bf16[16,16384]{1,0:T(8,128)(2,1)S(1)} %collective-permute-done, bf16[128,16384]{1,0:T(8,128)(2,1)S(1)} %copy-done.1, bf16[32,128]{1,0:T(8,128)(2,1)S(1)} %convolution_convert_fusion.2), kind=kOutput, calls=%fused_computation.90 | convolution fusion | flops 67895296 | bytes 6295552 | tf_op jit(solution)/shard_map/dot_general | solution.py:55
  7.7 0.0 copy-start.3
  7.7 0.2 fusion.38
  7.9 0.0 copy-start.2
  7.9 3.0 %collective-permute-start.1 = (bf16[4,16384]{1,0:T(4,128)(2,1)S(1)}, bf16[4,16384]{1,0:T(4,128)(2,1)S(1)}, u32[]{:S(2)}, u32[]{:S(2)}) collective-permute-start(bf16[4,16384]{1,0:T(4,128)(2,1)S(1)} %get-tuple-element.5), channel_id=1, source_target_pairs={{0,4},{1,5},{2,6},{3,7},{4,0},{5,1},{6,2},{7,3},{8,12},{9,13},{10,... | collective-permute-start | bytes 393224 | tf_op jit(solution)/shard_map/ppermute | solution.py:26
  10.9 1.4 %collective-permute-start.3 = (bf16[4,16384]{1,0:T(4,128)(2,1)S(1)}, bf16[4,16384]{1,0:T(4,128)(2,1)S(1)}, u32[]{:S(2)}, u32[]{:S(2)}) collective-permute-start(bf16[4,16384]{1,0:T(4,128)(2,1)S(1)} %get-tuple-element.6), channel_id=1, source_target_pairs={{0,6},{1,7},{2,4},{3,5},{4,2},{5,3},{6,0},{7,1},{8,14},{9,15},{10,... | collective-permute-start | bytes 393224 | tf_op jit(solution)/shard_map/ppermute | solution.py:26
  12.3 0.1 collective-permute-start.2
  12.4 2.6 %collective-permute-done.1 = bf16[4,16384]{1,0:T(4,128)(2,1)S(1)} collective-permute-done((bf16[4,16384]{1,0:T(4,128)(2,1)S(1)}, bf16[4,16384]{1,0:T(4,128)(2,1)S(1)}, u32[]{:S(2)}, u32[]{:S(2)}) %collective-permute-start.1) | collective-permute-done | bytes 131104 | tf_op jit(solution)/shard_map/ppermute | solution.py:26
  15.0 3.7 %collective-permute-done.3 = bf16[4,16384]{1,0:T(4,128)(2,1)S(1)} collective-permute-done((bf16[4,16384]{1,0:T(4,128)(2,1)S(1)}, bf16[4,16384]{1,0:T(4,128)(2,1)S(1)}, u32[]{:S(2)}, u32[]{:S(2)}) %collective-permute-start.3) | collective-permute-done | bytes 131104 | tf_op jit(solution)/shard_map/ppermute | solution.py:26
  18.7 1.4 %collective-permute-done.2 = bf16[4,16384]{1,0:T(4,128)(2,1)S(1)} collective-permute-done((bf16[4,16384]{1,0:T(4,128)(2,1)S(1)}, bf16[4,16384]{1,0:T(4,128)(2,1)S(1)}, u32[]{:S(2)}, u32[]{:S(2)}) %collective-permute-start.2) | collective-permute-done | bytes 131104 | tf_op jit(solution)/shard_map/ppermute | solution.py:26
  20.1 0.1 fusion.5
  20.2 0.0 copy-done.4
  20.2 0.1 slice_bitcast_fusion.3
  20.4 0.1 fusion.7
  20.5 2.6 %collective-permute-start.4 = (bf16[4,16384]{1,0:T(4,128)(2,1)S(1)}, bf16[4,16384]{1,0:T(4,128)(2,1)S(1)}, u32[]{:S(2)}, u32[]{:S(2)}) collective-permute-start(bf16[4,16384]{1,0:T(4,128)(2,1)S(1)} %fusion.7), channel_id=1, source_target_pairs={{0,8},{1,9},{2,10},{3,11},{4,12},{5,13},{6,14},{7,15},{8,0},{9,1},... | collective-permute-start | bytes 393224 | tf_op jit(solution)/shard_map/ppermute | solution.py:26
  23.2 5.6 %collective-permute-done.4 = bf16[4,16384]{1,0:T(4,128)(2,1)S(1)} collective-permute-done((bf16[4,16384]{1,0:T(4,128)(2,1)S(1)}, bf16[4,16384]{1,0:T(4,128)(2,1)S(1)}, u32[]{:S(2)}, u32[]{:S(2)}) %collective-permute-start.4) | collective-permute-done | bytes 131104 | tf_op jit(solution)/shard_map/ppermute | solution.py:26
  28.8 0.1 slice_bitcast_fusion.2
  28.9 0.1 abs_reduce_fusion
  29.1 0.2 multiply_reduce_fusion
  29.3 0.1 fusion.39
  29.4 0.0 copy-done.3
  29.4 0.4 fusion.3
  29.9 0.5 %collective-permute-start.7 = (bf16[4,16384]{1,0:T(4,128)(2,1)S(1)}, bf16[4,16384]{1,0:T(4,128)(2,1)S(1)}, u32[]{:S(2)}, u32[]{:S(2)}) collective-permute-start(bf16[4,16384]{1,0:T(4,128)(2,1)S(1)} %fusion.3), channel_id=1, source_target_pairs={{0,6},{1,7},{2,4},{3,5},{4,2},{5,3},{6,0},{7,1},{8,14},{9,15},{10,... | collective-permute-start | bytes 393224 | tf_op jit(solution)/shard_map/ppermute | solution.py:26
  30.4 1.7 %collective-permute-start.6 = (bf16[4,16384]{1,0:T(4,128)(2,1)S(1)}, bf16[4,16384]{1,0:T(4,128)(2,1)S(1)}, u32[]{:S(2)}, u32[]{:S(2)}) collective-permute-start(bf16[4,16384]{1,0:T(4,128)(2,1)S(1)} %fusion.3), channel_id=1, source_target_pairs={{0,2},{1,3},{2,0},{3,1},{4,6},{5,7},{6,4},{7,5},{8,10},{9,11},{10,... | collective-permute-start | bytes 393224 | tf_op jit(solution)/shard_map/ppermute | solution.py:26
  32.0 1.4 %collective-permute-start.5 = (bf16[4,16384]{1,0:T(4,128)(2,1)S(1)}, bf16[4,16384]{1,0:T(4,128)(2,1)S(1)}, u32[]{:S(2)}, u32[]{:S(2)}) collective-permute-start(bf16[4,16384]{1,0:T(4,128)(2,1)S(1)} %fusion.3), channel_id=1, source_target_pairs={{0,4},{1,5},{2,6},{3,7},{4,0},{5,1},{6,2},{7,3},{8,12},{9,13},{10,... | collective-permute-start | bytes 393224 | tf_op jit(solution)/shard_map/ppermute | solution.py:26
  33.4 0.6 %slice.54 = f32[2,128]{1,0:T(2,128)} slice(f32[4,128]{1,0:T(4,128)S(1)} %broadcast_add_fusion), slice={[0:2], [0:128]} | slice | bytes 2048 | tf_op jit(solution)/shard_map/slice | solution.py:87
  34.0 2.7 %collective-permute-done.7 = bf16[4,16384]{1,0:T(4,128)(2,1)S(1)} collective-permute-done((bf16[4,16384]{1,0:T(4,128)(2,1)S(1)}, bf16[4,16384]{1,0:T(4,128)(2,1)S(1)}, u32[]{:S(2)}, u32[]{:S(2)}) %collective-permute-start.7) | collective-permute-done | bytes 131104 | tf_op jit(solution)/shard_map/ppermute | solution.py:26
  36.7 1.1 %collective-permute-done.6 = bf16[4,16384]{1,0:T(4,128)(2,1)S(1)} collective-permute-done((bf16[4,16384]{1,0:T(4,128)(2,1)S(1)}, bf16[4,16384]{1,0:T(4,128)(2,1)S(1)}, u32[]{:S(2)}, u32[]{:S(2)}) %collective-permute-start.6) | collective-permute-done | bytes 131104 | tf_op jit(solution)/shard_map/ppermute | solution.py:26
  37.8 0.0 collective-permute-done.5
  37.8 0.3 pad_maximum_fusion
  38.1 0.1 collective-permute-start.8
  38.2 0.7 %copy.22 = bf16[1,2,128,128]{3,1,2,0:T(2,128)(2,1)} copy(bf16[1,2,128,128]{3,2,1,0:T(8,128)(2,1)S(1)} %slice_bitcast_fusion) | data formatting | bytes 131072
  38.9 0.0 copy-done.2
  38.9 0.8 %convolution_convert_fusion.5 = bf16[16,128]{1,0:T(8,128)(2,1)S(1)} fusion(bf16[16384,128]{1,0:T(8,128)(2,1)S(1)} %copy-done.2, bf16[4,16384]{1,0:T(4,128)(2,1)S(1)} %collective-permute-done.7, bf16[4,16384]{1,0:T(4,128)(2,1)S(1)} %collective-permute-done.6, bf16[4,16384]{1,0:T(4,128)(2,1)S(1)} %collective-permute-done.5, bf16[4,16384]{1,0:T(4,128)(2,1)S(1)} %fusion.3), kind=kOutput, calls=%fused_computation.7 | convolution fusion | flops 69208064 | bytes 4722688 | tf_op jit(solution)/shard_map/dot_general | solution.py:81
  39.7 0.4 collective-permute-done.8
  40.1 0.7 %convolution_convert_fusion.4 = bf16[16,128]{1,0:T(8,128)(2,1)S(1)} fusion(bf16[16,16384]{1,0:T(8,128)(2,1)S(1)} %collective-permute-done.8, bf16[16384,128]{1,0:T(8,128)(2,1)S(1)} %copy-done.2), kind=kOutput, calls=%fused_computation.6 | convolution fusion | flops 67110912 | bytes 4722688 | tf_op jit(solution)/shard_map/dot_general | solution.py:82
  40.8 0.7 %convolution_convert_fusion.1 = bf16[32,128]{1,0:T(8,128)(2,1)} fusion(bf16[16,128]{1,0:T(8,128)(2,1)S(1)} %convolution_convert_fusion.4, bf16[16,128]{1,0:T(8,128)(2,1)S(1)} %convolution_convert_fusion.5, s32[32]{0:T(128)S(1)} %fusion.24), kind=kOutput, calls=%fused_computation.3 | convolution fusion | flops 283648 | bytes 16512 | tf_op jit(solution)/shard_map/dot_general | solution.py:84
  (8 shorter events, 0.1 us)
Async XLA Ops:
  0.6 1.1 %copy-start = (bf16[32,1024]{1,0:T(8,128)(2,1)S(1)}, bf16[32,1024]{1,0:T(8,128)(2,1)}, u32[]{:S(2)}) copy-start(bf16[32,1024]{1,0:T(8,128)(2,1)} %param.10) | copy-start | bytes 196612
  1.7 5.3 %copy-start.1 = (bf16[128,16384]{1,0:T(8,128)(2,1)S(1)}, bf16[128,16384]{1,0:T(8,128)(2,1)}, u32[]{:S(2)}) copy-start(bf16[128,16384]{1,0:T(8,128)(2,1)} %param.11) | copy-start | bytes 12582916
  5.0 15.2 %copy-start.4 = (bf16[2,16384]{1,0:T(2,128)(2,1)S(1)}, bf16[2,16384]{1,0:T(2,128)(2,1)}, u32[]{:S(2)}) copy-start(bf16[2,16384]{1,0:T(2,128)(2,1)} %param.7) | copy-start | bytes 196612
  5.0 2.1 %collective-permute-start = (bf16[16,16384]{1,0:T(8,128)(2,1)S(1)}, bf16[16,16384]{1,0:T(8,128)(2,1)S(1)}, u32[]{:S(2)}, u32[]{:S(2)}) collective-permute-start(bf16[16,16384]{1,0:T(8,128)(2,1)S(1)} %convolution_convert_fusion), channel_id=1, source_target_pairs={{0,1},{1,0},{2,3},{3,2},{4,5},{5,4},{6,7},{7,6},{8,9},{9,8},{10,11... | collective-permute-start | bytes 1572872 | tf_op jit(solution)/shard_map/ppermute | solution.py:26
  7.7 21.8 %copy-start.3 = (f32[16384]{0:T(1024)S(1)}, f32[16384]{0:T(1024)}, u32[]{:S(2)}) copy-start(f32[16384]{0:T(1024)} %param.12) | copy-start | bytes 196612
  7.9 31.1 %copy-start.2 = (bf16[16384,128]{1,0:T(8,128)(2,1)S(1)}, bf16[16384,128]{1,0:T(8,128)(2,1)}, u32[]{:S(2)}) copy-start(bf16[16384,128]{1,0:T(8,128)(2,1)} %param.13) | copy-start | bytes 12582916
  7.9 7.1 %collective-permute-start.1 = (bf16[4,16384]{1,0:T(4,128)(2,1)S(1)}, bf16[4,16384]{1,0:T(4,128)(2,1)S(1)}, u32[]{:S(2)}, u32[]{:S(2)}) collective-permute-start(bf16[4,16384]{1,0:T(4,128)(2,1)S(1)} %get-tuple-element.5), channel_id=1, source_target_pairs={{0,4},{1,5},{2,6},{3,7},{4,0},{5,1},{6,2},{7,3},{8,12},{9,13},{10,... | collective-permute-start | bytes 393224 | tf_op jit(solution)/shard_map/ppermute | solution.py:26
  10.9 7.8 %collective-permute-start.3 = (bf16[4,16384]{1,0:T(4,128)(2,1)S(1)}, bf16[4,16384]{1,0:T(4,128)(2,1)S(1)}, u32[]{:S(2)}, u32[]{:S(2)}) collective-permute-start(bf16[4,16384]{1,0:T(4,128)(2,1)S(1)} %get-tuple-element.6), channel_id=1, source_target_pairs={{0,6},{1,7},{2,4},{3,5},{4,2},{5,3},{6,0},{7,1},{8,14},{9,15},{10,... | collective-permute-start | bytes 393224 | tf_op jit(solution)/shard_map/ppermute | solution.py:26
  12.3 7.8 %collective-permute-start.2 = (bf16[4,16384]{1,0:T(4,128)(2,1)S(1)}, bf16[4,16384]{1,0:T(4,128)(2,1)S(1)}, u32[]{:S(2)}, u32[]{:S(2)}) collective-permute-start(bf16[4,16384]{1,0:T(4,128)(2,1)S(1)} %get-tuple-element.7), channel_id=1, source_target_pairs={{0,2},{1,3},{2,0},{3,1},{4,6},{5,7},{6,4},{7,5},{8,10},{9,11},{10,... | collective-permute-start | bytes 393224 | tf_op jit(solution)/shard_map/ppermute | solution.py:26
  20.5 8.3 %collective-permute-start.4 = (bf16[4,16384]{1,0:T(4,128)(2,1)S(1)}, bf16[4,16384]{1,0:T(4,128)(2,1)S(1)}, u32[]{:S(2)}, u32[]{:S(2)}) collective-permute-start(bf16[4,16384]{1,0:T(4,128)(2,1)S(1)} %fusion.7), channel_id=1, source_target_pairs={{0,8},{1,9},{2,10},{3,11},{4,12},{5,13},{6,14},{7,15},{8,0},{9,1},... | collective-permute-start | bytes 393224 | tf_op jit(solution)/shard_map/ppermute | solution.py:26
  29.9 6.9 %collective-permute-start.7 = (bf16[4,16384]{1,0:T(4,128)(2,1)S(1)}, bf16[4,16384]{1,0:T(4,128)(2,1)S(1)}, u32[]{:S(2)}, u32[]{:S(2)}) collective-permute-start(bf16[4,16384]{1,0:T(4,128)(2,1)S(1)} %fusion.3), channel_id=1, source_target_pairs={{0,6},{1,7},{2,4},{3,5},{4,2},{5,3},{6,0},{7,1},{8,14},{9,15},{10,... | collective-permute-start | bytes 393224 | tf_op jit(solution)/shard_map/ppermute | solution.py:26
  30.4 7.4 %collective-permute-start.6 = (bf16[4,16384]{1,0:T(4,128)(2,1)S(1)}, bf16[4,16384]{1,0:T(4,128)(2,1)S(1)}, u32[]{:S(2)}, u32[]{:S(2)}) collective-permute-start(bf16[4,16384]{1,0:T(4,128)(2,1)S(1)} %fusion.3), channel_id=1, source_target_pairs={{0,2},{1,3},{2,0},{3,1},{4,6},{5,7},{6,4},{7,5},{8,10},{9,11},{10,... | collective-permute-start | bytes 393224 | tf_op jit(solution)/shard_map/ppermute | solution.py:26
  32.0 5.8 %collective-permute-start.5 = (bf16[4,16384]{1,0:T(4,128)(2,1)S(1)}, bf16[4,16384]{1,0:T(4,128)(2,1)S(1)}, u32[]{:S(2)}, u32[]{:S(2)}) collective-permute-start(bf16[4,16384]{1,0:T(4,128)(2,1)S(1)} %fusion.3), channel_id=1, source_target_pairs={{0,4},{1,5},{2,6},{3,7},{4,0},{5,1},{6,2},{7,3},{8,12},{9,13},{10,... | collective-permute-start | bytes 393224 | tf_op jit(solution)/shard_map/ppermute | solution.py:26
  38.1 2.0 %collective-permute-start.8 = (bf16[16,16384]{1,0:T(8,128)(2,1)S(1)}, bf16[16,16384]{1,0:T(8,128)(2,1)S(1)}, u32[]{:S(2)}, u32[]{:S(2)}) collective-permute-start(bf16[16,16384]{1,0:T(8,128)(2,1)S(1)} %pad_maximum_fusion), channel_id=1, source_target_pairs={{0,1},{1,0},{2,3},{3,2},{4,5},{5,4},{6,7},{7,6},{8,9},{9,8},{10,11... | collective-permute-start | bytes 1572872 | tf_op jit(solution)/shard_map/ppermute | solution.py:26

commit v6 on v5

v6 whole, which is shorter than its diff:
```python
import functools

import jax
import jax.numpy as jnp
from jax import lax
from jax.experimental import pallas as pl
from jax.experimental.pallas import tpu as pltpu
from jax.sharding import PartitionSpec as P

HD = 128
QB = 128
EPS = 1e-06
F32 = jnp.float32
BF16 = jnp.bfloat16
CHUNKS = 8


def late_levels(n):
    return [1 << b for b in range(3, n.bit_length() - 1)]


def owner_token(row, device, n, local):
    bits = [(1, 1), (2, 4), (4, 2)] + [(d, d) for d in late_levels(n)]
    block = row // local
    side = (device + block // (n // 2)) % 2
    distance = jnp.zeros_like(row)
    for place, (even, odd) in enumerate(bits):
        bit = (block >> (len(bits) - 1 - place)) % 2
        distance = distance + bit * jnp.where(side == 0, even, odd)
    return (device ^ distance) * local + row % local


def project_kernel(n, local, queries, keys, values, weight, sent, kept, held, sems):
    device = lax.axis_index("tp")
    tokens = queries.shape[0]
    heads = queries.shape[1] // HD
    group = heads * n // (keys.shape[1] // HD)
    width = held.shape[1] // CHUNKS
    copies = []
    for c in range(CHUNKS):
        part = pl.ds(c * width, width)
        copies.append(pltpu.make_async_copy(weight.at[:, part], held.at[:, part], sems.at[c]))
        copies[-1].start()
    row = lax.broadcasted_iota(jnp.int32, (tokens, tokens), 0)
    col = lax.broadcasted_iota(jnp.int32, (tokens, tokens), 1)
    token = owner_token(row, device, n, local)
    pick = (token == col).astype(F32).astype(BF16)
    ordered = jnp.dot(pick, queries[...], preferred_element_type=F32).astype(BF16)
    contexts = []
    for h in range(heads):
        at = pl.ds(pl.multiple_of(lax.div(device * heads + h, group) * HD, HD), HD)
        scores = lax.dot_general(
            ordered[:, h * HD : (h + 1) * HD],
            keys[:, at],
            (((1,), (1,)), ((), ())),
            preferred_element_type=F32,
        ) / jnp.sqrt(F32(HD))
        scores = jnp.where(col <= token, scores, F32(-1e30))
        weights = jnp.exp(scores - jnp.max(scores, axis=1, keepdims=True))
        probs = (weights / jnp.sum(weights, axis=1, keepdims=True)).astype(BF16)
        contexts.append(
            jnp.dot(probs, values[:, at], preferred_element_type=F32).astype(BF16)
        )
    context = contexts[0] if heads == 1 else jnp.concatenate(contexts, axis=1)
    half = tokens // 2
    for c in range(CHUNKS):
        part = pl.ds(c * width, width)
        copies[c].wait()
        partial = jnp.dot(context, held[:, part], preferred_element_type=F32)
        kept[:, part] = partial[:half]
        sent[:, part] = partial[half:].astype(BF16)


def project(n, local, queries, keys, values, weight):
    tokens, D = queries.shape[0], weight.shape[1]
    half = tokens // 2
    whole = pl.BlockSpec(memory_space=pltpu.VMEM)
    return pl.pallas_call(
        functools.partial(project_kernel, n, local),
        out_shape=[
            jax.ShapeDtypeStruct((half, D), BF16),
            jax.ShapeDtypeStruct((half, D), F32),
        ],
        in_specs=[whole, whole, whole, pl.BlockSpec(memory_space=pltpu.HBM)],
        out_specs=[whole, whole],
        scratch_shapes=[
            pltpu.VMEM(weight.shape, BF16),
            pltpu.SemaphoreType.DMA((CHUNKS,)),
        ],
        compiler_params=pltpu.CompilerParams(vmem_limit_bytes=24 << 20),
        cost_estimate=pl.CostEstimate(
            flops=2 * tokens * weight.size, bytes_accessed=2 * weight.size, transcendentals=0
        ),
        name="project",
    )(queries, keys, values, weight)


def on_device(residual, queries, key_rows, value_rows, out_weight, norm_gain, q_weight):
    n = lax.axis_size("tp")
    device = lax.axis_index("tp")
    tokens = queries.shape[0]
    local = residual.shape[0]
    D = residual.shape[1]
    levels = late_levels(n)
    square = [(1, (4, 2)), (2, (2, 4)), (3, (6, 6))]

    def swap(x, even, odd):
        return lax.ppermute(x, "tp", [(i, i ^ (odd if i % 2 else even)) for i in range(n)])

    half = tokens // 2
    sent, total = project(n, local, queries, key_rows, value_rows, out_weight)
    total = total + swap(sent, 1, 1).astype(F32)
    part = half // 4
    arrived = [
        swap(total[k * part : (k + 1) * part].astype(BF16), *distance)
        for k, distance in square[::-1]
    ]
    total = total[:part]
    for piece in arrived:
        total = total + piece.astype(F32)
    for level in levels[:-1]:
        kept = total.shape[0] // 2
        total = total[:kept] + swap(total[kept:].astype(BF16), level, level).astype(F32)
    total = jnp.concatenate([total[:local] + residual.astype(F32), total[local:]], axis=0)
    got = swap(total.astype(BF16), levels[-1], levels[-1]).astype(F32)
    stream = total + jnp.concatenate([got[local:], got[:local]], axis=0)
    rows = stream.shape[0]
    grouped = stream.reshape(rows, D // QB, QB)
    scales = jnp.max(jnp.abs(grouped), axis=2) + EPS
    codes = (grouped / scales[:, :, None]).astype(BF16)
    decoded = (codes.astype(F32) * scales[:, :, None]).reshape(rows, D)
    mean_sq = jnp.mean(decoded * decoded, axis=1, keepdims=True)
    held = (decoded * lax.rsqrt(mean_sq + 1e-05) * norm_gain[None, :]).astype(BF16)
    for level in levels[-2::-1]:
        held = jnp.concatenate([held, swap(held, level, level)], axis=0)
    arrived = [swap(held, *distance) for _, distance in square[::-1]]
    held = jnp.concatenate([held] + arrived[::-1], axis=0)
    other = swap(held, 1, 1)
    out_mine = jnp.dot(held, q_weight, preferred_element_type=F32).astype(BF16)
    out_other = jnp.dot(other, q_weight, preferred_element_type=F32).astype(BF16)
    found = jnp.concatenate([out_mine, out_other], axis=0)
    row = jnp.arange(tokens)
    pick = (owner_token(row, device, n, local)[:, None] == row[None, :]).astype(BF16)
    next_queries = lax.dot_general(
        pick, found, (((0,), (0,)), ((), ())), preferred_element_type=F32
    ).astype(BF16)
    return (codes.reshape(rows, D)[:local], scales[:local], next_queries)


def solution(mesh):
    in_specs = (
        P(("replica", "tp"), None),
        P("replica", "tp"),
        P("replica", None),
        P("replica", None),
        P("tp", None),
        P(),
        P(None, "tp"),
    )
    out_specs = (P(("replica", "tp"), None), P(("replica", "tp"), None), P("replica", "tp"))
    return jax.shard_map(
        on_device, mesh=mesh, in_specs=in_specs, out_specs=out_specs, check_vma=False
    )
```

time: 41.7 us -> 46.3 us (1.11)
  local copies, waits for them, and re-layouts: 1.69 us -> 6.23 us
  Pallas kernels: 0 us -> 2.6 us
  matrix products: 7.08 us -> 4.52 us
    dot_general x4 -> x0, matrix products: 4.88 us -> none  [the longest x1 2.99 us: on_device(): sent = jnp.dot(context[half:], out_weight, preferred_element_type=F32)]
    unnamed x13 -> x17, local copies, waits for them, and re-layouts: 0.84 us -> 5.38 us
    pallas_call x0 -> x1, Pallas kernels: none -> 2.6 us  [project(): pl.pallas_call(functools.partial(project_kernel, n, local), out_shape=[ja...]
    dot_general x1, matrix products: 0.79 us -> 2.97 us  [on_device(): out_mine = jnp.dot(held, q_weight, preferred_element_type=F32).astype(BF16)]
  transfers between devices with their start and end apart: 9 -> 9, of which waited for: 8 -> 7; matrix products, arithmetic and copies ran while one was open for 5% -> 9% of each run, Pallas kernels for 0% -> 0%
where the time goes in v6:
time: 46.3 us; the launch traced here: 46 us
  waiting for transfers between devices  18.8 us (41%)
  starting transfers between devices  11.4 us (25%)
  local copies, waits for them, and re-layouts  6.23 us (13%)
  matrix products  4.52 us (10%)
  Pallas kernels  2.6 us (6%)
  other arithmetic  1.65 us (4%)
  between operations  0.77 us (2%)
    ppermute x9, waiting for transfers between devices, swap(): lax.ppermute(x, 'tp', [(i, i ^ (odd if i % 2 else even)) for i in range(n)])  18.8 us
    ppermute x9, starting transfers between devices, swap(): lax.ppermute(x, 'tp', [(i, i ^ (odd if i % 2 else even)) for i in range(n)])  11.4 us
    unnamed x17, local copies, waits for them, and re-layouts  5.38 us
    dot_general x1, matrix products, on_device(): out_mine = jnp.dot(held, q_weight, preferred_element_type=F32).astype(BF16)  2.97 us
    pallas_call x1, Pallas kernels, project(): pl.pallas_call(functools.partial(project_kernel, n, local), out_shape=[ja...  2.6 us
  transfers between devices with their start and end apart: 9, of which 7 were waited for; matrix products, arithmetic and copies ran while one was open for 9% of the time, Pallas kernels for 0%

profile of v6, /device:TPU:0, one launch (start us, length us, event | category | flops | bytes accessed | tf_op | source)
XLA Modules:
  0.0 46.0 jit_solution(13937954703287964639)
XLA Ops:
  0.6 0.0 copy-start
  0.6 2.2 %copy-done = bf16[128,16384]{1,0:T(8,128)(2,1)S(1)} copy-done((bf16[128,16384]{1,0:T(8,128)(2,1)S(1)}, bf16[128,16384]{1,0:T(8,128)(2,1)}, u32[]{:S(2)}) %copy-start) | copy-done | bytes 4194328
  2.8 0.0 copy-start.1
  2.8 0.8 %copy-done.1 = bf16[32,1024]{1,0:T(8,128)(2,1)S(1)} copy-done((bf16[32,1024]{1,0:T(8,128)(2,1)S(1)}, bf16[32,1024]{1,0:T(8,128)(2,1)}, u32[]{:S(2)}) %copy-start.1) | copy-done | bytes 65560
  3.7 0.0 copy-start.2
  3.7 0.8 %copy-done.2 = bf16[32,1024]{1,0:T(8,128)(2,1)S(1)} copy-done((bf16[32,1024]{1,0:T(8,128)(2,1)S(1)}, bf16[32,1024]{1,0:T(8,128)(2,1)}, u32[]{:S(2)}) %copy-start.2) | copy-done | bytes 65560
  4.5 0.0 copy-start.3
  4.5 0.7 %copy-done.3 = bf16[32,128]{1,0:T(8,128)(2,1)S(1)} copy-done((bf16[32,128]{1,0:T(8,128)(2,1)S(1)}, bf16[32,128]{1,0:T(8,128)(2,1)}, u32[]{:S(2)}) %copy-start.3) | copy-done | bytes 8216
  5.2 0.0 copy-start.6
  5.2 2.6 %project.1 = (bf16[16,16384]{1,0:T(8,128)(2,1)S(1)}, f32[16,16384]{1,0:T(8,128)S(1)}) custom-call(bf16[32,128]{1,0:T(8,128)(2,1)S(1)} %copy-done.3, bf16[32,1024]{1,0:T(8,128)(2,1)S(1)} %copy-done.1, bf16[32,1024]{1,0:T(8,128)(2,1)S(1)} %copy-done.2, bf16[128,16384]{1,0:T(8,128)(2,1)S(1)} %copy-done), custom_call_target="tpu_custom_call" | custom-call | flops 134217728 | bytes 4194304 | tf_op jit(solution)/shard_map/project/pallas_call | solution.py:78
  7.8 0.5 %collective-permute-start = (bf16[16,16384]{1,0:T(8,128)(2,1)S(1)}, bf16[16,16384]{1,0:T(8,128)(2,1)S(1)}, u32[]{:S(2)}, u32[]{:S(2)}) collective-permute-start(bf16[16,16384]{1,0:T(8,128)(2,1)S(1)} %get-tuple-element.6), channel_id=1, source_target_pairs={{0,1},{1,0},{2,3},{3,2},{4,5},{5,4},{6,7},{7,6},{8,9},{9,8},{10,11... | collective-permute-start | bytes 1572872 | tf_op jit(solution)/shard_map/ppermute | solution.py:108
  8.3 1.5 %collective-permute-done = bf16[16,16384]{1,0:T(8,128)(2,1)S(1)} collective-permute-done((bf16[16,16384]{1,0:T(8,128)(2,1)S(1)}, bf16[16,16384]{1,0:T(8,128)(2,1)S(1)}, u32[]{:S(2)}, u32[]{:S(2)}) %collective-permute-start) | collective-permute-done | bytes 524320 | tf_op jit(solution)/shard_map/ppermute | solution.py:108
  9.9 0.0 copy-start.5
  9.9 0.1 fusion.24
  10.0 0.2 fusion.25
  10.1 4.0 %collective-permute-start.1 = (bf16[4,16384]{1,0:T(4,128)(2,1)S(1)}, bf16[4,16384]{1,0:T(4,128)(2,1)S(1)}, u32[]{:S(2)}, u32[]{:S(2)}) collective-permute-start(bf16[4,16384]{1,0:T(4,128)(2,1)S(1)} %get-tuple-element.11), channel_id=1, source_target_pairs={{0,6},{1,7},{2,4},{3,5},{4,2},{5,3},{6,0},{7,1},{8,14},{9,15},{10,... | collective-permute-start | bytes 393224 | tf_op jit(solution)/shard_map/ppermute | solution.py:108
  14.1 0.5 %collective-permute-start.2 = (bf16[4,16384]{1,0:T(4,128)(2,1)S(1)}, bf16[4,16384]{1,0:T(4,128)(2,1)S(1)}, u32[]{:S(2)}, u32[]{:S(2)}) collective-permute-start(bf16[4,16384]{1,0:T(4,128)(2,1)S(1)} %get-tuple-element.13), channel_id=1, source_target_pairs={{0,2},{1,5},{2,0},{3,7},{4,6},{5,1},{6,4},{7,3},{8,10},{9,13},{10,... | collective-permute-start | bytes 393224 | tf_op jit(solution)/shard_map/ppermute | solution.py:108
  14.6 0.1 collective-permute-start.3
  14.7 3.6 %collective-permute-done.1 = bf16[4,16384]{1,0:T(4,128)(2,1)S(1)} collective-permute-done((bf16[4,16384]{1,0:T(4,128)(2,1)S(1)}, bf16[4,16384]{1,0:T(4,128)(2,1)S(1)}, u32[]{:S(2)}, u32[]{:S(2)}) %collective-permute-start.1) | collective-permute-done | bytes 131104 | tf_op jit(solution)/shard_map/ppermute | solution.py:108
  18.4 2.3 %collective-permute-done.2 = bf16[4,16384]{1,0:T(4,128)(2,1)S(1)} collective-permute-done((bf16[4,16384]{1,0:T(4,128)(2,1)S(1)}, bf16[4,16384]{1,0:T(4,128)(2,1)S(1)}, u32[]{:S(2)}, u32[]{:S(2)}) %collective-permute-start.2) | collective-permute-done | bytes 131104 | tf_op jit(solution)/shard_map/ppermute | solution.py:108
  20.7 0.2 collective-permute-done.3
  20.9 0.1 fusion.4
  21.0 0.0 copy-done.6
  21.0 0.1 slice_bitcast_fusion.3
  21.2 0.1 fusion.6
  21.3 2.6 %collective-permute-start.4 = (bf16[4,16384]{1,0:T(4,128)(2,1)S(1)}, bf16[4,16384]{1,0:T(4,128)(2,1)S(1)}, u32[]{:S(2)}, u32[]{:S(2)}) collective-permute-start(bf16[4,16384]{1,0:T(4,128)(2,1)S(1)} %fusion.6), channel_id=1, source_target_pairs={{0,8},{1,9},{2,10},{3,11},{4,12},{5,13},{6,14},{7,15},{8,0},{9,1},... | collective-permute-start | bytes 393224 | tf_op jit(solution)/shard_map/ppermute | solution.py:108
  24.0 6.3 %collective-permute-done.4 = bf16[4,16384]{1,0:T(4,128)(2,1)S(1)} collective-permute-done((bf16[4,16384]{1,0:T(4,128)(2,1)S(1)}, bf16[4,16384]{1,0:T(4,128)(2,1)S(1)}, u32[]{:S(2)}, u32[]{:S(2)}) %collective-permute-start.4) | collective-permute-done | bytes 131104 | tf_op jit(solution)/shard_map/ppermute | solution.py:108
  30.3 0.1 slice_bitcast_fusion.2
  30.5 0.1 abs_reduce_fusion
  30.6 0.2 multiply_reduce_fusion
  30.9 0.1 fusion.26
  31.0 0.0 copy-done.5
  31.0 0.4 fusion.2
  31.4 0.7 %collective-permute-start.5 = (bf16[4,16384]{1,0:T(4,128)(2,1)S(1)}, bf16[4,16384]{1,0:T(4,128)(2,1)S(1)}, u32[]{:S(2)}, u32[]{:S(2)}) collective-permute-start(bf16[4,16384]{1,0:T(4,128)(2,1)S(1)} %fusion.2), channel_id=1, source_target_pairs={{0,4},{1,3},{2,6},{3,1},{4,0},{5,7},{6,2},{7,5},{8,12},{9,11},{10,... | collective-permute-start | bytes 393224 | tf_op jit(solution)/shard_map/ppermute | solution.py:108
  32.1 1.7 %collective-permute-start.6 = (bf16[4,16384]{1,0:T(4,128)(2,1)S(1)}, bf16[4,16384]{1,0:T(4,128)(2,1)S(1)}, u32[]{:S(2)}, u32[]{:S(2)}) collective-permute-start(bf16[4,16384]{1,0:T(4,128)(2,1)S(1)} %fusion.2), channel_id=1, source_target_pairs={{0,2},{1,5},{2,0},{3,7},{4,6},{5,1},{6,4},{7,3},{8,10},{9,13},{10,... | collective-permute-start | bytes 393224 | tf_op jit(solution)/shard_map/ppermute | solution.py:108
  33.8 1.2 %collective-permute-start.7 = (bf16[4,16384]{1,0:T(4,128)(2,1)S(1)}, bf16[4,16384]{1,0:T(4,128)(2,1)S(1)}, u32[]{:S(2)}, u32[]{:S(2)}) collective-permute-start(bf16[4,16384]{1,0:T(4,128)(2,1)S(1)} %fusion.2), channel_id=1, source_target_pairs={{0,6},{1,7},{2,4},{3,5},{4,2},{5,3},{6,0},{7,1},{8,14},{9,15},{10,... | collective-permute-start | bytes 393224 | tf_op jit(solution)/shard_map/ppermute | solution.py:108
  34.9 0.0 copy-start.4
  35.0 0.6 %slice.46 = f32[2,128]{1,0:T(2,128)} slice(f32[4,128]{1,0:T(4,128)S(1)} %broadcast_add_fusion), slice={[0:2], [0:128]} | slice | bytes 2048 | tf_op jit(solution)/shard_map/slice | solution.py:147
  35.5 2.2 %collective-permute-done.5 = bf16[4,16384]{1,0:T(4,128)(2,1)S(1)} collective-permute-done((bf16[4,16384]{1,0:T(4,128)(2,1)S(1)}, bf16[4,16384]{1,0:T(4,128)(2,1)S(1)}, u32[]{:S(2)}, u32[]{:S(2)}) %collective-permute-start.5) | collective-permute-done | bytes 131104 | tf_op jit(solution)/shard_map/ppermute | solution.py:108
  37.7 0.0 collective-permute-done.6
  37.7 2.6 %collective-permute-done.7 = bf16[4,16384]{1,0:T(4,128)(2,1)S(1)} collective-permute-done((bf16[4,16384]{1,0:T(4,128)(2,1)S(1)}, bf16[4,16384]{1,0:T(4,128)(2,1)S(1)}, u32[]{:S(2)}, u32[]{:S(2)}) %collective-permute-start.7) | collective-permute-done | bytes 131104 | tf_op jit(solution)/shard_map/ppermute | solution.py:108
  40.3 0.3 pad_maximum_fusion
  40.6 0.1 collective-permute-start.8
  40.7 0.7 %copy.22 = bf16[1,2,128,128]{3,1,2,0:T(2,128)(2,1)} copy(bf16[1,2,128,128]{3,2,1,0:T(8,128)(2,1)S(1)} %slice_bitcast_fusion) | data formatting | bytes 131072
  41.4 3.0 %convolution_convert_fusion.2 = bf16[16,128]{1,0:T(8,128)(2,1)S(1)} fusion(bf16[16384,128]{1,0:T(8,128)(2,1)} %param.13, bf16[4,16384]{1,0:T(4,128)(2,1)S(1)} %collective-permute-done.7, bf16[4,16384]{1,0:T(4,128)(2,1)S(1)} %collective-permute-done.6, bf16[4,16384]{1,0:T(4,128)(2,1)S(1)} %collective-permute-done.5, bf16[4,16384]{1,0:T(4,128)(2,1)S(1)} %fusion.2), kind=kOutput, calls=%fused_computation.2 | convolution fusion | flops 69208064 | bytes 4722688 | tf_op jit(solution)/shard_map/dot_general | solution.py:139
  44.4 0.0 collective-permute-done.8
  44.4 0.0 copy-done.4
  44.4 0.7 %convolution_convert_fusion.1 = bf16[16,128]{1,0:T(8,128)(2,1)S(1)} fusion(bf16[16,16384]{1,0:T(8,128)(2,1)S(1)} %collective-permute-done.8, bf16[16384,128]{1,0:T(8,128)(2,1)S(1)} %copy-done.4), kind=kOutput, calls=%fused_computation.1 | convolution fusion | flops 67110912 | bytes 4722688 | tf_op jit(solution)/shard_map/dot_general | solution.py:140
  45.1 0.9 %convolution_convert_fusion = bf16[32,128]{1,0:T(8,128)(2,1)} fusion(bf16[16,128]{1,0:T(8,128)(2,1)S(1)} %convolution_convert_fusion.1, bf16[16,128]{1,0:T(8,128)(2,1)S(1)} %convolution_convert_fusion.2, s32[32]{0:T(128)S(1)} %fusion.11), kind=kOutput, calls=%fused_computation | convolution fusion | flops 283648 | bytes 16512 | tf_op jit(solution)/shard_map/dot_general | solution.py:144
  (7 shorter events, 0.1 us)
Async XLA Ops:
  0.6 2.2 %copy-start = (bf16[128,16384]{1,0:T(8,128)(2,1)S(1)}, bf16[128,16384]{1,0:T(8,128)(2,1)}, u32[]{:S(2)}) copy-start(bf16[128,16384]{1,0:T(8,128)(2,1)} %weight.1) | copy-start | bytes 12582916
  2.8 0.8 %copy-start.1 = (bf16[32,1024]{1,0:T(8,128)(2,1)S(1)}, bf16[32,1024]{1,0:T(8,128)(2,1)}, u32[]{:S(2)}) copy-start(bf16[32,1024]{1,0:T(8,128)(2,1)} %keys.1) | copy-start | bytes 196612
  3.7 0.8 %copy-start.2 = (bf16[32,1024]{1,0:T(8,128)(2,1)S(1)}, bf16[32,1024]{1,0:T(8,128)(2,1)}, u32[]{:S(2)}) copy-start(bf16[32,1024]{1,0:T(8,128)(2,1)} %values.1) | copy-start | bytes 196612
  4.5 0.7 %copy-start.3 = (bf16[32,128]{1,0:T(8,128)(2,1)S(1)}, bf16[32,128]{1,0:T(8,128)(2,1)}, u32[]{:S(2)}) copy-start(bf16[32,128]{1,0:T(8,128)(2,1)} %queries.1) | copy-start | bytes 24580
  5.2 15.8 %copy-start.6 = (bf16[2,16384]{1,0:T(2,128)(2,1)S(1)}, bf16[2,16384]{1,0:T(2,128)(2,1)}, u32[]{:S(2)}) copy-start(bf16[2,16384]{1,0:T(2,128)(2,1)} %param.7) | copy-start | bytes 196612
  7.8 2.0 %collective-permute-start = (bf16[16,16384]{1,0:T(8,128)(2,1)S(1)}, bf16[16,16384]{1,0:T(8,128)(2,1)S(1)}, u32[]{:S(2)}, u32[]{:S(2)}) collective-permute-start(bf16[16,16384]{1,0:T(8,128)(2,1)S(1)} %get-tuple-element.6), channel_id=1, source_target_pairs={{0,1},{1,0},{2,3},{3,2},{4,5},{5,4},{6,7},{7,6},{8,9},{9,8},{10,11... | collective-permute-start | bytes 1572872 | tf_op jit(solution)/shard_map/ppermute | solution.py:108
  9.9 21.1 %copy-start.5 = (f32[16384]{0:T(1024)S(1)}, f32[16384]{0:T(1024)}, u32[]{:S(2)}) copy-start(f32[16384]{0:T(1024)} %param.12) | copy-start | bytes 196612
  10.1 8.3 %collective-permute-start.1 = (bf16[4,16384]{1,0:T(4,128)(2,1)S(1)}, bf16[4,16384]{1,0:T(4,128)(2,1)S(1)}, u32[]{:S(2)}, u32[]{:S(2)}) collective-permute-start(bf16[4,16384]{1,0:T(4,128)(2,1)S(1)} %get-tuple-element.11), channel_id=1, source_target_pairs={{0,6},{1,7},{2,4},{3,5},{4,2},{5,3},{6,0},{7,1},{8,14},{9,15},{10,... | collective-permute-start | bytes 393224 | tf_op jit(solution)/shard_map/ppermute | solution.py:108
  14.1 6.6 %collective-permute-start.2 = (bf16[4,16384]{1,0:T(4,128)(2,1)S(1)}, bf16[4,16384]{1,0:T(4,128)(2,1)S(1)}, u32[]{:S(2)}, u32[]{:S(2)}) collective-permute-start(bf16[4,16384]{1,0:T(4,128)(2,1)S(1)} %get-tuple-element.13), channel_id=1, source_target_pairs={{0,2},{1,5},{2,0},{3,7},{4,6},{5,1},{6,4},{7,3},{8,10},{9,13},{10,... | collective-permute-start | bytes 393224 | tf_op jit(solution)/shard_map/ppermute | solution.py:108
  14.6 6.3 %collective-permute-start.3 = (bf16[4,16384]{1,0:T(4,128)(2,1)S(1)}, bf16[4,16384]{1,0:T(4,128)(2,1)S(1)}, u32[]{:S(2)}, u32[]{:S(2)}) collective-permute-start(bf16[4,16384]{1,0:T(4,128)(2,1)S(1)} %get-tuple-element.12), channel_id=1, source_target_pairs={{0,4},{1,3},{2,6},{3,1},{4,0},{5,7},{6,2},{7,5},{8,12},{9,11},{10,... | collective-permute-start | bytes 393224 | tf_op jit(solution)/shard_map/ppermute | solution.py:108
  21.3 9.0 %collective-permute-start.4 = (bf16[4,16384]{1,0:T(4,128)(2,1)S(1)}, bf16[4,16384]{1,0:T(4,128)(2,1)S(1)}, u32[]{:S(2)}, u32[]{:S(2)}) collective-permute-start(bf16[4,16384]{1,0:T(4,128)(2,1)S(1)} %fusion.6), channel_id=1, source_target_pairs={{0,8},{1,9},{2,10},{3,11},{4,12},{5,13},{6,14},{7,15},{8,0},{9,1},... | collective-permute-start | bytes 393224 | tf_op jit(solution)/shard_map/ppermute | solution.py:108
  31.4 6.4 %collective-permute-start.5 = (bf16[4,16384]{1,0:T(4,128)(2,1)S(1)}, bf16[4,16384]{1,0:T(4,128)(2,1)S(1)}, u32[]{:S(2)}, u32[]{:S(2)}) collective-permute-start(bf16[4,16384]{1,0:T(4,128)(2,1)S(1)} %fusion.2), channel_id=1, source_target_pairs={{0,4},{1,3},{2,6},{3,1},{4,0},{5,7},{6,2},{7,5},{8,12},{9,11},{10,... | collective-permute-start | bytes 393224 | tf_op jit(solution)/shard_map/ppermute | solution.py:108
  32.1 5.6 %collective-permute-start.6 = (bf16[4,16384]{1,0:T(4,128)(2,1)S(1)}, bf16[4,16384]{1,0:T(4,128)(2,1)S(1)}, u32[]{:S(2)}, u32[]{:S(2)}) collective-permute-start(bf16[4,16384]{1,0:T(4,128)(2,1)S(1)} %fusion.2), channel_id=1, source_target_pairs={{0,2},{1,5},{2,0},{3,7},{4,6},{5,1},{6,4},{7,3},{8,10},{9,13},{10,... | collective-permute-start | bytes 393224 | tf_op jit(solution)/shard_map/ppermute | solution.py:108
  33.8 6.5 %collective-permute-start.7 = (bf16[4,16384]{1,0:T(4,128)(2,1)S(1)}, bf16[4,16384]{1,0:T(4,128)(2,1)S(1)}, u32[]{:S(2)}, u32[]{:S(2)}) collective-permute-start(bf16[4,16384]{1,0:T(4,128)(2,1)S(1)} %fusion.2), channel_id=1, source_target_pairs={{0,6},{1,7},{2,4},{3,5},{4,2},{5,3},{6,0},{7,1},{8,14},{9,15},{10,... | collective-permute-start | bytes 393224 | tf_op jit(solution)/shard_map/ppermute | solution.py:108
  34.9 9.5 %copy-start.4 = (bf16[16384,128]{1,0:T(8,128)(2,1)S(1)}, bf16[16384,128]{1,0:T(8,128)(2,1)}, u32[]{:S(2)}) copy-start(bf16[16384,128]{1,0:T(8,128)(2,1)} %param.13) | copy-start | bytes 12582916
  40.6 3.8 %collective-permute-start.8 = (bf16[16,16384]{1,0:T(8,128)(2,1)S(1)}, bf16[16,16384]{1,0:T(8,128)(2,1)S(1)}, u32[]{:S(2)}, u32[]{:S(2)}) collective-permute-start(bf16[16,16384]{1,0:T(8,128)(2,1)S(1)} %pad_maximum_fusion), channel_id=1, source_target_pairs={{0,1},{1,0},{2,3},{3,2},{4,5},{5,4},{6,7},{7,6},{8,9},{9,8},{10,11... | collective-permute-start | bytes 1572872 | tf_op jit(solution)/shard_map/ppermute | solution.py:108

commit v7 on v6

--- a/solution.py
+++ b/solution.py
@@ -13,6 +13,7 @@
 F32 = jnp.float32
 BF16 = jnp.bfloat16
 CHUNKS = 8
+VMEM = 32 << 20
 
 
 def late_levels(n):
@@ -20,22 +21,31 @@
 
 
 def owner_token(row, device, n, local):
-    bits = [(1, 1), (2, 4), (4, 2)] + [(d, d) for d in late_levels(n)]
+    bits = [(1, 1), (2, 4), (6, 6)] + [(d, d) for d in late_levels(n)]
     block = row // local
     side = (device + block // (n // 2)) % 2
     distance = jnp.zeros_like(row)
     for place, (even, odd) in enumerate(bits):
         bit = (block >> (len(bits) - 1 - place)) % 2
-        distance = distance + bit * jnp.where(side == 0, even, odd)
+        distance = distance ^ (bit * jnp.where(side == 0, even, odd))
     return (device ^ distance) * local + row % local
 
 
-def project_kernel(n, local, queries, keys, values, weight, sent, kept, held, sems):
+def project_kernel(
+    n, local, queries, keys, values, weight, sent, kept, query, key, value, held, small, sems
+):
     device = lax.axis_index("tp")
     tokens = queries.shape[0]
     heads = queries.shape[1] // HD
     group = heads * n // (keys.shape[1] // HD)
     width = held.shape[1] // CHUNKS
+    fetches = [pltpu.make_async_copy(queries, query, small.at[0])]
+    for h in range(heads):
+        at = pl.ds(pl.multiple_of(lax.div(device * heads + h, group) * HD, HD), HD)
+        fetches.append(pltpu.make_async_copy(keys.at[:, at], key.at[h], small.at[1 + 2 * h]))
+        fetches.append(pltpu.make_async_copy(values.at[:, at], value.at[h], small.at[2 + 2 * h]))
+    for fetch in fetches:
+        fetch.start()
     copies = []
     for c in range(CHUNKS):
         part = pl.ds(c * width, width)
@@ -45,13 +55,14 @@
     col = lax.broadcasted_iota(jnp.int32, (tokens, tokens), 1)
     token = owner_token(row, device, n, local)
     pick = (token == col).astype(F32).astype(BF16)
-    ordered = jnp.dot(pick, queries[...], preferred_element_type=F32).astype(BF16)
+    for fetch in fetches:
+        fetch.wait()
+    ordered = jnp.dot(pick, query[...], preferred_element_type=F32).astype(BF16)
     contexts = []
     for h in range(heads):
-        at = pl.ds(pl.multiple_of(lax.div(device * heads + h, group) * HD, HD), HD)
         scores = lax.dot_general(
             ordered[:, h * HD : (h + 1) * HD],
-            keys[:, at],
+            key[h],
             (((1,), (1,)), ((), ())),
             preferred_element_type=F32,
         ) / jnp.sqrt(F32(HD))
@@ -59,7 +70,7 @@
         weights = jnp.exp(scores - jnp.max(scores, axis=1, keepdims=True))
         probs = (weights / jnp.sum(weights, axis=1, keepdims=True)).astype(BF16)
         contexts.append(
-            jnp.dot(probs, values[:, at], preferred_element_type=F32).astype(BF16)
+            jnp.dot(probs, value[h], preferred_element_type=F32).astype(BF16)
         )
     context = contexts[0] if heads == 1 else jnp.concatenate(contexts, axis=1)
     half = tokens // 2
@@ -74,6 +85,10 @@
 def project(n, local, queries, keys, values, weight):
     tokens, D = queries.shape[0], weight.shape[1]
     half = tokens // 2
+    heads = queries.shape[1] // HD
+    operands = [
+        pltpu.with_memory_space_constraint(x, pltpu.HBM) for x in (queries, keys, values, weight)
+    ]
     whole = pl.BlockSpec(memory_space=pltpu.VMEM)
     return pl.pallas_call(
         functools.partial(project_kernel, n, local),
@@ -81,18 +96,22 @@
             jax.ShapeDtypeStruct((half, D), BF16),
             jax.ShapeDtypeStruct((half, D), F32),
         ],
-        in_specs=[whole, whole, whole, pl.BlockSpec(memory_space=pltpu.HBM)],
+        in_specs=[pl.BlockSpec(memory_space=pltpu.HBM)] * 4,
         out_specs=[whole, whole],
         scratch_shapes=[
+            pltpu.VMEM(queries.shape, BF16),
+            pltpu.VMEM((heads, tokens, HD), BF16),
+            pltpu.VMEM((heads, tokens, HD), BF16),
             pltpu.VMEM(weight.shape, BF16),
+            pltpu.SemaphoreType.DMA((1 + 2 * heads,)),
             pltpu.SemaphoreType.DMA((CHUNKS,)),
         ],
-        compiler_params=pltpu.CompilerParams(vmem_limit_bytes=24 << 20),
+        compiler_params=pltpu.CompilerParams(vmem_limit_bytes=VMEM),
         cost_estimate=pl.CostEstimate(
             flops=2 * tokens * weight.size, bytes_accessed=2 * weight.size, transcendentals=0
         ),
         name="project",
-    )(queries, keys, values, weight)
+    )(*operands)
 
 
 def on_device(residual, queries, key_rows, value_rows, out_weight, norm_gain, q_weight):
@@ -102,7 +121,7 @@
     local = residual.shape[0]
     D = residual.shape[1]
     levels = late_levels(n)
-    square = [(1, (4, 2)), (2, (2, 4)), (3, (6, 6))]
+    square = [(1, (6, 6)), (2, (2, 4)), (3, (4, 2))]
 
     def swap(x, even, odd):
         return lax.ppermute(x, "tp", [(i, i ^ (odd if i % 2 else even)) for i in range(n)])
@@ -113,7 +132,7 @@
     part = half // 4
     arrived = [
         swap(total[k * part : (k + 1) * part].astype(BF16), *distance)
-        for k, distance in square[::-1]
+        for k, distance in square
     ]
     total = total[:part]
     for piece in arrived:
@@ -133,8 +152,7 @@
     held = (decoded * lax.rsqrt(mean_sq + 1e-05) * norm_gain[None, :]).astype(BF16)
     for level in levels[-2::-1]:
         held = jnp.concatenate([held, swap(held, level, level)], axis=0)
-    arrived = [swap(held, *distance) for _, distance in square[::-1]]
-    held = jnp.concatenate([held] + arrived[::-1], axis=0)
+    held = jnp.concatenate([held] + [swap(held, *distance) for _, distance in square], axis=0)
     other = swap(held, 1, 1)
     out_mine = jnp.dot(held, q_weight, preferred_element_type=F32).astype(BF16)
     out_other = jnp.dot(other, q_weight, preferred_element_type=F32).astype(BF16)

time: 46.3 us -> 43 us (0.929)
  local copies, waits for them, and re-layouts: 6.23 us -> 1.67 us
  Pallas kernels: 2.6 us -> 4.31 us
    unnamed x17 -> x9, local copies, waits for them, and re-layouts: 5.38 us -> 0.82 us
    pallas_call x1, Pallas kernels: 2.6 us -> 4.31 us  [project(): pl.pallas_call(functools.partial(project_kernel, n, local), out_shape=[ja...]
  transfers between devices with their start and end apart: 9 -> 9, of which waited for: 7 -> 7; matrix products, arithmetic and copies ran while one was open for 9% -> 10% of each run, Pallas kernels for 0% -> 0%
where the time goes in v7:
time: 43 us; the launch traced here: 42.8 us
  waiting for transfers between devices  18.6 us (43%)
  starting transfers between devices  11.3 us (26%)
  matrix products  4.52 us (11%)
  Pallas kernels  4.31 us (10%)
  local copies, waits for them, and re-layouts  1.67 us (4%)
  other arithmetic  1.65 us (4%)
  between operations  0.77 us (2%)
    ppermute x9, waiting for transfers between devices, swap(): lax.ppermute(x, 'tp', [(i, i ^ (odd if i % 2 else even)) for i in range(n)])  18.6 us
    ppermute x9, starting transfers between devices, swap(): lax.ppermute(x, 'tp', [(i, i ^ (odd if i % 2 else even)) for i in range(n)])  11.3 us
    pallas_call x1, Pallas kernels, project(): pl.pallas_call(functools.partial(project_kernel, n, local), out_shape=[ja...  4.31 us
    dot_general x1, matrix products, on_device(): out_mine = jnp.dot(held, q_weight, preferred_element_type=F32).astype(BF16)  2.97 us
    dot_general x1, matrix products, on_device(): lax.dot_general(pick, found, (((0,), (0,)), ((), ())), preferred_element_...  0.88 us
  transfers between devices with their start and end apart: 9, of which 7 were waited for; matrix products, arithmetic and copies ran while one was open for 10% of the time, Pallas kernels for 0%

profile of v7, /device:TPU:0, one launch (start us, length us, event | category | flops | bytes accessed | tf_op | source)
XLA Modules:
  0.0 42.8 jit_solution(8049333433387910167)
XLA Ops:
  0.6 0.0 copy-start.2
  0.6 4.3 %project.1 = (bf16[16,16384]{1,0:T(8,128)(2,1)S(1)}, f32[16,16384]{1,0:T(8,128)S(1)}) custom-call(bf16[32,128]{1,0:T(8,128)(2,1)} %queries.1, bf16[32,1024]{1,0:T(8,128)(2,1)} %keys.1, bf16[32,1024]{1,0:T(8,128)(2,1)} %values.1, bf16[128,16384]{1,0:T(8,128)(2,1)} %weight.1), custom_call_target="tpu_custom_call" | custom-call | flops 134217728 | bytes 4194304 | tf_op jit(solution)/shard_map/project/pallas_call | solution.py:93
  5.0 0.5 %collective-permute-start = (bf16[16,16384]{1,0:T(8,128)(2,1)S(1)}, bf16[16,16384]{1,0:T(8,128)(2,1)S(1)}, u32[]{:S(2)}, u32[]{:S(2)}) collective-permute-start(bf16[16,16384]{1,0:T(8,128)(2,1)S(1)} %get-tuple-element.6), channel_id=1, source_target_pairs={{0,1},{1,0},{2,3},{3,2},{4,5},{5,4},{6,7},{7,6},{8,9},{9,8},{10,11... | collective-permute-start | bytes 1572872 | tf_op jit(solution)/shard_map/ppermute | solution.py:127
  5.5 1.5 %collective-permute-done = bf16[16,16384]{1,0:T(8,128)(2,1)S(1)} collective-permute-done((bf16[16,16384]{1,0:T(8,128)(2,1)S(1)}, bf16[16,16384]{1,0:T(8,128)(2,1)S(1)}, u32[]{:S(2)}, u32[]{:S(2)}) %collective-permute-start) | collective-permute-done | bytes 524320 | tf_op jit(solution)/shard_map/ppermute | solution.py:127
  7.0 0.0 copy-start.1
  7.0 0.1 fusion.24
  7.1 0.2 fusion.25
  7.3 4.0 %collective-permute-start.1 = (bf16[4,16384]{1,0:T(4,128)(2,1)S(1)}, bf16[4,16384]{1,0:T(4,128)(2,1)S(1)}, u32[]{:S(2)}, u32[]{:S(2)}) collective-permute-start(bf16[4,16384]{1,0:T(4,128)(2,1)S(1)} %get-tuple-element.11), channel_id=1, source_target_pairs={{0,6},{1,7},{2,4},{3,5},{4,2},{5,3},{6,0},{7,1},{8,14},{9,15},{10,... | collective-permute-start | bytes 393224 | tf_op jit(solution)/shard_map/ppermute | solution.py:127
  11.3 0.5 %collective-permute-start.2 = (bf16[4,16384]{1,0:T(4,128)(2,1)S(1)}, bf16[4,16384]{1,0:T(4,128)(2,1)S(1)}, u32[]{:S(2)}, u32[]{:S(2)}) collective-permute-start(bf16[4,16384]{1,0:T(4,128)(2,1)S(1)} %get-tuple-element.13), channel_id=1, source_target_pairs={{0,2},{1,5},{2,0},{3,7},{4,6},{5,1},{6,4},{7,3},{8,10},{9,13},{10,... | collective-permute-start | bytes 393224 | tf_op jit(solution)/shard_map/ppermute | solution.py:127
  11.8 0.1 collective-permute-start.3
  11.9 3.6 %collective-permute-done.1 = bf16[4,16384]{1,0:T(4,128)(2,1)S(1)} collective-permute-done((bf16[4,16384]{1,0:T(4,128)(2,1)S(1)}, bf16[4,16384]{1,0:T(4,128)(2,1)S(1)}, u32[]{:S(2)}, u32[]{:S(2)}) %collective-permute-start.1) | collective-permute-done | bytes 131104 | tf_op jit(solution)/shard_map/ppermute | solution.py:127
  15.5 2.3 %collective-permute-done.2 = bf16[4,16384]{1,0:T(4,128)(2,1)S(1)} collective-permute-done((bf16[4,16384]{1,0:T(4,128)(2,1)S(1)}, bf16[4,16384]{1,0:T(4,128)(2,1)S(1)}, u32[]{:S(2)}, u32[]{:S(2)}) %collective-permute-start.2) | collective-permute-done | bytes 131104 | tf_op jit(solution)/shard_map/ppermute | solution.py:127
  17.9 0.2 collective-permute-done.3
  18.1 0.1 fusion.4
  18.2 0.0 copy-done.2
  18.2 0.1 slice_bitcast_fusion.3
  18.4 0.1 fusion.6
  18.5 2.6 %collective-permute-start.4 = (bf16[4,16384]{1,0:T(4,128)(2,1)S(1)}, bf16[4,16384]{1,0:T(4,128)(2,1)S(1)}, u32[]{:S(2)}, u32[]{:S(2)}) collective-permute-start(bf16[4,16384]{1,0:T(4,128)(2,1)S(1)} %fusion.6), channel_id=1, source_target_pairs={{0,8},{1,9},{2,10},{3,11},{4,12},{5,13},{6,14},{7,15},{8,0},{9,1},... | collective-permute-start | bytes 393224 | tf_op jit(solution)/shard_map/ppermute | solution.py:127
  21.1 6.3 %collective-permute-done.4 = bf16[4,16384]{1,0:T(4,128)(2,1)S(1)} collective-permute-done((bf16[4,16384]{1,0:T(4,128)(2,1)S(1)}, bf16[4,16384]{1,0:T(4,128)(2,1)S(1)}, u32[]{:S(2)}, u32[]{:S(2)}) %collective-permute-start.4) | collective-permute-done | bytes 131104 | tf_op jit(solution)/shard_map/ppermute | solution.py:127
  27.5 0.1 slice_bitcast_fusion.2
  27.6 0.1 abs_reduce_fusion
  27.8 0.2 multiply_reduce_fusion
  28.0 0.1 fusion.26
  28.1 0.0 copy-done.1
  28.1 0.4 fusion.2
  28.5 1.8 %collective-permute-start.5 = (bf16[4,16384]{1,0:T(4,128)(2,1)S(1)}, bf16[4,16384]{1,0:T(4,128)(2,1)S(1)}, u32[]{:S(2)}, u32[]{:S(2)}) collective-permute-start(bf16[4,16384]{1,0:T(4,128)(2,1)S(1)} %fusion.2), channel_id=1, source_target_pairs={{0,6},{1,7},{2,4},{3,5},{4,2},{5,3},{6,0},{7,1},{8,14},{9,15},{10,... | collective-permute-start | bytes 393224 | tf_op jit(solution)/shard_map/ppermute | solution.py:127
  30.4 0.3 collective-permute-start.6
  30.7 1.4 %collective-permute-start.7 = (bf16[4,16384]{1,0:T(4,128)(2,1)S(1)}, bf16[4,16384]{1,0:T(4,128)(2,1)S(1)}, u32[]{:S(2)}, u32[]{:S(2)}) collective-permute-start(bf16[4,16384]{1,0:T(4,128)(2,1)S(1)} %fusion.2), channel_id=1, source_target_pairs={{0,4},{1,3},{2,6},{3,1},{4,0},{5,7},{6,2},{7,5},{8,12},{9,11},{10,... | collective-permute-start | bytes 393224 | tf_op jit(solution)/shard_map/ppermute | solution.py:127
  32.1 0.0 copy-start
  32.1 0.6 %slice.46 = f32[2,128]{1,0:T(2,128)} slice(f32[4,128]{1,0:T(4,128)S(1)} %broadcast_add_fusion), slice={[0:2], [0:128]} | slice | bytes 2048 | tf_op jit(solution)/shard_map/slice | solution.py:165
  32.7 2.9 %collective-permute-done.5 = bf16[4,16384]{1,0:T(4,128)(2,1)S(1)} collective-permute-done((bf16[4,16384]{1,0:T(4,128)(2,1)S(1)}, bf16[4,16384]{1,0:T(4,128)(2,1)S(1)}, u32[]{:S(2)}, u32[]{:S(2)}) %collective-permute-start.5) | collective-permute-done | bytes 131104 | tf_op jit(solution)/shard_map/ppermute | solution.py:127
  35.6 1.6 %collective-permute-done.6 = bf16[4,16384]{1,0:T(4,128)(2,1)S(1)} collective-permute-done((bf16[4,16384]{1,0:T(4,128)(2,1)S(1)}, bf16[4,16384]{1,0:T(4,128)(2,1)S(1)}, u32[]{:S(2)}, u32[]{:S(2)}) %collective-permute-start.6) | collective-permute-done | bytes 131104 | tf_op jit(solution)/shard_map/ppermute | solution.py:127
  37.2 0.0 collective-permute-done.7
  37.2 0.3 pad_maximum_fusion
  37.5 0.1 collective-permute-start.8
  37.6 0.7 %copy.22 = bf16[1,2,128,128]{3,1,2,0:T(2,128)(2,1)} copy(bf16[1,2,128,128]{3,2,1,0:T(8,128)(2,1)S(1)} %slice_bitcast_fusion) | data formatting | bytes 131072
  38.3 3.0 %convolution_convert_fusion.2 = bf16[16,128]{1,0:T(8,128)(2,1)S(1)} fusion(bf16[16384,128]{1,0:T(8,128)(2,1)} %param.13, bf16[4,16384]{1,0:T(4,128)(2,1)S(1)} %collective-permute-done.7, bf16[4,16384]{1,0:T(4,128)(2,1)S(1)} %collective-permute-done.6, bf16[4,16384]{1,0:T(4,128)(2,1)S(1)} %collective-permute-done.5, bf16[4,16384]{1,0:T(4,128)(2,1)S(1)} %fusion.2), kind=kOutput, calls=%fused_computation.2 | convolution fusion | flops 69208064 | bytes 4722688 | tf_op jit(solution)/shard_map/dot_general | solution.py:157
  41.3 0.0 collective-permute-done.8
  41.3 0.0 copy-done
  41.3 0.7 %convolution_convert_fusion.1 = bf16[16,128]{1,0:T(8,128)(2,1)S(1)} fusion(bf16[16,16384]{1,0:T(8,128)(2,1)S(1)} %collective-permute-done.8, bf16[16384,128]{1,0:T(8,128)(2,1)S(1)} %copy-done), kind=kOutput, calls=%fused_computation.1 | convolution fusion | flops 67110912 | bytes 4722688 | tf_op jit(solution)/shard_map/dot_general | solution.py:158
  42.0 0.9 %convolution_convert_fusion = bf16[32,128]{1,0:T(8,128)(2,1)} fusion(bf16[16,128]{1,0:T(8,128)(2,1)S(1)} %convolution_convert_fusion.1, bf16[16,128]{1,0:T(8,128)(2,1)S(1)} %convolution_convert_fusion.2, s32[32]{0:T(128)S(1)} %fusion.11), kind=kOutput, calls=%fused_computation | convolution fusion | flops 283648 | bytes 16512 | tf_op jit(solution)/shard_map/dot_general | solution.py:162
  (7 shorter events, 0.1 us)
Async XLA Ops:
  0.6 17.6 %copy-start.2 = (bf16[2,16384]{1,0:T(2,128)(2,1)S(1)}, bf16[2,16384]{1,0:T(2,128)(2,1)}, u32[]{:S(2)}) copy-start(bf16[2,16384]{1,0:T(2,128)(2,1)} %param.7) | copy-start | bytes 196612
  5.0 2.1 %collective-permute-start = (bf16[16,16384]{1,0:T(8,128)(2,1)S(1)}, bf16[16,16384]{1,0:T(8,128)(2,1)S(1)}, u32[]{:S(2)}, u32[]{:S(2)}) collective-permute-start(bf16[16,16384]{1,0:T(8,128)(2,1)S(1)} %get-tuple-element.6), channel_id=1, source_target_pairs={{0,1},{1,0},{2,3},{3,2},{4,5},{5,4},{6,7},{7,6},{8,9},{9,8},{10,11... | collective-permute-start | bytes 1572872 | tf_op jit(solution)/shard_map/ppermute | solution.py:127
  7.0 21.1 %copy-start.1 = (f32[16384]{0:T(1024)S(1)}, f32[16384]{0:T(1024)}, u32[]{:S(2)}) copy-start(f32[16384]{0:T(1024)} %param.12) | copy-start | bytes 196612
  7.3 8.2 %collective-permute-start.1 = (bf16[4,16384]{1,0:T(4,128)(2,1)S(1)}, bf16[4,16384]{1,0:T(4,128)(2,1)S(1)}, u32[]{:S(2)}, u32[]{:S(2)}) collective-permute-start(bf16[4,16384]{1,0:T(4,128)(2,1)S(1)} %get-tuple-element.11), channel_id=1, source_target_pairs={{0,6},{1,7},{2,4},{3,5},{4,2},{5,3},{6,0},{7,1},{8,14},{9,15},{10,... | collective-permute-start | bytes 393224 | tf_op jit(solution)/shard_map/ppermute | solution.py:127
  11.3 6.6 %collective-permute-start.2 = (bf16[4,16384]{1,0:T(4,128)(2,1)S(1)}, bf16[4,16384]{1,0:T(4,128)(2,1)S(1)}, u32[]{:S(2)}, u32[]{:S(2)}) collective-permute-start(bf16[4,16384]{1,0:T(4,128)(2,1)S(1)} %get-tuple-element.13), channel_id=1, source_target_pairs={{0,2},{1,5},{2,0},{3,7},{4,6},{5,1},{6,4},{7,3},{8,10},{9,13},{10,... | collective-permute-start | bytes 393224 | tf_op jit(solution)/shard_map/ppermute | solution.py:127
  11.8 6.3 %collective-permute-start.3 = (bf16[4,16384]{1,0:T(4,128)(2,1)S(1)}, bf16[4,16384]{1,0:T(4,128)(2,1)S(1)}, u32[]{:S(2)}, u32[]{:S(2)}) collective-permute-start(bf16[4,16384]{1,0:T(4,128)(2,1)S(1)} %get-tuple-element.12), channel_id=1, source_target_pairs={{0,4},{1,3},{2,6},{3,1},{4,0},{5,7},{6,2},{7,5},{8,12},{9,11},{10,... | collective-permute-start | bytes 393224 | tf_op jit(solution)/shard_map/ppermute | solution.py:127
  18.5 8.9 %collective-permute-start.4 = (bf16[4,16384]{1,0:T(4,128)(2,1)S(1)}, bf16[4,16384]{1,0:T(4,128)(2,1)S(1)}, u32[]{:S(2)}, u32[]{:S(2)}) collective-permute-start(bf16[4,16384]{1,0:T(4,128)(2,1)S(1)} %fusion.6), channel_id=1, source_target_pairs={{0,8},{1,9},{2,10},{3,11},{4,12},{5,13},{6,14},{7,15},{8,0},{9,1},... | collective-permute-start | bytes 393224 | tf_op jit(solution)/shard_map/ppermute | solution.py:127
  28.5 7.0 %collective-permute-start.5 = (bf16[4,16384]{1,0:T(4,128)(2,1)S(1)}, bf16[4,16384]{1,0:T(4,128)(2,1)S(1)}, u32[]{:S(2)}, u32[]{:S(2)}) collective-permute-start(bf16[4,16384]{1,0:T(4,128)(2,1)S(1)} %fusion.2), channel_id=1, source_target_pairs={{0,6},{1,7},{2,4},{3,5},{4,2},{5,3},{6,0},{7,1},{8,14},{9,15},{10,... | collective-permute-start | bytes 393224 | tf_op jit(solution)/shard_map/ppermute | solution.py:127
  30.4 6.8 %collective-permute-start.6 = (bf16[4,16384]{1,0:T(4,128)(2,1)S(1)}, bf16[4,16384]{1,0:T(4,128)(2,1)S(1)}, u32[]{:S(2)}, u32[]{:S(2)}) collective-permute-start(bf16[4,16384]{1,0:T(4,128)(2,1)S(1)} %fusion.2), channel_id=1, source_target_pairs={{0,2},{1,5},{2,0},{3,7},{4,6},{5,1},{6,4},{7,3},{8,10},{9,13},{10,... | collective-permute-start | bytes 393224 | tf_op jit(solution)/shard_map/ppermute | solution.py:127
  30.7 6.5 %collective-permute-start.7 = (bf16[4,16384]{1,0:T(4,128)(2,1)S(1)}, bf16[4,16384]{1,0:T(4,128)(2,1)S(1)}, u32[]{:S(2)}, u32[]{:S(2)}) collective-permute-start(bf16[4,16384]{1,0:T(4,128)(2,1)S(1)} %fusion.2), channel_id=1, source_target_pairs={{0,4},{1,3},{2,6},{3,1},{4,0},{5,7},{6,2},{7,5},{8,12},{9,11},{10,... | collective-permute-start | bytes 393224 | tf_op jit(solution)/shard_map/ppermute | solution.py:127
  32.1 9.2 %copy-start = (bf16[16384,128]{1,0:T(8,128)(2,1)S(1)}, bf16[16384,128]{1,0:T(8,128)(2,1)}, u32[]{:S(2)}) copy-start(bf16[16384,128]{1,0:T(8,128)(2,1)} %param.13) | copy-start | bytes 12582916
  37.5 3.8 %collective-permute-start.8 = (bf16[16,16384]{1,0:T(8,128)(2,1)S(1)}, bf16[16,16384]{1,0:T(8,128)(2,1)S(1)}, u32[]{:S(2)}, u32[]{:S(2)}) collective-permute-start(bf16[16,16384]{1,0:T(8,128)(2,1)S(1)} %pad_maximum_fusion), channel_id=1, source_target_pairs={{0,1},{1,0},{2,3},{3,2},{4,5},{5,4},{6,7},{7,6},{8,9},{9,8},{10,11... | collective-permute-start | bytes 1572872 | tf_op jit(solution)/shard_map/ppermute | solution.py:127

commit v8 on v7

v8 whole, which is shorter than its diff:
```python
import functools

import jax
import jax.numpy as jnp
from jax import lax
from jax.experimental import pallas as pl
from jax.experimental.pallas import tpu as pltpu
from jax.sharding import PartitionSpec as P

HD = 128
QB = 128
EPS = 1e-06
F32 = jnp.float32
BF16 = jnp.bfloat16
PIECES = 4
VMEM_LIMIT = 24 << 20


def late_levels(n):
    return [1 << b for b in range(3, n.bit_length() - 1)]


def owner_token(row, device, n, local):
    bits = [1, 2, 6] + late_levels(n)
    shift = local.bit_length() - 1
    block = row >> shift
    distance = jnp.zeros_like(row)
    for place, bit in enumerate(bits):
        distance = distance ^ (((block >> (len(bits) - 1 - place)) & 1) * bit)
    return ((device ^ distance) << shift) | (row & (local - 1))


def attend_kernel(
    n, local, queries, keys, values, weight, context, held, query, key, value, small, large
):
    device = lax.axis_index("tp")
    tokens = queries.shape[0]
    heads = queries.shape[1] // HD
    group = heads * n // (keys.shape[1] // HD)
    copies = [pltpu.make_async_copy(queries, query, small.at[0])]
    for h in range(heads):
        at = pl.ds(pl.multiple_of(lax.div(device * heads + h, group) * HD, HD), HD)
        copies.append(pltpu.make_async_copy(keys.at[:, at], key.at[h], small.at[1 + 2 * h]))
        copies.append(pltpu.make_async_copy(values.at[:, at], value.at[h], small.at[2 + 2 * h]))
    depth = held.shape[0] // PIECES
    late = []
    for c in range(PIECES):
        part = pl.ds(c * depth, depth)
        late.append(pltpu.make_async_copy(weight.at[part], held.at[part], large.at[c]))
    for copy in copies + late:
        copy.start()
    row = lax.broadcasted_iota(jnp.int32, (tokens, tokens), 0)
    col = lax.broadcasted_iota(jnp.int32, (tokens, tokens), 1)
    token = owner_token(row, device, n, local)
    pick = (token == col).astype(F32).astype(BF16)
    for copy in copies:
        copy.wait()
    ordered = jnp.dot(pick, query[...], preferred_element_type=F32).astype(BF16)
    for h in range(heads):
        scores = lax.dot_general(
            ordered[:, h * HD : (h + 1) * HD],
            key[h],
            (((1,), (1,)), ((), ())),
            preferred_element_type=F32,
        ) / jnp.sqrt(F32(HD))
        scores = jnp.where(col <= token, scores, F32(-1e30))
        weights = jnp.exp(scores - jnp.max(scores, axis=1, keepdims=True))
        probs = (weights / jnp.sum(weights, axis=1, keepdims=True)).astype(BF16)
        context[:, h * HD : (h + 1) * HD] = jnp.dot(
            probs, value[h], preferred_element_type=F32
        ).astype(BF16)
    for copy in late:
        copy.wait()


def in_hbm(*arrays):
    return [pltpu.with_memory_space_constraint(x, pltpu.HBM) for x in arrays]


def attend(n, local, queries, keys, values, weight):
    tokens = queries.shape[0]
    heads = queries.shape[1] // HD
    whole = pl.BlockSpec(memory_space=pltpu.VMEM)
    return pl.pallas_call(
        functools.partial(attend_kernel, n, local),
        out_shape=[
            jax.ShapeDtypeStruct(queries.shape, BF16),
            pltpu.VMEM(weight.shape, BF16),
        ],
        in_specs=[pl.BlockSpec(memory_space=pltpu.HBM)] * 4,
        out_specs=[whole, whole],
        scratch_shapes=[
            pltpu.VMEM(queries.shape, BF16),
            pltpu.VMEM((heads, tokens, HD), BF16),
            pltpu.VMEM((heads, tokens, HD), BF16),
            pltpu.SemaphoreType.DMA((1 + 2 * heads,)),
            pltpu.SemaphoreType.DMA((PIECES,)),
        ],
        compiler_params=pltpu.CompilerParams(vmem_limit_bytes=VMEM_LIMIT),
        cost_estimate=pl.CostEstimate(
            flops=0, bytes_accessed=2 * weight.size, transcendentals=0
        ),
        name="attend",
    )(*in_hbm(queries, keys, values, weight))


def fetch_kernel(source, target, sems):
    depth = source.shape[0] // PIECES
    copies = []
    for c in range(PIECES):
        part = pl.ds(c * depth, depth)
        copies.append(pltpu.make_async_copy(source.at[part], target.at[part], sems.at[c]))
        copies[-1].start()
    for copy in copies:
        copy.wait()


def fetch(weight):
    return pl.pallas_call(
        fetch_kernel,
        out_shape=pltpu.VMEM(weight.shape, BF16),
        in_specs=[pl.BlockSpec(memory_space=pltpu.HBM)],
        out_specs=pl.BlockSpec(memory_space=pltpu.VMEM),
        scratch_shapes=[pltpu.SemaphoreType.DMA((PIECES,))],
        compiler_params=pltpu.CompilerParams(vmem_limit_bytes=VMEM_LIMIT),
        cost_estimate=pl.CostEstimate(
            flops=0, bytes_accessed=4 * weight.size, transcendentals=0
        ),
        name="fetch",
    )(*in_hbm(weight))


def on_device(residual, queries, key_rows, value_rows, out_weight, norm_gain, q_weight):
    n = lax.axis_size("tp")
    device = lax.axis_index("tp")
    tokens = queries.shape[0]
    local = residual.shape[0]
    D = residual.shape[1]
    levels = late_levels(n)
    square = (6, 2, 4)

    def swap(x, distance):
        return lax.ppermute(x, "tp", [(i, i ^ distance) for i in range(n)])

    half = tokens // 2
    context, weight = attend(n, local, queries, key_rows, value_rows, out_weight)
    sent = jnp.dot(context[half:], weight, preferred_element_type=F32).astype(BF16)
    got = swap(sent, 1)
    total = jnp.dot(context[:half], weight, preferred_element_type=F32)
    total = lax.optimization_barrier(total) + got.astype(F32)
    part = half // 4
    pieces = [total[k * part : (k + 1) * part].astype(BF16) for k in range(1, 4)]
    arrived = [swap(piece, distance) for piece, distance in zip(pieces, square)]
    arrived[0], q_weight = lax.optimization_barrier((arrived[0], q_weight))
    total, q_weight = lax.optimization_barrier(
        (total[:part] + arrived[0].astype(F32), fetch(q_weight))
    )
    for piece in arrived[1:]:
        total = total + piece.astype(F32)
    for level in levels[:-1]:
        kept = total.shape[0] // 2
        total = total[:kept] + swap(total[kept:].astype(BF16), level).astype(F32)
    total = jnp.concatenate([total[:local] + residual.astype(F32), total[local:]], axis=0)
    got = swap(total.astype(BF16), levels[-1]).astype(F32)
    stream = total + jnp.concatenate([got[local:], got[:local]], axis=0)
    rows = stream.shape[0]
    grouped = stream.reshape(rows, D // QB, QB)
    scales = jnp.max(jnp.abs(grouped), axis=2) + EPS
    codes = (grouped / scales[:, :, None]).astype(BF16)
    decoded = (codes.astype(F32) * scales[:, :, None]).reshape(rows, D)
    mean_sq = jnp.mean(decoded * decoded, axis=1, keepdims=True)
    held = (decoded * lax.rsqrt(mean_sq + 1e-05) * norm_gain[None, :]).astype(BF16)
    for level in levels[-2::-1]:
        held = jnp.concatenate([held, swap(held, level)], axis=0)
    held = jnp.concatenate([held] + [swap(held, distance) for distance in square], axis=0)
    other = swap(held, 1)
    out_mine = jnp.dot(held, q_weight, preferred_element_type=F32).astype(BF16)
    out_other = jnp.dot(other, q_weight, preferred_element_type=F32).astype(BF16)
    found = jnp.concatenate([out_mine, out_other], axis=0)
    row = jnp.arange(tokens)
    pick = (owner_token(row, device, n, local)[:, None] == row[None, :]).astype(BF16)
    next_queries = lax.dot_general(
        pick, found, (((0,), (0,)), ((), ())), preferred_element_type=F32
    ).astype(BF16)
    return (codes.reshape(rows, D)[:local], scales[:local], next_queries)


def solution(mesh):
    in_specs = (
        P(("replica", "tp"), None),
        P("replica", "tp"),
        P("replica", None),
        P("replica", None),
        P("tp", None),
        P(),
        P(None, "tp"),
    )
    out_specs = (P(("replica", "tp"), None), P(("replica", "tp"), None), P("replica", "tp"))
    return jax.shard_map(
        on_device, mesh=mesh, in_specs=in_specs, out_specs=out_specs, check_vma=False
    )
```

time: 43 us -> 41.9 us (0.974)
  waiting for transfers between devices: 18.6 us -> 13.6 us
  local copies, waits for them, and re-layouts: 1.67 us -> 3.64 us
  matrix products: 4.52 us -> 5.83 us
    ppermute x9, waiting for transfers between devices: 18.6 us -> 13.6 us  [swap(): return lax.ppermute(x, 'tp', [(i, i ^ distance) for i in range(n)])]
    unnamed x9 -> x11, local copies, waits for them, and re-layouts: 0.82 us -> 2.78 us
    dot_general x0 -> x2, matrix products: none -> 1.31 us  [the longest x1 0.66 us: on_device(): total = jnp.dot(context[:half], weight, preferred_element_type=F32)]
    pallas_call x1 -> x2, Pallas kernels: 4.31 us -> 4.52 us  [the longest x1 2.28 us: attend(): pl.pallas_call(functools.partial(attend_kernel, n, local), out_shape=[jax...]
  transfers between devices with their start and end apart: 9 -> 9, of which waited for: 7 -> 6; matrix products, arithmetic and copies ran while one was open for 10% -> 12% of each run, Pallas kernels for 0% -> 5%
where the time goes in v8:
time: 41.9 us; the launch traced here: 41.7 us
  waiting for transfers between devices  13.6 us (32%)
  starting transfers between devices  11.6 us (28%)
  matrix products  5.83 us (14%)
  Pallas kernels  4.52 us (11%)
  local copies, waits for them, and re-layouts  3.64 us (9%)
  other arithmetic  1.69 us (4%)
  between operations  0.8 us (2%)
    ppermute x9, waiting for transfers between devices, swap(): return lax.ppermute(x, 'tp', [(i, i ^ distance) for i in range(n)])  13.6 us
    ppermute x9, starting transfers between devices, swap(): return lax.ppermute(x, 'tp', [(i, i ^ distance) for i in range(n)])  11.6 us
    dot_general x1, matrix products, on_device(): out_mine = jnp.dot(held, q_weight, preferred_element_type=F32).astype(BF16)  2.97 us
    unnamed x11, local copies, waits for them, and re-layouts  2.78 us
    pallas_call x1, Pallas kernels, attend(): pl.pallas_call(functools.partial(attend_kernel, n, local), out_shape=[jax...  2.28 us
    pallas_call x1, Pallas kernels, fetch(): pl.pallas_call(fetch_kernel, out_shape=pltpu.VMEM(weight.shape, BF16), in...  2.24 us
    dot_general x1, matrix products, on_device(): lax.dot_general(pick, found, (((0,), (0,)), ((), ())), preferred_element_...  0.88 us
  transfers between devices with their start and end apart: 9, of which 6 were waited for; matrix products, arithmetic and copies ran while one was open for 12% of the time, Pallas kernels for 5%

profile of v8, /device:TPU:0, one launch (start us, length us, event | category | flops | bytes accessed | tf_op | source)
XLA Modules:
  0.0 41.7 jit_solution(10184309149832033495)
XLA Ops:
  0.6 2.3 %attend.1 = (bf16[32,128]{1,0:T(8,128)(2,1)S(1)}, bf16[128,16384]{1,0:T(8,128)(2,1)S(1)}) custom-call(bf16[32,128]{1,0:T(8,128)(2,1)} %queries.1, bf16[32,1024]{1,0:T(8,128)(2,1)} %keys.1, bf16[32,1024]{1,0:T(8,128)(2,1)} %values.1, bf16[128,16384]{1,0:T(8,128)(2,1)} %weight.1), custom_call_target="tpu_custom_call" | custom-call | bytes 4194304 | tf_op jit(solution)/shard_map/attend/pallas_call | solution.py:84
  2.9 0.7 %convolution_convert_fusion = bf16[16,16384]{1,0:T(8,128)(2,1)S(1)} fusion(bf16[128,16384]{1,0:T(8,128)(2,1)S(1)} %get-tuple-element.10, bf16[32,128]{1,0:T(8,128)(2,1)S(1)} %get-tuple-element.9), kind=kOutput, calls=%fused_computation | convolution fusion | flops 67371008 | bytes 4722688 | tf_op jit(solution)/shard_map/dot_general | solution.py:147
  3.6 0.5 %collective-permute-start = (bf16[16,16384]{1,0:T(8,128)(2,1)S(1)}, bf16[16,16384]{1,0:T(8,128)(2,1)S(1)}, u32[]{:S(2)}, u32[]{:S(2)}) collective-permute-start(bf16[16,16384]{1,0:T(8,128)(2,1)S(1)} %convolution_convert_fusion), channel_id=1, source_target_pairs={{0,1},{1,0},{2,3},{3,2},{4,5},{5,4},{6,7},{7,6},{8,9},{9,8},{10,11... | collective-permute-start | bytes 1572872 | tf_op jit(solution)/shard_map/ppermute | solution.py:143
  4.1 0.7 %fusion.10 = f32[16,16384]{1,0:T(8,128)S(1)} fusion(bf16[128,16384]{1,0:T(8,128)(2,1)S(1)} %get-tuple-element.10, bf16[32,128]{1,0:T(8,128)(2,1)S(1)} %get-tuple-element.9), kind=kOutput, calls=%fused_computation.35 | convolution fusion | flops 67108864 | bytes 5246976 | tf_op jit(solution)/shard_map/dot_general | solution.py:149
  4.7 0.9 %collective-permute-done = bf16[16,16384]{1,0:T(8,128)(2,1)S(1)} collective-permute-done((bf16[16,16384]{1,0:T(8,128)(2,1)S(1)}, bf16[16,16384]{1,0:T(8,128)(2,1)S(1)}, u32[]{:S(2)}, u32[]{:S(2)}) %collective-permute-start) | collective-permute-done | bytes 524320 | tf_op jit(solution)/shard_map/ppermute | solution.py:143
  5.6 0.1 fusion.13
  5.7 0.2 fusion.14
  5.9 4.0 %collective-permute-start.1 = (bf16[4,16384]{1,0:T(4,128)(2,1)S(1)}, bf16[4,16384]{1,0:T(4,128)(2,1)S(1)}, u32[]{:S(2)}, u32[]{:S(2)}) collective-permute-start(bf16[4,16384]{1,0:T(4,128)(2,1)S(1)} %get-tuple-element.21), channel_id=1, source_target_pairs={{0,6},{1,7},{2,4},{3,5},{4,2},{5,3},{6,0},{7,1},{8,14},{9,15},{10,... | collective-permute-start | bytes 393224 | tf_op jit(solution)/shard_map/ppermute | solution.py:143
  9.9 0.5 %collective-permute-start.2 = (bf16[4,16384]{1,0:T(4,128)(2,1)S(1)}, bf16[4,16384]{1,0:T(4,128)(2,1)S(1)}, u32[]{:S(2)}, u32[]{:S(2)}) collective-permute-start(bf16[4,16384]{1,0:T(4,128)(2,1)S(1)} %get-tuple-element.19), channel_id=1, source_target_pairs={{0,2},{1,3},{2,0},{3,1},{4,6},{5,7},{6,4},{7,5},{8,10},{9,11},{10,... | collective-permute-start | bytes 393224 | tf_op jit(solution)/shard_map/ppermute | solution.py:143
  10.4 0.1 collective-permute-start.3
  10.5 3.3 %collective-permute-done.1 = bf16[4,16384]{1,0:T(4,128)(2,1)S(1)} collective-permute-done((bf16[4,16384]{1,0:T(4,128)(2,1)S(1)}, bf16[4,16384]{1,0:T(4,128)(2,1)S(1)}, u32[]{:S(2)}, u32[]{:S(2)}) %collective-permute-start.1) | collective-permute-done | bytes 131104 | tf_op jit(solution)/shard_map/ppermute | solution.py:143
  13.8 0.1 slice_add_fusion
  13.9 0.0 copy-start.3
  13.9 2.2 %fetch.1 = bf16[16384,128]{1,0:T(8,128)(2,1)S(1)} custom-call(bf16[16384,128]{1,0:T(8,128)(2,1)} %source), custom_call_target="tpu_custom_call" | custom-call | bytes 8388608 | tf_op jit(solution)/shard_map/fetch/pallas_call | solution.py:119
  16.1 0.0 copy-start
  16.1 2.0 %copy-done = bf16[16384,128]{1,0:T(8,128)(2,1)} copy-done((bf16[16384,128]{1,0:T(8,128)(2,1)}, bf16[16384,128]{1,0:T(8,128)(2,1)S(1)}, u32[]{:S(2)}) %copy-start) | copy-done | bytes 4194328
  18.1 0.0 copy-start.2
  18.1 0.0 collective-permute-done.2
  18.1 0.0 collective-permute-done.3
  18.1 0.1 convert_add_fusion.1
  18.2 0.0 copy-done.3
  18.2 0.1 slice_bitcast_fusion.3
  18.4 0.1 fusion.4
  18.5 2.9 %collective-permute-start.4 = (bf16[4,16384]{1,0:T(4,128)(2,1)S(1)}, bf16[4,16384]{1,0:T(4,128)(2,1)S(1)}, u32[]{:S(2)}, u32[]{:S(2)}) collective-permute-start(bf16[4,16384]{1,0:T(4,128)(2,1)S(1)} %fusion.4), channel_id=1, source_target_pairs={{0,8},{1,9},{2,10},{3,11},{4,12},{5,13},{6,14},{7,15},{8,0},{9,1},... | collective-permute-start | bytes 393224 | tf_op jit(solution)/shard_map/ppermute | solution.py:143
  21.4 5.8 %collective-permute-done.4 = bf16[4,16384]{1,0:T(4,128)(2,1)S(1)} collective-permute-done((bf16[4,16384]{1,0:T(4,128)(2,1)S(1)}, bf16[4,16384]{1,0:T(4,128)(2,1)S(1)}, u32[]{:S(2)}, u32[]{:S(2)}) %collective-permute-start.4) | collective-permute-done | bytes 131104 | tf_op jit(solution)/shard_map/ppermute | solution.py:143
  27.2 0.1 slice_bitcast_fusion.2
  27.4 0.1 abs_reduce_fusion
  27.5 0.2 multiply_reduce_fusion
  27.8 0.1 fusion.15
  27.9 0.0 copy-done.2
  27.9 0.4 fusion.2
  28.3 1.5 %collective-permute-start.5 = (bf16[4,16384]{1,0:T(4,128)(2,1)S(1)}, bf16[4,16384]{1,0:T(4,128)(2,1)S(1)}, u32[]{:S(2)}, u32[]{:S(2)}) collective-permute-start(bf16[4,16384]{1,0:T(4,128)(2,1)S(1)} %fusion.2), channel_id=1, source_target_pairs={{0,6},{1,7},{2,4},{3,5},{4,2},{5,3},{6,0},{7,1},{8,14},{9,15},{10,... | collective-permute-start | bytes 393224 | tf_op jit(solution)/shard_map/ppermute | solution.py:143
  29.8 0.5 %collective-permute-start.6 = (bf16[4,16384]{1,0:T(4,128)(2,1)S(1)}, bf16[4,16384]{1,0:T(4,128)(2,1)S(1)}, u32[]{:S(2)}, u32[]{:S(2)}) collective-permute-start(bf16[4,16384]{1,0:T(4,128)(2,1)S(1)} %fusion.2), channel_id=1, source_target_pairs={{0,2},{1,3},{2,0},{3,1},{4,6},{5,7},{6,4},{7,5},{8,10},{9,11},{10,... | collective-permute-start | bytes 393224 | tf_op jit(solution)/shard_map/ppermute | solution.py:143
  30.3 1.6 %collective-permute-start.7 = (bf16[4,16384]{1,0:T(4,128)(2,1)S(1)}, bf16[4,16384]{1,0:T(4,128)(2,1)S(1)}, u32[]{:S(2)}, u32[]{:S(2)}) collective-permute-start(bf16[4,16384]{1,0:T(4,128)(2,1)S(1)} %fusion.2), channel_id=1, source_target_pairs={{0,4},{1,5},{2,6},{3,7},{4,0},{5,1},{6,2},{7,3},{8,12},{9,13},{10,... | collective-permute-start | bytes 393224 | tf_op jit(solution)/shard_map/ppermute | solution.py:143
  31.8 0.0 copy-start.1
  31.9 0.6 %slice.54 = f32[2,128]{1,0:T(2,128)} slice(f32[4,128]{1,0:T(4,128)S(1)} %broadcast_add_fusion), slice={[0:2], [0:128]} | slice | bytes 2048 | tf_op jit(solution)/shard_map/slice | solution.py:185
  32.4 2.5 %collective-permute-done.5 = bf16[4,16384]{1,0:T(4,128)(2,1)S(1)} collective-permute-done((bf16[4,16384]{1,0:T(4,128)(2,1)S(1)}, bf16[4,16384]{1,0:T(4,128)(2,1)S(1)}, u32[]{:S(2)}, u32[]{:S(2)}) %collective-permute-start.5) | collective-permute-done | bytes 131104 | tf_op jit(solution)/shard_map/ppermute | solution.py:143
  34.9 1.0 %collective-permute-done.6 = bf16[4,16384]{1,0:T(4,128)(2,1)S(1)} collective-permute-done((bf16[4,16384]{1,0:T(4,128)(2,1)S(1)}, bf16[4,16384]{1,0:T(4,128)(2,1)S(1)}, u32[]{:S(2)}, u32[]{:S(2)}) %collective-permute-start.6) | collective-permute-done | bytes 131104 | tf_op jit(solution)/shard_map/ppermute | solution.py:143
  35.9 0.2 collective-permute-done.7
  36.1 0.3 pad_maximum_fusion
  36.4 0.1 collective-permute-start.8
  36.5 0.7 %copy.22 = bf16[1,2,128,128]{3,1,2,0:T(2,128)(2,1)} copy(bf16[1,2,128,128]{3,2,1,0:T(8,128)(2,1)S(1)} %slice_bitcast_fusion) | data formatting | bytes 131072
  37.2 3.0 %convolution_convert_fusion.3 = bf16[16,128]{1,0:T(8,128)(2,1)S(1)} fusion(bf16[16384,128]{1,0:T(8,128)(2,1)} %copy-done, bf16[4,16384]{1,0:T(4,128)(2,1)S(1)} %collective-permute-done.7, bf16[4,16384]{1,0:T(4,128)(2,1)S(1)} %collective-permute-done.6, bf16[4,16384]{1,0:T(4,128)(2,1)S(1)} %collective-permute-done.5, bf16[4,16384]{1,0:T(4,128)(2,1)S(1)} %fusion.2), kind=kOutput, calls=%fused_computation.3 | convolution fusion | flops 69208064 | bytes 4722688 | tf_op jit(solution)/shard_map/dot_general | solution.py:177
  40.2 0.0 collective-permute-done.8
  40.2 0.0 copy-done.1
  40.2 0.7 %convolution_convert_fusion.2 = bf16[16,128]{1,0:T(8,128)(2,1)S(1)} fusion(bf16[16,16384]{1,0:T(8,128)(2,1)S(1)} %collective-permute-done.8, bf16[16384,128]{1,0:T(8,128)(2,1)S(1)} %copy-done.1), kind=kOutput, calls=%fused_computation.2 | convolution fusion | flops 67110912 | bytes 4722688 | tf_op jit(solution)/shard_map/dot_general | solution.py:178
  40.9 0.9 %convolution_convert_fusion.1 = bf16[32,128]{1,0:T(8,128)(2,1)} fusion(bf16[16,128]{1,0:T(8,128)(2,1)S(1)} %convolution_convert_fusion.2, bf16[16,128]{1,0:T(8,128)(2,1)S(1)} %convolution_convert_fusion.3, s32[32]{0:T(128)S(1)} %and_or_fusion), kind=kOutput, calls=%fused_computation.1 | convolution fusion | flops 283648 | bytes 16512 | tf_op jit(solution)/shard_map/dot_general | solution.py:182
  (7 shorter events, 0.1 us)
Async XLA Ops:
  3.6 2.0 %collective-permute-start = (bf16[16,16384]{1,0:T(8,128)(2,1)S(1)}, bf16[16,16384]{1,0:T(8,128)(2,1)S(1)}, u32[]{:S(2)}, u32[]{:S(2)}) collective-permute-start(bf16[16,16384]{1,0:T(8,128)(2,1)S(1)} %convolution_convert_fusion), channel_id=1, source_target_pairs={{0,1},{1,0},{2,3},{3,2},{4,5},{5,4},{6,7},{7,6},{8,9},{9,8},{10,11... | collective-permute-start | bytes 1572872 | tf_op jit(solution)/shard_map/ppermute | solution.py:143
  5.9 7.9 %collective-permute-start.1 = (bf16[4,16384]{1,0:T(4,128)(2,1)S(1)}, bf16[4,16384]{1,0:T(4,128)(2,1)S(1)}, u32[]{:S(2)}, u32[]{:S(2)}) collective-permute-start(bf16[4,16384]{1,0:T(4,128)(2,1)S(1)} %get-tuple-element.21), channel_id=1, source_target_pairs={{0,6},{1,7},{2,4},{3,5},{4,2},{5,3},{6,0},{7,1},{8,14},{9,15},{10,... | collective-permute-start | bytes 393224 | tf_op jit(solution)/shard_map/ppermute | solution.py:143
  9.9 8.2 %collective-permute-start.2 = (bf16[4,16384]{1,0:T(4,128)(2,1)S(1)}, bf16[4,16384]{1,0:T(4,128)(2,1)S(1)}, u32[]{:S(2)}, u32[]{:S(2)}) collective-permute-start(bf16[4,16384]{1,0:T(4,128)(2,1)S(1)} %get-tuple-element.19), channel_id=1, source_target_pairs={{0,2},{1,3},{2,0},{3,1},{4,6},{5,7},{6,4},{7,5},{8,10},{9,11},{10,... | collective-permute-start | bytes 393224 | tf_op jit(solution)/shard_map/ppermute | solution.py:143
  10.4 7.7 %collective-permute-start.3 = (bf16[4,16384]{1,0:T(4,128)(2,1)S(1)}, bf16[4,16384]{1,0:T(4,128)(2,1)S(1)}, u32[]{:S(2)}, u32[]{:S(2)}) collective-permute-start(bf16[4,16384]{1,0:T(4,128)(2,1)S(1)} %get-tuple-element.20), channel_id=1, source_target_pairs={{0,4},{1,5},{2,6},{3,7},{4,0},{5,1},{6,2},{7,3},{8,12},{9,13},{10,... | collective-permute-start | bytes 393224 | tf_op jit(solution)/shard_map/ppermute | solution.py:143
  13.9 4.3 %copy-start.3 = (bf16[2,16384]{1,0:T(2,128)(2,1)S(1)}, bf16[2,16384]{1,0:T(2,128)(2,1)}, u32[]{:S(2)}) copy-start(bf16[2,16384]{1,0:T(2,128)(2,1)} %param.7) | copy-start | bytes 196612
  16.1 2.0 %copy-start = (bf16[16384,128]{1,0:T(8,128)(2,1)}, bf16[16384,128]{1,0:T(8,128)(2,1)S(1)}, u32[]{:S(2)}) copy-start(bf16[16384,128]{1,0:T(8,128)(2,1)S(1)} %fetch.1) | copy-start | bytes 12582916
  18.1 9.8 %copy-start.2 = (f32[16384]{0:T(1024)S(1)}, f32[16384]{0:T(1024)}, u32[]{:S(2)}) copy-start(f32[16384]{0:T(1024)} %param.12) | copy-start | bytes 196612
  18.5 8.7 %collective-permute-start.4 = (bf16[4,16384]{1,0:T(4,128)(2,1)S(1)}, bf16[4,16384]{1,0:T(4,128)(2,1)S(1)}, u32[]{:S(2)}, u32[]{:S(2)}) collective-permute-start(bf16[4,16384]{1,0:T(4,128)(2,1)S(1)} %fusion.4), channel_id=1, source_target_pairs={{0,8},{1,9},{2,10},{3,11},{4,12},{5,13},{6,14},{7,15},{8,0},{9,1},... | collective-permute-start | bytes 393224 | tf_op jit(solution)/shard_map/ppermute | solution.py:143
  28.3 6.6 %collective-permute-start.5 = (bf16[4,16384]{1,0:T(4,128)(2,1)S(1)}, bf16[4,16384]{1,0:T(4,128)(2,1)S(1)}, u32[]{:S(2)}, u32[]{:S(2)}) collective-permute-start(bf16[4,16384]{1,0:T(4,128)(2,1)S(1)} %fusion.2), channel_id=1, source_target_pairs={{0,6},{1,7},{2,4},{3,5},{4,2},{5,3},{6,0},{7,1},{8,14},{9,15},{10,... | collective-permute-start | bytes 393224 | tf_op jit(solution)/shard_map/ppermute | solution.py:143
  29.8 6.1 %collective-permute-start.6 = (bf16[4,16384]{1,0:T(4,128)(2,1)S(1)}, bf16[4,16384]{1,0:T(4,128)(2,1)S(1)}, u32[]{:S(2)}, u32[]{:S(2)}) collective-permute-start(bf16[4,16384]{1,0:T(4,128)(2,1)S(1)} %fusion.2), channel_id=1, source_target_pairs={{0,2},{1,3},{2,0},{3,1},{4,6},{5,7},{6,4},{7,5},{8,10},{9,11},{10,... | collective-permute-start | bytes 393224 | tf_op jit(solution)/shard_map/ppermute | solution.py:143
  30.3 5.8 %collective-permute-start.7 = (bf16[4,16384]{1,0:T(4,128)(2,1)S(1)}, bf16[4,16384]{1,0:T(4,128)(2,1)S(1)}, u32[]{:S(2)}, u32[]{:S(2)}) collective-permute-start(bf16[4,16384]{1,0:T(4,128)(2,1)S(1)} %fusion.2), channel_id=1, source_target_pairs={{0,4},{1,5},{2,6},{3,7},{4,0},{5,1},{6,2},{7,3},{8,12},{9,13},{10,... | collective-permute-start | bytes 393224 | tf_op jit(solution)/shard_map/ppermute | solution.py:143
  31.8 8.3 %copy-start.1 = (bf16[16384,128]{1,0:T(8,128)(2,1)S(1)}, bf16[16384,128]{1,0:T(8,128)(2,1)}, u32[]{:S(2)}) copy-start(bf16[16384,128]{1,0:T(8,128)(2,1)} %copy-done) | copy-start | bytes 12582916
  36.4 3.8 %collective-permute-start.8 = (bf16[16,16384]{1,0:T(8,128)(2,1)S(1)}, bf16[16,16384]{1,0:T(8,128)(2,1)S(1)}, u32[]{:S(2)}, u32[]{:S(2)}) collective-permute-start(bf16[16,16384]{1,0:T(8,128)(2,1)S(1)} %pad_maximum_fusion), channel_id=1, source_target_pairs={{0,1},{1,0},{2,3},{3,2},{4,5},{5,4},{6,7},{7,6},{8,9},{9,8},{10,11... | collective-permute-start | bytes 1572872 | tf_op jit(solution)/shard_map/ppermute | solution.py:143

commit v9 on v8

--- a/solution.py
+++ b/solution.py
@@ -13,6 +13,7 @@
 F32 = jnp.float32
 BF16 = jnp.bfloat16
 PIECES = 4
+STEPS = 8
 VMEM_LIMIT = 24 << 20
 
 
@@ -104,30 +105,47 @@
     )(*in_hbm(queries, keys, values, weight))
 
 
-def fetch_kernel(source, target, sems):
-    depth = source.shape[0] // PIECES
-    copies = []
-    for c in range(PIECES):
+def times(rows, weight):
+    depth = weight.shape[0] // STEPS
+    total = jnp.zeros((rows.shape[0], weight.shape[1]), F32)
+    for c in range(STEPS):
         part = pl.ds(c * depth, depth)
-        copies.append(pltpu.make_async_copy(source.at[part], target.at[part], sems.at[c]))
-        copies[-1].start()
-    for copy in copies:
-        copy.wait()
-
-
-def fetch(weight):
+        total += jnp.dot(rows[:, part], weight[part], preferred_element_type=F32)
+    return total
+
+
+def first_dot_kernel(rows, weight, out):
+    out[...] = times(rows, weight).astype(BF16)
+
+
+def last_dot_kernel(n, local, rows, weight, near, out):
+    device = lax.axis_index("tp")
+    tokens, half = out.shape[0], rows.shape[0]
+    row = lax.broadcasted_iota(jnp.int32, (tokens, half), 1) ^ (3 * half // 4)
+    token = lax.broadcasted_iota(jnp.int32, (tokens, half), 0)
+    far = times(rows, weight).astype(BF16)
+    total = jnp.zeros(out.shape, F32)
+    for start, values in ((0, near[...]), (half, far)):
+        pick = (owner_token(row + start, device, n, local) == token).astype(F32).astype(BF16)
+        total += jnp.dot(pick, values, preferred_element_type=F32)
+    out[...] = total.astype(BF16)
+
+
+def small_call(kernel, shape, name, *operands):
+    spec = pl.BlockSpec(memory_space=pltpu.VMEM)
     return pl.pallas_call(
-        fetch_kernel,
-        out_shape=pltpu.VMEM(weight.shape, BF16),
-        in_specs=[pl.BlockSpec(memory_space=pltpu.HBM)],
-        out_specs=pl.BlockSpec(memory_space=pltpu.VMEM),
-        scratch_shapes=[pltpu.SemaphoreType.DMA((PIECES,))],
+        kernel,
+        out_shape=jax.ShapeDtypeStruct(shape, BF16),
+        in_specs=[spec] * len(operands),
+        out_specs=spec,
         compiler_params=pltpu.CompilerParams(vmem_limit_bytes=VMEM_LIMIT),
         cost_estimate=pl.CostEstimate(
-            flops=0, bytes_accessed=4 * weight.size, transcendentals=0
+            flops=2 * operands[0].size * operands[1].shape[1],
+            bytes_accessed=2 * operands[1].size,
+            transcendentals=0,
         ),
-        name="fetch",
-    )(*in_hbm(weight))
+        name=name,
+    )(*operands)
 
 
 def on_device(residual, queries, key_rows, value_rows, out_weight, norm_gain, q_weight):
@@ -151,11 +169,8 @@
     part = half // 4
     pieces = [total[k * part : (k + 1) * part].astype(BF16) for k in range(1, 4)]
     arrived = [swap(piece, distance) for piece, distance in zip(pieces, square)]
-    arrived[0], q_weight = lax.optimization_barrier((arrived[0], q_weight))
-    total, q_weight = lax.optimization_barrier(
-        (total[:part] + arrived[0].astype(F32), fetch(q_weight))
-    )
-    for piece in arrived[1:]:
+    total = total[:part]
+    for piece in arrived:
         total = total + piece.astype(F32)
     for level in levels[:-1]:
         kept = total.shape[0] // 2
@@ -172,16 +187,13 @@
     held = (decoded * lax.rsqrt(mean_sq + 1e-05) * norm_gain[None, :]).astype(BF16)
     for level in levels[-2::-1]:
         held = jnp.concatenate([held, swap(held, level)], axis=0)
-    held = jnp.concatenate([held] + [swap(held, distance) for distance in square], axis=0)
+    arrived = [swap(held, distance) for distance in square]
+    held = jnp.concatenate(arrived[::-1] + [held], axis=0)
     other = swap(held, 1)
-    out_mine = jnp.dot(held, q_weight, preferred_element_type=F32).astype(BF16)
-    out_other = jnp.dot(other, q_weight, preferred_element_type=F32).astype(BF16)
-    found = jnp.concatenate([out_mine, out_other], axis=0)
-    row = jnp.arange(tokens)
-    pick = (owner_token(row, device, n, local)[:, None] == row[None, :]).astype(BF16)
-    next_queries = lax.dot_general(
-        pick, found, (((0,), (0,)), ((), ())), preferred_element_type=F32
-    ).astype(BF16)
+    near = small_call(first_dot_kernel, (half, q_weight.shape[1]), "first_dot", held, q_weight)
+    last = functools.partial(last_dot_kernel, n, local)
+    shape = (tokens, q_weight.shape[1])
+    next_queries = small_call(last, shape, "last_dot", other, q_weight, near)
     return (codes.reshape(rows, D)[:local], scales[:local], next_queries)
 
 

time: 41.9 us -> 39.7 us (0.947)
  waiting for transfers between devices: 13.6 us -> 18.4 us
  matrix products: 5.83 us -> 1.31 us
  local copies, waits for them, and re-layouts: 3.64 us -> 1.67 us
    ppermute x9, waiting for transfers between devices: 13.6 us -> 18.4 us  [swap(): return lax.ppermute(x, 'tp', [(i, i ^ distance) for i in range(n)])]
    dot_general x3 -> x0, matrix products: 4.52 us -> none  [the longest x1 2.97 us: on_device(): out_mine = jnp.dot(held, q_weight, preferred_element_type=F32).astype(BF16)]
    unnamed x11 -> x9, local copies, waits for them, and re-layouts: 2.78 us -> 0.82 us
    pallas_call x1 -> x2, Pallas kernels: 2.24 us -> 2.07 us  [small_call(): pl.pallas_call(kernel, out_shape=jax.ShapeDtypeStruct(shape, BF16), in_sp...]
  transfers between devices with their start and end apart: 9 -> 9, of which waited for: 6 -> 7; matrix products, arithmetic and copies ran while one was open for 12% -> 5% of each run, Pallas kernels for 5% -> 2%
where the time goes in v9:
time: 39.7 us; the launch traced here: 39.5 us
  waiting for transfers between devices  18.4 us (46%)
  starting transfers between devices  11.4 us (29%)
  Pallas kernels  4.36 us (11%)
  local copies, waits for them, and re-layouts  1.67 us (4%)
  other arithmetic  1.63 us (4%)
  matrix products  1.31 us (3%)
  between operations  0.76 us (2%)
    ppermute x9, waiting for transfers between devices, swap(): return lax.ppermute(x, 'tp', [(i, i ^ distance) for i in range(n)])  18.4 us
    ppermute x9, starting transfers between devices, swap(): return lax.ppermute(x, 'tp', [(i, i ^ distance) for i in range(n)])  11.4 us
    pallas_call x1, Pallas kernels, attend(): pl.pallas_call(functools.partial(attend_kernel, n, local), out_shape=[jax...  2.28 us
    pallas_call x2, Pallas kernels, small_call(): pl.pallas_call(kernel, out_shape=jax.ShapeDtypeStruct(shape, BF16), in_sp...  2.07 us
    unnamed x9, local copies, waits for them, and re-layouts  0.82 us
  transfers between devices with their start and end apart: 9, of which 7 were waited for; matrix products, arithmetic and copies ran while one was open for 5% of the time, Pallas kernels for 2%

profile of v9, /device:TPU:0, one launch (start us, length us, event | category | flops | bytes accessed | tf_op | source)
XLA Modules:
  0.0 39.5 jit_solution(6862568465272061282)
XLA Ops:
  0.6 2.3 %attend.1 = (bf16[32,128]{1,0:T(8,128)(2,1)S(1)}, bf16[128,16384]{1,0:T(8,128)(2,1)S(1)}) custom-call(bf16[32,128]{1,0:T(8,128)(2,1)} %queries.1, bf16[32,1024]{1,0:T(8,128)(2,1)} %keys.1, bf16[32,1024]{1,0:T(8,128)(2,1)} %values.1, bf16[128,16384]{1,0:T(8,128)(2,1)} %weight.3), custom_call_target="tpu_custom_call" | custom-call | bytes 4194304 | tf_op jit(solution)/shard_map/attend/pallas_call | solution.py:85
  2.9 0.7 %convolution_convert_fusion = bf16[16,16384]{1,0:T(8,128)(2,1)S(1)} fusion(bf16[128,16384]{1,0:T(8,128)(2,1)S(1)} %get-tuple-element.6, bf16[32,128]{1,0:T(8,128)(2,1)S(1)} %get-tuple-element.5), kind=kOutput, calls=%fused_computation | convolution fusion | flops 67371008 | bytes 4722688 | tf_op jit(solution)/shard_map/dot_general | solution.py:165
  3.6 0.0 copy-start.2
  3.6 0.5 %collective-permute-start = (bf16[16,16384]{1,0:T(8,128)(2,1)S(1)}, bf16[16,16384]{1,0:T(8,128)(2,1)S(1)}, u32[]{:S(2)}, u32[]{:S(2)}) collective-permute-start(bf16[16,16384]{1,0:T(8,128)(2,1)S(1)} %convolution_convert_fusion), channel_id=1, source_target_pairs={{0,1},{1,0},{2,3},{3,2},{4,5},{5,4},{6,7},{7,6},{8,9},{9,8},{10,11... | collective-permute-start | bytes 1572872 | tf_op jit(solution)/shard_map/ppermute | solution.py:161
  4.1 0.7 %fusion.8 = f32[16,16384]{1,0:T(8,128)S(1)} fusion(bf16[128,16384]{1,0:T(8,128)(2,1)S(1)} %get-tuple-element.6, bf16[32,128]{1,0:T(8,128)(2,1)S(1)} %get-tuple-element.5), kind=kOutput, calls=%fused_computation.28 | convolution fusion | flops 67108864 | bytes 5246976 | tf_op jit(solution)/shard_map/dot_general | solution.py:167
  4.8 0.0 copy-start.1
  4.8 0.9 %collective-permute-done = bf16[16,16384]{1,0:T(8,128)(2,1)S(1)} collective-permute-done((bf16[16,16384]{1,0:T(8,128)(2,1)S(1)}, bf16[16,16384]{1,0:T(8,128)(2,1)S(1)}, u32[]{:S(2)}, u32[]{:S(2)}) %collective-permute-start) | collective-permute-done | bytes 524320 | tf_op jit(solution)/shard_map/ppermute | solution.py:161
  5.6 0.1 fusion.10
  5.7 0.2 fusion.11
  5.9 0.0 copy-start
  5.9 4.0 %collective-permute-start.1 = (bf16[4,16384]{1,0:T(4,128)(2,1)S(1)}, bf16[4,16384]{1,0:T(4,128)(2,1)S(1)}, u32[]{:S(2)}, u32[]{:S(2)}) collective-permute-start(bf16[4,16384]{1,0:T(4,128)(2,1)S(1)} %get-tuple-element.11), channel_id=1, source_target_pairs={{0,6},{1,7},{2,4},{3,5},{4,2},{5,3},{6,0},{7,1},{8,14},{9,15},{10,... | collective-permute-start | bytes 393224 | tf_op jit(solution)/shard_map/ppermute | solution.py:161
  9.9 0.5 %collective-permute-start.3 = (bf16[4,16384]{1,0:T(4,128)(2,1)S(1)}, bf16[4,16384]{1,0:T(4,128)(2,1)S(1)}, u32[]{:S(2)}, u32[]{:S(2)}) collective-permute-start(bf16[4,16384]{1,0:T(4,128)(2,1)S(1)} %get-tuple-element.12), channel_id=1, source_target_pairs={{0,4},{1,5},{2,6},{3,7},{4,0},{5,1},{6,2},{7,3},{8,12},{9,13},{10,... | collective-permute-start | bytes 393224 | tf_op jit(solution)/shard_map/ppermute | solution.py:161
  10.4 0.2 collective-permute-start.2
  10.5 3.6 %collective-permute-done.1 = bf16[4,16384]{1,0:T(4,128)(2,1)S(1)} collective-permute-done((bf16[4,16384]{1,0:T(4,128)(2,1)S(1)}, bf16[4,16384]{1,0:T(4,128)(2,1)S(1)}, u32[]{:S(2)}, u32[]{:S(2)}) %collective-permute-start.1) | collective-permute-done | bytes 131104 | tf_op jit(solution)/shard_map/ppermute | solution.py:161
  14.2 2.5 %collective-permute-done.3 = bf16[4,16384]{1,0:T(4,128)(2,1)S(1)} collective-permute-done((bf16[4,16384]{1,0:T(4,128)(2,1)S(1)}, bf16[4,16384]{1,0:T(4,128)(2,1)S(1)}, u32[]{:S(2)}, u32[]{:S(2)}) %collective-permute-start.3) | collective-permute-done | bytes 131104 | tf_op jit(solution)/shard_map/ppermute | solution.py:161
  16.7 0.0 collective-permute-done.2
  16.7 0.1 fusion.4
  16.8 0.0 copy-done.2
  16.8 0.1 slice_bitcast_fusion.3
  17.0 0.1 fusion.6
  17.1 2.6 %collective-permute-start.4 = (bf16[4,16384]{1,0:T(4,128)(2,1)S(1)}, bf16[4,16384]{1,0:T(4,128)(2,1)S(1)}, u32[]{:S(2)}, u32[]{:S(2)}) collective-permute-start(bf16[4,16384]{1,0:T(4,128)(2,1)S(1)} %fusion.6), channel_id=1, source_target_pairs={{0,8},{1,9},{2,10},{3,11},{4,12},{5,13},{6,14},{7,15},{8,0},{9,1},... | collective-permute-start | bytes 393224 | tf_op jit(solution)/shard_map/ppermute | solution.py:161
  19.8 6.0 %collective-permute-done.4 = bf16[4,16384]{1,0:T(4,128)(2,1)S(1)} collective-permute-done((bf16[4,16384]{1,0:T(4,128)(2,1)S(1)}, bf16[4,16384]{1,0:T(4,128)(2,1)S(1)}, u32[]{:S(2)}, u32[]{:S(2)}) %collective-permute-start.4) | collective-permute-done | bytes 131104 | tf_op jit(solution)/shard_map/ppermute | solution.py:161
  25.8 0.1 slice_bitcast_fusion.2
  26.0 0.1 abs_reduce_fusion
  26.1 0.2 multiply_reduce_fusion
  26.4 0.1 fusion.12
  26.5 0.0 copy-done.1
  26.5 0.4 %fusion.2 = bf16[4,16384]{1,0:T(4,128)(2,1)S(1)} fusion(f32[2,16384]{1,0:T(2,128)S(1)} %get-tuple-element.20, f32[2,16384]{1,0:T(2,128)S(1)} %get-tuple-element.19, f32[1,4,128,128]{3,2,1,0:T(8,128)S(1)} %get-tuple-element.21, f32[2,16384]{1,0:T(2,128)S(1)} %get-tuple-element.15, f32[2,16384]{1,0:T(2,128)S(1)} %get-tuple-element.16, f32[16384]{0:T(1024)S(1)} %copy-done.1, ...), kind=kLoop, calls=%fused_computation.7 | loop fusion | flops 655360 | bytes 983056 | tf_op jit(solution)/shard_map/convert_element_type | solution.py:187
  26.9 2.1 %collective-permute-start.7 = (bf16[4,16384]{1,0:T(4,128)(2,1)S(1)}, bf16[4,16384]{1,0:T(4,128)(2,1)S(1)}, u32[]{:S(2)}, u32[]{:S(2)}) collective-permute-start(bf16[4,16384]{1,0:T(4,128)(2,1)S(1)} %fusion.2), channel_id=1, source_target_pairs={{0,6},{1,7},{2,4},{3,5},{4,2},{5,3},{6,0},{7,1},{8,14},{9,15},{10,... | collective-permute-start | bytes 393224 | tf_op jit(solution)/shard_map/ppermute | solution.py:161
  29.0 0.1 collective-permute-start.6
  29.1 1.3 %collective-permute-start.5 = (bf16[4,16384]{1,0:T(4,128)(2,1)S(1)}, bf16[4,16384]{1,0:T(4,128)(2,1)S(1)}, u32[]{:S(2)}, u32[]{:S(2)}) collective-permute-start(bf16[4,16384]{1,0:T(4,128)(2,1)S(1)} %fusion.2), channel_id=1, source_target_pairs={{0,4},{1,5},{2,6},{3,7},{4,0},{5,1},{6,2},{7,3},{8,12},{9,13},{10,... | collective-permute-start | bytes 393224 | tf_op jit(solution)/shard_map/ppermute | solution.py:161
  30.4 2.8 %collective-permute-done.7 = bf16[4,16384]{1,0:T(4,128)(2,1)S(1)} collective-permute-done((bf16[4,16384]{1,0:T(4,128)(2,1)S(1)}, bf16[4,16384]{1,0:T(4,128)(2,1)S(1)}, u32[]{:S(2)}, u32[]{:S(2)}) %collective-permute-start.7) | collective-permute-done | bytes 131104 | tf_op jit(solution)/shard_map/ppermute | solution.py:161
  33.2 2.4 %collective-permute-done.6 = bf16[4,16384]{1,0:T(4,128)(2,1)S(1)} collective-permute-done((bf16[4,16384]{1,0:T(4,128)(2,1)S(1)}, bf16[4,16384]{1,0:T(4,128)(2,1)S(1)}, u32[]{:S(2)}, u32[]{:S(2)}) %collective-permute-start.6) | collective-permute-done | bytes 131104 | tf_op jit(solution)/shard_map/ppermute | solution.py:161
  35.5 0.2 collective-permute-done.5
  35.7 0.3 pad_maximum_fusion.rows
  36.0 0.1 collective-permute-start.8
  36.1 0.6 %slice.54 = f32[2,128]{1,0:T(2,128)} slice(f32[4,128]{1,0:T(4,128)S(1)} %broadcast_add_fusion), slice={[0:2], [0:128]} | slice | bytes 2048 | tf_op jit(solution)/shard_map/slice | solution.py:197
  36.7 0.7 %copy.22 = bf16[1,2,128,128]{3,1,2,0:T(2,128)(2,1)} copy(bf16[1,2,128,128]{3,2,1,0:T(8,128)(2,1)S(1)} %slice_bitcast_fusion) | data formatting | bytes 131072
  37.4 0.0 copy-done
  37.4 0.7 %first_dot.1.near = bf16[16,128]{1,0:T(8,128)(2,1)S(1)} custom-call(bf16[16,16384]{1,0:T(8,128)(2,1)S(1)} %pad_maximum_fusion.rows, bf16[16384,128]{1,0:T(8,128)(2,1)S(1)} %copy-done), custom_call_target="tpu_custom_call" | custom-call | flops 67108864 | bytes 4194304 | tf_op jit(solution)/shard_map/first_dot/pallas_call | solution.py:136
  38.1 0.0 collective-permute-done.8.rows
  38.1 1.4 %last_dot.1 = bf16[32,128]{1,0:T(8,128)(2,1)} custom-call(bf16[16,16384]{1,0:T(8,128)(2,1)S(1)} %collective-permute-done.8.rows, bf16[16384,128]{1,0:T(8,128)(2,1)S(1)} %copy-done, bf16[16,128]{1,0:T(8,128)(2,1)S(1)} %first_dot.1.near), custom_call_target="tpu_custom_call" | custom-call | flops 67108864 | bytes 4194304 | tf_op jit(solution)/shard_map/last_dot/pallas_call | solution.py:136
  (6 shorter events, 0.1 us)
Async XLA Ops:
  3.6 13.2 %copy-start.2 = (bf16[2,16384]{1,0:T(2,128)(2,1)S(1)}, bf16[2,16384]{1,0:T(2,128)(2,1)}, u32[]{:S(2)}) copy-start(bf16[2,16384]{1,0:T(2,128)(2,1)} %param.7) | copy-start | bytes 196612
  3.6 2.1 %collective-permute-start = (bf16[16,16384]{1,0:T(8,128)(2,1)S(1)}, bf16[16,16384]{1,0:T(8,128)(2,1)S(1)}, u32[]{:S(2)}, u32[]{:S(2)}) collective-permute-start(bf16[16,16384]{1,0:T(8,128)(2,1)S(1)} %convolution_convert_fusion), channel_id=1, source_target_pairs={{0,1},{1,0},{2,3},{3,2},{4,5},{5,4},{6,7},{7,6},{8,9},{9,8},{10,11... | collective-permute-start | bytes 1572872 | tf_op jit(solution)/shard_map/ppermute | solution.py:161
  4.8 21.7 %copy-start.1 = (f32[16384]{0:T(1024)S(1)}, f32[16384]{0:T(1024)}, u32[]{:S(2)}) copy-start(f32[16384]{0:T(1024)} %param.12) | copy-start | bytes 196612
  5.9 31.5 %copy-start = (bf16[16384,128]{1,0:T(8,128)(2,1)S(1)}, bf16[16384,128]{1,0:T(8,128)(2,1)}, u32[]{:S(2)}) copy-start(bf16[16384,128]{1,0:T(8,128)(2,1)} %weight.5) | copy-start | bytes 12582916
  5.9 8.2 %collective-permute-start.1 = (bf16[4,16384]{1,0:T(4,128)(2,1)S(1)}, bf16[4,16384]{1,0:T(4,128)(2,1)S(1)}, u32[]{:S(2)}, u32[]{:S(2)}) collective-permute-start(bf16[4,16384]{1,0:T(4,128)(2,1)S(1)} %get-tuple-element.11), channel_id=1, source_target_pairs={{0,6},{1,7},{2,4},{3,5},{4,2},{5,3},{6,0},{7,1},{8,14},{9,15},{10,... | collective-permute-start | bytes 393224 | tf_op jit(solution)/shard_map/ppermute | solution.py:161
  9.9 6.8 %collective-permute-start.3 = (bf16[4,16384]{1,0:T(4,128)(2,1)S(1)}, bf16[4,16384]{1,0:T(4,128)(2,1)S(1)}, u32[]{:S(2)}, u32[]{:S(2)}) collective-permute-start(bf16[4,16384]{1,0:T(4,128)(2,1)S(1)} %get-tuple-element.12), channel_id=1, source_target_pairs={{0,4},{1,5},{2,6},{3,7},{4,0},{5,1},{6,2},{7,3},{8,12},{9,13},{10,... | collective-permute-start | bytes 393224 | tf_op jit(solution)/shard_map/ppermute | solution.py:161
  10.4 6.3 %collective-permute-start.2 = (bf16[4,16384]{1,0:T(4,128)(2,1)S(1)}, bf16[4,16384]{1,0:T(4,128)(2,1)S(1)}, u32[]{:S(2)}, u32[]{:S(2)}) collective-permute-start(bf16[4,16384]{1,0:T(4,128)(2,1)S(1)} %get-tuple-element.13), channel_id=1, source_target_pairs={{0,2},{1,3},{2,0},{3,1},{4,6},{5,7},{6,4},{7,5},{8,10},{9,11},{10,... | collective-permute-start | bytes 393224 | tf_op jit(solution)/shard_map/ppermute | solution.py:161
  17.1 8.7 %collective-permute-start.4 = (bf16[4,16384]{1,0:T(4,128)(2,1)S(1)}, bf16[4,16384]{1,0:T(4,128)(2,1)S(1)}, u32[]{:S(2)}, u32[]{:S(2)}) collective-permute-start(bf16[4,16384]{1,0:T(4,128)(2,1)S(1)} %fusion.6), channel_id=1, source_target_pairs={{0,8},{1,9},{2,10},{3,11},{4,12},{5,13},{6,14},{7,15},{8,0},{9,1},... | collective-permute-start | bytes 393224 | tf_op jit(solution)/shard_map/ppermute | solution.py:161
  26.9 6.3 %collective-permute-start.7 = (bf16[4,16384]{1,0:T(4,128)(2,1)S(1)}, bf16[4,16384]{1,0:T(4,128)(2,1)S(1)}, u32[]{:S(2)}, u32[]{:S(2)}) collective-permute-start(bf16[4,16384]{1,0:T(4,128)(2,1)S(1)} %fusion.2), channel_id=1, source_target_pairs={{0,6},{1,7},{2,4},{3,5},{4,2},{5,3},{6,0},{7,1},{8,14},{9,15},{10,... | collective-permute-start | bytes 393224 | tf_op jit(solution)/shard_map/ppermute | solution.py:161
  29.0 6.5 %collective-permute-start.6 = (bf16[4,16384]{1,0:T(4,128)(2,1)S(1)}, bf16[4,16384]{1,0:T(4,128)(2,1)S(1)}, u32[]{:S(2)}, u32[]{:S(2)}) collective-permute-start(bf16[4,16384]{1,0:T(4,128)(2,1)S(1)} %fusion.2), channel_id=1, source_target_pairs={{0,2},{1,3},{2,0},{3,1},{4,6},{5,7},{6,4},{7,5},{8,10},{9,11},{10,... | collective-permute-start | bytes 393224 | tf_op jit(solution)/shard_map/ppermute | solution.py:161
  29.1 6.6 %collective-permute-start.5 = (bf16[4,16384]{1,0:T(4,128)(2,1)S(1)}, bf16[4,16384]{1,0:T(4,128)(2,1)S(1)}, u32[]{:S(2)}, u32[]{:S(2)}) collective-permute-start(bf16[4,16384]{1,0:T(4,128)(2,1)S(1)} %fusion.2), channel_id=1, source_target_pairs={{0,4},{1,5},{2,6},{3,7},{4,0},{5,1},{6,2},{7,3},{8,12},{9,13},{10,... | collective-permute-start | bytes 393224 | tf_op jit(solution)/shard_map/ppermute | solution.py:161
  36.0 2.0 %collective-permute-start.8 = (bf16[16,16384]{1,0:T(8,128)(2,1)S(1)}, bf16[16,16384]{1,0:T(8,128)(2,1)S(1)}, u32[]{:S(2)}, u32[]{:S(2)}) collective-permute-start(bf16[16,16384]{1,0:T(8,128)(2,1)S(1)} %pad_maximum_fusion.rows), channel_id=1, source_target_pairs={{0,1},{1,0},{2,3},{3,2},{4,5},{5,4},{6,7},{7,6},{8,9},{9,8},{10,11... | collective-permute-start | bytes 1572872 | tf_op jit(solution)/shard_map/ppermute | solution.py:161

commit v10 on v9

--- a/solution.py
+++ b/solution.py
@@ -22,17 +22,19 @@
 
 
 def owner_token(row, device, n, local):
-    bits = [1, 2, 6] + late_levels(n)
-    shift = local.bit_length() - 1
+    bits = [2, 6] + late_levels(n)
+    shift = local.bit_length() - 2
     block = row >> shift
-    distance = jnp.zeros_like(row)
+    distance = block >> (len(bits) + 1)
+    part = (block >> len(bits)) & 1
     for place, bit in enumerate(bits):
         distance = distance ^ (((block >> (len(bits) - 1 - place)) & 1) * bit)
-    return ((device ^ distance) << shift) | (row & (local - 1))
+    own = (part << shift) | (row & (local // 2 - 1))
+    return ((device ^ distance) << (shift + 1)) | own
 
 
 def attend_kernel(
-    n, local, queries, keys, values, weight, context, held, query, key, value, small, large
+    n, local, queries, keys, values, weight, old, context, held, fresh, query, key, value, small, large
 ):
     device = lax.axis_index("tp")
     tokens = queries.shape[0]
@@ -44,7 +46,7 @@
         copies.append(pltpu.make_async_copy(keys.at[:, at], key.at[h], small.at[1 + 2 * h]))
         copies.append(pltpu.make_async_copy(values.at[:, at], value.at[h], small.at[2 + 2 * h]))
     depth = held.shape[0] // PIECES
-    late = []
+    late = [pltpu.make_async_copy(old, fresh, small.at[1 + 2 * heads])]
     for c in range(PIECES):
         part = pl.ds(c * depth, depth)
         late.append(pltpu.make_async_copy(weight.at[part], held.at[part], large.at[c]))
@@ -78,7 +80,7 @@
     return [pltpu.with_memory_space_constraint(x, pltpu.HBM) for x in arrays]
 
 
-def attend(n, local, queries, keys, values, weight):
+def attend(n, local, queries, keys, values, weight, old):
     tokens = queries.shape[0]
     heads = queries.shape[1] // HD
     whole = pl.BlockSpec(memory_space=pltpu.VMEM)
@@ -87,14 +89,15 @@
         out_shape=[
             jax.ShapeDtypeStruct(queries.shape, BF16),
             pltpu.VMEM(weight.shape, BF16),
+            pltpu.VMEM(old.shape, BF16),
         ],
-        in_specs=[pl.BlockSpec(memory_space=pltpu.HBM)] * 4,
-        out_specs=[whole, whole],
+        in_specs=[pl.BlockSpec(memory_space=pltpu.HBM)] * 5,
+        out_specs=[whole] * 3,
         scratch_shapes=[
             pltpu.VMEM(queries.shape, BF16),
             pltpu.VMEM((heads, tokens, HD), BF16),
             pltpu.VMEM((heads, tokens, HD), BF16),
-            pltpu.SemaphoreType.DMA((1 + 2 * heads,)),
+            pltpu.SemaphoreType.DMA((2 + 2 * heads,)),
             pltpu.SemaphoreType.DMA((PIECES,)),
         ],
         compiler_params=pltpu.CompilerParams(vmem_limit_bytes=VMEM_LIMIT),
@@ -102,7 +105,7 @@
             flops=0, bytes_accessed=2 * weight.size, transcendentals=0
         ),
         name="attend",
-    )(*in_hbm(queries, keys, values, weight))
+    )(*in_hbm(queries, keys, values, weight, old))
 
 
 def times(rows, weight):
@@ -118,14 +121,19 @@
     out[...] = times(rows, weight).astype(BF16)
 
 
-def last_dot_kernel(n, local, rows, weight, near, out):
+def last_dot_kernel(n, local, rows, weight, early, near, out):
     device = lax.axis_index("tp")
-    tokens, half = out.shape[0], rows.shape[0]
-    row = lax.broadcasted_iota(jnp.int32, (tokens, half), 1) ^ (3 * half // 4)
-    token = lax.broadcasted_iota(jnp.int32, (tokens, half), 0)
+    tokens, quarter = out.shape[0], rows.shape[0]
+    token = lax.broadcasted_iota(jnp.int32, (tokens, quarter), 0)
+    row = lax.broadcasted_iota(jnp.int32, (tokens, quarter), 1) ^ (3 * quarter // 4)
     far = times(rows, weight).astype(BF16)
     total = jnp.zeros(out.shape, F32)
-    for start, values in ((0, near[...]), (half, far)):
+    for start, values in (
+        (0, early[:quarter]),
+        (2 * quarter, early[quarter:]),
+        (quarter, near[...]),
+        (3 * quarter, far),
+    ):
         pick = (owner_token(row + start, device, n, local) == token).astype(F32).astype(BF16)
         total += jnp.dot(pick, values, preferred_element_type=F32)
     out[...] = total.astype(BF16)
@@ -160,41 +168,75 @@
     def swap(x, distance):
         return lax.ppermute(x, "tp", [(i, i ^ distance) for i in range(n)])
 
-    half = tokens // 2
-    context, weight = attend(n, local, queries, key_rows, value_rows, out_weight)
-    sent = jnp.dot(context[half:], weight, preferred_element_type=F32).astype(BF16)
-    got = swap(sent, 1)
-    total = jnp.dot(context[:half], weight, preferred_element_type=F32)
-    total = lax.optimization_barrier(total) + got.astype(F32)
-    part = half // 4
-    pieces = [total[k * part : (k + 1) * part].astype(BF16) for k in range(1, 4)]
-    arrived = [swap(piece, distance) for piece, distance in zip(pieces, square)]
-    total = total[:part]
-    for piece in arrived:
-        total = total + piece.astype(F32)
-    for level in levels[:-1]:
-        kept = total.shape[0] // 2
-        total = total[:kept] + swap(total[kept:].astype(BF16), level).astype(F32)
-    total = jnp.concatenate([total[:local] + residual.astype(F32), total[local:]], axis=0)
-    got = swap(total.astype(BF16), levels[-1]).astype(F32)
-    stream = total + jnp.concatenate([got[local:], got[:local]], axis=0)
-    rows = stream.shape[0]
-    grouped = stream.reshape(rows, D // QB, QB)
-    scales = jnp.max(jnp.abs(grouped), axis=2) + EPS
-    codes = (grouped / scales[:, :, None]).astype(BF16)
-    decoded = (codes.astype(F32) * scales[:, :, None]).reshape(rows, D)
-    mean_sq = jnp.mean(decoded * decoded, axis=1, keepdims=True)
-    held = (decoded * lax.rsqrt(mean_sq + 1e-05) * norm_gain[None, :]).astype(BF16)
-    for level in levels[-2::-1]:
-        held = jnp.concatenate([held, swap(held, level)], axis=0)
-    arrived = [swap(held, distance) for distance in square]
-    held = jnp.concatenate(arrived[::-1] + [held], axis=0)
-    other = swap(held, 1)
-    near = small_call(first_dot_kernel, (half, q_weight.shape[1]), "first_dot", held, q_weight)
+    half, quarter = tokens // 2, tokens // 4
+    context, weight, fresh = attend(
+        n, local, queries, key_rows, value_rows, out_weight, residual
+    )
+
+    def project(start):
+        rows = context[start : start + quarter]
+        return lax.optimization_barrier(jnp.dot(rows, weight, preferred_element_type=F32))
+
+    got = [swap(project(half + h * quarter).astype(BF16), 1) for h in range(2)]
+    kept = [project(h * quarter) for h in range(2)]
+
+    def after(values, earlier):
+        return list(lax.optimization_barrier((*values, *earlier))[: len(values)])
+
+    def reduce(total, old, earlier):
+        part = total.shape[0] // 4
+        pieces = [total[k * part : (k + 1) * part].astype(BF16) for k in range(1, 4)]
+        arrived = [swap(piece, distance) for piece, distance in zip(pieces, square)]
+        arrived = after(arrived[::-1], earlier)
+        total = total[:part]
+        for piece in arrived:
+            total = total + piece.astype(F32)
+        for level in levels[:-1]:
+            rest = total.shape[0] // 2
+            total = total[:rest] + swap(total[rest:].astype(BF16), level).astype(F32)
+        own = old.shape[0]
+        return jnp.concatenate([total[:own] + old.astype(F32), total[own:]], axis=0)
+
+    def finish(total, own, earlier):
+        (arrived,) = after([swap(total.astype(BF16), levels[-1])], earlier)
+        arrived = arrived.astype(F32)
+        stream = total + jnp.concatenate([arrived[own:], arrived[:own]], axis=0)
+        rows = stream.shape[0]
+        grouped = stream.reshape(rows, D // QB, QB)
+        scales = jnp.max(jnp.abs(grouped), axis=2) + EPS
+        codes = (grouped / scales[:, :, None]).astype(BF16)
+        decoded = (codes.astype(F32) * scales[:, :, None]).reshape(rows, D)
+        mean_sq = jnp.mean(decoded * decoded, axis=1, keepdims=True)
+        normed = (decoded * lax.rsqrt(mean_sq + 1e-05) * norm_gain[None, :]).astype(BF16)
+        return codes.reshape(rows, D)[:own], scales[:own], normed
+
+    def gather(held, earlier):
+        for level in levels[-2::-1]:
+            held = jnp.concatenate([held, swap(held, level)], axis=0)
+        arrived = after([swap(held, distance) for distance in square[::-1]], earlier)
+        return jnp.concatenate(arrived + [held], axis=0)
+
+    part = local // 2
+    codes, scales, normed, sums, held = [], [], [], [], []
+    for h in range(2):
+        old = (residual, fresh)[h][h * part : (h + 1) * part]
+        sums.append(reduce(kept[h] + got[h].astype(F32), old, sums[:h]))
+    for h in range(2):
+        out = finish(sums[h], part, normed[:h])
+        codes.append(out[0])
+        scales.append(out[1])
+        normed.append(out[2])
+    for h in range(2):
+        held.append(gather(normed[h], held[:h]))
+    early = jnp.concatenate([held[0], swap(held[0], 1)], axis=0)
+    early = small_call(first_dot_kernel, (half, q_weight.shape[1]), "early_dot", early, q_weight)
+    other = swap(held[1], 1)
+    shape = (quarter, q_weight.shape[1])
+    near = small_call(first_dot_kernel, shape, "near_dot", held[1], q_weight)
     last = functools.partial(last_dot_kernel, n, local)
     shape = (tokens, q_weight.shape[1])
-    next_queries = small_call(last, shape, "last_dot", other, q_weight, near)
-    return (codes.reshape(rows, D)[:local], scales[:local], next_queries)
+    next_queries = small_call(last, shape, "last_dot", other, q_weight, early, near)
+    return jnp.concatenate(codes, axis=0), jnp.concatenate(scales, axis=0), next_queries
 
 
 def solution(mesh):

time: 39.7 us -> 43.7 us (1.10)
  waiting for transfers between devices: 18.4 us -> 4.18 us
  starting transfers between devices: 11.4 us -> 21.5 us
  local copies, waits for them, and re-layouts: 1.67 us -> 4.9 us
  other arithmetic: 1.63 us -> 4.16 us
  matrix products: 1.31 us -> 2.6 us
  Pallas kernels: 4.36 us -> 5 us
    ppermute x9 -> x18, waiting for transfers between devices: 18.4 us -> 4.18 us  [swap(): return lax.ppermute(x, 'tp', [(i, i ^ distance) for i in range(n)])]
    ppermute x9 -> x18, starting transfers between devices: 11.4 us -> 21.5 us  [swap(): return lax.ppermute(x, 'tp', [(i, i ^ distance) for i in range(n)])]
    unnamed x9 -> x12, local copies, waits for them, and re-layouts: 0.82 us -> 3.72 us
    concatenate x1 -> x4, other arithmetic: 0.31 us -> 1.96 us  [the longest x1 0.78 us: on_device(): jnp.concatenate(codes, axis=0)]
    dot_general x2 -> x4, matrix products: 1.31 us -> 2.6 us  [project(): jnp.dot(rows, weight, preferred_element_type=F32)]
    pallas_call x2 -> x3, Pallas kernels: 2.07 us -> 2.69 us  [small_call(): pl.pallas_call(kernel, out_shape=jax.ShapeDtypeStruct(shape, BF16), in_sp...]
    concatenate x2 -> x1, local copies, waits for them, and re-layouts: 0.04 us -> 0.54 us  [on_device(): early = jnp.concatenate([held[0], swap(held[0], 1)], axis=0)]
    convert_element_type x3 -> x4, other arithmetic: 0.55 us -> 0.92 us  [the longest x2 0.68 us: finish(): (decoded * lax.rsqrt(mean_sq + 1e-05) * norm_gain[None, :]).astype(BF16)]
  transfers between devices with their start and end apart: 9 -> 18, of which waited for: 7 -> 6; matrix products, arithmetic and copies ran while one was open for 5% -> 17% of each run, Pallas kernels for 2% -> 3%
where the time goes in v10:
time: 43.7 us; the launch traced here: 43.2 us
  starting transfers between devices  21.5 us (49%)
  Pallas kernels  5 us (11%)
  local copies, waits for them, and re-layouts  4.9 us (11%)
  waiting for transfers between devices  4.18 us (10%)
  other arithmetic  4.16 us (10%)
  matrix products  2.6 us (6%)
  between operations  0.82 us (2%)
    ppermute x18, starting transfers between devices, swap(): return lax.ppermute(x, 'tp', [(i, i ^ distance) for i in range(n)])  21.5 us
    ppermute x18, waiting for transfers between devices, swap(): return lax.ppermute(x, 'tp', [(i, i ^ distance) for i in range(n)])  4.18 us
    unnamed x12, local copies, waits for them, and re-layouts  3.72 us
    pallas_call x3, Pallas kernels, small_call(): pl.pallas_call(kernel, out_shape=jax.ShapeDtypeStruct(shape, BF16), in_sp...  2.69 us
    dot_general x4, matrix products, project(): jnp.dot(rows, weight, preferred_element_type=F32)  2.6 us
    pallas_call x1, Pallas kernels, attend(): pl.pallas_call(functools.partial(attend_kernel, n, local), out_shape=[jax...  2.31 us
  transfers between devices with their start and end apart: 18, of which 6 were waited for; matrix products, arithmetic and copies ran while one was open for 17% of the time, Pallas kernels for 3%

profile of v10, /device:TPU:0, one launch (start us, length us, event | category | flops | bytes accessed | tf_op | source)
XLA Modules:
  0.0 43.2 jit_solution(5216619771585761778)
XLA Ops:
  0.6 2.3 %attend.1 = (bf16[32,128]{1,0:T(8,128)(2,1)S(1)}, bf16[128,16384]{1,0:T(8,128)(2,1)S(1)}, bf16[2,16384]{1,0:T(2,128)(2,1)S(1)}) custom-call(bf16[32,128]{1,0:T(8,128)(2,1)} %queries.1, bf16[32,1024]{1,0:T(8,128)(2,1)} %keys.1, bf16[32,1024]{1,0:T(8,128)(2,1)} %values.1, bf16[128,16384]{1,0:T(8,128)(2,1)} %weight.4, bf16[2,16384]{1,0:T(2,128)(2,1)} %old.1), custom_call_target="tpu_custom_call" | custom-call | bytes 4194304 | tf_op jit(solution)/shard_map/attend/pallas_call | solution.py:87
  2.9 0.6 %fusion.17 = bf16[8,16384]{1,0:T(8,128)(2,1)S(1)} fusion(bf16[128,16384]{1,0:T(8,128)(2,1)S(1)} %get-tuple-element.20, bf16[32,128]{1,0:T(8,128)(2,1)S(1)} %get-tuple-element.19), kind=kOutput, calls=%fused_computation.48 | convolution fusion | flops 33554432 | bytes 4458496 | tf_op jit(solution)/shard_map/dot_general | solution.py:178
  3.6 0.5 %collective-permute-start = (bf16[8,16384]{1,0:T(8,128)(2,1)S(1)}, bf16[8,16384]{1,0:T(8,128)(2,1)S(1)}, u32[]{:S(2)}, u32[]{:S(2)}) collective-permute-start(bf16[8,16384]{1,0:T(8,128)(2,1)S(1)} %fusion.17), channel_id=1, source_target_pairs={{0,1},{1,0},{2,3},{3,2},{4,5},{5,4},{6,7},{7,6},{8,9},{9,8},{10,11... | collective-permute-start | bytes 786440 | tf_op jit(solution)/shard_map/ppermute | solution.py:169
  4.1 0.6 %fusion.13 = bf16[8,16384]{1,0:T(8,128)(2,1)S(1)} fusion(bf16[128,16384]{1,0:T(8,128)(2,1)S(1)} %get-tuple-element.20, bf16[32,128]{1,0:T(8,128)(2,1)S(1)} %get-tuple-element.19), kind=kOutput, calls=%fused_computation.44 | convolution fusion | flops 33554432 | bytes 4458496 | tf_op jit(solution)/shard_map/dot_general | solution.py:178
  4.7 0.1 collective-permute-start.5
  4.8 0.7 %fusion.19 = f32[8,16384]{1,0:T(8,128)S(1)} fusion(bf16[128,16384]{1,0:T(8,128)(2,1)S(1)} %get-tuple-element.20, bf16[32,128]{1,0:T(8,128)(2,1)S(1)} %get-tuple-element.19), kind=kOutput, calls=%fused_computation.50 | convolution fusion | flops 33554432 | bytes 4720640 | tf_op jit(solution)/shard_map/dot_general | solution.py:178
  5.5 0.7 %fusion.15 = f32[8,16384]{1,0:T(8,128)S(1)} fusion(bf16[128,16384]{1,0:T(8,128)(2,1)S(1)} %get-tuple-element.20, bf16[32,128]{1,0:T(8,128)(2,1)S(1)} %get-tuple-element.19), kind=kOutput, calls=%fused_computation.46 | convolution fusion | flops 33554432 | bytes 4720640 | tf_op jit(solution)/shard_map/dot_general | solution.py:178
  6.2 0.1 fusion.22
  6.2 0.2 fusion.24
  6.4 4.0 %collective-permute-start.3 = (bf16[2,16384]{1,0:T(2,128)(2,1)S(1)}, bf16[2,16384]{1,0:T(2,128)(2,1)S(1)}, u32[]{:S(2)}, u32[]{:S(2)}) collective-permute-start(bf16[2,16384]{1,0:T(2,128)(2,1)S(1)} %get-tuple-element.43), channel_id=1, source_target_pairs={{0,6},{1,7},{2,4},{3,5},{4,2},{5,3},{6,0},{7,1},{8,14},{9,15},{10,... | collective-permute-start | bytes 196616 | tf_op jit(solution)/shard_map/ppermute | solution.py:169
  10.5 0.5 %collective-permute-start.2 = (bf16[2,16384]{1,0:T(2,128)(2,1)S(1)}, bf16[2,16384]{1,0:T(2,128)(2,1)S(1)}, u32[]{:S(2)}, u32[]{:S(2)}) collective-permute-start(bf16[2,16384]{1,0:T(2,128)(2,1)S(1)} %get-tuple-element.44), channel_id=1, source_target_pairs={{0,2},{1,3},{2,0},{3,1},{4,6},{5,7},{6,4},{7,5},{8,10},{9,11},{10,... | collective-permute-start | bytes 196616 | tf_op jit(solution)/shard_map/ppermute | solution.py:169
  11.0 0.1 collective-permute-start.1
  11.1 0.1 fusion.23
  11.2 0.2 fusion.25
  11.3 2.9 %collective-permute-start.8 = (bf16[2,16384]{1,0:T(2,128)(2,1)S(1)}, bf16[2,16384]{1,0:T(2,128)(2,1)S(1)}, u32[]{:S(2)}, u32[]{:S(2)}) collective-permute-start(bf16[2,16384]{1,0:T(2,128)(2,1)S(1)} %get-tuple-element.46), channel_id=1, source_target_pairs={{0,6},{1,7},{2,4},{3,5},{4,2},{5,3},{6,0},{7,1},{8,14},{9,15},{10,... | collective-permute-start | bytes 196616 | tf_op jit(solution)/shard_map/ppermute | solution.py:169
  14.3 0.5 %collective-permute-start.7 = (bf16[2,16384]{1,0:T(2,128)(2,1)S(1)}, bf16[2,16384]{1,0:T(2,128)(2,1)S(1)}, u32[]{:S(2)}, u32[]{:S(2)}) collective-permute-start(bf16[2,16384]{1,0:T(2,128)(2,1)S(1)} %get-tuple-element.47), channel_id=1, source_target_pairs={{0,2},{1,3},{2,0},{3,1},{4,6},{5,7},{6,4},{7,5},{8,10},{9,11},{10,... | collective-permute-start | bytes 196616 | tf_op jit(solution)/shard_map/ppermute | solution.py:169
  14.8 0.0 collective-permute-done.3
  14.8 0.2 collective-permute-start.6
  15.0 0.0 collective-permute-done.2
  15.0 0.9 %collective-permute-done.1 = bf16[2,16384]{1,0:T(2,128)(2,1)S(1)} collective-permute-done((bf16[2,16384]{1,0:T(2,128)(2,1)S(1)}, bf16[2,16384]{1,0:T(2,128)(2,1)S(1)}, u32[]{:S(2)}, u32[]{:S(2)}) %collective-permute-start.1) | collective-permute-done | bytes 65568 | tf_op jit(solution)/shard_map/ppermute | solution.py:169
  15.9 0.1 fusion.9
  16.0 0.1 slice_add_fusion.3
  16.1 0.1 fusion.21
  16.2 2.6 %collective-permute-start.4 = (bf16[2,16384]{1,0:T(2,128)(2,1)S(1)}, bf16[2,16384]{1,0:T(2,128)(2,1)S(1)}, u32[]{:S(2)}, u32[]{:S(2)}) collective-permute-start(bf16[2,16384]{1,0:T(2,128)(2,1)S(1)} %fusion.21), channel_id=1, source_target_pairs={{0,8},{1,9},{2,10},{3,11},{4,12},{5,13},{6,14},{7,15},{8,0},{9,1},... | collective-permute-start | bytes 196616 | tf_op jit(solution)/shard_map/ppermute | solution.py:169
  18.9 0.1 collective-permute-done.6
  19.0 0.1 fusion.7
  19.2 0.1 slice_add_fusion.2
  19.3 0.1 fusion.12
  19.4 2.7 %collective-permute-start.9 = (bf16[2,16384]{1,0:T(2,128)(2,1)S(1)}, bf16[2,16384]{1,0:T(2,128)(2,1)S(1)}, u32[]{:S(2)}, u32[]{:S(2)}) collective-permute-start(bf16[2,16384]{1,0:T(2,128)(2,1)S(1)} %fusion.12), channel_id=1, source_target_pairs={{0,8},{1,9},{2,10},{3,11},{4,12},{5,13},{6,14},{7,15},{8,0},{9,1},... | collective-permute-start | bytes 196616 | tf_op jit(solution)/shard_map/ppermute | solution.py:169
  22.1 1.3 %collective-permute-done.4 = bf16[2,16384]{1,0:T(2,128)(2,1)S(1)} collective-permute-done((bf16[2,16384]{1,0:T(2,128)(2,1)S(1)}, bf16[2,16384]{1,0:T(2,128)(2,1)S(1)}, u32[]{:S(2)}, u32[]{:S(2)}) %collective-permute-start.4) | collective-permute-done | bytes 65568 | tf_op jit(solution)/shard_map/ppermute | solution.py:169
  23.4 0.1 fusion.27
  23.5 0.1 abs_reduce_fusion.1
  23.6 0.2 multiply_reduce_fusion.1
  23.8 0.3 fusion.5
  24.2 1.2 %collective-permute-start.15 = (bf16[2,16384]{1,0:T(2,128)(2,1)S(1)}, bf16[2,16384]{1,0:T(2,128)(2,1)S(1)}, u32[]{:S(2)}, u32[]{:S(2)}) collective-permute-start(bf16[2,16384]{1,0:T(2,128)(2,1)S(1)} %fusion.5), channel_id=1, source_target_pairs={{0,6},{1,7},{2,4},{3,5},{4,2},{5,3},{6,0},{7,1},{8,14},{9,15},{10,... | collective-permute-start | bytes 196616 | tf_op jit(solution)/shard_map/ppermute | solution.py:169
  25.4 0.2 collective-permute-start.14
  25.7 2.1 %collective-permute-start.13 = (bf16[2,16384]{1,0:T(2,128)(2,1)S(1)}, bf16[2,16384]{1,0:T(2,128)(2,1)S(1)}, u32[]{:S(2)}, u32[]{:S(2)}) collective-permute-start(bf16[2,16384]{1,0:T(2,128)(2,1)S(1)} %fusion.5), channel_id=1, source_target_pairs={{0,4},{1,5},{2,6},{3,7},{4,0},{5,1},{6,2},{7,3},{8,12},{9,13},{10,... | collective-permute-start | bytes 196616 | tf_op jit(solution)/shard_map/ppermute | solution.py:169
  27.7 0.0 collective-permute-done.9
  27.7 0.1 fusion.26
  27.8 0.1 abs_reduce_fusion
  28.0 0.2 multiply_reduce_fusion
  28.2 0.3 fusion.2
  28.5 1.2 %collective-permute-start.12 = (bf16[2,16384]{1,0:T(2,128)(2,1)S(1)}, bf16[2,16384]{1,0:T(2,128)(2,1)S(1)}, u32[]{:S(2)}, u32[]{:S(2)}) collective-permute-start(bf16[2,16384]{1,0:T(2,128)(2,1)S(1)} %fusion.2), channel_id=1, source_target_pairs={{0,6},{1,7},{2,4},{3,5},{4,2},{5,3},{6,0},{7,1},{8,14},{9,15},{10,... | collective-permute-start | bytes 196616 | tf_op jit(solution)/shard_map/ppermute | solution.py:169
  29.8 0.3 collective-permute-start.11
  30.0 0.1 copy_bitcast_fusion
  30.2 2.1 %collective-permute-start.10 = (bf16[2,16384]{1,0:T(2,128)(2,1)S(1)}, bf16[2,16384]{1,0:T(2,128)(2,1)S(1)}, u32[]{:S(2)}, u32[]{:S(2)}) collective-permute-start(bf16[2,16384]{1,0:T(2,128)(2,1)S(1)} %fusion.2), channel_id=1, source_target_pairs={{0,4},{1,5},{2,6},{3,7},{4,0},{5,1},{6,2},{7,3},{8,12},{9,13},{10,... | collective-permute-start | bytes 196616 | tf_op jit(solution)/shard_map/ppermute | solution.py:169
  32.3 0.0 collective-permute-done.14
  32.3 0.0 collective-permute-done.13
  32.3 0.3 pad_maximum_fusion
  32.6 0.1 collective-permute-start.17
  32.6 1.1 %collective-permute-done.12 = bf16[2,16384]{1,0:T(2,128)(2,1)S(1)} collective-permute-done((bf16[2,16384]{1,0:T(2,128)(2,1)S(1)}, bf16[2,16384]{1,0:T(2,128)(2,1)S(1)}, u32[]{:S(2)}, u32[]{:S(2)}) %collective-permute-start.12) | collective-permute-done | bytes 65568 | tf_op jit(solution)/shard_map/ppermute | solution.py:169
  33.8 0.7 %collective-permute-done.11 = bf16[2,16384]{1,0:T(2,128)(2,1)S(1)} collective-permute-done((bf16[2,16384]{1,0:T(2,128)(2,1)S(1)}, bf16[2,16384]{1,0:T(2,128)(2,1)S(1)}, u32[]{:S(2)}, u32[]{:S(2)}) %collective-permute-start.11) | collective-permute-done | bytes 65568 | tf_op jit(solution)/shard_map/ppermute | solution.py:169
  34.4 0.1 collective-permute-done.10
  34.5 0.3 pad_maximum_fusion.1.rows
  34.8 0.1 collective-permute-start.16
  34.9 0.8 %pad_maximum_fusion.4 = bf16[2,16384]{1,0:T(2,128)(2,1)} fusion(bf16[1,16384]{1,0:T(2,128)(2,1)S(1)} %get-tuple-element.59, bf16[1,16384]{1,0:T(2,128)(2,1)S(1)} %get-tuple-element.60), kind=kLoop, calls=%fused_computation.38 | loop fusion | flops 131072 | bytes 131072 | tf_op jit(solution)/shard_map/concatenate | solution.py:239
  35.7 0.6 %pad_maximum_fusion.5 = f32[2,128]{1,0:T(2,128)} fusion(f32[1,128]{1,0:T(1,128)S(1)} %slice.117, f32[1,128]{1,0:T(1,128)S(1)} %slice.116), kind=kLoop, calls=%fused_computation.52 | loop fusion | flops 256 | bytes 2048 | tf_op jit(solution)/shard_map/concatenate | solution.py:239
  36.2 0.6 %near_dot.1.near = bf16[8,128]{1,0:T(8,128)(2,1)S(1)} custom-call(bf16[8,16384]{1,0:T(8,128)(2,1)S(1)} %pad_maximum_fusion.1.rows, bf16[16384,128]{1,0:T(8,128)(2,1)S(1)} %copy-done), custom_call_target="tpu_custom_call" | custom-call | flops 33554432 | bytes 4194304 | tf_op jit(solution)/shard_map/near_dot/pallas_call | solution.py:144
  36.9 0.5 %concatenate.84.rows = bf16[16,16384]{1,0:T(8,128)(2,1)S(1)} concatenate(bf16[2,16384]{1,0:T(2,128)(2,1)S(1)} %collective-permute-done.13, bf16[2,16384]{1,0:T(2,128)(2,1)S(1)} %collective-permute-done.14, bf16[2,16384]{1,0:T(2,128)(2,1)S(1)} %collective-permute-done.15, bf16[2,16384]{1,0:T(2,128)(2,1)S(1)} %fusion.5, bf16[8,16384]{1,0:T(8,128)(2,1)S(1)} %collective-permute-done.17), dimensions={0} | concatenate | bytes 1048576 | tf_op jit(solution)/shard_map/concatenate | solution.py:231
  37.4 0.0 copy-start.1
  37.5 2.2 %copy-done.1 = bf16[16384,128]{1,0:T(8,128)(2,1)S(1)} copy-done((bf16[16384,128]{1,0:T(8,128)(2,1)S(1)}, bf16[16384,128]{1,0:T(8,128)(2,1)}, u32[]{:S(2)}) %copy-start.1) | copy-done | bytes 4194328
  39.6 0.7 %early_dot.1.early = bf16[16,128]{1,0:T(8,128)(2,1)S(1)} custom-call(bf16[16,16384]{1,0:T(8,128)(2,1)S(1)} %concatenate.84.rows, bf16[16384,128]{1,0:T(8,128)(2,1)S(1)} %copy-done.1), custom_call_target="tpu_custom_call" | custom-call | flops 67108864 | bytes 4194304 | tf_op jit(solution)/shard_map/early_dot/pallas_call | solution.py:144
  40.3 1.5 %copy-done.2 = bf16[16384,128]{1,0:T(8,128)(2,1)S(1)} copy-done((bf16[16384,128]{1,0:T(8,128)(2,1)S(1)}, bf16[16384,128]{1,0:T(8,128)(2,1)}, u32[]{:S(2)}) %copy-start.2) | copy-done | bytes 4194328
  41.8 1.4 %last_dot.1 = bf16[32,128]{1,0:T(8,128)(2,1)} custom-call(bf16[8,16384]{1,0:T(8,128)(2,1)S(1)} %collective-permute-done.16.rows, bf16[16384,128]{1,0:T(8,128)(2,1)S(1)} %copy-done.2, bf16[16,128]{1,0:T(8,128)(2,1)S(1)} %early_dot.1.early, bf16[8,128]{1,0:T(8,128)(2,1)S(1)} %near_dot.1.near), custom_call_target="tpu_custom_call" | custom-call | flops 33554432 | bytes 4194304 | tf_op jit(solution)/shard_map/last_dot/pallas_call | solution.py:144
  (22 shorter events, 0.1 us)
Async XLA Ops:
  3.6 2.6 %collective-permute-start = (bf16[8,16384]{1,0:T(8,128)(2,1)S(1)}, bf16[8,16384]{1,0:T(8,128)(2,1)S(1)}, u32[]{:S(2)}, u32[]{:S(2)}) collective-permute-start(bf16[8,16384]{1,0:T(8,128)(2,1)S(1)} %fusion.17), channel_id=1, source_target_pairs={{0,1},{1,0},{2,3},{3,2},{4,5},{5,4},{6,7},{7,6},{8,9},{9,8},{10,11... | collective-permute-start | bytes 786440 | tf_op jit(solution)/shard_map/ppermute | solution.py:169
  4.7 6.4 %collective-permute-start.5 = (bf16[8,16384]{1,0:T(8,128)(2,1)S(1)}, bf16[8,16384]{1,0:T(8,128)(2,1)S(1)}, u32[]{:S(2)}, u32[]{:S(2)}) collective-permute-start(bf16[8,16384]{1,0:T(8,128)(2,1)S(1)} %fusion.13), channel_id=1, source_target_pairs={{0,1},{1,0},{2,3},{3,2},{4,5},{5,4},{6,7},{7,6},{8,9},{9,8},{10,11... | collective-permute-start | bytes 786440 | tf_op jit(solution)/shard_map/ppermute | solution.py:169
  5.5 10.5 %copy-start.3 = (bf16[2,16384]{1,0:T(2,128)(2,1)S(1)}, bf16[2,16384]{1,0:T(2,128)(2,1)}, u32[]{:S(2)}) copy-start(bf16[2,16384]{1,0:T(2,128)(2,1)} %old.1) | copy-start | bytes 196612
  6.2 17.7 %copy-start.4 = (f32[16384]{0:T(1024)S(1)}, f32[16384]{0:T(1024)}, u32[]{:S(2)}) copy-start(f32[16384]{0:T(1024)} %param.12) | copy-start | bytes 196612
  6.4 8.4 %collective-permute-start.3 = (bf16[2,16384]{1,0:T(2,128)(2,1)S(1)}, bf16[2,16384]{1,0:T(2,128)(2,1)S(1)}, u32[]{:S(2)}, u32[]{:S(2)}) collective-permute-start(bf16[2,16384]{1,0:T(2,128)(2,1)S(1)} %get-tuple-element.43), channel_id=1, source_target_pairs={{0,6},{1,7},{2,4},{3,5},{4,2},{5,3},{6,0},{7,1},{8,14},{9,15},{10,... | collective-permute-start | bytes 196616 | tf_op jit(solution)/shard_map/ppermute | solution.py:169
  10.5 4.5 %collective-permute-start.2 = (bf16[2,16384]{1,0:T(2,128)(2,1)S(1)}, bf16[2,16384]{1,0:T(2,128)(2,1)S(1)}, u32[]{:S(2)}, u32[]{:S(2)}) collective-permute-start(bf16[2,16384]{1,0:T(2,128)(2,1)S(1)} %get-tuple-element.44), channel_id=1, source_target_pairs={{0,2},{1,3},{2,0},{3,1},{4,6},{5,7},{6,4},{7,5},{8,10},{9,11},{10,... | collective-permute-start | bytes 196616 | tf_op jit(solution)/shard_map/ppermute | solution.py:169
  11.0 25.3 %copy-start = (bf16[16384,128]{1,0:T(8,128)(2,1)S(1)}, bf16[16384,128]{1,0:T(8,128)(2,1)}, u32[]{:S(2)}) copy-start(bf16[16384,128]{1,0:T(8,128)(2,1)} %weight.7) | copy-start | bytes 12582916
  11.0 4.9 %collective-permute-start.1 = (bf16[2,16384]{1,0:T(2,128)(2,1)S(1)}, bf16[2,16384]{1,0:T(2,128)(2,1)S(1)}, u32[]{:S(2)}, u32[]{:S(2)}) collective-permute-start(bf16[2,16384]{1,0:T(2,128)(2,1)S(1)} %get-tuple-element.45), channel_id=1, source_target_pairs={{0,4},{1,5},{2,6},{3,7},{4,0},{5,1},{6,2},{7,3},{8,12},{9,13},{10,... | collective-permute-start | bytes 196616 | tf_op jit(solution)/shard_map/ppermute | solution.py:169
  11.3 7.6 %collective-permute-start.8 = (bf16[2,16384]{1,0:T(2,128)(2,1)S(1)}, bf16[2,16384]{1,0:T(2,128)(2,1)S(1)}, u32[]{:S(2)}, u32[]{:S(2)}) collective-permute-start(bf16[2,16384]{1,0:T(2,128)(2,1)S(1)} %get-tuple-element.46), channel_id=1, source_target_pairs={{0,6},{1,7},{2,4},{3,5},{4,2},{5,3},{6,0},{7,1},{8,14},{9,15},{10,... | collective-permute-start | bytes 196616 | tf_op jit(solution)/shard_map/ppermute | solution.py:169
  14.3 4.6 %collective-permute-start.7 = (bf16[2,16384]{1,0:T(2,128)(2,1)S(1)}, bf16[2,16384]{1,0:T(2,128)(2,1)S(1)}, u32[]{:S(2)}, u32[]{:S(2)}) collective-permute-start(bf16[2,16384]{1,0:T(2,128)(2,1)S(1)} %get-tuple-element.47), channel_id=1, source_target_pairs={{0,2},{1,3},{2,0},{3,1},{4,6},{5,7},{6,4},{7,5},{8,10},{9,11},{10,... | collective-permute-start | bytes 196616 | tf_op jit(solution)/shard_map/ppermute | solution.py:169
  14.8 4.3 %collective-permute-start.6 = (bf16[2,16384]{1,0:T(2,128)(2,1)S(1)}, bf16[2,16384]{1,0:T(2,128)(2,1)S(1)}, u32[]{:S(2)}, u32[]{:S(2)}) collective-permute-start(bf16[2,16384]{1,0:T(2,128)(2,1)S(1)} %get-tuple-element.48), channel_id=1, source_target_pairs={{0,4},{1,5},{2,6},{3,7},{4,0},{5,1},{6,2},{7,3},{8,12},{9,13},{10,... | collective-permute-start | bytes 196616 | tf_op jit(solution)/shard_map/ppermute | solution.py:169
  16.2 7.1 %collective-permute-start.4 = (bf16[2,16384]{1,0:T(2,128)(2,1)S(1)}, bf16[2,16384]{1,0:T(2,128)(2,1)S(1)}, u32[]{:S(2)}, u32[]{:S(2)}) collective-permute-start(bf16[2,16384]{1,0:T(2,128)(2,1)S(1)} %fusion.21), channel_id=1, source_target_pairs={{0,8},{1,9},{2,10},{3,11},{4,12},{5,13},{6,14},{7,15},{8,0},{9,1},... | collective-permute-start | bytes 196616 | tf_op jit(solution)/shard_map/ppermute | solution.py:169
  19.4 8.3 %collective-permute-start.9 = (bf16[2,16384]{1,0:T(2,128)(2,1)S(1)}, bf16[2,16384]{1,0:T(2,128)(2,1)S(1)}, u32[]{:S(2)}, u32[]{:S(2)}) collective-permute-start(bf16[2,16384]{1,0:T(2,128)(2,1)S(1)} %fusion.12), channel_id=1, source_target_pairs={{0,8},{1,9},{2,10},{3,11},{4,12},{5,13},{6,14},{7,15},{8,0},{9,1},... | collective-permute-start | bytes 196616 | tf_op jit(solution)/shard_map/ppermute | solution.py:169
  24.2 6.0 %collective-permute-start.15 = (bf16[2,16384]{1,0:T(2,128)(2,1)S(1)}, bf16[2,16384]{1,0:T(2,128)(2,1)S(1)}, u32[]{:S(2)}, u32[]{:S(2)}) collective-permute-start(bf16[2,16384]{1,0:T(2,128)(2,1)S(1)} %fusion.5), channel_id=1, source_target_pairs={{0,6},{1,7},{2,4},{3,5},{4,2},{5,3},{6,0},{7,1},{8,14},{9,15},{10,... | collective-permute-start | bytes 196616 | tf_op jit(solution)/shard_map/ppermute | solution.py:169
  25.4 6.8 %collective-permute-start.14 = (bf16[2,16384]{1,0:T(2,128)(2,1)S(1)}, bf16[2,16384]{1,0:T(2,128)(2,1)S(1)}, u32[]{:S(2)}, u32[]{:S(2)}) collective-permute-start(bf16[2,16384]{1,0:T(2,128)(2,1)S(1)} %fusion.5), channel_id=1, source_target_pairs={{0,2},{1,3},{2,0},{3,1},{4,6},{5,7},{6,4},{7,5},{8,10},{9,11},{10,... | collective-permute-start | bytes 196616 | tf_op jit(solution)/shard_map/ppermute | solution.py:169
  25.7 6.6 %collective-permute-start.13 = (bf16[2,16384]{1,0:T(2,128)(2,1)S(1)}, bf16[2,16384]{1,0:T(2,128)(2,1)S(1)}, u32[]{:S(2)}, u32[]{:S(2)}) collective-permute-start(bf16[2,16384]{1,0:T(2,128)(2,1)S(1)} %fusion.5), channel_id=1, source_target_pairs={{0,4},{1,5},{2,6},{3,7},{4,0},{5,1},{6,2},{7,3},{8,12},{9,13},{10,... | collective-permute-start | bytes 196616 | tf_op jit(solution)/shard_map/ppermute | solution.py:169
  28.5 5.3 %collective-permute-start.12 = (bf16[2,16384]{1,0:T(2,128)(2,1)S(1)}, bf16[2,16384]{1,0:T(2,128)(2,1)S(1)}, u32[]{:S(2)}, u32[]{:S(2)}) collective-permute-start(bf16[2,16384]{1,0:T(2,128)(2,1)S(1)} %fusion.2), channel_id=1, source_target_pairs={{0,6},{1,7},{2,4},{3,5},{4,2},{5,3},{6,0},{7,1},{8,14},{9,15},{10,... | collective-permute-start | bytes 196616 | tf_op jit(solution)/shard_map/ppermute | solution.py:169
  29.8 4.7 %collective-permute-start.11 = (bf16[2,16384]{1,0:T(2,128)(2,1)S(1)}, bf16[2,16384]{1,0:T(2,128)(2,1)S(1)}, u32[]{:S(2)}, u32[]{:S(2)}) collective-permute-start(bf16[2,16384]{1,0:T(2,128)(2,1)S(1)} %fusion.2), channel_id=1, source_target_pairs={{0,2},{1,3},{2,0},{3,1},{4,6},{5,7},{6,4},{7,5},{8,10},{9,11},{10,... | collective-permute-start | bytes 196616 | tf_op jit(solution)/shard_map/ppermute | solution.py:169
  30.2 4.3 %collective-permute-start.10 = (bf16[2,16384]{1,0:T(2,128)(2,1)S(1)}, bf16[2,16384]{1,0:T(2,128)(2,1)S(1)}, u32[]{:S(2)}, u32[]{:S(2)}) collective-permute-start(bf16[2,16384]{1,0:T(2,128)(2,1)S(1)} %fusion.2), channel_id=1, source_target_pairs={{0,4},{1,5},{2,6},{3,7},{4,0},{5,1},{6,2},{7,3},{8,12},{9,13},{10,... | collective-permute-start | bytes 196616 | tf_op jit(solution)/shard_map/ppermute | solution.py:169
  32.6 4.3 %collective-permute-start.17 = (bf16[8,16384]{1,0:T(8,128)(2,1)S(1)}, bf16[8,16384]{1,0:T(8,128)(2,1)S(1)}, u32[]{:S(2)}, u32[]{:S(2)}) collective-permute-start(bf16[8,16384]{1,0:T(8,128)(2,1)S(1)} %pad_maximum_fusion), channel_id=1, source_target_pairs={{0,1},{1,0},{2,3},{3,2},{4,5},{5,4},{6,7},{7,6},{8,9},{9,8},{10,11... | collective-permute-start | bytes 786440 | tf_op jit(solution)/shard_map/ppermute | solution.py:169
  34.8 5.5 %collective-permute-start.16 = (bf16[8,16384]{1,0:T(8,128)(2,1)S(1)}, bf16[8,16384]{1,0:T(8,128)(2,1)S(1)}, u32[]{:S(2)}, u32[]{:S(2)}) collective-permute-start(bf16[8,16384]{1,0:T(8,128)(2,1)S(1)} %pad_maximum_fusion.1.rows), channel_id=1, source_target_pairs={{0,1},{1,0},{2,3},{3,2},{4,5},{5,4},{6,7},{7,6},{8,9},{9,8},{10,11... | collective-permute-start | bytes 786440 | tf_op jit(solution)/shard_map/ppermute | solution.py:169
  37.4 2.2 %copy-start.1 = (bf16[16384,128]{1,0:T(8,128)(2,1)S(1)}, bf16[16384,128]{1,0:T(8,128)(2,1)}, u32[]{:S(2)}) copy-start(bf16[16384,128]{1,0:T(8,128)(2,1)} %weight.7) | copy-start | bytes 12582916
  39.6 2.2 %copy-start.2 = (bf16[16384,128]{1,0:T(8,128)(2,1)S(1)}, bf16[16384,128]{1,0:T(8,128)(2,1)}, u32[]{:S(2)}) copy-start(bf16[16384,128]{1,0:T(8,128)(2,1)} %weight.7) | copy-start | bytes 12582916

commit v11 on v10

--- a/solution.py
+++ b/solution.py
@@ -22,15 +22,17 @@
 
 
 def owner_token(row, device, n, local):
-    bits = [2, 6] + late_levels(n)
+    bits = late_levels(n)
     shift = local.bit_length() - 2
     block = row >> shift
-    distance = block >> (len(bits) + 1)
-    part = (block >> len(bits)) & 1
-    for place, bit in enumerate(bits):
-        distance = distance ^ (((block >> (len(bits) - 1 - place)) & 1) * bit)
+    distance = block >> (len(bits) + 3)
+    part = (block >> (len(bits) + 2)) & 1
+    place = (block >> len(bits)) & 3
+    for order, bit in enumerate(bits):
+        distance = distance ^ (((block >> (len(bits) - 1 - order)) & 1) * bit)
     own = (part << shift) | (row & (local // 2 - 1))
-    return ((device ^ distance) << (shift + 1)) | own
+    owner = ((device ^ distance) & ~6) | (place << 1)
+    return (owner << (shift + 1)) | own
 
 
 def attend_kernel(
@@ -117,39 +119,40 @@
     return total
 
 
-def first_dot_kernel(rows, weight, out):
-    out[...] = times(rows, weight).astype(BF16)
-
-
-def last_dot_kernel(n, local, rows, weight, early, near, out):
+def first_dot_kernel(early, near, weight, out):
+    split = early.shape[0]
+    out[:split] = times(early, weight)
+    out[split:] = times(near, weight)
+
+
+def last_dot_kernel(n, local, rows, before, weight, out):
     device = lax.axis_index("tp")
     tokens, quarter = out.shape[0], rows.shape[0]
     token = lax.broadcasted_iota(jnp.int32, (tokens, quarter), 0)
-    row = lax.broadcasted_iota(jnp.int32, (tokens, quarter), 1) ^ (3 * quarter // 4)
-    far = times(rows, weight).astype(BF16)
+    row = lax.broadcasted_iota(jnp.int32, (tokens, quarter), 1)
     total = jnp.zeros(out.shape, F32)
     for start, values in (
-        (0, early[:quarter]),
-        (2 * quarter, early[quarter:]),
-        (quarter, near[...]),
-        (3 * quarter, far),
+        (0, before[:quarter]),
+        (2 * quarter, before[quarter : 2 * quarter]),
+        (quarter, before[2 * quarter :]),
+        (3 * quarter, times(rows, weight)),
     ):
         pick = (owner_token(row + start, device, n, local) == token).astype(F32).astype(BF16)
-        total += jnp.dot(pick, values, preferred_element_type=F32)
+        total += jnp.dot(pick, values.astype(BF16), preferred_element_type=F32)
     out[...] = total.astype(BF16)
 
 
-def small_call(kernel, shape, name, *operands):
+def small_call(kernel, shape, dtype, name, *operands):
     spec = pl.BlockSpec(memory_space=pltpu.VMEM)
     return pl.pallas_call(
         kernel,
-        out_shape=jax.ShapeDtypeStruct(shape, BF16),
+        out_shape=jax.ShapeDtypeStruct(shape, dtype),
         in_specs=[spec] * len(operands),
         out_specs=spec,
         compiler_params=pltpu.CompilerParams(vmem_limit_bytes=VMEM_LIMIT),
         cost_estimate=pl.CostEstimate(
-            flops=2 * operands[0].size * operands[1].shape[1],
-            bytes_accessed=2 * operands[1].size,
+            flops=2 * operands[0].size * operands[-1].shape[1],
+            bytes_accessed=2 * operands[-1].size,
             transcendentals=0,
         ),
         name=name,
@@ -163,7 +166,10 @@
     local = residual.shape[0]
     D = residual.shape[1]
     levels = late_levels(n)
-    square = (6, 2, 4)
+    squares = [[b + c + 2 * k for k in range(4)] for b in range(0, n, 8) for c in range(2)]
+
+    def exchange(x):
+        return lax.all_to_all(x, "tp", 0, 0, axis_index_groups=squares, tiled=True)
 
     def swap(x, distance):
         return lax.ppermute(x, "tp", [(i, i ^ distance) for i in range(n)])
@@ -184,13 +190,9 @@
         return list(lax.optimization_barrier((*values, *earlier))[: len(values)])
 
     def reduce(total, old, earlier):
-        part = total.shape[0] // 4
-        pieces = [total[k * part : (k + 1) * part].astype(BF16) for k in range(1, 4)]
-        arrived = [swap(piece, distance) for piece, distance in zip(pieces, square)]
-        arrived = after(arrived[::-1], earlier)
-        total = total[:part]
-        for piece in arrived:
-            total = total + piece.astype(F32)
+        pieces = total.astype(BF16).reshape(4, total.shape[0] // 4, D)
+        (arrived,) = after([exchange(pieces)], earlier)
+        total = jnp.sum(arrived.astype(F32), axis=0)
         for level in levels[:-1]:
             rest = total.shape[0] // 2
             total = total[:rest] + swap(total[rest:].astype(BF16), level).astype(F32)
@@ -213,8 +215,9 @@
     def gather(held, earlier):
         for level in levels[-2::-1]:
             held = jnp.concatenate([held, swap(held, level)], axis=0)
-        arrived = after([swap(held, distance) for distance in square[::-1]], earlier)
-        return jnp.concatenate(arrived + [held], axis=0)
+        copies = jnp.broadcast_to(held[None], (4, *held.shape))
+        (arrived,) = after([exchange(copies)], earlier)
+        return arrived.reshape(-1, D)
 
     part = local // 2
     codes, scales, normed, sums, held = [], [], [], [], []
@@ -229,13 +232,12 @@
     for h in range(2):
         held.append(gather(normed[h], held[:h]))
     early = jnp.concatenate([held[0], swap(held[0], 1)], axis=0)
-    early = small_call(first_dot_kernel, (half, q_weight.shape[1]), "early_dot", early, q_weight)
     other = swap(held[1], 1)
-    shape = (quarter, q_weight.shape[1])
-    near = small_call(first_dot_kernel, shape, "near_dot", held[1], q_weight)
+    width = q_weight.shape[1]
+    shape = (3 * quarter, width)
+    before = small_call(first_dot_kernel, shape, F32, "first_dots", early, held[1], q_weight)
     last = functools.partial(last_dot_kernel, n, local)
-    shape = (tokens, q_weight.shape[1])
-    next_queries = small_call(last, shape, "last_dot", other, q_weight, early, near)
+    next_queries = small_call(last, (tokens, width), BF16, "last_dot", other, before, q_weight)
     return jnp.concatenate(codes, axis=0), jnp.concatenate(scales, axis=0), next_queries
 
 

time: 43.7 us -> 60.3 us (1.38)
  waiting for transfers between devices: 4.18 us -> 19.3 us
  local copies, waits for them, and re-layouts: 4.9 us -> 7.14 us
    all_to_all x0 -> x4, waiting for transfers between devices: none -> 16.1 us  [exchange(): return lax.all_to_all(x, 'tp', 0, 0, axis_index_groups=squares, tiled=True)]
    ppermute x18 -> x6, starting transfers between devices: 21.5 us -> 5.73 us  [swap(): return lax.ppermute(x, 'tp', [(i, i ^ distance) for i in range(n)])]
    all_to_all x0 -> x4, starting transfers between devices: none -> 15.5 us  [exchange(): return lax.all_to_all(x, 'tp', 0, 0, axis_index_groups=squares, tiled=True)]
    reshape x0 -> x4, local copies, waits for them, and re-layouts: none -> 1.98 us  [the longest x2 1.77 us: reduce(): pieces = total.astype(BF16).reshape(4, total.shape[0] // 4, D)]
    broadcast_in_dim x0 -> x2, local copies, waits for them, and re-layouts: none -> 1.7 us  [gather(): copies = jnp.broadcast_to(held[None], (4, *held.shape))]
    ppermute x18 -> x6, waiting for transfers between devices: 4.18 us -> 3.17 us  [swap(): return lax.ppermute(x, 'tp', [(i, i ^ distance) for i in range(n)])]
    unnamed x12 -> x10, local copies, waits for them, and re-layouts: 3.72 us -> 3.18 us
    pallas_call x3 -> x2, Pallas kernels: 2.69 us -> 2.59 us  [small_call(): pl.pallas_call(kernel, out_shape=jax.ShapeDtypeStruct(shape, dtype), in_s...]
  transfers between devices with their start and end apart: 18 -> 10, of which waited for: 6 -> 5; matrix products, arithmetic and copies ran while one was open for 17% -> 12% of each run, Pallas kernels for 3% -> 2%
where the time goes in v11:
time: 60.3 us; the launch traced here: 59.7 us
  starting transfers between devices  21.2 us (35%)
  waiting for transfers between devices  19.3 us (32%)
  local copies, waits for them, and re-layouts  7.14 us (12%)
  Pallas kernels  4.9 us (8%)
  other arithmetic  3.77 us (6%)
  matrix products  2.6 us (4%)
  between operations  0.84 us (1%)
    all_to_all x4, waiting for transfers between devices, exchange(): return lax.all_to_all(x, 'tp', 0, 0, axis_index_groups=squares, tiled=True)  16.1 us
    all_to_all x4, starting transfers between devices, exchange(): return lax.all_to_all(x, 'tp', 0, 0, axis_index_groups=squares, tiled=True)  15.5 us
    ppermute x6, starting transfers between devices, swap(): return lax.ppermute(x, 'tp', [(i, i ^ distance) for i in range(n)])  5.73 us
    unnamed x10, local copies, waits for them, and re-layouts  3.18 us
    ppermute x6, waiting for transfers between devices, swap(): return lax.ppermute(x, 'tp', [(i, i ^ distance) for i in range(n)])  3.17 us
    dot_general x4, matrix products, project(): jnp.dot(rows, weight, preferred_element_type=F32)  2.6 us
    pallas_call x2, Pallas kernels, small_call(): pl.pallas_call(kernel, out_shape=jax.ShapeDtypeStruct(shape, dtype), in_s...  2.59 us
    pallas_call x1, Pallas kernels, attend(): pl.pallas_call(functools.partial(attend_kernel, n, local), out_shape=[jax...  2.31 us
  transfers between devices with their start and end apart: 10, of which 5 were waited for; matrix products, arithmetic and copies ran while one was open for 12% of the time, Pallas kernels for 2%

profile of v11, /device:TPU:0, one launch (start us, length us, event | category | flops | bytes accessed | tf_op | source)
XLA Modules:
  0.0 59.7 jit_solution(7149497574815092885)
XLA Ops:
  0.6 2.3 %attend.1 = (bf16[32,128]{1,0:T(8,128)(2,1)S(1)}, bf16[128,16384]{1,0:T(8,128)(2,1)S(1)}, bf16[2,16384]{1,0:T(2,128)(2,1)S(1)}) custom-call(bf16[32,128]{1,0:T(8,128)(2,1)} %queries.1, bf16[32,1024]{1,0:T(8,128)(2,1)} %keys.1, bf16[32,1024]{1,0:T(8,128)(2,1)} %values.1, bf16[128,16384]{1,0:T(8,128)(2,1)} %weight.3, bf16[2,16384]{1,0:T(2,128)(2,1)} %old.1), custom_call_target="tpu_custom_call" | custom-call | bytes 4194304 | tf_op jit(solution)/shard_map/attend/pallas_call | solution.py:89
  2.9 0.6 %fusion.9 = bf16[8,16384]{1,0:T(8,128)(2,1)S(1)} fusion(bf16[128,16384]{1,0:T(8,128)(2,1)S(1)} %get-tuple-element.9, bf16[32,128]{1,0:T(8,128)(2,1)S(1)} %get-tuple-element.8), kind=kOutput, calls=%fused_computation.39 | convolution fusion | flops 33554432 | bytes 4458496 | tf_op jit(solution)/shard_map/dot_general | solution.py:184
  3.6 0.5 collective-permute-start.2
  4.1 0.6 %fusion.13 = bf16[8,16384]{1,0:T(8,128)(2,1)S(1)} fusion(bf16[128,16384]{1,0:T(8,128)(2,1)S(1)} %get-tuple-element.9, bf16[32,128]{1,0:T(8,128)(2,1)S(1)} %get-tuple-element.8), kind=kOutput, calls=%fused_computation.43 | convolution fusion | flops 33554432 | bytes 4458496 | tf_op jit(solution)/shard_map/dot_general | solution.py:184
  4.7 0.1 collective-permute-start
  4.8 0.7 %fusion.11 = f32[8,16384]{1,0:T(8,128)S(1)} fusion(bf16[128,16384]{1,0:T(8,128)(2,1)S(1)} %get-tuple-element.9, bf16[32,128]{1,0:T(8,128)(2,1)S(1)} %get-tuple-element.8), kind=kOutput, calls=%fused_computation.41 | convolution fusion | flops 33554432 | bytes 4720640 | tf_op jit(solution)/shard_map/dot_general | solution.py:184
  5.5 0.0 copy-start.2
  5.5 0.7 %fusion.15 = f32[8,16384]{1,0:T(8,128)S(1)} fusion(bf16[128,16384]{1,0:T(8,128)(2,1)S(1)} %get-tuple-element.9, bf16[32,128]{1,0:T(8,128)(2,1)S(1)} %get-tuple-element.8), kind=kOutput, calls=%fused_computation.45 | convolution fusion | flops 33554432 | bytes 4720640 | tf_op jit(solution)/shard_map/dot_general | solution.py:184
  6.2 0.0 copy-start.3
  6.2 0.0 collective-permute-done.2
  6.2 0.9 %reshape.228 = bf16[4,2,16384]{2,1,0:T(2,128)(2,1)} reshape(bf16[8,16384]{1,0:T(8,128)(2,1)S(1)} %add_convert_fusion) | data formatting | bytes 524288 | tf_op jit(solution)/shard_map/reshape | solution.py:193
  7.1 5.2 %all-to-all-start.1 = ((bf16[4,2,16384]{2,1,0:T(2,128)(2,1)}), bf16[4,2,16384]{2,1,0:T(2,128)(2,1)S(1)}, u32[]{:S(2)}, u32[]{:S(2)}) async-start(bf16[4,2,16384]{2,1,0:T(2,128)(2,1)} %reshape.228), calls=%async_computation.1 | async-start | bytes 524288 | tf_op jit(solution)/shard_map/all_to_all | solution.py:172
  12.4 0.0 collective-permute-done
  12.4 0.9 %reshape.227 = bf16[4,2,16384]{2,1,0:T(2,128)(2,1)} reshape(bf16[8,16384]{1,0:T(8,128)(2,1)S(1)} %add_convert_fusion.1) | data formatting | bytes 524288 | tf_op jit(solution)/shard_map/reshape | solution.py:193
  13.3 4.6 %all-to-all-done.1 = bf16[4,2,16384]{2,1,0:T(2,128)(2,1)S(1)} async-done(((bf16[4,2,16384]{2,1,0:T(2,128)(2,1)}), bf16[4,2,16384]{2,1,0:T(2,128)(2,1)S(1)}, u32[]{:S(2)}, u32[]{:S(2)}) %all-to-all-start.1) | async-done | bytes 262176 | tf_op jit(solution)/shard_map/all_to_all | solution.py:172
  17.9 3.4 %all-to-all-start = ((bf16[4,2,16384]{2,1,0:T(2,128)(2,1)}), bf16[4,2,16384]{2,1,0:T(2,128)(2,1)S(1)}, u32[]{:S(2)}, u32[]{:S(2)}) async-start(bf16[4,2,16384]{2,1,0:T(2,128)(2,1)} %reshape.227), calls=%async_computation | async-start | bytes 524288 | tf_op jit(solution)/shard_map/all_to_all | solution.py:172
  21.3 0.2 convert_reduce_fusion
  21.6 0.1 slice_add_fusion
  21.7 0.1 fusion.8
  21.8 2.7 %collective-permute-start.3 = (bf16[2,16384]{1,0:T(2,128)(2,1)S(1)}, bf16[2,16384]{1,0:T(2,128)(2,1)S(1)}, u32[]{:S(2)}, u32[]{:S(2)}) collective-permute-start(bf16[2,16384]{1,0:T(2,128)(2,1)S(1)} %fusion.8), channel_id=1, source_target_pairs={{0,8},{1,9},{2,10},{3,11},{4,12},{5,13},{6,14},{7,15},{8,0},{9,1},... | collective-permute-start | bytes 196616 | tf_op jit(solution)/shard_map/ppermute | solution.py:175
  24.5 2.5 %all-to-all-done = bf16[4,2,16384]{2,1,0:T(2,128)(2,1)S(1)} async-done(((bf16[4,2,16384]{2,1,0:T(2,128)(2,1)}), bf16[4,2,16384]{2,1,0:T(2,128)(2,1)S(1)}, u32[]{:S(2)}, u32[]{:S(2)}) %all-to-all-start) | async-done | bytes 262176 | tf_op jit(solution)/shard_map/all_to_all | solution.py:172
  27.0 0.2 convert_reduce_fusion.1
  27.2 0.0 copy-done.2
  27.2 0.1 slice_add_fusion.1
  27.4 0.1 fusion.17
  27.5 2.3 %collective-permute-start.1 = (bf16[2,16384]{1,0:T(2,128)(2,1)S(1)}, bf16[2,16384]{1,0:T(2,128)(2,1)S(1)}, u32[]{:S(2)}, u32[]{:S(2)}) collective-permute-start(bf16[2,16384]{1,0:T(2,128)(2,1)S(1)} %fusion.17), channel_id=1, source_target_pairs={{0,8},{1,9},{2,10},{3,11},{4,12},{5,13},{6,14},{7,15},{8,0},{9,1},... | collective-permute-start | bytes 196616 | tf_op jit(solution)/shard_map/ppermute | solution.py:175
  29.8 0.0 collective-permute-done.3
  29.8 0.1 fusion.19
  29.9 0.1 abs_reduce_fusion
  30.1 0.2 multiply_reduce_fusion.1
  30.3 3.2 %collective-permute-done.1 = bf16[2,16384]{1,0:T(2,128)(2,1)S(1)} collective-permute-done((bf16[2,16384]{1,0:T(2,128)(2,1)S(1)}, bf16[2,16384]{1,0:T(2,128)(2,1)S(1)}, u32[]{:S(2)}, u32[]{:S(2)}) %collective-permute-start.1) | collective-permute-done | bytes 65568 | tf_op jit(solution)/shard_map/ppermute | solution.py:175
  33.4 0.1 fusion.18
  33.5 0.1 abs_reduce_fusion.1
  33.7 0.2 multiply_reduce_fusion
  33.9 0.0 copy-done.3
  33.9 0.6 %fusion.2 = (bf16[2,16384]{1,0:T(2,128)(2,1)S(1)}, bf16[2,16384]{1,0:T(2,128)(2,1)S(1)}) fusion(f32[1,16384]{1,0:T(1,128)S(1)} %get-tuple-element.24, f32[1,16384]{1,0:T(1,128)S(1)} %get-tuple-element.23, f32[1,2,128,128]{3,2,1,0:T(8,128)S(1)} %get-tuple-element.27, f32[2]{0:T(128)S(1)} %get-tuple-element.31, f32[16384]{0:T(1024)S(1)} %copy-done.3, ...), kind=kLoop, calls=%fused_computation.9 | loop fusion | flops 655360 | bytes 983056 | tf_op jit(solution)/shard_map/convert_element_type | solution.py:212
  34.5 0.8 %broadcast_in_dim.5 = bf16[4,2,16384]{2,1,0:T(2,128)(2,1)} broadcast(bf16[2,16384]{1,0:T(2,128)(2,1)S(1)} %get-tuple-element.21), dimensions={1,2} | broadcast | bytes 327680 | tf_op jit(solution)/shard_map/broadcast_in_dim | solution.py:218
  35.4 3.4 %all-to-all-start.3 = ((bf16[4,2,16384]{2,1,0:T(2,128)(2,1)}), bf16[4,2,16384]{2,1,0:T(2,128)(2,1)S(1)}, u32[]{:S(2)}, u32[]{:S(2)}) async-start(bf16[4,2,16384]{2,1,0:T(2,128)(2,1)} %broadcast_in_dim.5), calls=%async_computation.3 | async-start | bytes 524288 | tf_op jit(solution)/shard_map/all_to_all | solution.py:172
  38.8 0.1 copy_bitcast_fusion
  38.9 5.2 %all-to-all-done.3 = bf16[4,2,16384]{2,1,0:T(2,128)(2,1)S(1)} async-done(((bf16[4,2,16384]{2,1,0:T(2,128)(2,1)}), bf16[4,2,16384]{2,1,0:T(2,128)(2,1)S(1)}, u32[]{:S(2)}, u32[]{:S(2)}) %all-to-all-start.3) | async-done | bytes 262176 | tf_op jit(solution)/shard_map/all_to_all | solution.py:172
  44.1 0.8 %broadcast_in_dim.4 = bf16[4,2,16384]{2,1,0:T(2,128)(2,1)} broadcast(bf16[2,16384]{1,0:T(2,128)(2,1)S(1)} %get-tuple-element.22), dimensions={1,2} | broadcast | bytes 327680 | tf_op jit(solution)/shard_map/broadcast_in_dim | solution.py:218
  45.0 3.4 %all-to-all-start.2 = ((bf16[4,2,16384]{2,1,0:T(2,128)(2,1)}), bf16[4,2,16384]{2,1,0:T(2,128)(2,1)S(1)}, u32[]{:S(2)}, u32[]{:S(2)}) async-start(bf16[4,2,16384]{2,1,0:T(2,128)(2,1)} %broadcast_in_dim.4), calls=%async_computation.2 | async-start | bytes 524288 | tf_op jit(solution)/shard_map/all_to_all | solution.py:172
  48.4 0.1 reshape.229
  48.5 0.1 collective-permute-start.5
  48.6 0.8 %pad_maximum_fusion.3 = bf16[2,16384]{1,0:T(2,128)(2,1)} fusion(bf16[1,16384]{1,0:T(2,128)(2,1)S(1)} %get-tuple-element.29, bf16[1,16384]{1,0:T(2,128)(2,1)S(1)} %get-tuple-element.30), kind=kLoop, calls=%fused_computation.33 | loop fusion | flops 131072 | bytes 131072 | tf_op jit(solution)/shard_map/concatenate | solution.py:241
  49.4 0.6 pad_maximum_fusion.4
  49.9 3.8 %all-to-all-done.2 = bf16[4,2,16384]{2,1,0:T(2,128)(2,1)S(1)} async-done(((bf16[4,2,16384]{2,1,0:T(2,128)(2,1)}), bf16[4,2,16384]{2,1,0:T(2,128)(2,1)S(1)}, u32[]{:S(2)}, u32[]{:S(2)}) %all-to-all-start.2) | async-done | bytes 262176 | tf_op jit(solution)/shard_map/all_to_all | solution.py:172
  53.7 0.1 reshape.230.near
  53.8 0.1 collective-permute-start.4
  53.9 0.0 collective-permute-done.5
  54.0 0.0 copy-start
  54.0 2.2 %copy-done = bf16[16384,128]{1,0:T(8,128)(2,1)S(1)} copy-done((bf16[16384,128]{1,0:T(8,128)(2,1)S(1)}, bf16[16384,128]{1,0:T(8,128)(2,1)}, u32[]{:S(2)}) %copy-start) | copy-done | bytes 4194328
  56.2 0.0 copy-start.1
  56.2 1.2 %first_dots.1.before = f32[24,128]{1,0:T(8,128)S(1)} custom-call(bf16[16,16384]{1,0:T(8,128)(2,1)S(1)} %pad_maximum_fusion.early, bf16[8,16384]{1,0:T(8,128)(2,1)S(1)} %reshape.230.near, bf16[16384,128]{1,0:T(8,128)(2,1)S(1)} %copy-done), custom_call_target="tpu_custom_call" | custom-call | flops 67108864 | bytes 4194304 | tf_op jit(solution)/shard_map/first_dots/pallas_call | solution.py:147
  57.4 0.0 collective-permute-done.4.rows
  57.4 1.0 %copy-done.1 = bf16[16384,128]{1,0:T(8,128)(2,1)S(1)} copy-done((bf16[16384,128]{1,0:T(8,128)(2,1)S(1)}, bf16[16384,128]{1,0:T(8,128)(2,1)}, u32[]{:S(2)}) %copy-start.1) | copy-done | bytes 4194328
  58.4 1.4 %last_dot.1 = bf16[32,128]{1,0:T(8,128)(2,1)} custom-call(bf16[8,16384]{1,0:T(8,128)(2,1)S(1)} %collective-permute-done.4.rows, f32[24,128]{1,0:T(8,128)S(1)} %first_dots.1.before, bf16[16384,128]{1,0:T(8,128)(2,1)S(1)} %copy-done.1), custom_call_target="tpu_custom_call" | custom-call | flops 33554432 | bytes 4194304 | tf_op jit(solution)/shard_map/last_dot/pallas_call | solution.py:147
  (10 shorter events, 0.2 us)
Async XLA Ops:
  3.6 2.6 %collective-permute-start.2 = (bf16[8,16384]{1,0:T(8,128)(2,1)S(1)}, bf16[8,16384]{1,0:T(8,128)(2,1)S(1)}, u32[]{:S(2)}, u32[]{:S(2)}) collective-permute-start(bf16[8,16384]{1,0:T(8,128)(2,1)S(1)} %fusion.9), channel_id=1, source_target_pairs={{0,1},{1,0},{2,3},{3,2},{4,5},{5,4},{6,7},{7,6},{8,9},{9,8},{10,11... | collective-permute-start | bytes 786440 | tf_op jit(solution)/shard_map/ppermute | solution.py:175
  4.7 7.6 %collective-permute-start = (bf16[8,16384]{1,0:T(8,128)(2,1)S(1)}, bf16[8,16384]{1,0:T(8,128)(2,1)S(1)}, u32[]{:S(2)}, u32[]{:S(2)}) collective-permute-start(bf16[8,16384]{1,0:T(8,128)(2,1)S(1)} %fusion.13), channel_id=1, source_target_pairs={{0,1},{1,0},{2,3},{3,2},{4,5},{5,4},{6,7},{7,6},{8,9},{9,8},{10,11... | collective-permute-start | bytes 786440 | tf_op jit(solution)/shard_map/ppermute | solution.py:175
  5.5 21.7 %copy-start.2 = (bf16[2,16384]{1,0:T(2,128)(2,1)S(1)}, bf16[2,16384]{1,0:T(2,128)(2,1)}, u32[]{:S(2)}) copy-start(bf16[2,16384]{1,0:T(2,128)(2,1)} %old.1) | copy-start | bytes 196612
  6.2 27.7 %copy-start.3 = (f32[16384]{0:T(1024)S(1)}, f32[16384]{0:T(1024)}, u32[]{:S(2)}) copy-start(f32[16384]{0:T(1024)} %param.12) | copy-start | bytes 196612
  7.1 10.8 %all-to-all-start.1 = ((bf16[4,2,16384]{2,1,0:T(2,128)(2,1)}), bf16[4,2,16384]{2,1,0:T(2,128)(2,1)S(1)}, u32[]{:S(2)}, u32[]{:S(2)}) async-start(bf16[4,2,16384]{2,1,0:T(2,128)(2,1)} %reshape.228), calls=%async_computation.1 | async-start | bytes 524288 | tf_op jit(solution)/shard_map/all_to_all | solution.py:172
  17.9 9.1 %all-to-all-start = ((bf16[4,2,16384]{2,1,0:T(2,128)(2,1)}), bf16[4,2,16384]{2,1,0:T(2,128)(2,1)S(1)}, u32[]{:S(2)}, u32[]{:S(2)}) async-start(bf16[4,2,16384]{2,1,0:T(2,128)(2,1)} %reshape.227), calls=%async_computation | async-start | bytes 524288 | tf_op jit(solution)/shard_map/all_to_all | solution.py:172
  21.8 8.0 %collective-permute-start.3 = (bf16[2,16384]{1,0:T(2,128)(2,1)S(1)}, bf16[2,16384]{1,0:T(2,128)(2,1)S(1)}, u32[]{:S(2)}, u32[]{:S(2)}) collective-permute-start(bf16[2,16384]{1,0:T(2,128)(2,1)S(1)} %fusion.8), channel_id=1, source_target_pairs={{0,8},{1,9},{2,10},{3,11},{4,12},{5,13},{6,14},{7,15},{8,0},{9,1},... | collective-permute-start | bytes 196616 | tf_op jit(solution)/shard_map/ppermute | solution.py:175
  27.5 5.9 %collective-permute-start.1 = (bf16[2,16384]{1,0:T(2,128)(2,1)S(1)}, bf16[2,16384]{1,0:T(2,128)(2,1)S(1)}, u32[]{:S(2)}, u32[]{:S(2)}) collective-permute-start(bf16[2,16384]{1,0:T(2,128)(2,1)S(1)} %fusion.17), channel_id=1, source_target_pairs={{0,8},{1,9},{2,10},{3,11},{4,12},{5,13},{6,14},{7,15},{8,0},{9,1},... | collective-permute-start | bytes 196616 | tf_op jit(solution)/shard_map/ppermute | solution.py:175
  35.4 8.8 %all-to-all-start.3 = ((bf16[4,2,16384]{2,1,0:T(2,128)(2,1)}), bf16[4,2,16384]{2,1,0:T(2,128)(2,1)S(1)}, u32[]{:S(2)}, u32[]{:S(2)}) async-start(bf16[4,2,16384]{2,1,0:T(2,128)(2,1)} %broadcast_in_dim.5), calls=%async_computation.3 | async-start | bytes 524288 | tf_op jit(solution)/shard_map/all_to_all | solution.py:172
  45.0 8.8 %all-to-all-start.2 = ((bf16[4,2,16384]{2,1,0:T(2,128)(2,1)}), bf16[4,2,16384]{2,1,0:T(2,128)(2,1)S(1)}, u32[]{:S(2)}, u32[]{:S(2)}) async-start(bf16[4,2,16384]{2,1,0:T(2,128)(2,1)} %broadcast_in_dim.4), calls=%async_computation.2 | async-start | bytes 524288 | tf_op jit(solution)/shard_map/all_to_all | solution.py:172
  48.5 5.4 %collective-permute-start.5 = (bf16[8,16384]{1,0:T(8,128)(2,1)S(1)}, bf16[8,16384]{1,0:T(8,128)(2,1)S(1)}, u32[]{:S(2)}, u32[]{:S(2)}) collective-permute-start(bf16[8,16384]{1,0:T(8,128)(2,1)S(1)} %reshape.229), channel_id=1, source_target_pairs={{0,1},{1,0},{2,3},{3,2},{4,5},{5,4},{6,7},{7,6},{8,9},{9,8},{10,11... | collective-permute-start | bytes 786440 | tf_op jit(solution)/shard_map/ppermute | solution.py:175
  53.8 3.5 %collective-permute-start.4 = (bf16[8,16384]{1,0:T(8,128)(2,1)S(1)}, bf16[8,16384]{1,0:T(8,128)(2,1)S(1)}, u32[]{:S(2)}, u32[]{:S(2)}) collective-permute-start(bf16[8,16384]{1,0:T(8,128)(2,1)S(1)} %reshape.230.near), channel_id=1, source_target_pairs={{0,1},{1,0},{2,3},{3,2},{4,5},{5,4},{6,7},{7,6},{8,9},{9,8},{10,11... | collective-permute-start | bytes 786440 | tf_op jit(solution)/shard_map/ppermute | solution.py:175
  54.0 2.2 %copy-start = (bf16[16384,128]{1,0:T(8,128)(2,1)S(1)}, bf16[16384,128]{1,0:T(8,128)(2,1)}, u32[]{:S(2)}) copy-start(bf16[16384,128]{1,0:T(8,128)(2,1)} %weight.5) | copy-start | bytes 12582916
  56.2 2.2 %copy-start.1 = (bf16[16384,128]{1,0:T(8,128)(2,1)S(1)}, bf16[16384,128]{1,0:T(8,128)(2,1)}, u32[]{:S(2)}) copy-start(bf16[16384,128]{1,0:T(8,128)(2,1)} %weight.5) | copy-start | bytes 12582916

commit v12 on v9

v12 whole, which is shorter than its diff:
```python
import functools

import jax
import jax.numpy as jnp
from jax import lax
from jax.experimental import pallas as pl
from jax.experimental.pallas import tpu as pltpu
from jax.sharding import PartitionSpec as P

HD = 128
QB = 128
EPS = 1e-06
F32 = jnp.float32
BF16 = jnp.bfloat16
PIECES = 4
STEPS = 8
VMEM_LIMIT = 24 << 20
SMALL_LIMIT = 16 << 20


def late_levels(n):
    return [1 << b for b in range(3, n.bit_length() - 1)]


def owner_token(row, device, n):
    bits = [2, 6] + late_levels(n)
    distance = row >> (len(bits) + 1)
    which = (row >> len(bits)) & 1
    block = row ^ which
    for place, bit in enumerate(bits):
        distance = distance ^ (((block >> (len(bits) - 1 - place)) & 1) * bit)
    return ((device ^ distance) << 1) | which


def attend_kernel(
    n, queries, keys, values, weight, context, held, query, key, value, small, large
):
    device = lax.axis_index("tp")
    tokens = queries.shape[0]
    heads = queries.shape[1] // HD
    group = heads * n // (keys.shape[1] // HD)
    copies = [pltpu.make_async_copy(queries, query, small.at[0])]
    for h in range(heads):
        at = pl.ds(pl.multiple_of(lax.div(device * heads + h, group) * HD, HD), HD)
        copies.append(pltpu.make_async_copy(keys.at[:, at], key.at[h], small.at[1 + 2 * h]))
        copies.append(pltpu.make_async_copy(values.at[:, at], value.at[h], small.at[2 + 2 * h]))
    depth = held.shape[0] // PIECES
    late = []
    for c in range(PIECES):
        part = pl.ds(c * depth, depth)
        late.append(pltpu.make_async_copy(weight.at[part], held.at[part], large.at[c]))
    for copy in copies + late:
        copy.start()
    row = lax.broadcasted_iota(jnp.int32, (tokens, tokens), 0)
    col = lax.broadcasted_iota(jnp.int32, (tokens, tokens), 1)
    token = owner_token(row, device, n)
    pick = (token == col).astype(F32).astype(BF16)
    for copy in copies:
        copy.wait()
    ordered = jnp.dot(pick, query[...], preferred_element_type=F32).astype(BF16)
    for h in range(heads):
        scores = lax.dot_general(
            ordered[:, h * HD : (h + 1) * HD],
            key[h],
            (((1,), (1,)), ((), ())),
            preferred_element_type=F32,
        ) / jnp.sqrt(F32(HD))
        scores = jnp.where(col <= token, scores, F32(-1e30))
        weights = jnp.exp(scores - jnp.max(scores, axis=1, keepdims=True))
        probs = (weights / jnp.sum(weights, axis=1, keepdims=True)).astype(BF16)
        context[:, h * HD : (h + 1) * HD] = jnp.dot(
            probs, value[h], preferred_element_type=F32
        ).astype(BF16)
    for copy in late:
        copy.wait()


def in_hbm(*arrays):
    return [pltpu.with_memory_space_constraint(x, pltpu.HBM) for x in arrays]


def attend(n, queries, keys, values, weight):
    tokens = queries.shape[0]
    heads = queries.shape[1] // HD
    whole = pl.BlockSpec(memory_space=pltpu.VMEM)
    return pl.pallas_call(
        functools.partial(attend_kernel, n),
        out_shape=[
            jax.ShapeDtypeStruct(queries.shape, BF16),
            pltpu.VMEM(weight.shape, BF16),
        ],
        in_specs=[pl.BlockSpec(memory_space=pltpu.HBM)] * 4,
        out_specs=[whole] * 2,
        scratch_shapes=[
            pltpu.VMEM(queries.shape, BF16),
            pltpu.VMEM((heads, tokens, HD), BF16),
            pltpu.VMEM((heads, tokens, HD), BF16),
            pltpu.SemaphoreType.DMA((1 + 2 * heads,)),
            pltpu.SemaphoreType.DMA((PIECES,)),
        ],
        compiler_params=pltpu.CompilerParams(vmem_limit_bytes=VMEM_LIMIT),
        cost_estimate=pl.CostEstimate(
            flops=0, bytes_accessed=2 * weight.size, transcendentals=0
        ),
        name="attend",
    )(*in_hbm(queries, keys, values, weight))


def parts(ref):
    width = ref.shape[1] // STEPS
    return [pl.ds(c * width, width) for c in range(STEPS)]


def split_kernel(which, kept, got, own, *pieces):
    rows = got.shape[0]
    part = rows // 4
    for at in parts(got):
        total = kept[which * rows : (which + 1) * rows, at] + got[:, at].astype(F32)
        own[:, at] = total[:part]
        for k, piece in enumerate(pieces, 1):
            piece[:, at] = total[k * part : (k + 1) * part].astype(BF16)


def settle_kernel(which, own, old, *refs):
    *arrived, total, turned = refs
    for at in parts(own):
        value = own[:, at]
        for piece in arrived:
            value = value + piece[:, at].astype(F32)
        row = lax.broadcasted_iota(jnp.int32, value.shape, 0)
        value = value + jnp.where(row == which, old[:, at].astype(F32), F32(0))
        total[:, at] = value
        turned[:, at] = jnp.concatenate([value[1:], value[:1]], axis=0).astype(BF16)


def encode_kernel(total, arrived, gain, *refs):
    *before, normed, codes, scales, decoded = refs
    blocks = total.shape[1] // QB
    row = lax.broadcasted_iota(jnp.int32, (total.shape[0], QB), 0)
    lane = lax.broadcasted_iota(jnp.int32, (total.shape[0], blocks), 1)
    all_scales = jnp.zeros(scales.shape, F32)
    squares = jnp.zeros(row.shape, F32)
    for b in range(blocks):
        at = pl.ds(b * QB, QB)
        stream = total[:, at] + arrived[:, at].astype(F32)
        scale = jnp.max(jnp.abs(stream), axis=1, keepdims=True) + EPS
        code = (stream / scale).astype(BF16).astype(F32)
        value = code * scale
        squares += value * value
        decoded[:, at] = value
        if before:
            code = jnp.where(row == 0, before[0][:, at].astype(F32), code)
        codes[:, at] = code.astype(BF16)
        all_scales = jnp.where(lane == b, scale, all_scales)
    if before:
        all_scales = jnp.where(
            lax.broadcasted_iota(jnp.int32, scales.shape, 0) == 0, before[1][...], all_scales
        )
    scales[...] = all_scales
    mean_sq = jnp.sum(squares, axis=1, keepdims=True) / total.shape[1]
    factor = lax.rsqrt(mean_sq + 1e-05)
    for at in parts(total):
        normed[:, at] = (decoded[:, at] * factor * gain[:, at]).astype(BF16)


def times(rows, weight):
    depth = weight.shape[0] // STEPS
    count = sum(r.shape[0] for r in rows)
    total = jnp.zeros((count, weight.shape[1]), F32)
    for c in range(STEPS):
        part = pl.ds(c * depth, depth)
        block = jnp.concatenate([r[:, part] for r in rows], axis=0)
        total += jnp.dot(block, weight[part], preferred_element_type=F32)
    return total


def first_dots_kernel(early, early_other, near, weight, out):
    out[...] = times([early, early_other, near], weight)


def last_dot_kernel(n, rows, before, weight, out):
    device = lax.axis_index("tp")
    tokens, quarter = out.shape[0], rows.shape[0]
    token = lax.broadcasted_iota(jnp.int32, (tokens, quarter), 0)
    row = lax.broadcasted_iota(jnp.int32, (tokens, quarter), 1) ^ (3 * quarter // 4)
    total = jnp.zeros(out.shape, F32)
    for start, values in (
        (0, before[:quarter]),
        (2 * quarter, before[quarter : 2 * quarter]),
        (quarter, before[2 * quarter :]),
        (3 * quarter, times([rows], weight)),
    ):
        pick = (owner_token(row + start, device, n) == token).astype(F32).astype(BF16)
        total += jnp.dot(pick, values.astype(BF16), preferred_element_type=F32)
    out[...] = total.astype(BF16)


def local_call(kernel, shapes, name, *operands, scratch=()):
    spec = pl.BlockSpec(memory_space=pltpu.VMEM)
    return pl.pallas_call(
        kernel,
        out_shape=[jax.ShapeDtypeStruct(shape, dtype) for shape, dtype in shapes],
        in_specs=[spec] * len(operands),
        out_specs=[spec] * len(shapes),
        scratch_shapes=list(scratch),
        compiler_params=pltpu.CompilerParams(vmem_limit_bytes=SMALL_LIMIT),
        cost_estimate=pl.CostEstimate(
            flops=0, bytes_accessed=sum(2 * x.size for x in operands), transcendentals=0
        ),
        name=name,
    )(*operands)


def on_device(residual, queries, key_rows, value_rows, out_weight, norm_gain, q_weight):
    n = lax.axis_size("tp")
    tokens = queries.shape[0]
    D = residual.shape[1]
    levels = late_levels(n)
    square = (6, 2, 4)

    def swap(x, distance):
        return lax.ppermute(x, "tp", [(i, i ^ distance) for i in range(n)])

    half, quarter = tokens // 2, tokens // 4
    part, pair = quarter // 4, (2, D)
    gain = norm_gain.reshape(1, D)
    context, weight = attend(n, queries, key_rows, value_rows, out_weight)
    sent = jnp.dot(context[half:], weight, preferred_element_type=F32).astype(BF16)
    got = [swap(sent[:quarter], 1), swap(sent[quarter:], 1)]
    kept = jnp.dot(context[:half], weight, preferred_element_type=F32)

    def reduce(which):
        shapes = [((part, D), F32)] + [((part, D), BF16)] * 3
        kernel = functools.partial(split_kernel, which)
        total, *pieces = local_call(kernel, shapes, f"split{which}", kept, got[which])
        arrived = [swap(piece, distance) for piece, distance in zip(pieces, square)]
        if len(levels) > 1:
            for piece in arrived:
                total = total + piece.astype(F32)
            arrived = []
        for level in levels[:-1]:
            rest = total.shape[0] // 2
            total = total[:rest] + swap(total[rest:].astype(BF16), level).astype(F32)
        kernel = functools.partial(settle_kernel, which)
        shapes = [(pair, F32), (pair, BF16)]
        return local_call(kernel, shapes, f"settle{which}", total, residual, *arrived)

    def gather(held):
        for level in levels[-2::-1]:
            held = jnp.concatenate([held, swap(held, level)], axis=0)
        arrived = [swap(held, distance) for distance in square]
        return jnp.concatenate(arrived[::-1] + [held], axis=0)

    sums = [reduce(which) for which in range(2)]
    sums = [(total, swap(turned, levels[-1])) for total, turned in sums]
    outs, held = [], []
    for which in range(2):
        shapes = [(pair, BF16), (pair, BF16), ((2, D // QB), F32)]
        normed, *outs = local_call(
            encode_kernel,
            shapes,
            f"encode{which}",
            *sums[which],
            gain,
            *outs,
            scratch=[pltpu.VMEM(pair, F32)],
        )
        held.append(gather(normed))
    others = [swap(rows, 1) for rows in held]
    width = q_weight.shape[1]
    shapes = [((3 * quarter, width), F32)]
    (before,) = local_call(
        first_dots_kernel, shapes, "first_dots", held[0], others[0], held[1], q_weight
    )
    kernel = functools.partial(last_dot_kernel, n)
    shapes = [((tokens, width), BF16)]
    (next_queries,) = local_call(kernel, shapes, "last_dot", others[1], before, q_weight)
    return (*outs, next_queries)


def solution(mesh):
    in_specs = (
        P(("replica", "tp"), None),
        P("replica", "tp"),
        P("replica", None),
        P("replica", None),
        P("tp", None),
        P(),
        P(None, "tp"),
    )
    out_specs = (P(("replica", "tp"), None), P(("replica", "tp"), None), P("replica", "tp"))
    return jax.shard_map(
        on_device, mesh=mesh, in_specs=in_specs, out_specs=out_specs, check_vma=False
    )
```

time: 39.7 us -> 36.4 us (0.917)
  waiting for transfers between devices: 18.4 us -> 5.89 us
  starting transfers between devices: 11.4 us -> 21.3 us
  Pallas kernels: 4.36 us -> 6.34 us
  local copies, waits for them, and re-layouts: 1.67 us -> 0.06 us
  other arithmetic: 1.63 us -> 0.6 us
    ppermute x9 -> x18, waiting for transfers between devices: 18.4 us -> 5.89 us  [swap(): return lax.ppermute(x, 'tp', [(i, i ^ distance) for i in range(n)])]
    ppermute x9 -> x18, starting transfers between devices: 11.4 us -> 21.3 us  [swap(): return lax.ppermute(x, 'tp', [(i, i ^ distance) for i in range(n)])]
    pallas_call x3 -> x9, Pallas kernels: 4.36 us -> 6.34 us  [the longest x8 4.06 us: local_call(): pl.pallas_call(kernel, out_shape=[jax.ShapeDtypeStruct(shape, dtype) for...]
    unnamed x9 -> x6, local copies, waits for them, and re-layouts: 0.82 us -> 0.01 us
    slice x3 -> x1, local copies, waits for them, and re-layouts: 0.82 us -> 0.04 us  [on_device(): got = [swap(sent[:quarter], 1), swap(sent[quarter:], 1)]]
    convert_element_type x3 -> x0, other arithmetic: 0.55 us -> none  [the longest x1 0.4 us: on_device(): (decoded * lax.rsqrt(mean_sq + 1e-05) * norm_gain[None, :]).astype(BF16)]
  transfers between devices with their start and end apart: 9 -> 18, of which waited for: 7 -> 7; matrix products, arithmetic and copies ran while one was open for 5% -> 3% of each run, Pallas kernels for 2% -> 7%
where the time goes in v12:
time: 36.4 us; the launch traced here: 36.3 us
  starting transfers between devices  21.3 us (59%)
  Pallas kernels  6.34 us (17%)
  waiting for transfers between devices  5.89 us (16%)
  matrix products  1.31 us (4%)
  between operations  0.74 us (2%)
  other arithmetic  0.6 us (2%)
    ppermute x18, starting transfers between devices, swap(): return lax.ppermute(x, 'tp', [(i, i ^ distance) for i in range(n)])  21.3 us
    ppermute x18, waiting for transfers between devices, swap(): return lax.ppermute(x, 'tp', [(i, i ^ distance) for i in range(n)])  5.89 us
    pallas_call x8, Pallas kernels, local_call(): pl.pallas_call(kernel, out_shape=[jax.ShapeDtypeStruct(shape, dtype) for...  4.06 us
    pallas_call x1, Pallas kernels, attend(): pl.pallas_call(functools.partial(attend_kernel, n), out_shape=[jax.ShapeD...  2.28 us
  transfers between devices with their start and end apart: 18, of which 7 were waited for; matrix products, arithmetic and copies ran while one was open for 3% of the time, Pallas kernels for 7%

profile of v12, /device:TPU:0, one launch (start us, length us, event | category | flops | bytes accessed | tf_op | source)
XLA Modules:
  0.0 36.3 jit_solution(15285745195181605563)
XLA Ops:
  0.6 2.3 %attend.1 = (bf16[32,128]{1,0:T(8,128)(2,1)S(1)}, bf16[128,16384]{1,0:T(8,128)(2,1)S(1)}) custom-call(bf16[32,128]{1,0:T(8,128)(2,1)} %queries.1, bf16[32,1024]{1,0:T(8,128)(2,1)} %keys.1, bf16[32,1024]{1,0:T(8,128)(2,1)} %values.1, bf16[128,16384]{1,0:T(8,128)(2,1)} %weight.3), custom_call_target="tpu_custom_call" | custom-call | bytes 4194304 | tf_op jit(solution)/shard_map/attend/pallas_call | solution.py:86
  2.9 0.7 %convolution_convert_fusion = bf16[16,16384]{1,0:T(8,128)(2,1)S(1)} fusion(bf16[128,16384]{1,0:T(8,128)(2,1)S(1)} %get-tuple-element.24, bf16[32,128]{1,0:T(8,128)(2,1)S(1)} %get-tuple-element.23), kind=kOutput, calls=%fused_computation | convolution fusion | flops 67371008 | bytes 4722688 | tf_op jit(solution)/shard_map/dot_general | solution.py:228
  3.6 0.0 copy-start.2
  3.6 0.5 %collective-permute-start.5 = (bf16[8,16384]{1,0:T(8,128)(2,1)S(1)}, bf16[8,16384]{1,0:T(8,128)(2,1)S(1)}, u32[]{:S(2)}, u32[]{:S(2)}) collective-permute-start(bf16[8,16384]{1,0:T(8,128)(2,1)S(1)} %get-tuple-element.43), channel_id=1, source_target_pairs={{0,1},{1,0},{2,3},{3,2},{4,5},{5,4},{6,7},{7,6},{8,9},{9,8},{10,11... | collective-permute-start | bytes 786440 | tf_op jit(solution)/shard_map/ppermute | solution.py:222
  4.2 0.0 copy-start.1
  4.2 0.0 copy-start
  4.2 0.1 collective-permute-start
  4.3 0.7 %fusion.1.kept = f32[16,16384]{1,0:T(8,128)S(1)} fusion(bf16[128,16384]{1,0:T(8,128)(2,1)S(1)} %get-tuple-element.24, bf16[32,128]{1,0:T(8,128)(2,1)S(1)} %get-tuple-element.23), kind=kOutput, calls=%fused_computation.4 | convolution fusion | flops 67108864 | bytes 5246976 | tf_op jit(solution)/shard_map/dot_general | solution.py:230
  4.9 0.4 %collective-permute-done.5.got = bf16[8,16384]{1,0:T(8,128)(2,1)S(1)} collective-permute-done((bf16[8,16384]{1,0:T(8,128)(2,1)S(1)}, bf16[8,16384]{1,0:T(8,128)(2,1)S(1)}, u32[]{:S(2)}, u32[]{:S(2)}) %collective-permute-start.5) | collective-permute-done | bytes 262176 | tf_op jit(solution)/shard_map/ppermute | solution.py:222
  5.3 0.1 split0.1
  5.4 4.0 %collective-permute-start.6 = (bf16[2,16384]{1,0:T(2,128)(2,1)S(1)}, bf16[2,16384]{1,0:T(2,128)(2,1)S(1)}, u32[]{:S(2)}, u32[]{:S(2)}) collective-permute-start(bf16[2,16384]{1,0:T(2,128)(2,1)S(1)} %get-tuple-element.32), channel_id=1, source_target_pairs={{0,6},{1,7},{2,4},{3,5},{4,2},{5,3},{6,0},{7,1},{8,14},{9,15},{10,... | collective-permute-start | bytes 196616 | tf_op jit(solution)/shard_map/ppermute | solution.py:222
  9.4 0.5 %collective-permute-start.7 = (bf16[2,16384]{1,0:T(2,128)(2,1)S(1)}, bf16[2,16384]{1,0:T(2,128)(2,1)S(1)}, u32[]{:S(2)}, u32[]{:S(2)}) collective-permute-start(bf16[2,16384]{1,0:T(2,128)(2,1)S(1)} %get-tuple-element.33), channel_id=1, source_target_pairs={{0,2},{1,3},{2,0},{3,1},{4,6},{5,7},{6,4},{7,5},{8,10},{9,11},{10,... | collective-permute-start | bytes 196616 | tf_op jit(solution)/shard_map/ppermute | solution.py:222
  9.9 0.1 collective-permute-start.8
  10.0 0.0 collective-permute-done.got
  10.0 0.1 split1.1
  10.1 2.9 %collective-permute-start.1 = (bf16[2,16384]{1,0:T(2,128)(2,1)S(1)}, bf16[2,16384]{1,0:T(2,128)(2,1)S(1)}, u32[]{:S(2)}, u32[]{:S(2)}) collective-permute-start(bf16[2,16384]{1,0:T(2,128)(2,1)S(1)} %get-tuple-element.26), channel_id=1, source_target_pairs={{0,6},{1,7},{2,4},{3,5},{4,2},{5,3},{6,0},{7,1},{8,14},{9,15},{10,... | collective-permute-start | bytes 196616 | tf_op jit(solution)/shard_map/ppermute | solution.py:222
  13.1 0.5 %collective-permute-start.2 = (bf16[2,16384]{1,0:T(2,128)(2,1)S(1)}, bf16[2,16384]{1,0:T(2,128)(2,1)S(1)}, u32[]{:S(2)}, u32[]{:S(2)}) collective-permute-start(bf16[2,16384]{1,0:T(2,128)(2,1)S(1)} %get-tuple-element.27), channel_id=1, source_target_pairs={{0,2},{1,3},{2,0},{3,1},{4,6},{5,7},{6,4},{7,5},{8,10},{9,11},{10,... | collective-permute-start | bytes 196616 | tf_op jit(solution)/shard_map/ppermute | solution.py:222
  13.6 0.0 collective-permute-done.6.refs_0_
  13.6 0.2 collective-permute-start.3
  13.8 0.0 collective-permute-done.7.refs_1_
  13.8 1.0 %collective-permute-done.8.refs_2_ = bf16[2,16384]{1,0:T(2,128)(2,1)S(1)} collective-permute-done((bf16[2,16384]{1,0:T(2,128)(2,1)S(1)}, bf16[2,16384]{1,0:T(2,128)(2,1)S(1)}, u32[]{:S(2)}, u32[]{:S(2)}) %collective-permute-start.8) | collective-permute-done | bytes 65568 | tf_op jit(solution)/shard_map/ppermute | solution.py:222
  14.8 0.0 copy-done.2
  14.8 0.2 settle0.1
  15.0 2.6 %collective-permute-start.9 = (bf16[2,16384]{1,0:T(2,128)(2,1)S(1)}, bf16[2,16384]{1,0:T(2,128)(2,1)S(1)}, u32[]{:S(2)}, u32[]{:S(2)}) collective-permute-start(bf16[2,16384]{1,0:T(2,128)(2,1)S(1)} %get-tuple-element.36), channel_id=1, source_target_pairs={{0,8},{1,9},{2,10},{3,11},{4,12},{5,13},{6,14},{7,15},{8,0},{9,1},... | collective-permute-start | bytes 196616 | tf_op jit(solution)/shard_map/ppermute | solution.py:222
  17.6 0.0 collective-permute-done.1.refs_0_
  17.6 0.0 collective-permute-done.2.refs_1_
  17.6 0.2 collective-permute-done.3.refs_2_
  17.8 0.2 settle1.1
  18.0 2.7 %collective-permute-start.4 = (bf16[2,16384]{1,0:T(2,128)(2,1)S(1)}, bf16[2,16384]{1,0:T(2,128)(2,1)S(1)}, u32[]{:S(2)}, u32[]{:S(2)}) collective-permute-start(bf16[2,16384]{1,0:T(2,128)(2,1)S(1)} %get-tuple-element.30), channel_id=1, source_target_pairs={{0,8},{1,9},{2,10},{3,11},{4,12},{5,13},{6,14},{7,15},{8,0},{9,1},... | collective-permute-start | bytes 196616 | tf_op jit(solution)/shard_map/ppermute | solution.py:222
  20.7 1.4 %collective-permute-done.9.arrived = bf16[2,16384]{1,0:T(2,128)(2,1)S(1)} collective-permute-done((bf16[2,16384]{1,0:T(2,128)(2,1)S(1)}, bf16[2,16384]{1,0:T(2,128)(2,1)S(1)}, u32[]{:S(2)}, u32[]{:S(2)}) %collective-permute-start.9) | collective-permute-done | bytes 65568 | tf_op jit(solution)/shard_map/ppermute | solution.py:222
  22.1 0.0 copy-done.1
  22.1 0.4 %encode0.1 = (bf16[2,16384]{1,0:T(2,128)(2,1)S(1)}, bf16[2,16384]{1,0:T(2,128)(2,1)S(1)}, f32[2,128]{1,0:T(2,128)S(1)}) custom-call(f32[2,16384]{1,0:T(2,128)S(1)} %get-tuple-element.35.total, bf16[2,16384]{1,0:T(2,128)(2,1)S(1)} %collective-permute-done.9.arrived, f32[1,16384]{1,0:T(1,128)S(1)} %bitcast.3), custom_call_target="tpu_custom_call" | custom-call | bytes 163840 | tf_op jit(solution)/shard_map/encode0/pallas_call | solution.py:200
  22.5 1.2 %collective-permute-start.16 = (bf16[2,16384]{1,0:T(2,128)(2,1)S(1)}, bf16[2,16384]{1,0:T(2,128)(2,1)S(1)}, u32[]{:S(2)}, u32[]{:S(2)}) collective-permute-start(bf16[2,16384]{1,0:T(2,128)(2,1)S(1)} %get-tuple-element.42), channel_id=1, source_target_pairs={{0,6},{1,7},{2,4},{3,5},{4,2},{5,3},{6,0},{7,1},{8,14},{9,15},{10,... | collective-permute-start | bytes 196616 | tf_op jit(solution)/shard_map/ppermute | solution.py:222
  23.8 0.2 collective-permute-start.15
  24.0 2.1 %collective-permute-start.14 = (bf16[2,16384]{1,0:T(2,128)(2,1)S(1)}, bf16[2,16384]{1,0:T(2,128)(2,1)S(1)}, u32[]{:S(2)}, u32[]{:S(2)}) collective-permute-start(bf16[2,16384]{1,0:T(2,128)(2,1)S(1)} %get-tuple-element.42), channel_id=1, source_target_pairs={{0,4},{1,5},{2,6},{3,7},{4,0},{5,1},{6,2},{7,3},{8,12},{9,13},{10,... | collective-permute-start | bytes 196616 | tf_op jit(solution)/shard_map/ppermute | solution.py:222
  26.1 0.0 collective-permute-done.4.arrived
  26.1 1.0 %encode1.1 = (bf16[2,16384]{1,0:T(2,128)(2,1)S(1)}, bf16[2,16384]{1,0:T(2,128)(2,1)}, f32[2,128]{1,0:T(2,128)}) custom-call(f32[2,16384]{1,0:T(2,128)S(1)} %get-tuple-element.29.total, bf16[2,16384]{1,0:T(2,128)(2,1)S(1)} %collective-permute-done.4.arrived, f32[1,16384]{1,0:T(1,128)S(1)} %bitcast.4, bf16[2,16384]{1,0:T(2,128)(2,1)S(1)} %get-tuple-element.37.refs_0_, ...), custom_call_target="tpu_custom_call" | custom-call | bytes 229888 | tf_op jit(solution)/shard_map/encode1/pallas_call | solution.py:200
  27.1 1.2 %collective-permute-start.12 = (bf16[2,16384]{1,0:T(2,128)(2,1)S(1)}, bf16[2,16384]{1,0:T(2,128)(2,1)S(1)}, u32[]{:S(2)}, u32[]{:S(2)}) collective-permute-start(bf16[2,16384]{1,0:T(2,128)(2,1)S(1)} %get-tuple-element.41), channel_id=1, source_target_pairs={{0,6},{1,7},{2,4},{3,5},{4,2},{5,3},{6,0},{7,1},{8,14},{9,15},{10,... | collective-permute-start | bytes 196616 | tf_op jit(solution)/shard_map/ppermute | solution.py:222
  28.3 0.3 collective-permute-start.11
  28.6 0.0 collective-permute-done.16
  28.6 2.0 %collective-permute-start.10 = (bf16[2,16384]{1,0:T(2,128)(2,1)S(1)}, bf16[2,16384]{1,0:T(2,128)(2,1)S(1)}, u32[]{:S(2)}, u32[]{:S(2)}) collective-permute-start(bf16[2,16384]{1,0:T(2,128)(2,1)S(1)} %get-tuple-element.41), channel_id=1, source_target_pairs={{0,4},{1,5},{2,6},{3,7},{4,0},{5,1},{6,2},{7,3},{8,12},{9,13},{10,... | collective-permute-start | bytes 196616 | tf_op jit(solution)/shard_map/ppermute | solution.py:222
  30.6 0.0 collective-permute-done.15
  30.6 0.0 collective-permute-done.14
  30.6 0.3 pad_maximum_fusion.1.early
  30.9 0.1 collective-permute-start.17
  31.0 1.3 %collective-permute-done.12 = bf16[2,16384]{1,0:T(2,128)(2,1)S(1)} collective-permute-done((bf16[2,16384]{1,0:T(2,128)(2,1)S(1)}, bf16[2,16384]{1,0:T(2,128)(2,1)S(1)}, u32[]{:S(2)}, u32[]{:S(2)}) %collective-permute-start.12) | collective-permute-done | bytes 65568 | tf_op jit(solution)/shard_map/ppermute | solution.py:222
  32.3 0.7 %collective-permute-done.11 = bf16[2,16384]{1,0:T(2,128)(2,1)S(1)} collective-permute-done((bf16[2,16384]{1,0:T(2,128)(2,1)S(1)}, bf16[2,16384]{1,0:T(2,128)(2,1)S(1)}, u32[]{:S(2)}, u32[]{:S(2)}) %collective-permute-start.11) | collective-permute-done | bytes 65568 | tf_op jit(solution)/shard_map/ppermute | solution.py:222
  33.0 0.0 collective-permute-done.10
  33.0 0.3 pad_maximum_fusion.near
  33.3 0.1 collective-permute-start.13
  33.3 0.0 collective-permute-done.17.early_other
  33.4 0.0 copy-done
  33.4 0.7 %first_dots.1.before = f32[24,128]{1,0:T(8,128)S(1)} custom-call(bf16[8,16384]{1,0:T(8,128)(2,1)S(1)} %pad_maximum_fusion.1.early, bf16[8,16384]{1,0:T(8,128)(2,1)S(1)} %collective-permute-done.17.early_other, bf16[8,16384]{1,0:T(8,128)(2,1)S(1)} %pad_maximum_fusion.near, bf16[16384,128]{1,0:T(8,128)(2,1)S(1)} %copy-done), custom_call_target="tpu_custom_call" | custom-call | bytes 4980736 | tf_op jit(solution)/shard_map/first_dots/pallas_call | solution.py:200
  34.1 0.8 %collective-permute-done.13.rows = bf16[8,16384]{1,0:T(8,128)(2,1)S(1)} collective-permute-done((bf16[8,16384]{1,0:T(8,128)(2,1)S(1)}, bf16[8,16384]{1,0:T(8,128)(2,1)S(1)}, u32[]{:S(2)}, u32[]{:S(2)}) %collective-permute-start.13) | collective-permute-done | bytes 262176 | tf_op jit(solution)/shard_map/ppermute | solution.py:222
  34.9 1.4 %last_dot.1 = bf16[32,128]{1,0:T(8,128)(2,1)} custom-call(bf16[8,16384]{1,0:T(8,128)(2,1)S(1)} %collective-permute-done.13.rows, f32[24,128]{1,0:T(8,128)S(1)} %first_dots.1.before, bf16[16384,128]{1,0:T(8,128)(2,1)S(1)} %copy-done), custom_call_target="tpu_custom_call" | custom-call | bytes 4462592 | tf_op jit(solution)/shard_map/last_dot/pallas_call | solution.py:200
  (1 shorter events, 0.0 us)
Async XLA Ops:
  3.6 11.2 %copy-start.2 = (bf16[2,16384]{1,0:T(2,128)(2,1)S(1)}, bf16[2,16384]{1,0:T(2,128)(2,1)}, u32[]{:S(2)}) copy-start(bf16[2,16384]{1,0:T(2,128)(2,1)} %old.3) | copy-start | bytes 196612
  3.6 1.7 %collective-permute-start.5 = (bf16[8,16384]{1,0:T(8,128)(2,1)S(1)}, bf16[8,16384]{1,0:T(8,128)(2,1)S(1)}, u32[]{:S(2)}, u32[]{:S(2)}) collective-permute-start(bf16[8,16384]{1,0:T(8,128)(2,1)S(1)} %get-tuple-element.43), channel_id=1, source_target_pairs={{0,1},{1,0},{2,3},{3,2},{4,5},{5,4},{6,7},{7,6},{8,9},{9,8},{10,11... | collective-permute-start | bytes 786440 | tf_op jit(solution)/shard_map/ppermute | solution.py:222
  4.2 18.0 %copy-start.1 = (f32[16384]{0:T(1024)S(1)}, f32[16384]{0:T(1024)}, u32[]{:S(2)}) copy-start(f32[16384]{0:T(1024)} %param.12) | copy-start | bytes 196612
  4.2 29.2 %copy-start = (bf16[16384,128]{1,0:T(8,128)(2,1)S(1)}, bf16[16384,128]{1,0:T(8,128)(2,1)}, u32[]{:S(2)}) copy-start(bf16[16384,128]{1,0:T(8,128)(2,1)} %weight.5) | copy-start | bytes 12582916
  4.2 5.9 %collective-permute-start = (bf16[8,16384]{1,0:T(8,128)(2,1)S(1)}, bf16[8,16384]{1,0:T(8,128)(2,1)S(1)}, u32[]{:S(2)}, u32[]{:S(2)}) collective-permute-start(bf16[8,16384]{1,0:T(8,128)(2,1)S(1)} %get-tuple-element.44), channel_id=1, source_target_pairs={{0,1},{1,0},{2,3},{3,2},{4,5},{5,4},{6,7},{7,6},{8,9},{9,8},{10,11... | collective-permute-start | bytes 786440 | tf_op jit(solution)/shard_map/ppermute | solution.py:222
  5.4 8.1 %collective-permute-start.6 = (bf16[2,16384]{1,0:T(2,128)(2,1)S(1)}, bf16[2,16384]{1,0:T(2,128)(2,1)S(1)}, u32[]{:S(2)}, u32[]{:S(2)}) collective-permute-start(bf16[2,16384]{1,0:T(2,128)(2,1)S(1)} %get-tuple-element.32), channel_id=1, source_target_pairs={{0,6},{1,7},{2,4},{3,5},{4,2},{5,3},{6,0},{7,1},{8,14},{9,15},{10,... | collective-permute-start | bytes 196616 | tf_op jit(solution)/shard_map/ppermute | solution.py:222
  9.4 4.4 %collective-permute-start.7 = (bf16[2,16384]{1,0:T(2,128)(2,1)S(1)}, bf16[2,16384]{1,0:T(2,128)(2,1)S(1)}, u32[]{:S(2)}, u32[]{:S(2)}) collective-permute-start(bf16[2,16384]{1,0:T(2,128)(2,1)S(1)} %get-tuple-element.33), channel_id=1, source_target_pairs={{0,2},{1,3},{2,0},{3,1},{4,6},{5,7},{6,4},{7,5},{8,10},{9,11},{10,... | collective-permute-start | bytes 196616 | tf_op jit(solution)/shard_map/ppermute | solution.py:222
  9.9 4.9 %collective-permute-start.8 = (bf16[2,16384]{1,0:T(2,128)(2,1)S(1)}, bf16[2,16384]{1,0:T(2,128)(2,1)S(1)}, u32[]{:S(2)}, u32[]{:S(2)}) collective-permute-start(bf16[2,16384]{1,0:T(2,128)(2,1)S(1)} %get-tuple-element.34), channel_id=1, source_target_pairs={{0,4},{1,5},{2,6},{3,7},{4,0},{5,1},{6,2},{7,3},{8,12},{9,13},{10,... | collective-permute-start | bytes 196616 | tf_op jit(solution)/shard_map/ppermute | solution.py:222
  10.1 7.5 %collective-permute-start.1 = (bf16[2,16384]{1,0:T(2,128)(2,1)S(1)}, bf16[2,16384]{1,0:T(2,128)(2,1)S(1)}, u32[]{:S(2)}, u32[]{:S(2)}) collective-permute-start(bf16[2,16384]{1,0:T(2,128)(2,1)S(1)} %get-tuple-element.26), channel_id=1, source_target_pairs={{0,6},{1,7},{2,4},{3,5},{4,2},{5,3},{6,0},{7,1},{8,14},{9,15},{10,... | collective-permute-start | bytes 196616 | tf_op jit(solution)/shard_map/ppermute | solution.py:222
  13.1 4.6 %collective-permute-start.2 = (bf16[2,16384]{1,0:T(2,128)(2,1)S(1)}, bf16[2,16384]{1,0:T(2,128)(2,1)S(1)}, u32[]{:S(2)}, u32[]{:S(2)}) collective-permute-start(bf16[2,16384]{1,0:T(2,128)(2,1)S(1)} %get-tuple-element.27), channel_id=1, source_target_pairs={{0,2},{1,3},{2,0},{3,1},{4,6},{5,7},{6,4},{7,5},{8,10},{9,11},{10,... | collective-permute-start | bytes 196616 | tf_op jit(solution)/shard_map/ppermute | solution.py:222
  13.6 4.3 %collective-permute-start.3 = (bf16[2,16384]{1,0:T(2,128)(2,1)S(1)}, bf16[2,16384]{1,0:T(2,128)(2,1)S(1)}, u32[]{:S(2)}, u32[]{:S(2)}) collective-permute-start(bf16[2,16384]{1,0:T(2,128)(2,1)S(1)} %get-tuple-element.28), channel_id=1, source_target_pairs={{0,4},{1,5},{2,6},{3,7},{4,0},{5,1},{6,2},{7,3},{8,12},{9,13},{10,... | collective-permute-start | bytes 196616 | tf_op jit(solution)/shard_map/ppermute | solution.py:222
  15.0 7.1 %collective-permute-start.9 = (bf16[2,16384]{1,0:T(2,128)(2,1)S(1)}, bf16[2,16384]{1,0:T(2,128)(2,1)S(1)}, u32[]{:S(2)}, u32[]{:S(2)}) collective-permute-start(bf16[2,16384]{1,0:T(2,128)(2,1)S(1)} %get-tuple-element.36), channel_id=1, source_target_pairs={{0,8},{1,9},{2,10},{3,11},{4,12},{5,13},{6,14},{7,15},{8,0},{9,1},... | collective-permute-start | bytes 196616 | tf_op jit(solution)/shard_map/ppermute | solution.py:222
  18.0 8.1 %collective-permute-start.4 = (bf16[2,16384]{1,0:T(2,128)(2,1)S(1)}, bf16[2,16384]{1,0:T(2,128)(2,1)S(1)}, u32[]{:S(2)}, u32[]{:S(2)}) collective-permute-start(bf16[2,16384]{1,0:T(2,128)(2,1)S(1)} %get-tuple-element.30), channel_id=1, source_target_pairs={{0,8},{1,9},{2,10},{3,11},{4,12},{5,13},{6,14},{7,15},{8,0},{9,1},... | collective-permute-start | bytes 196616 | tf_op jit(solution)/shard_map/ppermute | solution.py:222
  22.5 6.0 %collective-permute-start.16 = (bf16[2,16384]{1,0:T(2,128)(2,1)S(1)}, bf16[2,16384]{1,0:T(2,128)(2,1)S(1)}, u32[]{:S(2)}, u32[]{:S(2)}) collective-permute-start(bf16[2,16384]{1,0:T(2,128)(2,1)S(1)} %get-tuple-element.42), channel_id=1, source_target_pairs={{0,6},{1,7},{2,4},{3,5},{4,2},{5,3},{6,0},{7,1},{8,14},{9,15},{10,... | collective-permute-start | bytes 196616 | tf_op jit(solution)/shard_map/ppermute | solution.py:222
  23.8 6.8 %collective-permute-start.15 = (bf16[2,16384]{1,0:T(2,128)(2,1)S(1)}, bf16[2,16384]{1,0:T(2,128)(2,1)S(1)}, u32[]{:S(2)}, u32[]{:S(2)}) collective-permute-start(bf16[2,16384]{1,0:T(2,128)(2,1)S(1)} %get-tuple-element.42), channel_id=1, source_target_pairs={{0,2},{1,3},{2,0},{3,1},{4,6},{5,7},{6,4},{7,5},{8,10},{9,11},{10,... | collective-permute-start | bytes 196616 | tf_op jit(solution)/shard_map/ppermute | solution.py:222
  24.0 6.6 %collective-permute-start.14 = (bf16[2,16384]{1,0:T(2,128)(2,1)S(1)}, bf16[2,16384]{1,0:T(2,128)(2,1)S(1)}, u32[]{:S(2)}, u32[]{:S(2)}) collective-permute-start(bf16[2,16384]{1,0:T(2,128)(2,1)S(1)} %get-tuple-element.42), channel_id=1, source_target_pairs={{0,4},{1,5},{2,6},{3,7},{4,0},{5,1},{6,2},{7,3},{8,12},{9,13},{10,... | collective-permute-start | bytes 196616 | tf_op jit(solution)/shard_map/ppermute | solution.py:222
  27.1 5.2 %collective-permute-start.12 = (bf16[2,16384]{1,0:T(2,128)(2,1)S(1)}, bf16[2,16384]{1,0:T(2,128)(2,1)S(1)}, u32[]{:S(2)}, u32[]{:S(2)}) collective-permute-start(bf16[2,16384]{1,0:T(2,128)(2,1)S(1)} %get-tuple-element.41), channel_id=1, source_target_pairs={{0,6},{1,7},{2,4},{3,5},{4,2},{5,3},{6,0},{7,1},{8,14},{9,15},{10,... | collective-permute-start | bytes 196616 | tf_op jit(solution)/shard_map/ppermute | solution.py:222
  28.3 4.7 %collective-permute-start.11 = (bf16[2,16384]{1,0:T(2,128)(2,1)S(1)}, bf16[2,16384]{1,0:T(2,128)(2,1)S(1)}, u32[]{:S(2)}, u32[]{:S(2)}) collective-permute-start(bf16[2,16384]{1,0:T(2,128)(2,1)S(1)} %get-tuple-element.41), channel_id=1, source_target_pairs={{0,2},{1,3},{2,0},{3,1},{4,6},{5,7},{6,4},{7,5},{8,10},{9,11},{10,... | collective-permute-start | bytes 196616 | tf_op jit(solution)/shard_map/ppermute | solution.py:222
  28.6 4.4 %collective-permute-start.10 = (bf16[2,16384]{1,0:T(2,128)(2,1)S(1)}, bf16[2,16384]{1,0:T(2,128)(2,1)S(1)}, u32[]{:S(2)}, u32[]{:S(2)}) collective-permute-start(bf16[2,16384]{1,0:T(2,128)(2,1)S(1)} %get-tuple-element.41), channel_id=1, source_target_pairs={{0,4},{1,5},{2,6},{3,7},{4,0},{5,1},{6,2},{7,3},{8,12},{9,13},{10,... | collective-permute-start | bytes 196616 | tf_op jit(solution)/shard_map/ppermute | solution.py:222
  30.9 2.5 %collective-permute-start.17 = (bf16[8,16384]{1,0:T(8,128)(2,1)S(1)}, bf16[8,16384]{1,0:T(8,128)(2,1)S(1)}, u32[]{:S(2)}, u32[]{:S(2)}) collective-permute-start(bf16[8,16384]{1,0:T(8,128)(2,1)S(1)} %pad_maximum_fusion.1.early), channel_id=1, source_target_pairs={{0,1},{1,0},{2,3},{3,2},{4,5},{5,4},{6,7},{7,6},{8,9},{9,8},{10,11... | collective-permute-start | bytes 786440 | tf_op jit(solution)/shard_map/ppermute | solution.py:222
  33.3 1.6 %collective-permute-start.13 = (bf16[8,16384]{1,0:T(8,128)(2,1)S(1)}, bf16[8,16384]{1,0:T(8,128)(2,1)S(1)}, u32[]{:S(2)}, u32[]{:S(2)}) collective-permute-start(bf16[8,16384]{1,0:T(8,128)(2,1)S(1)} %pad_maximum_fusion.near), channel_id=1, source_target_pairs={{0,1},{1,0},{2,3},{3,2},{4,5},{5,4},{6,7},{7,6},{8,9},{9,8},{10,11... | collective-permute-start | bytes 786440 | tf_op jit(solution)/shard_map/ppermute | solution.py:222

commit v13 on v12

--- a/solution.py
+++ b/solution.py
@@ -174,13 +174,24 @@
     return total
 
 
-def first_dots_kernel(early, early_other, near, weight, out):
-    out[...] = times([early, early_other, near], weight)
-
-
-def last_dot_kernel(n, rows, before, weight, out):
+def first_dots_kernel(*refs):
+    *rows, weight, codes, scales, out, codes_out, scales_out, sems = refs
+    copies = [
+        pltpu.make_async_copy(codes, codes_out, sems.at[0]),
+        pltpu.make_async_copy(scales, scales_out, sems.at[1]),
+    ]
+    for copy in copies:
+        copy.start()
+    out[...] = times(rows, weight)
+    for copy in copies:
+        copy.wait()
+
+
+def last_dot_kernel(n, *refs):
+    *rows, before, weight, out = refs
     device = lax.axis_index("tp")
-    tokens, quarter = out.shape[0], rows.shape[0]
+    tokens = out.shape[0]
+    quarter = tokens // 4
     token = lax.broadcasted_iota(jnp.int32, (tokens, quarter), 0)
     row = lax.broadcasted_iota(jnp.int32, (tokens, quarter), 1) ^ (3 * quarter // 4)
     total = jnp.zeros(out.shape, F32)
@@ -188,7 +199,7 @@
         (0, before[:quarter]),
         (2 * quarter, before[quarter : 2 * quarter]),
         (quarter, before[2 * quarter :]),
-        (3 * quarter, times([rows], weight)),
+        (3 * quarter, times(rows, weight)),
     ):
         pick = (owner_token(row + start, device, n) == token).astype(F32).astype(BF16)
         total += jnp.dot(pick, values.astype(BF16), preferred_element_type=F32)
@@ -197,11 +208,15 @@
 
 def local_call(kernel, shapes, name, *operands, scratch=()):
     spec = pl.BlockSpec(memory_space=pltpu.VMEM)
+    spaces = [space[0] if space else pltpu.VMEM for _, _, *space in shapes]
     return pl.pallas_call(
         kernel,
-        out_shape=[jax.ShapeDtypeStruct(shape, dtype) for shape, dtype in shapes],
+        out_shape=[
+            (space[0] if space else jax.ShapeDtypeStruct)(shape, dtype)
+            for shape, dtype, *space in shapes
+        ],
         in_specs=[spec] * len(operands),
-        out_specs=[spec] * len(shapes),
+        out_specs=[pl.BlockSpec(memory_space=space) for space in spaces],
         scratch_shapes=list(scratch),
         compiler_params=pltpu.CompilerParams(vmem_limit_bytes=SMALL_LIMIT),
         cost_estimate=pl.CostEstimate(
@@ -248,14 +263,13 @@
     def gather(held):
         for level in levels[-2::-1]:
             held = jnp.concatenate([held, swap(held, level)], axis=0)
-        arrived = [swap(held, distance) for distance in square]
-        return jnp.concatenate(arrived[::-1] + [held], axis=0)
+        return [swap(held, distance) for distance in square][::-1] + [held]
 
     sums = [reduce(which) for which in range(2)]
     sums = [(total, swap(turned, levels[-1])) for total, turned in sums]
     outs, held = [], []
     for which in range(2):
-        shapes = [(pair, BF16), (pair, BF16), ((2, D // QB), F32)]
+        shapes = [(pair, BF16), (pair, BF16, pltpu.VMEM), ((2, D // QB), F32, pltpu.VMEM)]
         normed, *outs = local_call(
             encode_kernel,
             shapes,
@@ -266,15 +280,20 @@
             scratch=[pltpu.VMEM(pair, F32)],
         )
         held.append(gather(normed))
-    others = [swap(rows, 1) for rows in held]
+    early, near = (jnp.concatenate(pieces, axis=0) for pieces in held)
+    early_other, near_other = swap(early, 1), swap(near, 1)
     width = q_weight.shape[1]
-    shapes = [((3 * quarter, width), F32)]
-    (before,) = local_call(
-        first_dots_kernel, shapes, "first_dots", held[0], others[0], held[1], q_weight
+    shapes = [((3 * quarter, width), F32)] + [(x.shape, x.dtype, pltpu.HBM) for x in outs]
+    before, *outs = local_call(
+        first_dots_kernel,
+        shapes,
+        "first_dots",
+        *(early, early_other, near, q_weight, *outs),
+        scratch=[pltpu.SemaphoreType.DMA((2,))],
     )
     kernel = functools.partial(last_dot_kernel, n)
     shapes = [((tokens, width), BF16)]
-    (next_queries,) = local_call(kernel, shapes, "last_dot", others[1], before, q_weight)
+    (next_queries,) = local_call(kernel, shapes, "last_dot", near_other, before, q_weight)
     return (*outs, next_queries)
 
 

time: 36.4 us -> 36.3 us (level)
  no operation moved by 1% of the time
where the time goes in v13:
time: 36.3 us; the launch traced here: 36.2 us
  starting transfers between devices  21.4 us (59%)
  Pallas kernels  6.35 us (17%)
  waiting for transfers between devices  5.77 us (16%)
  matrix products  1.31 us (4%)
  between operations  0.74 us (2%)
  other arithmetic  0.6 us (2%)
    ppermute x18, starting transfers between devices, swap(): return lax.ppermute(x, 'tp', [(i, i ^ distance) for i in range(n)])  21.4 us
    ppermute x18, waiting for transfers between devices, swap(): return lax.ppermute(x, 'tp', [(i, i ^ distance) for i in range(n)])  5.77 us
    pallas_call x8, Pallas kernels, local_call(): pl.pallas_call(kernel, out_shape=[(space[0] if space else jax.ShapeDtypeS...  4.07 us
    pallas_call x1, Pallas kernels, attend(): pl.pallas_call(functools.partial(attend_kernel, n), out_shape=[jax.ShapeD...  2.28 us
  transfers between devices with their start and end apart: 18, of which 7 were waited for; matrix products, arithmetic and copies ran while one was open for 3% of the time, Pallas kernels for 7%

profile of v13, /device:TPU:0, one launch (start us, length us, event | category | flops | bytes accessed | tf_op | source)
XLA Modules:
  0.0 36.2 jit_solution(6636311176649680596)
XLA Ops:
  0.6 2.3 %attend.1 = (bf16[32,128]{1,0:T(8,128)(2,1)S(1)}, bf16[128,16384]{1,0:T(8,128)(2,1)S(1)}) custom-call(bf16[32,128]{1,0:T(8,128)(2,1)} %queries.1, bf16[32,1024]{1,0:T(8,128)(2,1)} %keys.1, bf16[32,1024]{1,0:T(8,128)(2,1)} %values.1, bf16[128,16384]{1,0:T(8,128)(2,1)} %weight.1), custom_call_target="tpu_custom_call" | custom-call | bytes 4194304 | tf_op jit(solution)/shard_map/attend/pallas_call | solution.py:86
  2.9 0.7 %convolution_convert_fusion = bf16[16,16384]{1,0:T(8,128)(2,1)S(1)} fusion(bf16[128,16384]{1,0:T(8,128)(2,1)S(1)} %get-tuple-element.27, bf16[32,128]{1,0:T(8,128)(2,1)S(1)} %get-tuple-element.26), kind=kOutput, calls=%fused_computation | convolution fusion | flops 67371008 | bytes 4722688 | tf_op jit(solution)/shard_map/dot_general | solution.py:243
  3.6 0.0 copy-start.2
  3.6 0.5 %collective-permute-start.9 = (bf16[8,16384]{1,0:T(8,128)(2,1)S(1)}, bf16[8,16384]{1,0:T(8,128)(2,1)S(1)}, u32[]{:S(2)}, u32[]{:S(2)}) collective-permute-start(bf16[8,16384]{1,0:T(8,128)(2,1)S(1)} %get-tuple-element.49), channel_id=1, source_target_pairs={{0,1},{1,0},{2,3},{3,2},{4,5},{5,4},{6,7},{7,6},{8,9},{9,8},{10,11... | collective-permute-start | bytes 786440 | tf_op jit(solution)/shard_map/ppermute | solution.py:237
  4.2 0.0 copy-start.1
  4.2 0.0 copy-start
  4.2 0.1 collective-permute-start
  4.3 0.7 %fusion.1.kept = f32[16,16384]{1,0:T(8,128)S(1)} fusion(bf16[128,16384]{1,0:T(8,128)(2,1)S(1)} %get-tuple-element.27, bf16[32,128]{1,0:T(8,128)(2,1)S(1)} %get-tuple-element.26), kind=kOutput, calls=%fused_computation.4 | convolution fusion | flops 67108864 | bytes 5246976 | tf_op jit(solution)/shard_map/dot_general | solution.py:245
  4.9 0.8 %collective-permute-done.got = bf16[8,16384]{1,0:T(8,128)(2,1)S(1)} collective-permute-done((bf16[8,16384]{1,0:T(8,128)(2,1)S(1)}, bf16[8,16384]{1,0:T(8,128)(2,1)S(1)}, u32[]{:S(2)}, u32[]{:S(2)}) %collective-permute-start) | collective-permute-done | bytes 262176 | tf_op jit(solution)/shard_map/ppermute | solution.py:237
  5.7 0.1 split0.1
  5.8 4.0 %collective-permute-start.1 = (bf16[2,16384]{1,0:T(2,128)(2,1)S(1)}, bf16[2,16384]{1,0:T(2,128)(2,1)S(1)}, u32[]{:S(2)}, u32[]{:S(2)}) collective-permute-start(bf16[2,16384]{1,0:T(2,128)(2,1)S(1)} %get-tuple-element.29), channel_id=1, source_target_pairs={{0,6},{1,7},{2,4},{3,5},{4,2},{5,3},{6,0},{7,1},{8,14},{9,15},{10,... | collective-permute-start | bytes 196616 | tf_op jit(solution)/shard_map/ppermute | solution.py:237
  9.8 0.5 %collective-permute-start.2 = (bf16[2,16384]{1,0:T(2,128)(2,1)S(1)}, bf16[2,16384]{1,0:T(2,128)(2,1)S(1)}, u32[]{:S(2)}, u32[]{:S(2)}) collective-permute-start(bf16[2,16384]{1,0:T(2,128)(2,1)S(1)} %get-tuple-element.30), channel_id=1, source_target_pairs={{0,2},{1,3},{2,0},{3,1},{4,6},{5,7},{6,4},{7,5},{8,10},{9,11},{10,... | collective-permute-start | bytes 196616 | tf_op jit(solution)/shard_map/ppermute | solution.py:237
  10.3 0.1 collective-permute-start.3
  10.4 0.0 collective-permute-done.9.got
  10.4 0.1 split1.1
  10.5 2.9 %collective-permute-start.10 = (bf16[2,16384]{1,0:T(2,128)(2,1)S(1)}, bf16[2,16384]{1,0:T(2,128)(2,1)S(1)}, u32[]{:S(2)}, u32[]{:S(2)}) collective-permute-start(bf16[2,16384]{1,0:T(2,128)(2,1)S(1)} %get-tuple-element.36), channel_id=1, source_target_pairs={{0,6},{1,7},{2,4},{3,5},{4,2},{5,3},{6,0},{7,1},{8,14},{9,15},{10,... | collective-permute-start | bytes 196616 | tf_op jit(solution)/shard_map/ppermute | solution.py:237
  13.4 0.5 %collective-permute-start.11 = (bf16[2,16384]{1,0:T(2,128)(2,1)S(1)}, bf16[2,16384]{1,0:T(2,128)(2,1)S(1)}, u32[]{:S(2)}, u32[]{:S(2)}) collective-permute-start(bf16[2,16384]{1,0:T(2,128)(2,1)S(1)} %get-tuple-element.37), channel_id=1, source_target_pairs={{0,2},{1,3},{2,0},{3,1},{4,6},{5,7},{6,4},{7,5},{8,10},{9,11},{10,... | collective-permute-start | bytes 196616 | tf_op jit(solution)/shard_map/ppermute | solution.py:237
  13.9 0.0 collective-permute-done.1.refs_0_
  13.9 0.2 collective-permute-start.12
  14.1 0.0 collective-permute-done.2.refs_1_
  14.1 1.0 %collective-permute-done.3.refs_2_ = bf16[2,16384]{1,0:T(2,128)(2,1)S(1)} collective-permute-done((bf16[2,16384]{1,0:T(2,128)(2,1)S(1)}, bf16[2,16384]{1,0:T(2,128)(2,1)S(1)}, u32[]{:S(2)}, u32[]{:S(2)}) %collective-permute-start.3) | collective-permute-done | bytes 65568 | tf_op jit(solution)/shard_map/ppermute | solution.py:237
  15.2 0.0 copy-done.2
  15.2 0.2 settle0.1
  15.4 2.6 %collective-permute-start.4 = (bf16[2,16384]{1,0:T(2,128)(2,1)S(1)}, bf16[2,16384]{1,0:T(2,128)(2,1)S(1)}, u32[]{:S(2)}, u32[]{:S(2)}) collective-permute-start(bf16[2,16384]{1,0:T(2,128)(2,1)S(1)} %get-tuple-element.33), channel_id=1, source_target_pairs={{0,8},{1,9},{2,10},{3,11},{4,12},{5,13},{6,14},{7,15},{8,0},{9,1},... | collective-permute-start | bytes 196616 | tf_op jit(solution)/shard_map/ppermute | solution.py:237
  18.0 0.0 collective-permute-done.10.refs_0_
  18.0 0.0 collective-permute-done.11.refs_1_
  18.0 0.2 collective-permute-done.12.refs_2_
  18.2 0.2 settle1.1
  18.4 2.7 %collective-permute-start.13 = (bf16[2,16384]{1,0:T(2,128)(2,1)S(1)}, bf16[2,16384]{1,0:T(2,128)(2,1)S(1)}, u32[]{:S(2)}, u32[]{:S(2)}) collective-permute-start(bf16[2,16384]{1,0:T(2,128)(2,1)S(1)} %get-tuple-element.40), channel_id=1, source_target_pairs={{0,8},{1,9},{2,10},{3,11},{4,12},{5,13},{6,14},{7,15},{8,0},{9,1},... | collective-permute-start | bytes 196616 | tf_op jit(solution)/shard_map/ppermute | solution.py:237
  21.0 1.4 %collective-permute-done.4.arrived = bf16[2,16384]{1,0:T(2,128)(2,1)S(1)} collective-permute-done((bf16[2,16384]{1,0:T(2,128)(2,1)S(1)}, bf16[2,16384]{1,0:T(2,128)(2,1)S(1)}, u32[]{:S(2)}, u32[]{:S(2)}) %collective-permute-start.4) | collective-permute-done | bytes 65568 | tf_op jit(solution)/shard_map/ppermute | solution.py:237
  22.5 0.0 copy-done.1
  22.5 0.4 %encode0.1 = (bf16[2,16384]{1,0:T(2,128)(2,1)S(1)}, bf16[2,16384]{1,0:T(2,128)(2,1)S(1)}, f32[2,128]{1,0:T(2,128)S(1)}) custom-call(f32[2,16384]{1,0:T(2,128)S(1)} %get-tuple-element.32.total, bf16[2,16384]{1,0:T(2,128)(2,1)S(1)} %collective-permute-done.4.arrived, f32[1,16384]{1,0:T(1,128)S(1)} %bitcast.3), custom_call_target="tpu_custom_call" | custom-call | bytes 163840 | tf_op jit(solution)/shard_map/encode0/pallas_call | solution.py:212
  22.9 1.2 %collective-permute-start.7 = (bf16[2,16384]{1,0:T(2,128)(2,1)S(1)}, bf16[2,16384]{1,0:T(2,128)(2,1)S(1)}, u32[]{:S(2)}, u32[]{:S(2)}) collective-permute-start(bf16[2,16384]{1,0:T(2,128)(2,1)S(1)} %get-tuple-element.34), channel_id=1, source_target_pairs={{0,6},{1,7},{2,4},{3,5},{4,2},{5,3},{6,0},{7,1},{8,14},{9,15},{10,... | collective-permute-start | bytes 196616 | tf_op jit(solution)/shard_map/ppermute | solution.py:237
  24.1 0.2 collective-permute-start.6
  24.4 2.1 %collective-permute-start.5 = (bf16[2,16384]{1,0:T(2,128)(2,1)S(1)}, bf16[2,16384]{1,0:T(2,128)(2,1)S(1)}, u32[]{:S(2)}, u32[]{:S(2)}) collective-permute-start(bf16[2,16384]{1,0:T(2,128)(2,1)S(1)} %get-tuple-element.34), channel_id=1, source_target_pairs={{0,4},{1,5},{2,6},{3,7},{4,0},{5,1},{6,2},{7,3},{8,12},{9,13},{10,... | collective-permute-start | bytes 196616 | tf_op jit(solution)/shard_map/ppermute | solution.py:237
  26.5 0.0 collective-permute-done.13.arrived
  26.5 0.5 %encode1.1 = (bf16[2,16384]{1,0:T(2,128)(2,1)S(1)}, bf16[2,16384]{1,0:T(2,128)(2,1)S(1)}, f32[2,128]{1,0:T(2,128)S(1)}) custom-call(f32[2,16384]{1,0:T(2,128)S(1)} %get-tuple-element.39.total, bf16[2,16384]{1,0:T(2,128)(2,1)S(1)} %collective-permute-done.13.arrived, f32[1,16384]{1,0:T(1,128)S(1)} %bitcast.4, bf16[2,16384]{1,0:T(2,128)(2,1)S(1)} %get-tuple-element.41.refs_0_, ...), custom_call_target="tpu_custom_call" | custom-call | bytes 229888 | tf_op jit(solution)/shard_map/encode1/pallas_call | solution.py:212
  27.0 1.2 %collective-permute-start.16 = (bf16[2,16384]{1,0:T(2,128)(2,1)S(1)}, bf16[2,16384]{1,0:T(2,128)(2,1)S(1)}, u32[]{:S(2)}, u32[]{:S(2)}) collective-permute-start(bf16[2,16384]{1,0:T(2,128)(2,1)S(1)} %get-tuple-element.43), channel_id=1, source_target_pairs={{0,6},{1,7},{2,4},{3,5},{4,2},{5,3},{6,0},{7,1},{8,14},{9,15},{10,... | collective-permute-start | bytes 196616 | tf_op jit(solution)/shard_map/ppermute | solution.py:237
  28.2 0.3 collective-permute-start.15
  28.5 0.0 collective-permute-done.7
  28.5 2.0 %collective-permute-start.14 = (bf16[2,16384]{1,0:T(2,128)(2,1)S(1)}, bf16[2,16384]{1,0:T(2,128)(2,1)S(1)}, u32[]{:S(2)}, u32[]{:S(2)}) collective-permute-start(bf16[2,16384]{1,0:T(2,128)(2,1)S(1)} %get-tuple-element.43), channel_id=1, source_target_pairs={{0,4},{1,5},{2,6},{3,7},{4,0},{5,1},{6,2},{7,3},{8,12},{9,13},{10,... | collective-permute-start | bytes 196616 | tf_op jit(solution)/shard_map/ppermute | solution.py:237
  30.5 0.0 collective-permute-done.6
  30.5 0.0 collective-permute-done.5
  30.5 0.3 pad_maximum_fusion.refs_0_
  30.8 0.1 collective-permute-start.8
  30.9 1.3 %collective-permute-done.16 = bf16[2,16384]{1,0:T(2,128)(2,1)S(1)} collective-permute-done((bf16[2,16384]{1,0:T(2,128)(2,1)S(1)}, bf16[2,16384]{1,0:T(2,128)(2,1)S(1)}, u32[]{:S(2)}, u32[]{:S(2)}) %collective-permute-start.16) | collective-permute-done | bytes 65568 | tf_op jit(solution)/shard_map/ppermute | solution.py:237
  32.2 0.7 %collective-permute-done.15 = bf16[2,16384]{1,0:T(2,128)(2,1)S(1)} collective-permute-done((bf16[2,16384]{1,0:T(2,128)(2,1)S(1)}, bf16[2,16384]{1,0:T(2,128)(2,1)S(1)}, u32[]{:S(2)}, u32[]{:S(2)}) %collective-permute-start.15) | collective-permute-done | bytes 65568 | tf_op jit(solution)/shard_map/ppermute | solution.py:237
  32.9 0.0 collective-permute-done.14
  32.9 0.3 pad_maximum_fusion.1.refs_2_
  33.2 0.1 collective-permute-start.17
  33.3 0.0 collective-permute-done.8.refs_1_
  33.3 0.0 copy-done
  33.3 1.2 %first_dots.1 = (f32[24,128]{1,0:T(8,128)S(1)}, bf16[2,16384]{1,0:T(2,128)(2,1)}, f32[2,128]{1,0:T(2,128)}) custom-call(bf16[8,16384]{1,0:T(8,128)(2,1)S(1)} %pad_maximum_fusion.refs_0_, bf16[8,16384]{1,0:T(8,128)(2,1)S(1)} %collective-permute-done.8.refs_1_, bf16[8,16384]{1,0:T(8,128)(2,1)S(1)} %pad_maximum_fusion.1.refs_2_, ...), custom_call_target="tpu_custom_call" | custom-call | bytes 5046784 | tf_op jit(solution)/shard_map/first_dots/pallas_call | solution.py:212
  34.5 0.3 collective-permute-done.17.refs_0_
  34.8 1.4 %last_dot.1 = bf16[32,128]{1,0:T(8,128)(2,1)} custom-call(bf16[8,16384]{1,0:T(8,128)(2,1)S(1)} %collective-permute-done.17.refs_0_, f32[24,128]{1,0:T(8,128)S(1)} %get-tuple-element.48.refs_1_, bf16[16384,128]{1,0:T(8,128)(2,1)S(1)} %copy-done), custom_call_target="tpu_custom_call" | custom-call | bytes 4462592 | tf_op jit(solution)/shard_map/last_dot/pallas_call | solution.py:212
  (1 shorter events, 0.0 us)
Async XLA Ops:
  3.6 11.5 %copy-start.2 = (bf16[2,16384]{1,0:T(2,128)(2,1)S(1)}, bf16[2,16384]{1,0:T(2,128)(2,1)}, u32[]{:S(2)}) copy-start(bf16[2,16384]{1,0:T(2,128)(2,1)} %old.3) | copy-start | bytes 196612
  3.6 6.8 %collective-permute-start.9 = (bf16[8,16384]{1,0:T(8,128)(2,1)S(1)}, bf16[8,16384]{1,0:T(8,128)(2,1)S(1)}, u32[]{:S(2)}, u32[]{:S(2)}) collective-permute-start(bf16[8,16384]{1,0:T(8,128)(2,1)S(1)} %get-tuple-element.49), channel_id=1, source_target_pairs={{0,1},{1,0},{2,3},{3,2},{4,5},{5,4},{6,7},{7,6},{8,9},{9,8},{10,11... | collective-permute-start | bytes 786440 | tf_op jit(solution)/shard_map/ppermute | solution.py:237
  4.2 18.3 %copy-start.1 = (f32[16384]{0:T(1024)S(1)}, f32[16384]{0:T(1024)}, u32[]{:S(2)}) copy-start(f32[16384]{0:T(1024)} %param.12) | copy-start | bytes 196612
  4.2 29.1 %copy-start = (bf16[16384,128]{1,0:T(8,128)(2,1)S(1)}, bf16[16384,128]{1,0:T(8,128)(2,1)}, u32[]{:S(2)}) copy-start(bf16[16384,128]{1,0:T(8,128)(2,1)} %refs_2_.1) | copy-start | bytes 12582916
  4.2 1.5 %collective-permute-start = (bf16[8,16384]{1,0:T(8,128)(2,1)S(1)}, bf16[8,16384]{1,0:T(8,128)(2,1)S(1)}, u32[]{:S(2)}, u32[]{:S(2)}) collective-permute-start(bf16[8,16384]{1,0:T(8,128)(2,1)S(1)} %get-tuple-element.50), channel_id=1, source_target_pairs={{0,1},{1,0},{2,3},{3,2},{4,5},{5,4},{6,7},{7,6},{8,9},{9,8},{10,11... | collective-permute-start | bytes 786440 | tf_op jit(solution)/shard_map/ppermute | solution.py:237
  5.8 8.1 %collective-permute-start.1 = (bf16[2,16384]{1,0:T(2,128)(2,1)S(1)}, bf16[2,16384]{1,0:T(2,128)(2,1)S(1)}, u32[]{:S(2)}, u32[]{:S(2)}) collective-permute-start(bf16[2,16384]{1,0:T(2,128)(2,1)S(1)} %get-tuple-element.29), channel_id=1, source_target_pairs={{0,6},{1,7},{2,4},{3,5},{4,2},{5,3},{6,0},{7,1},{8,14},{9,15},{10,... | collective-permute-start | bytes 196616 | tf_op jit(solution)/shard_map/ppermute | solution.py:237
  9.8 4.4 %collective-permute-start.2 = (bf16[2,16384]{1,0:T(2,128)(2,1)S(1)}, bf16[2,16384]{1,0:T(2,128)(2,1)S(1)}, u32[]{:S(2)}, u32[]{:S(2)}) collective-permute-start(bf16[2,16384]{1,0:T(2,128)(2,1)S(1)} %get-tuple-element.30), channel_id=1, source_target_pairs={{0,2},{1,3},{2,0},{3,1},{4,6},{5,7},{6,4},{7,5},{8,10},{9,11},{10,... | collective-permute-start | bytes 196616 | tf_op jit(solution)/shard_map/ppermute | solution.py:237
  10.3 4.9 %collective-permute-start.3 = (bf16[2,16384]{1,0:T(2,128)(2,1)S(1)}, bf16[2,16384]{1,0:T(2,128)(2,1)S(1)}, u32[]{:S(2)}, u32[]{:S(2)}) collective-permute-start(bf16[2,16384]{1,0:T(2,128)(2,1)S(1)} %get-tuple-element.31), channel_id=1, source_target_pairs={{0,4},{1,5},{2,6},{3,7},{4,0},{5,1},{6,2},{7,3},{8,12},{9,13},{10,... | collective-permute-start | bytes 196616 | tf_op jit(solution)/shard_map/ppermute | solution.py:237
  10.5 7.5 %collective-permute-start.10 = (bf16[2,16384]{1,0:T(2,128)(2,1)S(1)}, bf16[2,16384]{1,0:T(2,128)(2,1)S(1)}, u32[]{:S(2)}, u32[]{:S(2)}) collective-permute-start(bf16[2,16384]{1,0:T(2,128)(2,1)S(1)} %get-tuple-element.36), channel_id=1, source_target_pairs={{0,6},{1,7},{2,4},{3,5},{4,2},{5,3},{6,0},{7,1},{8,14},{9,15},{10,... | collective-permute-start | bytes 196616 | tf_op jit(solution)/shard_map/ppermute | solution.py:237
  13.4 4.6 %collective-permute-start.11 = (bf16[2,16384]{1,0:T(2,128)(2,1)S(1)}, bf16[2,16384]{1,0:T(2,128)(2,1)S(1)}, u32[]{:S(2)}, u32[]{:S(2)}) collective-permute-start(bf16[2,16384]{1,0:T(2,128)(2,1)S(1)} %get-tuple-element.37), channel_id=1, source_target_pairs={{0,2},{1,3},{2,0},{3,1},{4,6},{5,7},{6,4},{7,5},{8,10},{9,11},{10,... | collective-permute-start | bytes 196616 | tf_op jit(solution)/shard_map/ppermute | solution.py:237
  13.9 4.3 %collective-permute-start.12 = (bf16[2,16384]{1,0:T(2,128)(2,1)S(1)}, bf16[2,16384]{1,0:T(2,128)(2,1)S(1)}, u32[]{:S(2)}, u32[]{:S(2)}) collective-permute-start(bf16[2,16384]{1,0:T(2,128)(2,1)S(1)} %get-tuple-element.38), channel_id=1, source_target_pairs={{0,4},{1,5},{2,6},{3,7},{4,0},{5,1},{6,2},{7,3},{8,12},{9,13},{10,... | collective-permute-start | bytes 196616 | tf_op jit(solution)/shard_map/ppermute | solution.py:237
  15.4 7.1 %collective-permute-start.4 = (bf16[2,16384]{1,0:T(2,128)(2,1)S(1)}, bf16[2,16384]{1,0:T(2,128)(2,1)S(1)}, u32[]{:S(2)}, u32[]{:S(2)}) collective-permute-start(bf16[2,16384]{1,0:T(2,128)(2,1)S(1)} %get-tuple-element.33), channel_id=1, source_target_pairs={{0,8},{1,9},{2,10},{3,11},{4,12},{5,13},{6,14},{7,15},{8,0},{9,1},... | collective-permute-start | bytes 196616 | tf_op jit(solution)/shard_map/ppermute | solution.py:237
  18.4 8.1 %collective-permute-start.13 = (bf16[2,16384]{1,0:T(2,128)(2,1)S(1)}, bf16[2,16384]{1,0:T(2,128)(2,1)S(1)}, u32[]{:S(2)}, u32[]{:S(2)}) collective-permute-start(bf16[2,16384]{1,0:T(2,128)(2,1)S(1)} %get-tuple-element.40), channel_id=1, source_target_pairs={{0,8},{1,9},{2,10},{3,11},{4,12},{5,13},{6,14},{7,15},{8,0},{9,1},... | collective-permute-start | bytes 196616 | tf_op jit(solution)/shard_map/ppermute | solution.py:237
  22.9 5.6 %collective-permute-start.7 = (bf16[2,16384]{1,0:T(2,128)(2,1)S(1)}, bf16[2,16384]{1,0:T(2,128)(2,1)S(1)}, u32[]{:S(2)}, u32[]{:S(2)}) collective-permute-start(bf16[2,16384]{1,0:T(2,128)(2,1)S(1)} %get-tuple-element.34), channel_id=1, source_target_pairs={{0,6},{1,7},{2,4},{3,5},{4,2},{5,3},{6,0},{7,1},{8,14},{9,15},{10,... | collective-permute-start | bytes 196616 | tf_op jit(solution)/shard_map/ppermute | solution.py:237
  24.1 6.4 %collective-permute-start.6 = (bf16[2,16384]{1,0:T(2,128)(2,1)S(1)}, bf16[2,16384]{1,0:T(2,128)(2,1)S(1)}, u32[]{:S(2)}, u32[]{:S(2)}) collective-permute-start(bf16[2,16384]{1,0:T(2,128)(2,1)S(1)} %get-tuple-element.34), channel_id=1, source_target_pairs={{0,2},{1,3},{2,0},{3,1},{4,6},{5,7},{6,4},{7,5},{8,10},{9,11},{10,... | collective-permute-start | bytes 196616 | tf_op jit(solution)/shard_map/ppermute | solution.py:237
  24.4 6.2 %collective-permute-start.5 = (bf16[2,16384]{1,0:T(2,128)(2,1)S(1)}, bf16[2,16384]{1,0:T(2,128)(2,1)S(1)}, u32[]{:S(2)}, u32[]{:S(2)}) collective-permute-start(bf16[2,16384]{1,0:T(2,128)(2,1)S(1)} %get-tuple-element.34), channel_id=1, source_target_pairs={{0,4},{1,5},{2,6},{3,7},{4,0},{5,1},{6,2},{7,3},{8,12},{9,13},{10,... | collective-permute-start | bytes 196616 | tf_op jit(solution)/shard_map/ppermute | solution.py:237
  27.0 5.3 %collective-permute-start.16 = (bf16[2,16384]{1,0:T(2,128)(2,1)S(1)}, bf16[2,16384]{1,0:T(2,128)(2,1)S(1)}, u32[]{:S(2)}, u32[]{:S(2)}) collective-permute-start(bf16[2,16384]{1,0:T(2,128)(2,1)S(1)} %get-tuple-element.43), channel_id=1, source_target_pairs={{0,6},{1,7},{2,4},{3,5},{4,2},{5,3},{6,0},{7,1},{8,14},{9,15},{10,... | collective-permute-start | bytes 196616 | tf_op jit(solution)/shard_map/ppermute | solution.py:237
  28.2 4.7 %collective-permute-start.15 = (bf16[2,16384]{1,0:T(2,128)(2,1)S(1)}, bf16[2,16384]{1,0:T(2,128)(2,1)S(1)}, u32[]{:S(2)}, u32[]{:S(2)}) collective-permute-start(bf16[2,16384]{1,0:T(2,128)(2,1)S(1)} %get-tuple-element.43), channel_id=1, source_target_pairs={{0,2},{1,3},{2,0},{3,1},{4,6},{5,7},{6,4},{7,5},{8,10},{9,11},{10,... | collective-permute-start | bytes 196616 | tf_op jit(solution)/shard_map/ppermute | solution.py:237
  28.5 4.4 %collective-permute-start.14 = (bf16[2,16384]{1,0:T(2,128)(2,1)S(1)}, bf16[2,16384]{1,0:T(2,128)(2,1)S(1)}, u32[]{:S(2)}, u32[]{:S(2)}) collective-permute-start(bf16[2,16384]{1,0:T(2,128)(2,1)S(1)} %get-tuple-element.43), channel_id=1, source_target_pairs={{0,4},{1,5},{2,6},{3,7},{4,0},{5,1},{6,2},{7,3},{8,12},{9,13},{10,... | collective-permute-start | bytes 196616 | tf_op jit(solution)/shard_map/ppermute | solution.py:237
  30.8 2.5 %collective-permute-start.8 = (bf16[8,16384]{1,0:T(8,128)(2,1)S(1)}, bf16[8,16384]{1,0:T(8,128)(2,1)S(1)}, u32[]{:S(2)}, u32[]{:S(2)}) collective-permute-start(bf16[8,16384]{1,0:T(8,128)(2,1)S(1)} %pad_maximum_fusion.refs_0_), channel_id=1, source_target_pairs={{0,1},{1,0},{2,3},{3,2},{4,5},{5,4},{6,7},{7,6},{8,9},{9,8},{10,11... | collective-permute-start | bytes 786440 | tf_op jit(solution)/shard_map/ppermute | solution.py:237
  33.2 1.6 %collective-permute-start.17 = (bf16[8,16384]{1,0:T(8,128)(2,1)S(1)}, bf16[8,16384]{1,0:T(8,128)(2,1)S(1)}, u32[]{:S(2)}, u32[]{:S(2)}) collective-permute-start(bf16[8,16384]{1,0:T(8,128)(2,1)S(1)} %pad_maximum_fusion.1.refs_2_), channel_id=1, source_target_pairs={{0,1},{1,0},{2,3},{3,2},{4,5},{5,4},{6,7},{7,6},{8,9},{9,8},{10,11... | collective-permute-start | bytes 786440 | tf_op jit(solution)/shard_map/ppermute | solution.py:237

commit v14 on v13

--- a/solution.py
+++ b/solution.py
@@ -134,7 +134,10 @@
 
 
 def encode_kernel(total, arrived, gain, *refs):
-    *before, normed, codes, scales, decoded = refs
+    if len(refs) > 4:
+        first, *before, normed, codes, scales, joint, decoded = refs
+    else:
+        before, (normed, codes, scales, decoded) = (), refs
     blocks = total.shape[1] // QB
     row = lax.broadcasted_iota(jnp.int32, (total.shape[0], QB), 0)
     lane = lax.broadcasted_iota(jnp.int32, (total.shape[0], blocks), 1)
@@ -160,7 +163,10 @@
     mean_sq = jnp.sum(squares, axis=1, keepdims=True) / total.shape[1]
     factor = lax.rsqrt(mean_sq + 1e-05)
     for at in parts(total):
-        normed[:, at] = (decoded[:, at] * factor * gain[:, at]).astype(BF16)
+        value = decoded[:, at] * factor * gain[:, at]
+        normed[:, at] = value.astype(BF16)
+        if before:
+            joint[:, at] = jnp.concatenate([first[:, at].astype(F32), value], axis=0).astype(BF16)
 
 
 def times(rows, weight):
@@ -187,21 +193,28 @@
         copy.wait()
 
 
-def last_dot_kernel(n, *refs):
+def last_dot_kernel(n, orders, *refs):
     *rows, before, weight, out = refs
     device = lax.axis_index("tp")
     tokens = out.shape[0]
-    quarter = tokens // 4
-    token = lax.broadcasted_iota(jnp.int32, (tokens, quarter), 0)
-    row = lax.broadcasted_iota(jnp.int32, (tokens, quarter), 1) ^ (3 * quarter // 4)
+    part = tokens // 16
     total = jnp.zeros(out.shape, F32)
-    for start, values in (
-        (0, before[:quarter]),
-        (2 * quarter, before[quarter : 2 * quarter]),
-        (quarter, before[2 * quarter :]),
-        (3 * quarter, times(rows, weight)),
-    ):
-        pick = (owner_token(row + start, device, n) == token).astype(F32).astype(BF16)
+    groups = [(0, 0), (1, 0), (0, 1), (1, 1)]
+    start = 0
+    for side, order in groups:
+        count = len(orders[order]) * part
+        if (side, order) == groups[-1]:
+            values = times(rows, weight)
+        else:
+            values = before[start : start + count]
+            start += count
+        at = lax.broadcasted_iota(jnp.int32, (tokens, count), 1)
+        row = at & (part - 1)
+        for k, (which, place) in enumerate(orders[order]):
+            here = (at >> (part.bit_length() - 1)) == k
+            row = row + jnp.where(here, (8 * side + 4 * which + place) * part, 0)
+        token = lax.broadcasted_iota(jnp.int32, (tokens, count), 0)
+        pick = (owner_token(row, device, n) == token).astype(F32).astype(BF16)
         total += jnp.dot(pick, values.astype(BF16), preferred_element_type=F32)
     out[...] = total.astype(BF16)
 
@@ -260,40 +273,42 @@
         shapes = [(pair, F32), (pair, BF16)]
         return local_call(kernel, shapes, f"settle{which}", total, residual, *arrived)
 
-    def gather(held):
+    def widen(held):
         for level in levels[-2::-1]:
             held = jnp.concatenate([held, swap(held, level)], axis=0)
-        return [swap(held, distance) for distance in square][::-1] + [held]
+        return held
 
     sums = [reduce(which) for which in range(2)]
     sums = [(total, swap(turned, levels[-1])) for total, turned in sums]
-    outs, held = [], []
-    for which in range(2):
-        shapes = [(pair, BF16), (pair, BF16, pltpu.VMEM), ((2, D // QB), F32, pltpu.VMEM)]
-        normed, *outs = local_call(
-            encode_kernel,
-            shapes,
-            f"encode{which}",
-            *sums[which],
-            gain,
-            *outs,
-            scratch=[pltpu.VMEM(pair, F32)],
-        )
-        held.append(gather(normed))
-    early, near = (jnp.concatenate(pieces, axis=0) for pieces in held)
-    early_other, near_other = swap(early, 1), swap(near, 1)
+    shapes = [(pair, BF16), (pair, BF16, pltpu.VMEM), ((2, D // QB), F32, pltpu.VMEM)]
+    scratch = [pltpu.VMEM(pair, F32)]
+    first = local_call(encode_kernel, shapes, "encode0", *sums[0], gain, scratch=scratch)
+    shapes.append(((4, D), BF16))
+    second = local_call(encode_kernel, shapes, "encode1", *sums[1], gain, *first, scratch=scratch)
+    held = [widen(first[0]), widen(second[0])]
+    joint = second[3] if len(levels) == 1 else jnp.concatenate(held, axis=0)
+    diagonal, near, far = square
+    early = [swap(held[0], near), swap(held[0], diagonal), held[0]]
+    early = jnp.concatenate(early, axis=0)
+    late = [swap(held[1], near), swap(joint, far), swap(held[1], diagonal), held[1]]
+    late = jnp.concatenate(late, axis=0)
+    orders = [(0, 2), (0, 1), (0, 0)], [(1, 2), (0, 3), (1, 3), (1, 1), (1, 0)]
+    early_other = swap(early, 1)
+    late, _ = lax.optimization_barrier((late, early_other))
+    late_other = swap(late, 1)
     width = q_weight.shape[1]
-    shapes = [((3 * quarter, width), F32)] + [(x.shape, x.dtype, pltpu.HBM) for x in outs]
+    outs = second[1:3]
+    shapes = [((half + 3 * part, width), F32)] + [(x.shape, x.dtype, pltpu.HBM) for x in outs]
     before, *outs = local_call(
         first_dots_kernel,
         shapes,
         "first_dots",
-        *(early, early_other, near, q_weight, *outs),
+        *(early, early_other, late, q_weight, *outs),
         scratch=[pltpu.SemaphoreType.DMA((2,))],
     )
-    kernel = functools.partial(last_dot_kernel, n)
+    kernel = functools.partial(last_dot_kernel, n, orders)
     shapes = [((tokens, width), BF16)]
-    (next_queries,) = local_call(kernel, shapes, "last_dot", near_other, before, q_weight)
+    (next_queries,) = local_call(kernel, shapes, "last_dot", late_other, before, q_weight)
     return (*outs, next_queries)
 
 

time: 36.3 us -> 37.4 us (1.030)
  waiting for transfers between devices: 5.77 us -> 8.77 us
  starting transfers between devices: 21.4 us -> 19.4 us
    ppermute x18 -> x17, waiting for transfers between devices: 5.77 us -> 8.77 us  [swap(): return lax.ppermute(x, 'tp', [(i, i ^ distance) for i in range(n)])]
    ppermute x18 -> x17, starting transfers between devices: 21.4 us -> 19.4 us  [swap(): return lax.ppermute(x, 'tp', [(i, i ^ distance) for i in range(n)])]
  transfers between devices with their start and end apart: 18 -> 17, of which waited for: 7 -> 9; matrix products, arithmetic and copies ran while one was open for 3% -> 3% of each run, Pallas kernels for 7% -> 7%
where the time goes in v14:
time: 37.4 us; the launch traced here: 37.3 us
  starting transfers between devices  19.4 us (52%)
  waiting for transfers between devices  8.77 us (23%)
  Pallas kernels  6.47 us (17%)
  matrix products  1.31 us (4%)
  between operations  0.74 us (2%)
  other arithmetic  0.58 us (2%)
    ppermute x17, starting transfers between devices, swap(): return lax.ppermute(x, 'tp', [(i, i ^ distance) for i in range(n)])  19.4 us
    ppermute x17, waiting for transfers between devices, swap(): return lax.ppermute(x, 'tp', [(i, i ^ distance) for i in range(n)])  8.77 us
    pallas_call x8, Pallas kernels, local_call(): pl.pallas_call(kernel, out_shape=[(space[0] if space else jax.ShapeDtypeS...  4.19 us
    pallas_call x1, Pallas kernels, attend(): pl.pallas_call(functools.partial(attend_kernel, n), out_shape=[jax.ShapeD...  2.28 us
  transfers between devices with their start and end apart: 17, of which 9 were waited for; matrix products, arithmetic and copies ran while one was open for 3% of the time, Pallas kernels for 7%

profile of v14, /device:TPU:0, one launch (start us, length us, event | category | flops | bytes accessed | tf_op | source)
XLA Modules:
  0.0 37.3 jit_solution(2271701723828919692)
XLA Ops:
  0.6 2.3 %attend.1 = (bf16[32,128]{1,0:T(8,128)(2,1)S(1)}, bf16[128,16384]{1,0:T(8,128)(2,1)S(1)}) custom-call(bf16[32,128]{1,0:T(8,128)(2,1)} %queries.1, bf16[32,1024]{1,0:T(8,128)(2,1)} %keys.1, bf16[32,1024]{1,0:T(8,128)(2,1)} %values.1, bf16[128,16384]{1,0:T(8,128)(2,1)} %weight.1), custom_call_target="tpu_custom_call" | custom-call | bytes 4194304 | tf_op jit(solution)/shard_map/attend/pallas_call | solution.py:86
  2.9 0.7 %convolution_convert_fusion = bf16[16,16384]{1,0:T(8,128)(2,1)S(1)} fusion(bf16[128,16384]{1,0:T(8,128)(2,1)S(1)} %get-tuple-element.29, bf16[32,128]{1,0:T(8,128)(2,1)S(1)} %get-tuple-element.28), kind=kOutput, calls=%fused_computation | convolution fusion | flops 67371008 | bytes 4722688 | tf_op jit(solution)/shard_map/dot_general | solution.py:256
  3.6 0.0 copy-start.1
  3.6 0.5 %collective-permute-start.8 = (bf16[8,16384]{1,0:T(8,128)(2,1)S(1)}, bf16[8,16384]{1,0:T(8,128)(2,1)S(1)}, u32[]{:S(2)}, u32[]{:S(2)}) collective-permute-start(bf16[8,16384]{1,0:T(8,128)(2,1)S(1)} %get-tuple-element.53), channel_id=1, source_target_pairs={{0,1},{1,0},{2,3},{3,2},{4,5},{5,4},{6,7},{7,6},{8,9},{9,8},{10,11... | collective-permute-start | bytes 786440 | tf_op jit(solution)/shard_map/ppermute | solution.py:250
  4.2 0.0 copy-start.2
  4.2 0.0 copy-start
  4.2 0.1 collective-permute-start
  4.3 0.7 %fusion.1.kept = f32[16,16384]{1,0:T(8,128)S(1)} fusion(bf16[128,16384]{1,0:T(8,128)(2,1)S(1)} %get-tuple-element.29, bf16[32,128]{1,0:T(8,128)(2,1)S(1)} %get-tuple-element.28), kind=kOutput, calls=%fused_computation.4 | convolution fusion | flops 67108864 | bytes 5246976 | tf_op jit(solution)/shard_map/dot_general | solution.py:258
  4.9 0.8 %collective-permute-done.got = bf16[8,16384]{1,0:T(8,128)(2,1)S(1)} collective-permute-done((bf16[8,16384]{1,0:T(8,128)(2,1)S(1)}, bf16[8,16384]{1,0:T(8,128)(2,1)S(1)}, u32[]{:S(2)}, u32[]{:S(2)}) %collective-permute-start) | collective-permute-done | bytes 262176 | tf_op jit(solution)/shard_map/ppermute | solution.py:250
  5.7 0.1 split0.1
  5.8 4.0 %collective-permute-start.1 = (bf16[2,16384]{1,0:T(2,128)(2,1)S(1)}, bf16[2,16384]{1,0:T(2,128)(2,1)S(1)}, u32[]{:S(2)}, u32[]{:S(2)}) collective-permute-start(bf16[2,16384]{1,0:T(2,128)(2,1)S(1)} %get-tuple-element.31), channel_id=1, source_target_pairs={{0,6},{1,7},{2,4},{3,5},{4,2},{5,3},{6,0},{7,1},{8,14},{9,15},{10,... | collective-permute-start | bytes 196616 | tf_op jit(solution)/shard_map/ppermute | solution.py:250
  9.8 0.5 %collective-permute-start.2 = (bf16[2,16384]{1,0:T(2,128)(2,1)S(1)}, bf16[2,16384]{1,0:T(2,128)(2,1)S(1)}, u32[]{:S(2)}, u32[]{:S(2)}) collective-permute-start(bf16[2,16384]{1,0:T(2,128)(2,1)S(1)} %get-tuple-element.32), channel_id=1, source_target_pairs={{0,2},{1,3},{2,0},{3,1},{4,6},{5,7},{6,4},{7,5},{8,10},{9,11},{10,... | collective-permute-start | bytes 196616 | tf_op jit(solution)/shard_map/ppermute | solution.py:250
  10.3 0.1 collective-permute-start.3
  10.4 0.0 collective-permute-done.8.got
  10.4 0.1 split1.1
  10.5 2.9 %collective-permute-start.9 = (bf16[2,16384]{1,0:T(2,128)(2,1)S(1)}, bf16[2,16384]{1,0:T(2,128)(2,1)S(1)}, u32[]{:S(2)}, u32[]{:S(2)}) collective-permute-start(bf16[2,16384]{1,0:T(2,128)(2,1)S(1)} %get-tuple-element.38), channel_id=1, source_target_pairs={{0,6},{1,7},{2,4},{3,5},{4,2},{5,3},{6,0},{7,1},{8,14},{9,15},{10,... | collective-permute-start | bytes 196616 | tf_op jit(solution)/shard_map/ppermute | solution.py:250
  13.4 0.5 %collective-permute-start.10 = (bf16[2,16384]{1,0:T(2,128)(2,1)S(1)}, bf16[2,16384]{1,0:T(2,128)(2,1)S(1)}, u32[]{:S(2)}, u32[]{:S(2)}) collective-permute-start(bf16[2,16384]{1,0:T(2,128)(2,1)S(1)} %get-tuple-element.39), channel_id=1, source_target_pairs={{0,2},{1,3},{2,0},{3,1},{4,6},{5,7},{6,4},{7,5},{8,10},{9,11},{10,... | collective-permute-start | bytes 196616 | tf_op jit(solution)/shard_map/ppermute | solution.py:250
  13.9 0.0 collective-permute-done.1.refs_0_
  13.9 0.2 collective-permute-start.11
  14.1 0.0 collective-permute-done.2.refs_1_
  14.1 1.0 %collective-permute-done.3.refs_2_ = bf16[2,16384]{1,0:T(2,128)(2,1)S(1)} collective-permute-done((bf16[2,16384]{1,0:T(2,128)(2,1)S(1)}, bf16[2,16384]{1,0:T(2,128)(2,1)S(1)}, u32[]{:S(2)}, u32[]{:S(2)}) %collective-permute-start.3) | collective-permute-done | bytes 65568 | tf_op jit(solution)/shard_map/ppermute | solution.py:250
  15.2 0.0 copy-done.1
  15.2 0.2 settle0.1
  15.4 2.6 %collective-permute-start.4 = (bf16[2,16384]{1,0:T(2,128)(2,1)S(1)}, bf16[2,16384]{1,0:T(2,128)(2,1)S(1)}, u32[]{:S(2)}, u32[]{:S(2)}) collective-permute-start(bf16[2,16384]{1,0:T(2,128)(2,1)S(1)} %get-tuple-element.35), channel_id=1, source_target_pairs={{0,8},{1,9},{2,10},{3,11},{4,12},{5,13},{6,14},{7,15},{8,0},{9,1},... | collective-permute-start | bytes 196616 | tf_op jit(solution)/shard_map/ppermute | solution.py:250
  18.0 0.0 collective-permute-done.9.refs_0_
  18.0 0.0 collective-permute-done.10.refs_1_
  18.0 0.2 collective-permute-done.11.refs_2_
  18.2 0.2 settle1.1
  18.4 2.7 %collective-permute-start.12 = (bf16[2,16384]{1,0:T(2,128)(2,1)S(1)}, bf16[2,16384]{1,0:T(2,128)(2,1)S(1)}, u32[]{:S(2)}, u32[]{:S(2)}) collective-permute-start(bf16[2,16384]{1,0:T(2,128)(2,1)S(1)} %get-tuple-element.42), channel_id=1, source_target_pairs={{0,8},{1,9},{2,10},{3,11},{4,12},{5,13},{6,14},{7,15},{8,0},{9,1},... | collective-permute-start | bytes 196616 | tf_op jit(solution)/shard_map/ppermute | solution.py:250
  21.0 1.4 %collective-permute-done.4.arrived = bf16[2,16384]{1,0:T(2,128)(2,1)S(1)} collective-permute-done((bf16[2,16384]{1,0:T(2,128)(2,1)S(1)}, bf16[2,16384]{1,0:T(2,128)(2,1)S(1)}, u32[]{:S(2)}, u32[]{:S(2)}) %collective-permute-start.4) | collective-permute-done | bytes 65568 | tf_op jit(solution)/shard_map/ppermute | solution.py:250
  22.5 0.0 copy-done.2
  22.5 0.4 %encode0.1 = (bf16[2,16384]{1,0:T(2,128)(2,1)S(1)}, bf16[2,16384]{1,0:T(2,128)(2,1)S(1)}, f32[2,128]{1,0:T(2,128)S(1)}) custom-call(f32[2,16384]{1,0:T(2,128)S(1)} %get-tuple-element.34.total, bf16[2,16384]{1,0:T(2,128)(2,1)S(1)} %collective-permute-done.4.arrived, f32[1,16384]{1,0:T(1,128)S(1)} %bitcast.3), custom_call_target="tpu_custom_call" | custom-call | bytes 163840 | tf_op jit(solution)/shard_map/encode0/pallas_call | solution.py:225
  22.9 1.2 %collective-permute-start.6 = (bf16[2,16384]{1,0:T(2,128)(2,1)S(1)}, bf16[2,16384]{1,0:T(2,128)(2,1)S(1)}, u32[]{:S(2)}, u32[]{:S(2)}) collective-permute-start(bf16[2,16384]{1,0:T(2,128)(2,1)S(1)} %get-tuple-element.36.refs_0_), channel_id=1, source_target_pairs={{0,6},{1,7},{2,4},{3,5},{4,2},{5,3},{6,0},{7,1},{8,14},{9,15},{10,... | collective-permute-start | bytes 196616 | tf_op jit(solution)/shard_map/ppermute | solution.py:250
  24.1 0.2 collective-permute-start.5
  24.4 0.0 collective-permute-done.12.arrived
  24.4 0.5 %encode1.1 = (bf16[2,16384]{1,0:T(2,128)(2,1)S(1)}, bf16[2,16384]{1,0:T(2,128)(2,1)S(1)}, f32[2,128]{1,0:T(2,128)S(1)}, bf16[4,16384]{1,0:T(4,128)(2,1)S(1)}) custom-call(f32[2,16384]{1,0:T(2,128)S(1)} %get-tuple-element.41.total, bf16[2,16384]{1,0:T(2,128)(2,1)S(1)} %collective-permute-done.12.arrived, f32[1,16384]{1,0:T(1,128)S(1)} %bitcast.4, ...), custom_call_target="tpu_custom_call" | custom-call | bytes 295424 | tf_op jit(solution)/shard_map/encode1/pallas_call | solution.py:225
  24.9 1.8 %collective-permute-start.15 = (bf16[2,16384]{1,0:T(2,128)(2,1)S(1)}, bf16[2,16384]{1,0:T(2,128)(2,1)S(1)}, u32[]{:S(2)}, u32[]{:S(2)}) collective-permute-start(bf16[2,16384]{1,0:T(2,128)(2,1)S(1)} %get-tuple-element.45), channel_id=1, source_target_pairs={{0,6},{1,7},{2,4},{3,5},{4,2},{5,3},{6,0},{7,1},{8,14},{9,15},{10,... | collective-permute-start | bytes 196616 | tf_op jit(solution)/shard_map/ppermute | solution.py:250
  26.7 1.9 %collective-permute-start.13 = (bf16[2,16384]{1,0:T(2,128)(2,1)S(1)}, bf16[2,16384]{1,0:T(2,128)(2,1)S(1)}, u32[]{:S(2)}, u32[]{:S(2)}) collective-permute-start(bf16[2,16384]{1,0:T(2,128)(2,1)S(1)} %get-tuple-element.45), channel_id=1, source_target_pairs={{0,2},{1,3},{2,0},{3,1},{4,6},{5,7},{6,4},{7,5},{8,10},{9,11},{10,... | collective-permute-start | bytes 196616 | tf_op jit(solution)/shard_map/ppermute | solution.py:250
  28.5 0.0 collective-permute-start.14
  28.6 0.0 collective-permute-done.6
  28.6 1.0 %collective-permute-done.5 = bf16[2,16384]{1,0:T(2,128)(2,1)S(1)} collective-permute-done((bf16[2,16384]{1,0:T(2,128)(2,1)S(1)}, bf16[2,16384]{1,0:T(2,128)(2,1)S(1)}, u32[]{:S(2)}, u32[]{:S(2)}) %collective-permute-start.5) | collective-permute-done | bytes 65568 | tf_op jit(solution)/shard_map/ppermute | solution.py:250
  29.5 0.2 pad_maximum_fusion.1.refs_0_
  29.8 0.1 collective-permute-start.7
  29.8 0.4 %collective-permute-done.15 = bf16[2,16384]{1,0:T(2,128)(2,1)S(1)} collective-permute-done((bf16[2,16384]{1,0:T(2,128)(2,1)S(1)}, bf16[2,16384]{1,0:T(2,128)(2,1)S(1)}, u32[]{:S(2)}, u32[]{:S(2)}) %collective-permute-start.15) | collective-permute-done | bytes 65568 | tf_op jit(solution)/shard_map/ppermute | solution.py:250
  30.3 0.7 %collective-permute-done.13 = bf16[2,16384]{1,0:T(2,128)(2,1)S(1)} collective-permute-done((bf16[2,16384]{1,0:T(2,128)(2,1)S(1)}, bf16[2,16384]{1,0:T(2,128)(2,1)S(1)}, u32[]{:S(2)}, u32[]{:S(2)}) %collective-permute-start.13) | collective-permute-done | bytes 65568 | tf_op jit(solution)/shard_map/ppermute | solution.py:250
  31.0 2.6 %collective-permute-done.14 = bf16[4,16384]{1,0:T(4,128)(2,1)S(1)} collective-permute-done((bf16[4,16384]{1,0:T(4,128)(2,1)S(1)}, bf16[4,16384]{1,0:T(4,128)(2,1)S(1)}, u32[]{:S(2)}, u32[]{:S(2)}) %collective-permute-start.14) | collective-permute-done | bytes 131104 | tf_op jit(solution)/shard_map/ppermute | solution.py:250
  33.5 0.4 pad_maximum_fusion.refs_2_
  33.9 0.0 collective-permute-done.7.refs_1_
  33.9 0.1 collective-permute-start.16
  34.0 0.0 copy-done
  34.0 1.3 %first_dots.1 = (f32[22,128]{1,0:T(8,128)S(1)}, bf16[2,16384]{1,0:T(2,128)(2,1)}, f32[2,128]{1,0:T(2,128)}) custom-call(bf16[6,16384]{1,0:T(8,128)(2,1)S(1)} %pad_maximum_fusion.1.refs_0_, bf16[6,16384]{1,0:T(8,128)(2,1)S(1)} %collective-permute-done.7.refs_1_, bf16[10,16384]{1,0:T(8,128)(2,1)S(1)} %pad_maximum_fusion.refs_2_, ...), custom_call_target="tpu_custom_call" | custom-call | bytes 4981248 | tf_op jit(solution)/shard_map/first_dots/pallas_call | solution.py:225
  35.2 0.6 %collective-permute-done.16.refs_0_ = bf16[10,16384]{1,0:T(8,128)(2,1)S(1)} collective-permute-done((bf16[10,16384]{1,0:T(8,128)(2,1)S(1)}, bf16[10,16384]{1,0:T(8,128)(2,1)S(1)}, u32[]{:S(2)}, u32[]{:S(2)}) %collective-permute-start.16) | collective-permute-done | bytes 327712 | tf_op jit(solution)/shard_map/ppermute | solution.py:250
  35.9 1.4 %last_dot.1 = bf16[32,128]{1,0:T(8,128)(2,1)} custom-call(bf16[10,16384]{1,0:T(8,128)(2,1)S(1)} %collective-permute-done.16.refs_0_, f32[22,128]{1,0:T(8,128)S(1)} %get-tuple-element.52.refs_1_, bf16[16384,128]{1,0:T(8,128)(2,1)S(1)} %copy-done), custom_call_target="tpu_custom_call" | custom-call | bytes 4527616 | tf_op jit(solution)/shard_map/last_dot/pallas_call | solution.py:225
  (1 shorter events, 0.0 us)
Async XLA Ops:
  3.6 11.5 %copy-start.1 = (bf16[2,16384]{1,0:T(2,128)(2,1)S(1)}, bf16[2,16384]{1,0:T(2,128)(2,1)}, u32[]{:S(2)}) copy-start(bf16[2,16384]{1,0:T(2,128)(2,1)} %old.3) | copy-start | bytes 196612
  3.6 6.8 %collective-permute-start.8 = (bf16[8,16384]{1,0:T(8,128)(2,1)S(1)}, bf16[8,16384]{1,0:T(8,128)(2,1)S(1)}, u32[]{:S(2)}, u32[]{:S(2)}) collective-permute-start(bf16[8,16384]{1,0:T(8,128)(2,1)S(1)} %get-tuple-element.53), channel_id=1, source_target_pairs={{0,1},{1,0},{2,3},{3,2},{4,5},{5,4},{6,7},{7,6},{8,9},{9,8},{10,11... | collective-permute-start | bytes 786440 | tf_op jit(solution)/shard_map/ppermute | solution.py:250
  4.2 18.3 %copy-start.2 = (f32[16384]{0:T(1024)S(1)}, f32[16384]{0:T(1024)}, u32[]{:S(2)}) copy-start(f32[16384]{0:T(1024)} %param.12) | copy-start | bytes 196612
  4.2 29.8 %copy-start = (bf16[16384,128]{1,0:T(8,128)(2,1)S(1)}, bf16[16384,128]{1,0:T(8,128)(2,1)}, u32[]{:S(2)}) copy-start(bf16[16384,128]{1,0:T(8,128)(2,1)} %refs_2_.1) | copy-start | bytes 12582916
  4.2 1.5 %collective-permute-start = (bf16[8,16384]{1,0:T(8,128)(2,1)S(1)}, bf16[8,16384]{1,0:T(8,128)(2,1)S(1)}, u32[]{:S(2)}, u32[]{:S(2)}) collective-permute-start(bf16[8,16384]{1,0:T(8,128)(2,1)S(1)} %get-tuple-element.54), channel_id=1, source_target_pairs={{0,1},{1,0},{2,3},{3,2},{4,5},{5,4},{6,7},{7,6},{8,9},{9,8},{10,11... | collective-permute-start | bytes 786440 | tf_op jit(solution)/shard_map/ppermute | solution.py:250
  5.8 8.1 %collective-permute-start.1 = (bf16[2,16384]{1,0:T(2,128)(2,1)S(1)}, bf16[2,16384]{1,0:T(2,128)(2,1)S(1)}, u32[]{:S(2)}, u32[]{:S(2)}) collective-permute-start(bf16[2,16384]{1,0:T(2,128)(2,1)S(1)} %get-tuple-element.31), channel_id=1, source_target_pairs={{0,6},{1,7},{2,4},{3,5},{4,2},{5,3},{6,0},{7,1},{8,14},{9,15},{10,... | collective-permute-start | bytes 196616 | tf_op jit(solution)/shard_map/ppermute | solution.py:250
  9.8 4.4 %collective-permute-start.2 = (bf16[2,16384]{1,0:T(2,128)(2,1)S(1)}, bf16[2,16384]{1,0:T(2,128)(2,1)S(1)}, u32[]{:S(2)}, u32[]{:S(2)}) collective-permute-start(bf16[2,16384]{1,0:T(2,128)(2,1)S(1)} %get-tuple-element.32), channel_id=1, source_target_pairs={{0,2},{1,3},{2,0},{3,1},{4,6},{5,7},{6,4},{7,5},{8,10},{9,11},{10,... | collective-permute-start | bytes 196616 | tf_op jit(solution)/shard_map/ppermute | solution.py:250
  10.3 4.9 %collective-permute-start.3 = (bf16[2,16384]{1,0:T(2,128)(2,1)S(1)}, bf16[2,16384]{1,0:T(2,128)(2,1)S(1)}, u32[]{:S(2)}, u32[]{:S(2)}) collective-permute-start(bf16[2,16384]{1,0:T(2,128)(2,1)S(1)} %get-tuple-element.33), channel_id=1, source_target_pairs={{0,4},{1,5},{2,6},{3,7},{4,0},{5,1},{6,2},{7,3},{8,12},{9,13},{10,... | collective-permute-start | bytes 196616 | tf_op jit(solution)/shard_map/ppermute | solution.py:250
  10.5 7.5 %collective-permute-start.9 = (bf16[2,16384]{1,0:T(2,128)(2,1)S(1)}, bf16[2,16384]{1,0:T(2,128)(2,1)S(1)}, u32[]{:S(2)}, u32[]{:S(2)}) collective-permute-start(bf16[2,16384]{1,0:T(2,128)(2,1)S(1)} %get-tuple-element.38), channel_id=1, source_target_pairs={{0,6},{1,7},{2,4},{3,5},{4,2},{5,3},{6,0},{7,1},{8,14},{9,15},{10,... | collective-permute-start | bytes 196616 | tf_op jit(solution)/shard_map/ppermute | solution.py:250
  13.4 4.6 %collective-permute-start.10 = (bf16[2,16384]{1,0:T(2,128)(2,1)S(1)}, bf16[2,16384]{1,0:T(2,128)(2,1)S(1)}, u32[]{:S(2)}, u32[]{:S(2)}) collective-permute-start(bf16[2,16384]{1,0:T(2,128)(2,1)S(1)} %get-tuple-element.39), channel_id=1, source_target_pairs={{0,2},{1,3},{2,0},{3,1},{4,6},{5,7},{6,4},{7,5},{8,10},{9,11},{10,... | collective-permute-start | bytes 196616 | tf_op jit(solution)/shard_map/ppermute | solution.py:250
  13.9 4.3 %collective-permute-start.11 = (bf16[2,16384]{1,0:T(2,128)(2,1)S(1)}, bf16[2,16384]{1,0:T(2,128)(2,1)S(1)}, u32[]{:S(2)}, u32[]{:S(2)}) collective-permute-start(bf16[2,16384]{1,0:T(2,128)(2,1)S(1)} %get-tuple-element.40), channel_id=1, source_target_pairs={{0,4},{1,5},{2,6},{3,7},{4,0},{5,1},{6,2},{7,3},{8,12},{9,13},{10,... | collective-permute-start | bytes 196616 | tf_op jit(solution)/shard_map/ppermute | solution.py:250
  15.4 7.1 %collective-permute-start.4 = (bf16[2,16384]{1,0:T(2,128)(2,1)S(1)}, bf16[2,16384]{1,0:T(2,128)(2,1)S(1)}, u32[]{:S(2)}, u32[]{:S(2)}) collective-permute-start(bf16[2,16384]{1,0:T(2,128)(2,1)S(1)} %get-tuple-element.35), channel_id=1, source_target_pairs={{0,8},{1,9},{2,10},{3,11},{4,12},{5,13},{6,14},{7,15},{8,0},{9,1},... | collective-permute-start | bytes 196616 | tf_op jit(solution)/shard_map/ppermute | solution.py:250
  18.4 6.0 %collective-permute-start.12 = (bf16[2,16384]{1,0:T(2,128)(2,1)S(1)}, bf16[2,16384]{1,0:T(2,128)(2,1)S(1)}, u32[]{:S(2)}, u32[]{:S(2)}) collective-permute-start(bf16[2,16384]{1,0:T(2,128)(2,1)S(1)} %get-tuple-element.42), channel_id=1, source_target_pairs={{0,8},{1,9},{2,10},{3,11},{4,12},{5,13},{6,14},{7,15},{8,0},{9,1},... | collective-permute-start | bytes 196616 | tf_op jit(solution)/shard_map/ppermute | solution.py:250
  22.9 5.6 %collective-permute-start.6 = (bf16[2,16384]{1,0:T(2,128)(2,1)S(1)}, bf16[2,16384]{1,0:T(2,128)(2,1)S(1)}, u32[]{:S(2)}, u32[]{:S(2)}) collective-permute-start(bf16[2,16384]{1,0:T(2,128)(2,1)S(1)} %get-tuple-element.36.refs_0_), channel_id=1, source_target_pairs={{0,6},{1,7},{2,4},{3,5},{4,2},{5,3},{6,0},{7,1},{8,14},{9,15},{10,... | collective-permute-start | bytes 196616 | tf_op jit(solution)/shard_map/ppermute | solution.py:250
  24.1 5.4 %collective-permute-start.5 = (bf16[2,16384]{1,0:T(2,128)(2,1)S(1)}, bf16[2,16384]{1,0:T(2,128)(2,1)S(1)}, u32[]{:S(2)}, u32[]{:S(2)}) collective-permute-start(bf16[2,16384]{1,0:T(2,128)(2,1)S(1)} %get-tuple-element.36.refs_0_), channel_id=1, source_target_pairs={{0,2},{1,3},{2,0},{3,1},{4,6},{5,7},{6,4},{7,5},{8,10},{9,11},{10,... | collective-permute-start | bytes 196616 | tf_op jit(solution)/shard_map/ppermute | solution.py:250
  24.9 5.4 %collective-permute-start.15 = (bf16[2,16384]{1,0:T(2,128)(2,1)S(1)}, bf16[2,16384]{1,0:T(2,128)(2,1)S(1)}, u32[]{:S(2)}, u32[]{:S(2)}) collective-permute-start(bf16[2,16384]{1,0:T(2,128)(2,1)S(1)} %get-tuple-element.45), channel_id=1, source_target_pairs={{0,6},{1,7},{2,4},{3,5},{4,2},{5,3},{6,0},{7,1},{8,14},{9,15},{10,... | collective-permute-start | bytes 196616 | tf_op jit(solution)/shard_map/ppermute | solution.py:250
  26.7 4.3 %collective-permute-start.13 = (bf16[2,16384]{1,0:T(2,128)(2,1)S(1)}, bf16[2,16384]{1,0:T(2,128)(2,1)S(1)}, u32[]{:S(2)}, u32[]{:S(2)}) collective-permute-start(bf16[2,16384]{1,0:T(2,128)(2,1)S(1)} %get-tuple-element.45), channel_id=1, source_target_pairs={{0,2},{1,3},{2,0},{3,1},{4,6},{5,7},{6,4},{7,5},{8,10},{9,11},{10,... | collective-permute-start | bytes 196616 | tf_op jit(solution)/shard_map/ppermute | solution.py:250
  28.5 5.0 %collective-permute-start.14 = (bf16[4,16384]{1,0:T(4,128)(2,1)S(1)}, bf16[4,16384]{1,0:T(4,128)(2,1)S(1)}, u32[]{:S(2)}, u32[]{:S(2)}) collective-permute-start(bf16[4,16384]{1,0:T(4,128)(2,1)S(1)} %get-tuple-element.46), channel_id=1, source_target_pairs={{0,4},{1,5},{2,6},{3,7},{4,0},{5,1},{6,2},{7,3},{8,12},{9,13},{10,... | collective-permute-start | bytes 393224 | tf_op jit(solution)/shard_map/ppermute | solution.py:250
  29.8 4.1 %collective-permute-start.7 = (bf16[6,16384]{1,0:T(8,128)(2,1)S(1)}, bf16[6,16384]{1,0:T(8,128)(2,1)S(1)}, u32[]{:S(2)}, u32[]{:S(2)}) collective-permute-start(bf16[6,16384]{1,0:T(8,128)(2,1)S(1)} %pad_maximum_fusion.1.refs_0_), channel_id=1, source_target_pairs={{0,1},{1,0},{2,3},{3,2},{4,5},{5,4},{6,7},{7,6},{8,9},{9,8},{10,11... | collective-permute-start | bytes 589832 | tf_op jit(solution)/shard_map/ppermute | solution.py:250
  33.9 2.0 %collective-permute-start.16 = (bf16[10,16384]{1,0:T(8,128)(2,1)S(1)}, bf16[10,16384]{1,0:T(8,128)(2,1)S(1)}, u32[]{:S(2)}, u32[]{:S(2)}) collective-permute-start(bf16[10,16384]{1,0:T(8,128)(2,1)S(1)} %pad_maximum_fusion.refs_2_), channel_id=1, source_target_pairs={{0,1},{1,0},{2,3},{3,2},{4,5},{5,4},{6,7},{7,6},{8,9},{9,8},{10,11... | collective-permute-start | bytes 983048 | tf_op jit(solution)/shard_map/ppermute | solution.py:250

commit v15 on v14

--- a/solution.py
+++ b/solution.py
@@ -199,7 +199,7 @@
     tokens = out.shape[0]
     part = tokens // 16
     total = jnp.zeros(out.shape, F32)
-    groups = [(0, 0), (1, 0), (0, 1), (1, 1)]
+    groups = [(side, order) for order in range(len(orders)) for side in range(2)]
     start = 0
     for side, order in groups:
         count = len(orders[order]) * part
@@ -290,25 +290,26 @@
     diagonal, near, far = square
     early = [swap(held[0], near), swap(held[0], diagonal), held[0]]
     early = jnp.concatenate(early, axis=0)
-    late = [swap(held[1], near), swap(joint, far), swap(held[1], diagonal), held[1]]
+    both = swap(joint, far)
+    late = [swap(held[1], near), swap(held[1], diagonal), held[1]]
     late = jnp.concatenate(late, axis=0)
-    orders = [(0, 2), (0, 1), (0, 0)], [(1, 2), (0, 3), (1, 3), (1, 1), (1, 0)]
     early_other = swap(early, 1)
     late, _ = lax.optimization_barrier((late, early_other))
-    late_other = swap(late, 1)
+    both_other, late_other = swap(both, 1), swap(late, 1)
+    orders = [(0, 2), (0, 1), (0, 0)], [(1, 2), (1, 1), (1, 0)], [(0, 3), (1, 3)]
     width = q_weight.shape[1]
     outs = second[1:3]
-    shapes = [((half + 3 * part, width), F32)] + [(x.shape, x.dtype, pltpu.HBM) for x in outs]
+    shapes = [((half + 6 * part, width), F32)] + [(x.shape, x.dtype, pltpu.HBM) for x in outs]
     before, *outs = local_call(
         first_dots_kernel,
         shapes,
         "first_dots",
-        *(early, early_other, late, q_weight, *outs),
+        *(early, early_other, late, late_other, both, q_weight, *outs),
         scratch=[pltpu.SemaphoreType.DMA((2,))],
     )
     kernel = functools.partial(last_dot_kernel, n, orders)
     shapes = [((tokens, width), BF16)]
-    (next_queries,) = local_call(kernel, shapes, "last_dot", late_other, before, q_weight)
+    (next_queries,) = local_call(kernel, shapes, "last_dot", both_other, before, q_weight)
     return (*outs, next_queries)
 
 

time: 37.4 us -> 36.4 us (0.973)
  Pallas kernels: 6.47 us -> 5.96 us
  waiting for transfers between devices: 8.77 us -> 8.37 us
    pallas_call x8, Pallas kernels: 4.19 us -> 3.68 us  [local_call(): pl.pallas_call(kernel, out_shape=[(space[0] if space else jax.ShapeDtypeS...]
    ppermute x17 -> x18, waiting for transfers between devices: 8.77 us -> 8.37 us  [swap(): return lax.ppermute(x, 'tp', [(i, i ^ distance) for i in range(n)])]
    ppermute x17 -> x18, starting transfers between devices: 19.4 us -> 19.4 us  [swap(): return lax.ppermute(x, 'tp', [(i, i ^ distance) for i in range(n)])]
  transfers between devices with their start and end apart: 17 -> 18, of which waited for: 9 -> 10; matrix products, arithmetic and copies ran while one was open for 3% -> 3% of each run, Pallas kernels for 7% -> 6%
where the time goes in v15:
time: 36.4 us; the launch traced here: 36.3 us
  starting transfers between devices  19.4 us (53%)
  waiting for transfers between devices  8.37 us (23%)
  Pallas kernels  5.96 us (16%)
  matrix products  1.31 us (4%)
  between operations  0.72 us (2%)
  other arithmetic  0.43 us (1%)
    ppermute x18, starting transfers between devices, swap(): return lax.ppermute(x, 'tp', [(i, i ^ distance) for i in range(n)])  19.4 us
    ppermute x18, waiting for transfers between devices, swap(): return lax.ppermute(x, 'tp', [(i, i ^ distance) for i in range(n)])  8.37 us
    pallas_call x8, Pallas kernels, local_call(): pl.pallas_call(kernel, out_shape=[(space[0] if space else jax.ShapeDtypeS...  3.68 us
    pallas_call x1, Pallas kernels, attend(): pl.pallas_call(functools.partial(attend_kernel, n), out_shape=[jax.ShapeD...  2.28 us
  transfers between devices with their start and end apart: 18, of which 10 were waited for; matrix products, arithmetic and copies ran while one was open for 3% of the time, Pallas kernels for 6%

profile of v15, /device:TPU:0, one launch (start us, length us, event | category | flops | bytes accessed | tf_op | source)
XLA Modules:
  0.0 36.3 jit_solution(7512245577910715795)
XLA Ops:
  0.6 2.3 %attend.1 = (bf16[32,128]{1,0:T(8,128)(2,1)S(1)}, bf16[128,16384]{1,0:T(8,128)(2,1)S(1)}) custom-call(bf16[32,128]{1,0:T(8,128)(2,1)} %queries.1, bf16[32,1024]{1,0:T(8,128)(2,1)} %keys.1, bf16[32,1024]{1,0:T(8,128)(2,1)} %values.1, bf16[128,16384]{1,0:T(8,128)(2,1)} %weight.1), custom_call_target="tpu_custom_call" | custom-call | bytes 4194304 | tf_op jit(solution)/shard_map/attend/pallas_call | solution.py:86
  2.9 0.7 %convolution_convert_fusion = bf16[16,16384]{1,0:T(8,128)(2,1)S(1)} fusion(bf16[128,16384]{1,0:T(8,128)(2,1)S(1)} %get-tuple-element.29, bf16[32,128]{1,0:T(8,128)(2,1)S(1)} %get-tuple-element.28), kind=kOutput, calls=%fused_computation | convolution fusion | flops 67371008 | bytes 4722688 | tf_op jit(solution)/shard_map/dot_general | solution.py:256
  3.6 0.0 copy-start.1
  3.6 0.5 %collective-permute-start.8 = (bf16[8,16384]{1,0:T(8,128)(2,1)S(1)}, bf16[8,16384]{1,0:T(8,128)(2,1)S(1)}, u32[]{:S(2)}, u32[]{:S(2)}) collective-permute-start(bf16[8,16384]{1,0:T(8,128)(2,1)S(1)} %get-tuple-element.53), channel_id=1, source_target_pairs={{0,1},{1,0},{2,3},{3,2},{4,5},{5,4},{6,7},{7,6},{8,9},{9,8},{10,11... | collective-permute-start | bytes 786440 | tf_op jit(solution)/shard_map/ppermute | solution.py:250
  4.2 0.0 copy-start.2
  4.2 0.0 copy-start
  4.2 0.1 collective-permute-start
  4.3 0.7 %fusion.1.kept = f32[16,16384]{1,0:T(8,128)S(1)} fusion(bf16[128,16384]{1,0:T(8,128)(2,1)S(1)} %get-tuple-element.29, bf16[32,128]{1,0:T(8,128)(2,1)S(1)} %get-tuple-element.28), kind=kOutput, calls=%fused_computation.4 | convolution fusion | flops 67108864 | bytes 5246976 | tf_op jit(solution)/shard_map/dot_general | solution.py:258
  4.9 0.8 %collective-permute-done.got = bf16[8,16384]{1,0:T(8,128)(2,1)S(1)} collective-permute-done((bf16[8,16384]{1,0:T(8,128)(2,1)S(1)}, bf16[8,16384]{1,0:T(8,128)(2,1)S(1)}, u32[]{:S(2)}, u32[]{:S(2)}) %collective-permute-start) | collective-permute-done | bytes 262176 | tf_op jit(solution)/shard_map/ppermute | solution.py:250
  5.7 0.1 split0.1
  5.8 4.0 %collective-permute-start.1 = (bf16[2,16384]{1,0:T(2,128)(2,1)S(1)}, bf16[2,16384]{1,0:T(2,128)(2,1)S(1)}, u32[]{:S(2)}, u32[]{:S(2)}) collective-permute-start(bf16[2,16384]{1,0:T(2,128)(2,1)S(1)} %get-tuple-element.31), channel_id=1, source_target_pairs={{0,6},{1,7},{2,4},{3,5},{4,2},{5,3},{6,0},{7,1},{8,14},{9,15},{10,... | collective-permute-start | bytes 196616 | tf_op jit(solution)/shard_map/ppermute | solution.py:250
  9.8 0.5 %collective-permute-start.2 = (bf16[2,16384]{1,0:T(2,128)(2,1)S(1)}, bf16[2,16384]{1,0:T(2,128)(2,1)S(1)}, u32[]{:S(2)}, u32[]{:S(2)}) collective-permute-start(bf16[2,16384]{1,0:T(2,128)(2,1)S(1)} %get-tuple-element.32), channel_id=1, source_target_pairs={{0,2},{1,3},{2,0},{3,1},{4,6},{5,7},{6,4},{7,5},{8,10},{9,11},{10,... | collective-permute-start | bytes 196616 | tf_op jit(solution)/shard_map/ppermute | solution.py:250
  10.3 0.1 collective-permute-start.3
  10.4 0.0 collective-permute-done.8.got
  10.4 0.1 split1.1
  10.5 2.9 %collective-permute-start.9 = (bf16[2,16384]{1,0:T(2,128)(2,1)S(1)}, bf16[2,16384]{1,0:T(2,128)(2,1)S(1)}, u32[]{:S(2)}, u32[]{:S(2)}) collective-permute-start(bf16[2,16384]{1,0:T(2,128)(2,1)S(1)} %get-tuple-element.38), channel_id=1, source_target_pairs={{0,6},{1,7},{2,4},{3,5},{4,2},{5,3},{6,0},{7,1},{8,14},{9,15},{10,... | collective-permute-start | bytes 196616 | tf_op jit(solution)/shard_map/ppermute | solution.py:250
  13.4 0.5 %collective-permute-start.10 = (bf16[2,16384]{1,0:T(2,128)(2,1)S(1)}, bf16[2,16384]{1,0:T(2,128)(2,1)S(1)}, u32[]{:S(2)}, u32[]{:S(2)}) collective-permute-start(bf16[2,16384]{1,0:T(2,128)(2,1)S(1)} %get-tuple-element.39), channel_id=1, source_target_pairs={{0,2},{1,3},{2,0},{3,1},{4,6},{5,7},{6,4},{7,5},{8,10},{9,11},{10,... | collective-permute-start | bytes 196616 | tf_op jit(solution)/shard_map/ppermute | solution.py:250
  13.9 0.0 collective-permute-done.1.refs_0_
  13.9 0.2 collective-permute-start.11
  14.1 0.0 collective-permute-done.2.refs_1_
  14.1 1.0 %collective-permute-done.3.refs_2_ = bf16[2,16384]{1,0:T(2,128)(2,1)S(1)} collective-permute-done((bf16[2,16384]{1,0:T(2,128)(2,1)S(1)}, bf16[2,16384]{1,0:T(2,128)(2,1)S(1)}, u32[]{:S(2)}, u32[]{:S(2)}) %collective-permute-start.3) | collective-permute-done | bytes 65568 | tf_op jit(solution)/shard_map/ppermute | solution.py:250
  15.2 0.0 copy-done.1
  15.2 0.2 settle0.1
  15.4 2.6 %collective-permute-start.4 = (bf16[2,16384]{1,0:T(2,128)(2,1)S(1)}, bf16[2,16384]{1,0:T(2,128)(2,1)S(1)}, u32[]{:S(2)}, u32[]{:S(2)}) collective-permute-start(bf16[2,16384]{1,0:T(2,128)(2,1)S(1)} %get-tuple-element.35), channel_id=1, source_target_pairs={{0,8},{1,9},{2,10},{3,11},{4,12},{5,13},{6,14},{7,15},{8,0},{9,1},... | collective-permute-start | bytes 196616 | tf_op jit(solution)/shard_map/ppermute | solution.py:250
  18.0 0.0 collective-permute-done.9.refs_0_
  18.0 0.0 collective-permute-done.10.refs_1_
  18.0 0.2 collective-permute-done.11.refs_2_
  18.2 0.2 settle1.1
  18.4 2.7 %collective-permute-start.12 = (bf16[2,16384]{1,0:T(2,128)(2,1)S(1)}, bf16[2,16384]{1,0:T(2,128)(2,1)S(1)}, u32[]{:S(2)}, u32[]{:S(2)}) collective-permute-start(bf16[2,16384]{1,0:T(2,128)(2,1)S(1)} %get-tuple-element.42), channel_id=1, source_target_pairs={{0,8},{1,9},{2,10},{3,11},{4,12},{5,13},{6,14},{7,15},{8,0},{9,1},... | collective-permute-start | bytes 196616 | tf_op jit(solution)/shard_map/ppermute | solution.py:250
  21.0 1.4 %collective-permute-done.4.arrived = bf16[2,16384]{1,0:T(2,128)(2,1)S(1)} collective-permute-done((bf16[2,16384]{1,0:T(2,128)(2,1)S(1)}, bf16[2,16384]{1,0:T(2,128)(2,1)S(1)}, u32[]{:S(2)}, u32[]{:S(2)}) %collective-permute-start.4) | collective-permute-done | bytes 65568 | tf_op jit(solution)/shard_map/ppermute | solution.py:250
  22.5 0.0 copy-done.2
  22.5 0.4 %encode0.1 = (bf16[2,16384]{1,0:T(2,128)(2,1)S(1)}, bf16[2,16384]{1,0:T(2,128)(2,1)S(1)}, f32[2,128]{1,0:T(2,128)S(1)}) custom-call(f32[2,16384]{1,0:T(2,128)S(1)} %get-tuple-element.34.total, bf16[2,16384]{1,0:T(2,128)(2,1)S(1)} %collective-permute-done.4.arrived, f32[1,16384]{1,0:T(1,128)S(1)} %bitcast.3), custom_call_target="tpu_custom_call" | custom-call | bytes 163840 | tf_op jit(solution)/shard_map/encode0/pallas_call | solution.py:225
  22.9 1.2 %collective-permute-start.6 = (bf16[2,16384]{1,0:T(2,128)(2,1)S(1)}, bf16[2,16384]{1,0:T(2,128)(2,1)S(1)}, u32[]{:S(2)}, u32[]{:S(2)}) collective-permute-start(bf16[2,16384]{1,0:T(2,128)(2,1)S(1)} %get-tuple-element.36.refs_0_), channel_id=1, source_target_pairs={{0,6},{1,7},{2,4},{3,5},{4,2},{5,3},{6,0},{7,1},{8,14},{9,15},{10,... | collective-permute-start | bytes 196616 | tf_op jit(solution)/shard_map/ppermute | solution.py:250
  24.1 0.2 collective-permute-start.5
  24.4 0.0 collective-permute-done.12.arrived
  24.4 0.5 %encode1.1 = (bf16[2,16384]{1,0:T(2,128)(2,1)S(1)}, bf16[2,16384]{1,0:T(2,128)(2,1)S(1)}, f32[2,128]{1,0:T(2,128)S(1)}, bf16[4,16384]{1,0:T(4,128)(2,1)S(1)}) custom-call(f32[2,16384]{1,0:T(2,128)S(1)} %get-tuple-element.41.total, bf16[2,16384]{1,0:T(2,128)(2,1)S(1)} %collective-permute-done.12.arrived, f32[1,16384]{1,0:T(1,128)S(1)} %bitcast.4, ...), custom_call_target="tpu_custom_call" | custom-call | bytes 295424 | tf_op jit(solution)/shard_map/encode1/pallas_call | solution.py:225
  24.9 1.8 %collective-permute-start.14 = (bf16[2,16384]{1,0:T(2,128)(2,1)S(1)}, bf16[2,16384]{1,0:T(2,128)(2,1)S(1)}, u32[]{:S(2)}, u32[]{:S(2)}) collective-permute-start(bf16[2,16384]{1,0:T(2,128)(2,1)S(1)} %get-tuple-element.45), channel_id=1, source_target_pairs={{0,6},{1,7},{2,4},{3,5},{4,2},{5,3},{6,0},{7,1},{8,14},{9,15},{10,... | collective-permute-start | bytes 196616 | tf_op jit(solution)/shard_map/ppermute | solution.py:250
  26.7 1.9 %collective-permute-start.13 = (bf16[2,16384]{1,0:T(2,128)(2,1)S(1)}, bf16[2,16384]{1,0:T(2,128)(2,1)S(1)}, u32[]{:S(2)}, u32[]{:S(2)}) collective-permute-start(bf16[2,16384]{1,0:T(2,128)(2,1)S(1)} %get-tuple-element.45), channel_id=1, source_target_pairs={{0,2},{1,3},{2,0},{3,1},{4,6},{5,7},{6,4},{7,5},{8,10},{9,11},{10,... | collective-permute-start | bytes 196616 | tf_op jit(solution)/shard_map/ppermute | solution.py:250
  28.6 0.0 collective-permute-start.16
  28.6 0.0 collective-permute-done.6
  28.6 1.0 %collective-permute-done.5 = bf16[2,16384]{1,0:T(2,128)(2,1)S(1)} collective-permute-done((bf16[2,16384]{1,0:T(2,128)(2,1)S(1)}, bf16[2,16384]{1,0:T(2,128)(2,1)S(1)}, u32[]{:S(2)}, u32[]{:S(2)}) %collective-permute-start.5) | collective-permute-done | bytes 65568 | tf_op jit(solution)/shard_map/ppermute | solution.py:250
  29.5 0.2 pad_maximum_fusion.refs_0_
  29.8 0.1 collective-permute-start.7
  29.8 0.4 %collective-permute-done.14 = bf16[2,16384]{1,0:T(2,128)(2,1)S(1)} collective-permute-done((bf16[2,16384]{1,0:T(2,128)(2,1)S(1)}, bf16[2,16384]{1,0:T(2,128)(2,1)S(1)}, u32[]{:S(2)}, u32[]{:S(2)}) %collective-permute-start.14) | collective-permute-done | bytes 65568 | tf_op jit(solution)/shard_map/ppermute | solution.py:250
  30.3 0.7 %collective-permute-done.13 = bf16[2,16384]{1,0:T(2,128)(2,1)S(1)} collective-permute-done((bf16[2,16384]{1,0:T(2,128)(2,1)S(1)}, bf16[2,16384]{1,0:T(2,128)(2,1)S(1)}, u32[]{:S(2)}, u32[]{:S(2)}) %collective-permute-start.13) | collective-permute-done | bytes 65568 | tf_op jit(solution)/shard_map/ppermute | solution.py:250
  31.0 0.2 pad_maximum_fusion.1.refs_2_
  31.2 0.2 collective-permute-done.7.refs_1_
  31.4 0.1 collective-permute-start.15
  31.5 2.0 %collective-permute-done.16.refs_4_ = bf16[4,16384]{1,0:T(4,128)(2,1)S(1)} collective-permute-done((bf16[4,16384]{1,0:T(4,128)(2,1)S(1)}, bf16[4,16384]{1,0:T(4,128)(2,1)S(1)}, u32[]{:S(2)}, u32[]{:S(2)}) %collective-permute-start.16) | collective-permute-done | bytes 131104 | tf_op jit(solution)/shard_map/ppermute | solution.py:250
  33.5 0.0 collective-permute-start.17
  33.5 0.0 collective-permute-done.15.refs_3_
  33.5 0.0 copy-done
  33.5 0.7 %first_dots.1 = (f32[28,128]{1,0:T(8,128)S(1)}, bf16[2,16384]{1,0:T(2,128)(2,1)}, f32[2,128]{1,0:T(2,128)}) custom-call(bf16[6,16384]{1,0:T(8,128)(2,1)S(1)} %pad_maximum_fusion.refs_0_, bf16[6,16384]{1,0:T(8,128)(2,1)S(1)} %collective-permute-done.7.refs_1_, bf16[6,16384]{1,0:T(8,128)(2,1)S(1)} %pad_maximum_fusion.1.refs_2_, ...), custom_call_target="tpu_custom_call" | custom-call | bytes 5177856 | tf_op jit(solution)/shard_map/first_dots/pallas_call | solution.py:225
  34.3 0.6 %collective-permute-done.17.refs_0_ = bf16[4,16384]{1,0:T(4,128)(2,1)S(1)} collective-permute-done((bf16[4,16384]{1,0:T(4,128)(2,1)S(1)}, bf16[4,16384]{1,0:T(4,128)(2,1)S(1)}, u32[]{:S(2)}, u32[]{:S(2)}) %collective-permute-start.17) | collective-permute-done | bytes 131104 | tf_op jit(solution)/shard_map/ppermute | solution.py:250
  34.9 1.4 %last_dot.1 = bf16[32,128]{1,0:T(8,128)(2,1)} custom-call(bf16[4,16384]{1,0:T(4,128)(2,1)S(1)} %collective-permute-done.17.refs_0_, f32[28,128]{1,0:T(8,128)S(1)} %get-tuple-element.52.refs_1_, bf16[16384,128]{1,0:T(8,128)(2,1)S(1)} %copy-done), custom_call_target="tpu_custom_call" | custom-call | bytes 4332544 | tf_op jit(solution)/shard_map/last_dot/pallas_call | solution.py:225
  (1 shorter events, 0.0 us)
Async XLA Ops:
  3.6 11.5 %copy-start.1 = (bf16[2,16384]{1,0:T(2,128)(2,1)S(1)}, bf16[2,16384]{1,0:T(2,128)(2,1)}, u32[]{:S(2)}) copy-start(bf16[2,16384]{1,0:T(2,128)(2,1)} %old.3) | copy-start | bytes 196612
  3.6 6.8 %collective-permute-start.8 = (bf16[8,16384]{1,0:T(8,128)(2,1)S(1)}, bf16[8,16384]{1,0:T(8,128)(2,1)S(1)}, u32[]{:S(2)}, u32[]{:S(2)}) collective-permute-start(bf16[8,16384]{1,0:T(8,128)(2,1)S(1)} %get-tuple-element.53), channel_id=1, source_target_pairs={{0,1},{1,0},{2,3},{3,2},{4,5},{5,4},{6,7},{7,6},{8,9},{9,8},{10,11... | collective-permute-start | bytes 786440 | tf_op jit(solution)/shard_map/ppermute | solution.py:250
  4.2 18.3 %copy-start.2 = (f32[16384]{0:T(1024)S(1)}, f32[16384]{0:T(1024)}, u32[]{:S(2)}) copy-start(f32[16384]{0:T(1024)} %param.12) | copy-start | bytes 196612
  4.2 29.4 %copy-start = (bf16[16384,128]{1,0:T(8,128)(2,1)S(1)}, bf16[16384,128]{1,0:T(8,128)(2,1)}, u32[]{:S(2)}) copy-start(bf16[16384,128]{1,0:T(8,128)(2,1)} %refs_2_.1) | copy-start | bytes 12582916
  4.2 1.5 %collective-permute-start = (bf16[8,16384]{1,0:T(8,128)(2,1)S(1)}, bf16[8,16384]{1,0:T(8,128)(2,1)S(1)}, u32[]{:S(2)}, u32[]{:S(2)}) collective-permute-start(bf16[8,16384]{1,0:T(8,128)(2,1)S(1)} %get-tuple-element.54), channel_id=1, source_target_pairs={{0,1},{1,0},{2,3},{3,2},{4,5},{5,4},{6,7},{7,6},{8,9},{9,8},{10,11... | collective-permute-start | bytes 786440 | tf_op jit(solution)/shard_map/ppermute | solution.py:250
  5.8 8.1 %collective-permute-start.1 = (bf16[2,16384]{1,0:T(2,128)(2,1)S(1)}, bf16[2,16384]{1,0:T(2,128)(2,1)S(1)}, u32[]{:S(2)}, u32[]{:S(2)}) collective-permute-start(bf16[2,16384]{1,0:T(2,128)(2,1)S(1)} %get-tuple-element.31), channel_id=1, source_target_pairs={{0,6},{1,7},{2,4},{3,5},{4,2},{5,3},{6,0},{7,1},{8,14},{9,15},{10,... | collective-permute-start | bytes 196616 | tf_op jit(solution)/shard_map/ppermute | solution.py:250
  9.8 4.4 %collective-permute-start.2 = (bf16[2,16384]{1,0:T(2,128)(2,1)S(1)}, bf16[2,16384]{1,0:T(2,128)(2,1)S(1)}, u32[]{:S(2)}, u32[]{:S(2)}) collective-permute-start(bf16[2,16384]{1,0:T(2,128)(2,1)S(1)} %get-tuple-element.32), channel_id=1, source_target_pairs={{0,2},{1,3},{2,0},{3,1},{4,6},{5,7},{6,4},{7,5},{8,10},{9,11},{10,... | collective-permute-start | bytes 196616 | tf_op jit(solution)/shard_map/ppermute | solution.py:250
  10.3 4.9 %collective-permute-start.3 = (bf16[2,16384]{1,0:T(2,128)(2,1)S(1)}, bf16[2,16384]{1,0:T(2,128)(2,1)S(1)}, u32[]{:S(2)}, u32[]{:S(2)}) collective-permute-start(bf16[2,16384]{1,0:T(2,128)(2,1)S(1)} %get-tuple-element.33), channel_id=1, source_target_pairs={{0,4},{1,5},{2,6},{3,7},{4,0},{5,1},{6,2},{7,3},{8,12},{9,13},{10,... | collective-permute-start | bytes 196616 | tf_op jit(solution)/shard_map/ppermute | solution.py:250
  10.5 7.5 %collective-permute-start.9 = (bf16[2,16384]{1,0:T(2,128)(2,1)S(1)}, bf16[2,16384]{1,0:T(2,128)(2,1)S(1)}, u32[]{:S(2)}, u32[]{:S(2)}) collective-permute-start(bf16[2,16384]{1,0:T(2,128)(2,1)S(1)} %get-tuple-element.38), channel_id=1, source_target_pairs={{0,6},{1,7},{2,4},{3,5},{4,2},{5,3},{6,0},{7,1},{8,14},{9,15},{10,... | collective-permute-start | bytes 196616 | tf_op jit(solution)/shard_map/ppermute | solution.py:250
  13.4 4.6 %collective-permute-start.10 = (bf16[2,16384]{1,0:T(2,128)(2,1)S(1)}, bf16[2,16384]{1,0:T(2,128)(2,1)S(1)}, u32[]{:S(2)}, u32[]{:S(2)}) collective-permute-start(bf16[2,16384]{1,0:T(2,128)(2,1)S(1)} %get-tuple-element.39), channel_id=1, source_target_pairs={{0,2},{1,3},{2,0},{3,1},{4,6},{5,7},{6,4},{7,5},{8,10},{9,11},{10,... | collective-permute-start | bytes 196616 | tf_op jit(solution)/shard_map/ppermute | solution.py:250
  13.9 4.3 %collective-permute-start.11 = (bf16[2,16384]{1,0:T(2,128)(2,1)S(1)}, bf16[2,16384]{1,0:T(2,128)(2,1)S(1)}, u32[]{:S(2)}, u32[]{:S(2)}) collective-permute-start(bf16[2,16384]{1,0:T(2,128)(2,1)S(1)} %get-tuple-element.40), channel_id=1, source_target_pairs={{0,4},{1,5},{2,6},{3,7},{4,0},{5,1},{6,2},{7,3},{8,12},{9,13},{10,... | collective-permute-start | bytes 196616 | tf_op jit(solution)/shard_map/ppermute | solution.py:250
  15.4 7.1 %collective-permute-start.4 = (bf16[2,16384]{1,0:T(2,128)(2,1)S(1)}, bf16[2,16384]{1,0:T(2,128)(2,1)S(1)}, u32[]{:S(2)}, u32[]{:S(2)}) collective-permute-start(bf16[2,16384]{1,0:T(2,128)(2,1)S(1)} %get-tuple-element.35), channel_id=1, source_target_pairs={{0,8},{1,9},{2,10},{3,11},{4,12},{5,13},{6,14},{7,15},{8,0},{9,1},... | collective-permute-start | bytes 196616 | tf_op jit(solution)/shard_map/ppermute | solution.py:250
  18.4 6.0 %collective-permute-start.12 = (bf16[2,16384]{1,0:T(2,128)(2,1)S(1)}, bf16[2,16384]{1,0:T(2,128)(2,1)S(1)}, u32[]{:S(2)}, u32[]{:S(2)}) collective-permute-start(bf16[2,16384]{1,0:T(2,128)(2,1)S(1)} %get-tuple-element.42), channel_id=1, source_target_pairs={{0,8},{1,9},{2,10},{3,11},{4,12},{5,13},{6,14},{7,15},{8,0},{9,1},... | collective-permute-start | bytes 196616 | tf_op jit(solution)/shard_map/ppermute | solution.py:250
  22.9 5.6 %collective-permute-start.6 = (bf16[2,16384]{1,0:T(2,128)(2,1)S(1)}, bf16[2,16384]{1,0:T(2,128)(2,1)S(1)}, u32[]{:S(2)}, u32[]{:S(2)}) collective-permute-start(bf16[2,16384]{1,0:T(2,128)(2,1)S(1)} %get-tuple-element.36.refs_0_), channel_id=1, source_target_pairs={{0,6},{1,7},{2,4},{3,5},{4,2},{5,3},{6,0},{7,1},{8,14},{9,15},{10,... | collective-permute-start | bytes 196616 | tf_op jit(solution)/shard_map/ppermute | solution.py:250
  24.1 5.4 %collective-permute-start.5 = (bf16[2,16384]{1,0:T(2,128)(2,1)S(1)}, bf16[2,16384]{1,0:T(2,128)(2,1)S(1)}, u32[]{:S(2)}, u32[]{:S(2)}) collective-permute-start(bf16[2,16384]{1,0:T(2,128)(2,1)S(1)} %get-tuple-element.36.refs_0_), channel_id=1, source_target_pairs={{0,2},{1,3},{2,0},{3,1},{4,6},{5,7},{6,4},{7,5},{8,10},{9,11},{10,... | collective-permute-start | bytes 196616 | tf_op jit(solution)/shard_map/ppermute | solution.py:250
  24.9 5.4 %collective-permute-start.14 = (bf16[2,16384]{1,0:T(2,128)(2,1)S(1)}, bf16[2,16384]{1,0:T(2,128)(2,1)S(1)}, u32[]{:S(2)}, u32[]{:S(2)}) collective-permute-start(bf16[2,16384]{1,0:T(2,128)(2,1)S(1)} %get-tuple-element.45), channel_id=1, source_target_pairs={{0,6},{1,7},{2,4},{3,5},{4,2},{5,3},{6,0},{7,1},{8,14},{9,15},{10,... | collective-permute-start | bytes 196616 | tf_op jit(solution)/shard_map/ppermute | solution.py:250
  26.7 4.3 %collective-permute-start.13 = (bf16[2,16384]{1,0:T(2,128)(2,1)S(1)}, bf16[2,16384]{1,0:T(2,128)(2,1)S(1)}, u32[]{:S(2)}, u32[]{:S(2)}) collective-permute-start(bf16[2,16384]{1,0:T(2,128)(2,1)S(1)} %get-tuple-element.45), channel_id=1, source_target_pairs={{0,2},{1,3},{2,0},{3,1},{4,6},{5,7},{6,4},{7,5},{8,10},{9,11},{10,... | collective-permute-start | bytes 196616 | tf_op jit(solution)/shard_map/ppermute | solution.py:250
  28.6 5.0 %collective-permute-start.16 = (bf16[4,16384]{1,0:T(4,128)(2,1)S(1)}, bf16[4,16384]{1,0:T(4,128)(2,1)S(1)}, u32[]{:S(2)}, u32[]{:S(2)}) collective-permute-start(bf16[4,16384]{1,0:T(4,128)(2,1)S(1)} %get-tuple-element.47), channel_id=1, source_target_pairs={{0,4},{1,5},{2,6},{3,7},{4,0},{5,1},{6,2},{7,3},{8,12},{9,13},{10,... | collective-permute-start | bytes 393224 | tf_op jit(solution)/shard_map/ppermute | solution.py:250
  29.8 1.6 %collective-permute-start.7 = (bf16[6,16384]{1,0:T(8,128)(2,1)S(1)}, bf16[6,16384]{1,0:T(8,128)(2,1)S(1)}, u32[]{:S(2)}, u32[]{:S(2)}) collective-permute-start(bf16[6,16384]{1,0:T(8,128)(2,1)S(1)} %pad_maximum_fusion.refs_0_), channel_id=1, source_target_pairs={{0,1},{1,0},{2,3},{3,2},{4,5},{5,4},{6,7},{7,6},{8,9},{9,8},{10,11... | collective-permute-start | bytes 589832 | tf_op jit(solution)/shard_map/ppermute | solution.py:250
  31.4 2.2 %collective-permute-start.15 = (bf16[6,16384]{1,0:T(8,128)(2,1)S(1)}, bf16[6,16384]{1,0:T(8,128)(2,1)S(1)}, u32[]{:S(2)}, u32[]{:S(2)}) collective-permute-start(bf16[6,16384]{1,0:T(8,128)(2,1)S(1)} %pad_maximum_fusion.1.refs_2_), channel_id=1, source_target_pairs={{0,1},{1,0},{2,3},{3,2},{4,5},{5,4},{6,7},{7,6},{8,9},{9,8},{10,11... | collective-permute-start | bytes 589832 | tf_op jit(solution)/shard_map/ppermute | solution.py:250
  33.5 1.3 %collective-permute-start.17 = (bf16[4,16384]{1,0:T(4,128)(2,1)S(1)}, bf16[4,16384]{1,0:T(4,128)(2,1)S(1)}, u32[]{:S(2)}, u32[]{:S(2)}) collective-permute-start(bf16[4,16384]{1,0:T(4,128)(2,1)S(1)} %collective-permute-done.16.refs_4_), channel_id=1, source_target_pairs={{0,1},{1,0},{2,3},{3,2},{4,5},{5,4},{6,7},{7,6},{8,9},{9,8},{10,11... | collective-permute-start | bytes 393224 | tf_op jit(solution)/shard_map/ppermute | solution.py:250

commit v16 on v15

--- a/solution.py
+++ b/solution.py
@@ -12,7 +12,7 @@
 EPS = 1e-06
 F32 = jnp.float32
 BF16 = jnp.bfloat16
-PIECES = 4
+PIECES = 16
 STEPS = 8
 VMEM_LIMIT = 24 << 20
 SMALL_LIMIT = 16 << 20
@@ -180,7 +180,20 @@
     return total
 
 
-def first_dots_kernel(*refs):
+def placed(n, tokens, values, side, order):
+    count = values.shape[0]
+    part = count // len(order)
+    at = lax.broadcasted_iota(jnp.int32, (tokens, count), 1)
+    row = at & (part - 1)
+    for k, (which, place) in enumerate(order):
+        here = (at >> (part.bit_length() - 1)) == k
+        row = row + jnp.where(here, (8 * side + 4 * which + place) * part, 0)
+    token = lax.broadcasted_iota(jnp.int32, (tokens, count), 0)
+    pick = (owner_token(row, lax.axis_index("tp"), n) == token).astype(F32).astype(BF16)
+    return jnp.dot(pick, values.astype(BF16), preferred_element_type=F32)
+
+
+def first_dots_kernel(n, groups, *refs):
     *rows, weight, codes, scales, out, codes_out, scales_out, sems = refs
     copies = [
         pltpu.make_async_copy(codes, codes_out, sems.at[0]),
@@ -188,35 +201,21 @@
     ]
     for copy in copies:
         copy.start()
-    out[...] = times(rows, weight)
+    values = times(rows, weight)
+    total = jnp.zeros(out.shape, F32)
+    start = 0
+    for ref, (side, order) in zip(rows, groups):
+        stop = start + ref.shape[0]
+        total += placed(n, out.shape[0], values[start:stop], side, order)
+        start = stop
+    out[...] = total
     for copy in copies:
         copy.wait()
 
 
-def last_dot_kernel(n, orders, *refs):
-    *rows, before, weight, out = refs
-    device = lax.axis_index("tp")
-    tokens = out.shape[0]
-    part = tokens // 16
-    total = jnp.zeros(out.shape, F32)
-    groups = [(side, order) for order in range(len(orders)) for side in range(2)]
-    start = 0
-    for side, order in groups:
-        count = len(orders[order]) * part
-        if (side, order) == groups[-1]:
-            values = times(rows, weight)
-        else:
-            values = before[start : start + count]
-            start += count
-        at = lax.broadcasted_iota(jnp.int32, (tokens, count), 1)
-        row = at & (part - 1)
-        for k, (which, place) in enumerate(orders[order]):
-            here = (at >> (part.bit_length() - 1)) == k
-            row = row + jnp.where(here, (8 * side + 4 * which + place) * part, 0)
-        token = lax.broadcasted_iota(jnp.int32, (tokens, count), 0)
-        pick = (owner_token(row, device, n) == token).astype(F32).astype(BF16)
-        total += jnp.dot(pick, values.astype(BF16), preferred_element_type=F32)
-    out[...] = total.astype(BF16)
+def last_dot_kernel(n, group, rows, before, weight, out):
+    values = times([rows], weight)
+    out[...] = (before[...] + placed(n, out.shape[0], values, *group)).astype(BF16)
 
 
 def local_call(kernel, shapes, name, *operands, scratch=()):
@@ -297,19 +296,21 @@
     late, _ = lax.optimization_barrier((late, early_other))
     both_other, late_other = swap(both, 1), swap(late, 1)
     orders = [(0, 2), (0, 1), (0, 0)], [(1, 2), (1, 1), (1, 0)], [(0, 3), (1, 3)]
-    width = q_weight.shape[1]
+    groups = [(side, order) for order in orders for side in range(2)]
+    shape = (tokens, q_weight.shape[1])
     outs = second[1:3]
-    shapes = [((half + 6 * part, width), F32)] + [(x.shape, x.dtype, pltpu.HBM) for x in outs]
+    shapes = [(shape, F32)] + [(x.shape, x.dtype, pltpu.HBM) for x in outs]
     before, *outs = local_call(
-        first_dots_kernel,
+        functools.partial(first_dots_kernel, n, groups[:-1]),
         shapes,
         "first_dots",
         *(early, early_other, late, late_other, both, q_weight, *outs),
         scratch=[pltpu.SemaphoreType.DMA((2,))],
     )
-    kernel = functools.partial(last_dot_kernel, n, orders)
-    shapes = [((tokens, width), BF16)]
-    (next_queries,) = local_call(kernel, shapes, "last_dot", both_other, before, q_weight)
+    kernel = functools.partial(last_dot_kernel, n, groups[-1])
+    (next_queries,) = local_call(
+        kernel, [(shape, BF16)], "last_dot", both_other, before, q_weight
+    )
     return (*outs, next_queries)
 
 

time: 36.4 us -> 36.7 us (level)
  Pallas kernels: 5.96 us -> 6.42 us
  transfers between devices with their start and end apart: 18 -> 18, of which waited for: 10 -> 10; matrix products, arithmetic and copies ran while one was open for 3% -> 3% of each run, Pallas kernels for 6% -> 7%
where the time goes in v16:
time: 36.7 us; the launch traced here: 36.5 us
  starting transfers between devices  19.3 us (53%)
  waiting for transfers between devices  8.32 us (23%)
  Pallas kernels  6.42 us (17%)
  matrix products  1.31 us (4%)
  between operations  0.72 us (2%)
  other arithmetic  0.43 us (1%)
    ppermute x18, starting transfers between devices, swap(): return lax.ppermute(x, 'tp', [(i, i ^ distance) for i in range(n)])  19.3 us
    ppermute x18, waiting for transfers between devices, swap(): return lax.ppermute(x, 'tp', [(i, i ^ distance) for i in range(n)])  8.32 us
    pallas_call x8, Pallas kernels, local_call(): pl.pallas_call(kernel, out_shape=[(space[0] if space else jax.ShapeDtypeS...  3.82 us
    pallas_call x1, Pallas kernels, attend(): pl.pallas_call(functools.partial(attend_kernel, n), out_shape=[jax.ShapeD...  2.6 us
  transfers between devices with their start and end apart: 18, of which 10 were waited for; matrix products, arithmetic and copies ran while one was open for 3% of the time, Pallas kernels for 7%

profile of v16, /device:TPU:0, one launch (start us, length us, event | category | flops | bytes accessed | tf_op | source)
XLA Modules:
  0.0 36.5 jit_solution(12692322316085240812)
XLA Ops:
  0.6 2.6 %attend.1 = (bf16[32,128]{1,0:T(8,128)(2,1)S(1)}, bf16[128,16384]{1,0:T(8,128)(2,1)S(1)}) custom-call(bf16[32,128]{1,0:T(8,128)(2,1)} %queries.1, bf16[32,1024]{1,0:T(8,128)(2,1)} %keys.1, bf16[32,1024]{1,0:T(8,128)(2,1)} %values.1, bf16[128,16384]{1,0:T(8,128)(2,1)} %weight.2), custom_call_target="tpu_custom_call" | custom-call | bytes 4194304 | tf_op jit(solution)/shard_map/attend/pallas_call | solution.py:86
  3.2 0.7 %convolution_convert_fusion = bf16[16,16384]{1,0:T(8,128)(2,1)S(1)} fusion(bf16[128,16384]{1,0:T(8,128)(2,1)S(1)} %get-tuple-element.29, bf16[32,128]{1,0:T(8,128)(2,1)S(1)} %get-tuple-element.28), kind=kOutput, calls=%fused_computation | convolution fusion | flops 67371008 | bytes 4722688 | tf_op jit(solution)/shard_map/dot_general | solution.py:255
  3.9 0.0 copy-start.1
  4.0 0.5 %collective-permute-start.8 = (bf16[8,16384]{1,0:T(8,128)(2,1)S(1)}, bf16[8,16384]{1,0:T(8,128)(2,1)S(1)}, u32[]{:S(2)}, u32[]{:S(2)}) collective-permute-start(bf16[8,16384]{1,0:T(8,128)(2,1)S(1)} %get-tuple-element.53), channel_id=1, source_target_pairs={{0,1},{1,0},{2,3},{3,2},{4,5},{5,4},{6,7},{7,6},{8,9},{9,8},{10,11... | collective-permute-start | bytes 786440 | tf_op jit(solution)/shard_map/ppermute | solution.py:249
  4.5 0.0 copy-start.2
  4.5 0.0 copy-start
  4.5 0.1 collective-permute-start
  4.6 0.7 %fusion.1.kept = f32[16,16384]{1,0:T(8,128)S(1)} fusion(bf16[128,16384]{1,0:T(8,128)(2,1)S(1)} %get-tuple-element.29, bf16[32,128]{1,0:T(8,128)(2,1)S(1)} %get-tuple-element.28), kind=kOutput, calls=%fused_computation.4 | convolution fusion | flops 67108864 | bytes 5246976 | tf_op jit(solution)/shard_map/dot_general | solution.py:257
  5.2 0.8 %collective-permute-done.got = bf16[8,16384]{1,0:T(8,128)(2,1)S(1)} collective-permute-done((bf16[8,16384]{1,0:T(8,128)(2,1)S(1)}, bf16[8,16384]{1,0:T(8,128)(2,1)S(1)}, u32[]{:S(2)}, u32[]{:S(2)}) %collective-permute-start) | collective-permute-done | bytes 262176 | tf_op jit(solution)/shard_map/ppermute | solution.py:249
  6.0 0.1 split0.1
  6.1 4.0 %collective-permute-start.1 = (bf16[2,16384]{1,0:T(2,128)(2,1)S(1)}, bf16[2,16384]{1,0:T(2,128)(2,1)S(1)}, u32[]{:S(2)}, u32[]{:S(2)}) collective-permute-start(bf16[2,16384]{1,0:T(2,128)(2,1)S(1)} %get-tuple-element.31), channel_id=1, source_target_pairs={{0,6},{1,7},{2,4},{3,5},{4,2},{5,3},{6,0},{7,1},{8,14},{9,15},{10,... | collective-permute-start | bytes 196616 | tf_op jit(solution)/shard_map/ppermute | solution.py:249
  10.1 0.5 %collective-permute-start.2 = (bf16[2,16384]{1,0:T(2,128)(2,1)S(1)}, bf16[2,16384]{1,0:T(2,128)(2,1)S(1)}, u32[]{:S(2)}, u32[]{:S(2)}) collective-permute-start(bf16[2,16384]{1,0:T(2,128)(2,1)S(1)} %get-tuple-element.32), channel_id=1, source_target_pairs={{0,2},{1,3},{2,0},{3,1},{4,6},{5,7},{6,4},{7,5},{8,10},{9,11},{10,... | collective-permute-start | bytes 196616 | tf_op jit(solution)/shard_map/ppermute | solution.py:249
  10.6 0.1 collective-permute-start.3
  10.7 0.0 collective-permute-done.8.got
  10.7 0.1 split1.1
  10.8 2.9 %collective-permute-start.9 = (bf16[2,16384]{1,0:T(2,128)(2,1)S(1)}, bf16[2,16384]{1,0:T(2,128)(2,1)S(1)}, u32[]{:S(2)}, u32[]{:S(2)}) collective-permute-start(bf16[2,16384]{1,0:T(2,128)(2,1)S(1)} %get-tuple-element.38), channel_id=1, source_target_pairs={{0,6},{1,7},{2,4},{3,5},{4,2},{5,3},{6,0},{7,1},{8,14},{9,15},{10,... | collective-permute-start | bytes 196616 | tf_op jit(solution)/shard_map/ppermute | solution.py:249
  13.7 0.5 %collective-permute-start.10 = (bf16[2,16384]{1,0:T(2,128)(2,1)S(1)}, bf16[2,16384]{1,0:T(2,128)(2,1)S(1)}, u32[]{:S(2)}, u32[]{:S(2)}) collective-permute-start(bf16[2,16384]{1,0:T(2,128)(2,1)S(1)} %get-tuple-element.39), channel_id=1, source_target_pairs={{0,2},{1,3},{2,0},{3,1},{4,6},{5,7},{6,4},{7,5},{8,10},{9,11},{10,... | collective-permute-start | bytes 196616 | tf_op jit(solution)/shard_map/ppermute | solution.py:249
  14.3 0.0 collective-permute-done.1.refs_0_
  14.3 0.1 collective-permute-start.11
  14.4 0.0 collective-permute-done.2.refs_1_
  14.4 1.1 %collective-permute-done.3.refs_2_ = bf16[2,16384]{1,0:T(2,128)(2,1)S(1)} collective-permute-done((bf16[2,16384]{1,0:T(2,128)(2,1)S(1)}, bf16[2,16384]{1,0:T(2,128)(2,1)S(1)}, u32[]{:S(2)}, u32[]{:S(2)}) %collective-permute-start.3) | collective-permute-done | bytes 65568 | tf_op jit(solution)/shard_map/ppermute | solution.py:249
  15.5 0.0 copy-done.1
  15.5 0.2 settle0.1
  15.7 2.6 %collective-permute-start.4 = (bf16[2,16384]{1,0:T(2,128)(2,1)S(1)}, bf16[2,16384]{1,0:T(2,128)(2,1)S(1)}, u32[]{:S(2)}, u32[]{:S(2)}) collective-permute-start(bf16[2,16384]{1,0:T(2,128)(2,1)S(1)} %get-tuple-element.35), channel_id=1, source_target_pairs={{0,8},{1,9},{2,10},{3,11},{4,12},{5,13},{6,14},{7,15},{8,0},{9,1},... | collective-permute-start | bytes 196616 | tf_op jit(solution)/shard_map/ppermute | solution.py:249
  18.3 0.0 collective-permute-done.9.refs_0_
  18.3 0.0 collective-permute-done.10.refs_1_
  18.3 0.3 collective-permute-done.11.refs_2_
  18.6 0.2 settle1.1
  18.8 2.6 %collective-permute-start.12 = (bf16[2,16384]{1,0:T(2,128)(2,1)S(1)}, bf16[2,16384]{1,0:T(2,128)(2,1)S(1)}, u32[]{:S(2)}, u32[]{:S(2)}) collective-permute-start(bf16[2,16384]{1,0:T(2,128)(2,1)S(1)} %get-tuple-element.42), channel_id=1, source_target_pairs={{0,8},{1,9},{2,10},{3,11},{4,12},{5,13},{6,14},{7,15},{8,0},{9,1},... | collective-permute-start | bytes 196616 | tf_op jit(solution)/shard_map/ppermute | solution.py:249
  21.4 1.4 %collective-permute-done.4.arrived = bf16[2,16384]{1,0:T(2,128)(2,1)S(1)} collective-permute-done((bf16[2,16384]{1,0:T(2,128)(2,1)S(1)}, bf16[2,16384]{1,0:T(2,128)(2,1)S(1)}, u32[]{:S(2)}, u32[]{:S(2)}) %collective-permute-start.4) | collective-permute-done | bytes 65568 | tf_op jit(solution)/shard_map/ppermute | solution.py:249
  22.8 0.0 copy-done.2
  22.8 0.4 %encode0.1 = (bf16[2,16384]{1,0:T(2,128)(2,1)S(1)}, bf16[2,16384]{1,0:T(2,128)(2,1)S(1)}, f32[2,128]{1,0:T(2,128)S(1)}) custom-call(f32[2,16384]{1,0:T(2,128)S(1)} %get-tuple-element.34.total, bf16[2,16384]{1,0:T(2,128)(2,1)S(1)} %collective-permute-done.4.arrived, f32[1,16384]{1,0:T(1,128)S(1)} %bitcast.3), custom_call_target="tpu_custom_call" | custom-call | bytes 163840 | tf_op jit(solution)/shard_map/encode0/pallas_call | solution.py:224
  23.2 1.4 %collective-permute-start.6 = (bf16[2,16384]{1,0:T(2,128)(2,1)S(1)}, bf16[2,16384]{1,0:T(2,128)(2,1)S(1)}, u32[]{:S(2)}, u32[]{:S(2)}) collective-permute-start(bf16[2,16384]{1,0:T(2,128)(2,1)S(1)} %get-tuple-element.36.refs_0_), channel_id=1, source_target_pairs={{0,6},{1,7},{2,4},{3,5},{4,2},{5,3},{6,0},{7,1},{8,14},{9,15},{10,... | collective-permute-start | bytes 196616 | tf_op jit(solution)/shard_map/ppermute | solution.py:249
  24.6 0.2 collective-permute-start.5
  24.7 0.0 collective-permute-done.12.arrived
  24.7 0.5 %encode1.1 = (bf16[2,16384]{1,0:T(2,128)(2,1)S(1)}, bf16[2,16384]{1,0:T(2,128)(2,1)S(1)}, f32[2,128]{1,0:T(2,128)S(1)}, bf16[4,16384]{1,0:T(4,128)(2,1)S(1)}) custom-call(f32[2,16384]{1,0:T(2,128)S(1)} %get-tuple-element.41.total, bf16[2,16384]{1,0:T(2,128)(2,1)S(1)} %collective-permute-done.12.arrived, f32[1,16384]{1,0:T(1,128)S(1)} %bitcast.4, ...), custom_call_target="tpu_custom_call" | custom-call | bytes 295424 | tf_op jit(solution)/shard_map/encode1/pallas_call | solution.py:224
  25.3 1.8 %collective-permute-start.14 = (bf16[2,16384]{1,0:T(2,128)(2,1)S(1)}, bf16[2,16384]{1,0:T(2,128)(2,1)S(1)}, u32[]{:S(2)}, u32[]{:S(2)}) collective-permute-start(bf16[2,16384]{1,0:T(2,128)(2,1)S(1)} %get-tuple-element.45), channel_id=1, source_target_pairs={{0,6},{1,7},{2,4},{3,5},{4,2},{5,3},{6,0},{7,1},{8,14},{9,15},{10,... | collective-permute-start | bytes 196616 | tf_op jit(solution)/shard_map/ppermute | solution.py:249
  27.0 1.8 %collective-permute-start.13 = (bf16[2,16384]{1,0:T(2,128)(2,1)S(1)}, bf16[2,16384]{1,0:T(2,128)(2,1)S(1)}, u32[]{:S(2)}, u32[]{:S(2)}) collective-permute-start(bf16[2,16384]{1,0:T(2,128)(2,1)S(1)} %get-tuple-element.45), channel_id=1, source_target_pairs={{0,2},{1,3},{2,0},{3,1},{4,6},{5,7},{6,4},{7,5},{8,10},{9,11},{10,... | collective-permute-start | bytes 196616 | tf_op jit(solution)/shard_map/ppermute | solution.py:249
  28.8 0.0 collective-permute-start.16
  28.9 0.0 collective-permute-done.6
  28.9 1.0 %collective-permute-done.5 = bf16[2,16384]{1,0:T(2,128)(2,1)S(1)} collective-permute-done((bf16[2,16384]{1,0:T(2,128)(2,1)S(1)}, bf16[2,16384]{1,0:T(2,128)(2,1)S(1)}, u32[]{:S(2)}, u32[]{:S(2)}) %collective-permute-start.5) | collective-permute-done | bytes 65568 | tf_op jit(solution)/shard_map/ppermute | solution.py:249
  29.8 0.2 pad_maximum_fusion.refs_0_
  30.0 0.1 collective-permute-start.7
  30.1 0.4 %collective-permute-done.14 = bf16[2,16384]{1,0:T(2,128)(2,1)S(1)} collective-permute-done((bf16[2,16384]{1,0:T(2,128)(2,1)S(1)}, bf16[2,16384]{1,0:T(2,128)(2,1)S(1)}, u32[]{:S(2)}, u32[]{:S(2)}) %collective-permute-start.14) | collective-permute-done | bytes 65568 | tf_op jit(solution)/shard_map/ppermute | solution.py:249
  30.6 0.8 %collective-permute-done.13 = bf16[2,16384]{1,0:T(2,128)(2,1)S(1)} collective-permute-done((bf16[2,16384]{1,0:T(2,128)(2,1)S(1)}, bf16[2,16384]{1,0:T(2,128)(2,1)S(1)}, u32[]{:S(2)}, u32[]{:S(2)}) %collective-permute-start.13) | collective-permute-done | bytes 65568 | tf_op jit(solution)/shard_map/ppermute | solution.py:249
  31.3 0.2 pad_maximum_fusion.1.refs_2_
  31.5 0.1 collective-permute-done.7.refs_1_
  31.6 0.1 collective-permute-start.15
  31.8 2.0 %collective-permute-done.16.refs_4_ = bf16[4,16384]{1,0:T(4,128)(2,1)S(1)} collective-permute-done((bf16[4,16384]{1,0:T(4,128)(2,1)S(1)}, bf16[4,16384]{1,0:T(4,128)(2,1)S(1)}, u32[]{:S(2)}, u32[]{:S(2)}) %collective-permute-start.16) | collective-permute-done | bytes 131104 | tf_op jit(solution)/shard_map/ppermute | solution.py:249
  33.8 0.0 collective-permute-start.17
  33.8 0.0 collective-permute-done.15.refs_3_
  33.8 0.0 copy-done
  33.8 0.9 %first_dots.1 = (f32[32,128]{1,0:T(8,128)S(1)}, bf16[2,16384]{1,0:T(2,128)(2,1)}, f32[2,128]{1,0:T(2,128)}) custom-call(bf16[6,16384]{1,0:T(8,128)(2,1)S(1)} %pad_maximum_fusion.refs_0_, bf16[6,16384]{1,0:T(8,128)(2,1)S(1)} %collective-permute-done.7.refs_1_, bf16[6,16384]{1,0:T(8,128)(2,1)S(1)} %pad_maximum_fusion.1.refs_2_, ...), custom_call_target="tpu_custom_call" | custom-call | bytes 5177856 | tf_op jit(solution)/shard_map/first_dots/pallas_call | solution.py:224
  34.8 0.4 %collective-permute-done.17.rows = bf16[4,16384]{1,0:T(4,128)(2,1)S(1)} collective-permute-done((bf16[4,16384]{1,0:T(4,128)(2,1)S(1)}, bf16[4,16384]{1,0:T(4,128)(2,1)S(1)}, u32[]{:S(2)}, u32[]{:S(2)}) %collective-permute-start.17) | collective-permute-done | bytes 131104 | tf_op jit(solution)/shard_map/ppermute | solution.py:249
  35.2 1.4 %last_dot.1 = bf16[32,128]{1,0:T(8,128)(2,1)} custom-call(bf16[4,16384]{1,0:T(4,128)(2,1)S(1)} %collective-permute-done.17.rows, f32[32,128]{1,0:T(8,128)S(1)} %get-tuple-element.52.before, bf16[16384,128]{1,0:T(8,128)(2,1)S(1)} %copy-done), custom_call_target="tpu_custom_call" | custom-call | bytes 4333568 | tf_op jit(solution)/shard_map/last_dot/pallas_call | solution.py:224
  (1 shorter events, 0.0 us)
Async XLA Ops:
  3.9 11.6 %copy-start.1 = (bf16[2,16384]{1,0:T(2,128)(2,1)S(1)}, bf16[2,16384]{1,0:T(2,128)(2,1)}, u32[]{:S(2)}) copy-start(bf16[2,16384]{1,0:T(2,128)(2,1)} %old.3) | copy-start | bytes 196612
  4.0 6.8 %collective-permute-start.8 = (bf16[8,16384]{1,0:T(8,128)(2,1)S(1)}, bf16[8,16384]{1,0:T(8,128)(2,1)S(1)}, u32[]{:S(2)}, u32[]{:S(2)}) collective-permute-start(bf16[8,16384]{1,0:T(8,128)(2,1)S(1)} %get-tuple-element.53), channel_id=1, source_target_pairs={{0,1},{1,0},{2,3},{3,2},{4,5},{5,4},{6,7},{7,6},{8,9},{9,8},{10,11... | collective-permute-start | bytes 786440 | tf_op jit(solution)/shard_map/ppermute | solution.py:249
  4.5 18.3 %copy-start.2 = (f32[16384]{0:T(1024)S(1)}, f32[16384]{0:T(1024)}, u32[]{:S(2)}) copy-start(f32[16384]{0:T(1024)} %param.12) | copy-start | bytes 196612
  4.5 29.3 %copy-start = (bf16[16384,128]{1,0:T(8,128)(2,1)S(1)}, bf16[16384,128]{1,0:T(8,128)(2,1)}, u32[]{:S(2)}) copy-start(bf16[16384,128]{1,0:T(8,128)(2,1)} %weight.3) | copy-start | bytes 12582916
  4.5 1.5 %collective-permute-start = (bf16[8,16384]{1,0:T(8,128)(2,1)S(1)}, bf16[8,16384]{1,0:T(8,128)(2,1)S(1)}, u32[]{:S(2)}, u32[]{:S(2)}) collective-permute-start(bf16[8,16384]{1,0:T(8,128)(2,1)S(1)} %get-tuple-element.54), channel_id=1, source_target_pairs={{0,1},{1,0},{2,3},{3,2},{4,5},{5,4},{6,7},{7,6},{8,9},{9,8},{10,11... | collective-permute-start | bytes 786440 | tf_op jit(solution)/shard_map/ppermute | solution.py:249
  6.1 8.1 %collective-permute-start.1 = (bf16[2,16384]{1,0:T(2,128)(2,1)S(1)}, bf16[2,16384]{1,0:T(2,128)(2,1)S(1)}, u32[]{:S(2)}, u32[]{:S(2)}) collective-permute-start(bf16[2,16384]{1,0:T(2,128)(2,1)S(1)} %get-tuple-element.31), channel_id=1, source_target_pairs={{0,6},{1,7},{2,4},{3,5},{4,2},{5,3},{6,0},{7,1},{8,14},{9,15},{10,... | collective-permute-start | bytes 196616 | tf_op jit(solution)/shard_map/ppermute | solution.py:249
  10.1 4.3 %collective-permute-start.2 = (bf16[2,16384]{1,0:T(2,128)(2,1)S(1)}, bf16[2,16384]{1,0:T(2,128)(2,1)S(1)}, u32[]{:S(2)}, u32[]{:S(2)}) collective-permute-start(bf16[2,16384]{1,0:T(2,128)(2,1)S(1)} %get-tuple-element.32), channel_id=1, source_target_pairs={{0,2},{1,3},{2,0},{3,1},{4,6},{5,7},{6,4},{7,5},{8,10},{9,11},{10,... | collective-permute-start | bytes 196616 | tf_op jit(solution)/shard_map/ppermute | solution.py:249
  10.6 4.9 %collective-permute-start.3 = (bf16[2,16384]{1,0:T(2,128)(2,1)S(1)}, bf16[2,16384]{1,0:T(2,128)(2,1)S(1)}, u32[]{:S(2)}, u32[]{:S(2)}) collective-permute-start(bf16[2,16384]{1,0:T(2,128)(2,1)S(1)} %get-tuple-element.33), channel_id=1, source_target_pairs={{0,4},{1,5},{2,6},{3,7},{4,0},{5,1},{6,2},{7,3},{8,12},{9,13},{10,... | collective-permute-start | bytes 196616 | tf_op jit(solution)/shard_map/ppermute | solution.py:249
  10.8 7.5 %collective-permute-start.9 = (bf16[2,16384]{1,0:T(2,128)(2,1)S(1)}, bf16[2,16384]{1,0:T(2,128)(2,1)S(1)}, u32[]{:S(2)}, u32[]{:S(2)}) collective-permute-start(bf16[2,16384]{1,0:T(2,128)(2,1)S(1)} %get-tuple-element.38), channel_id=1, source_target_pairs={{0,6},{1,7},{2,4},{3,5},{4,2},{5,3},{6,0},{7,1},{8,14},{9,15},{10,... | collective-permute-start | bytes 196616 | tf_op jit(solution)/shard_map/ppermute | solution.py:249
  13.7 4.6 %collective-permute-start.10 = (bf16[2,16384]{1,0:T(2,128)(2,1)S(1)}, bf16[2,16384]{1,0:T(2,128)(2,1)S(1)}, u32[]{:S(2)}, u32[]{:S(2)}) collective-permute-start(bf16[2,16384]{1,0:T(2,128)(2,1)S(1)} %get-tuple-element.39), channel_id=1, source_target_pairs={{0,2},{1,3},{2,0},{3,1},{4,6},{5,7},{6,4},{7,5},{8,10},{9,11},{10,... | collective-permute-start | bytes 196616 | tf_op jit(solution)/shard_map/ppermute | solution.py:249
  14.3 4.3 %collective-permute-start.11 = (bf16[2,16384]{1,0:T(2,128)(2,1)S(1)}, bf16[2,16384]{1,0:T(2,128)(2,1)S(1)}, u32[]{:S(2)}, u32[]{:S(2)}) collective-permute-start(bf16[2,16384]{1,0:T(2,128)(2,1)S(1)} %get-tuple-element.40), channel_id=1, source_target_pairs={{0,4},{1,5},{2,6},{3,7},{4,0},{5,1},{6,2},{7,3},{8,12},{9,13},{10,... | collective-permute-start | bytes 196616 | tf_op jit(solution)/shard_map/ppermute | solution.py:249
  15.7 7.1 %collective-permute-start.4 = (bf16[2,16384]{1,0:T(2,128)(2,1)S(1)}, bf16[2,16384]{1,0:T(2,128)(2,1)S(1)}, u32[]{:S(2)}, u32[]{:S(2)}) collective-permute-start(bf16[2,16384]{1,0:T(2,128)(2,1)S(1)} %get-tuple-element.35), channel_id=1, source_target_pairs={{0,8},{1,9},{2,10},{3,11},{4,12},{5,13},{6,14},{7,15},{8,0},{9,1},... | collective-permute-start | bytes 196616 | tf_op jit(solution)/shard_map/ppermute | solution.py:249
  18.8 6.0 %collective-permute-start.12 = (bf16[2,16384]{1,0:T(2,128)(2,1)S(1)}, bf16[2,16384]{1,0:T(2,128)(2,1)S(1)}, u32[]{:S(2)}, u32[]{:S(2)}) collective-permute-start(bf16[2,16384]{1,0:T(2,128)(2,1)S(1)} %get-tuple-element.42), channel_id=1, source_target_pairs={{0,8},{1,9},{2,10},{3,11},{4,12},{5,13},{6,14},{7,15},{8,0},{9,1},... | collective-permute-start | bytes 196616 | tf_op jit(solution)/shard_map/ppermute | solution.py:249
  23.2 5.6 %collective-permute-start.6 = (bf16[2,16384]{1,0:T(2,128)(2,1)S(1)}, bf16[2,16384]{1,0:T(2,128)(2,1)S(1)}, u32[]{:S(2)}, u32[]{:S(2)}) collective-permute-start(bf16[2,16384]{1,0:T(2,128)(2,1)S(1)} %get-tuple-element.36.refs_0_), channel_id=1, source_target_pairs={{0,6},{1,7},{2,4},{3,5},{4,2},{5,3},{6,0},{7,1},{8,14},{9,15},{10,... | collective-permute-start | bytes 196616 | tf_op jit(solution)/shard_map/ppermute | solution.py:249
  24.6 5.2 %collective-permute-start.5 = (bf16[2,16384]{1,0:T(2,128)(2,1)S(1)}, bf16[2,16384]{1,0:T(2,128)(2,1)S(1)}, u32[]{:S(2)}, u32[]{:S(2)}) collective-permute-start(bf16[2,16384]{1,0:T(2,128)(2,1)S(1)} %get-tuple-element.36.refs_0_), channel_id=1, source_target_pairs={{0,2},{1,3},{2,0},{3,1},{4,6},{5,7},{6,4},{7,5},{8,10},{9,11},{10,... | collective-permute-start | bytes 196616 | tf_op jit(solution)/shard_map/ppermute | solution.py:249
  25.3 5.3 %collective-permute-start.14 = (bf16[2,16384]{1,0:T(2,128)(2,1)S(1)}, bf16[2,16384]{1,0:T(2,128)(2,1)S(1)}, u32[]{:S(2)}, u32[]{:S(2)}) collective-permute-start(bf16[2,16384]{1,0:T(2,128)(2,1)S(1)} %get-tuple-element.45), channel_id=1, source_target_pairs={{0,6},{1,7},{2,4},{3,5},{4,2},{5,3},{6,0},{7,1},{8,14},{9,15},{10,... | collective-permute-start | bytes 196616 | tf_op jit(solution)/shard_map/ppermute | solution.py:249
  27.0 4.3 %collective-permute-start.13 = (bf16[2,16384]{1,0:T(2,128)(2,1)S(1)}, bf16[2,16384]{1,0:T(2,128)(2,1)S(1)}, u32[]{:S(2)}, u32[]{:S(2)}) collective-permute-start(bf16[2,16384]{1,0:T(2,128)(2,1)S(1)} %get-tuple-element.45), channel_id=1, source_target_pairs={{0,2},{1,3},{2,0},{3,1},{4,6},{5,7},{6,4},{7,5},{8,10},{9,11},{10,... | collective-permute-start | bytes 196616 | tf_op jit(solution)/shard_map/ppermute | solution.py:249
  28.8 5.0 %collective-permute-start.16 = (bf16[4,16384]{1,0:T(4,128)(2,1)S(1)}, bf16[4,16384]{1,0:T(4,128)(2,1)S(1)}, u32[]{:S(2)}, u32[]{:S(2)}) collective-permute-start(bf16[4,16384]{1,0:T(4,128)(2,1)S(1)} %get-tuple-element.47), channel_id=1, source_target_pairs={{0,4},{1,5},{2,6},{3,7},{4,0},{5,1},{6,2},{7,3},{8,12},{9,13},{10,... | collective-permute-start | bytes 393224 | tf_op jit(solution)/shard_map/ppermute | solution.py:249
  30.0 1.6 %collective-permute-start.7 = (bf16[6,16384]{1,0:T(8,128)(2,1)S(1)}, bf16[6,16384]{1,0:T(8,128)(2,1)S(1)}, u32[]{:S(2)}, u32[]{:S(2)}) collective-permute-start(bf16[6,16384]{1,0:T(8,128)(2,1)S(1)} %pad_maximum_fusion.refs_0_), channel_id=1, source_target_pairs={{0,1},{1,0},{2,3},{3,2},{4,5},{5,4},{6,7},{7,6},{8,9},{9,8},{10,11... | collective-permute-start | bytes 589832 | tf_op jit(solution)/shard_map/ppermute | solution.py:249
  31.6 2.2 %collective-permute-start.15 = (bf16[6,16384]{1,0:T(8,128)(2,1)S(1)}, bf16[6,16384]{1,0:T(8,128)(2,1)S(1)}, u32[]{:S(2)}, u32[]{:S(2)}) collective-permute-start(bf16[6,16384]{1,0:T(8,128)(2,1)S(1)} %pad_maximum_fusion.1.refs_2_), channel_id=1, source_target_pairs={{0,1},{1,0},{2,3},{3,2},{4,5},{5,4},{6,7},{7,6},{8,9},{9,8},{10,11... | collective-permute-start | bytes 589832 | tf_op jit(solution)/shard_map/ppermute | solution.py:249
  33.8 1.3 %collective-permute-start.17 = (bf16[4,16384]{1,0:T(4,128)(2,1)S(1)}, bf16[4,16384]{1,0:T(4,128)(2,1)S(1)}, u32[]{:S(2)}, u32[]{:S(2)}) collective-permute-start(bf16[4,16384]{1,0:T(4,128)(2,1)S(1)} %collective-permute-done.16.refs_4_), channel_id=1, source_target_pairs={{0,1},{1,0},{2,3},{3,2},{4,5},{5,4},{6,7},{7,6},{8,9},{9,8},{10,11... | collective-permute-start | bytes 393224 | tf_op jit(solution)/shard_map/ppermute | solution.py:249

commit v17 on v16

--- a/solution.py
+++ b/solution.py
@@ -12,7 +12,7 @@
 EPS = 1e-06
 F32 = jnp.float32
 BF16 = jnp.bfloat16
-PIECES = 16
+PIECES = 4
 STEPS = 8
 VMEM_LIMIT = 24 << 20
 SMALL_LIMIT = 16 << 20
@@ -135,7 +135,7 @@
 
 def encode_kernel(total, arrived, gain, *refs):
     if len(refs) > 4:
-        first, *before, normed, codes, scales, joint, decoded = refs
+        _, *before, normed, codes, scales, decoded = refs
     else:
         before, (normed, codes, scales, decoded) = (), refs
     blocks = total.shape[1] // QB
@@ -163,19 +163,21 @@
     mean_sq = jnp.sum(squares, axis=1, keepdims=True) / total.shape[1]
     factor = lax.rsqrt(mean_sq + 1e-05)
     for at in parts(total):
-        value = decoded[:, at] * factor * gain[:, at]
-        normed[:, at] = value.astype(BF16)
-        if before:
-            joint[:, at] = jnp.concatenate([first[:, at].astype(F32), value], axis=0).astype(BF16)
+        normed[:, at] = (decoded[:, at] * factor * gain[:, at]).astype(BF16)
 
 
 def times(rows, weight):
     depth = weight.shape[0] // STEPS
-    count = sum(r.shape[0] for r in rows)
+    count = sum(r[0].shape[0] if isinstance(r, tuple) else r.shape[0] for r in rows)
     total = jnp.zeros((count, weight.shape[1]), F32)
+    odd = (lax.axis_index("tp") & 1) == 1
     for c in range(STEPS):
         part = pl.ds(c * depth, depth)
-        block = jnp.concatenate([r[:, part] for r in rows], axis=0)
+        block = [
+            jnp.where(odd, r[0][:, part], r[1][:, part]) if isinstance(r, tuple) else r[:, part]
+            for r in rows
+        ]
+        block = jnp.concatenate(block, axis=0)
         total += jnp.dot(block, weight[part], preferred_element_type=F32)
     return total
 
@@ -201,11 +203,13 @@
     ]
     for copy in copies:
         copy.start()
+    *rows, a, b, c, d = rows
+    rows += [(a, b), (c, d)]
     values = times(rows, weight)
     total = jnp.zeros(out.shape, F32)
     start = 0
     for ref, (side, order) in zip(rows, groups):
-        stop = start + ref.shape[0]
+        stop = start + (ref[0] if isinstance(ref, tuple) else ref).shape[0]
         total += placed(n, out.shape[0], values[start:stop], side, order)
         start = stop
     out[...] = total
@@ -248,6 +252,9 @@
     def swap(x, distance):
         return lax.ppermute(x, "tp", [(i, i ^ distance) for i in range(n)])
 
+    def send(x, core, distance):
+        return lax.ppermute(x, "tp", [(i, i ^ distance) for i in range(core, n, 2)])
+
     half, quarter = tokens // 2, tokens // 4
     part, pair = quarter // 4, (2, D)
     gain = norm_gain.reshape(1, D)
@@ -282,34 +289,35 @@
     shapes = [(pair, BF16), (pair, BF16, pltpu.VMEM), ((2, D // QB), F32, pltpu.VMEM)]
     scratch = [pltpu.VMEM(pair, F32)]
     first = local_call(encode_kernel, shapes, "encode0", *sums[0], gain, scratch=scratch)
-    shapes.append(((4, D), BF16))
     second = local_call(encode_kernel, shapes, "encode1", *sums[1], gain, *first, scratch=scratch)
     held = [widen(first[0]), widen(second[0])]
-    joint = second[3] if len(levels) == 1 else jnp.concatenate(held, axis=0)
     diagonal, near, far = square
+    lent = send(held[0], 0, 1)
+    far_mine, far_other = send(held[0], 1, far), send(lent, 1, far)
+    back_other, back_mine = send(far_mine, 1, 1), send(far_other, 1, 1)
     early = [swap(held[0], near), swap(held[0], diagonal), held[0]]
     early = jnp.concatenate(early, axis=0)
-    both = swap(joint, far)
-    late = [swap(held[1], near), swap(held[1], diagonal), held[1]]
+    late = [swap(held[1], d) for d in square][::-1] + [held[1]]
     late = jnp.concatenate(late, axis=0)
     early_other = swap(early, 1)
-    late, _ = lax.optimization_barrier((late, early_other))
-    both_other, late_other = swap(both, 1), swap(late, 1)
-    orders = [(0, 2), (0, 1), (0, 0)], [(1, 2), (1, 1), (1, 0)], [(0, 3), (1, 3)]
-    groups = [(side, order) for order in orders for side in range(2)]
+    late, *_ = lax.optimization_barrier((late, early_other, back_mine, back_other))
+    late_other = swap(late, 1)
+    first_rows, far_rows = [(0, 2), (0, 1), (0, 0)], [(0, 3)]
+    last_rows = [(1, 3), (1, 2), (1, 1), (1, 0)]
+    groups = [(0, first_rows), (1, first_rows), (0, last_rows), (0, far_rows), (1, far_rows)]
     shape = (tokens, q_weight.shape[1])
     outs = second[1:3]
     shapes = [(shape, F32)] + [(x.shape, x.dtype, pltpu.HBM) for x in outs]
     before, *outs = local_call(
-        functools.partial(first_dots_kernel, n, groups[:-1]),
+        functools.partial(first_dots_kernel, n, groups),
         shapes,
         "first_dots",
-        *(early, early_other, late, late_other, both, q_weight, *outs),
+        *(early, early_other, late, far_mine, back_mine, far_other, back_other, q_weight, *outs),
         scratch=[pltpu.SemaphoreType.DMA((2,))],
     )
-    kernel = functools.partial(last_dot_kernel, n, groups[-1])
+    kernel = functools.partial(last_dot_kernel, n, (1, last_rows))
     (next_queries,) = local_call(
-        kernel, [(shape, BF16)], "last_dot", both_other, before, q_weight
+        kernel, [(shape, BF16)], "last_dot", late_other, before, q_weight
     )
     return (*outs, next_queries)
 

time: 36.7 us -> 39.9 us (1.087)
  starting transfers between devices: 19.3 us -> 24.6 us
  waiting for transfers between devices: 8.32 us -> 6.52 us
  Pallas kernels: 6.42 us -> 6 us
    ppermute x0 -> x5, starting transfers between devices: none -> 5.19 us  [send(): return lax.ppermute(x, 'tp', [(i, i ^ distance) for i in range(core, n, 2)])]
    ppermute x18 -> x17, waiting for transfers between devices: 8.32 us -> 4.72 us  [swap(): return lax.ppermute(x, 'tp', [(i, i ^ distance) for i in range(n)])]
    ppermute x0 -> x5, waiting for transfers between devices: none -> 1.79 us  [send(): return lax.ppermute(x, 'tp', [(i, i ^ distance) for i in range(core, n, 2)])]
    ppermute x18 -> x17, starting transfers between devices: 19.3 us -> 19.4 us  [swap(): return lax.ppermute(x, 'tp', [(i, i ^ distance) for i in range(n)])]
  transfers between devices with their start and end apart: 18 -> 22, of which waited for: 10 -> 9; matrix products, arithmetic and copies ran while one was open for 3% -> 3% of each run, Pallas kernels for 7% -> 6%
where the time goes in v17:
time: 39.9 us; the launch traced here: 39.7 us
  starting transfers between devices  24.6 us (62%)
  waiting for transfers between devices  6.52 us (16%)
  Pallas kernels  6 us (15%)
  matrix products  1.31 us (3%)
  between operations  0.79 us (2%)
  other arithmetic  0.52 us (1%)
    ppermute x17, starting transfers between devices, swap(): return lax.ppermute(x, 'tp', [(i, i ^ distance) for i in range(n)])  19.4 us
    ppermute x5, starting transfers between devices, send(): return lax.ppermute(x, 'tp', [(i, i ^ distance) for i in range(core, n, 2)])  5.19 us
    ppermute x17, waiting for transfers between devices, swap(): return lax.ppermute(x, 'tp', [(i, i ^ distance) for i in range(n)])  4.72 us
    pallas_call x8, Pallas kernels, local_call(): pl.pallas_call(kernel, out_shape=[(space[0] if space else jax.ShapeDtypeS...  3.71 us
    pallas_call x1, Pallas kernels, attend(): pl.pallas_call(functools.partial(attend_kernel, n), out_shape=[jax.ShapeD...  2.28 us
    ppermute x5, waiting for transfers between devices, send(): return lax.ppermute(x, 'tp', [(i, i ^ distance) for i in range(core, n, 2)])  1.79 us
  transfers between devices with their start and end apart: 22, of which 9 were waited for; matrix products, arithmetic and copies ran while one was open for 3% of the time, Pallas kernels for 6%

profile of v17, /device:TPU:0, one launch (start us, length us, event | category | flops | bytes accessed | tf_op | source)
XLA Modules:
  0.0 39.7 jit_solution(3194349215006524315)
XLA Ops:
  0.6 2.3 %attend.1 = (bf16[32,128]{1,0:T(8,128)(2,1)S(1)}, bf16[128,16384]{1,0:T(8,128)(2,1)S(1)}) custom-call(bf16[32,128]{1,0:T(8,128)(2,1)} %queries.1, bf16[32,1024]{1,0:T(8,128)(2,1)} %keys.1, bf16[32,1024]{1,0:T(8,128)(2,1)} %values.1, bf16[128,16384]{1,0:T(8,128)(2,1)} %weight.2), custom_call_target="tpu_custom_call" | custom-call | bytes 4194304 | tf_op jit(solution)/shard_map/attend/pallas_call | solution.py:86
  2.9 0.7 %convolution_convert_fusion = bf16[16,16384]{1,0:T(8,128)(2,1)S(1)} fusion(bf16[128,16384]{1,0:T(8,128)(2,1)S(1)} %get-tuple-element.28, bf16[32,128]{1,0:T(8,128)(2,1)S(1)} %get-tuple-element.27), kind=kOutput, calls=%fused_computation | convolution fusion | flops 67371008 | bytes 4722688 | tf_op jit(solution)/shard_map/dot_general | solution.py:262
  3.6 0.0 copy-start.1
  3.6 0.5 %collective-permute-start.8 = (bf16[8,16384]{1,0:T(8,128)(2,1)S(1)}, bf16[8,16384]{1,0:T(8,128)(2,1)S(1)}, u32[]{:S(2)}, u32[]{:S(2)}) collective-permute-start(bf16[8,16384]{1,0:T(8,128)(2,1)S(1)} %get-tuple-element.51), channel_id=1, source_target_pairs={{0,1},{1,0},{2,3},{3,2},{4,5},{5,4},{6,7},{7,6},{8,9},{9,8},{10,11... | collective-permute-start | bytes 786440 | tf_op jit(solution)/shard_map/ppermute | solution.py:253
  4.2 0.0 copy-start.2
  4.2 0.0 copy-start
  4.2 0.1 collective-permute-start
  4.3 0.7 %fusion.1.kept = f32[16,16384]{1,0:T(8,128)S(1)} fusion(bf16[128,16384]{1,0:T(8,128)(2,1)S(1)} %get-tuple-element.28, bf16[32,128]{1,0:T(8,128)(2,1)S(1)} %get-tuple-element.27), kind=kOutput, calls=%fused_computation.4 | convolution fusion | flops 67108864 | bytes 5246976 | tf_op jit(solution)/shard_map/dot_general | solution.py:264
  4.9 0.8 %collective-permute-done.got = bf16[8,16384]{1,0:T(8,128)(2,1)S(1)} collective-permute-done((bf16[8,16384]{1,0:T(8,128)(2,1)S(1)}, bf16[8,16384]{1,0:T(8,128)(2,1)S(1)}, u32[]{:S(2)}, u32[]{:S(2)}) %collective-permute-start) | collective-permute-done | bytes 262176 | tf_op jit(solution)/shard_map/ppermute | solution.py:253
  5.7 0.1 split0.1
  5.8 4.0 %collective-permute-start.1 = (bf16[2,16384]{1,0:T(2,128)(2,1)S(1)}, bf16[2,16384]{1,0:T(2,128)(2,1)S(1)}, u32[]{:S(2)}, u32[]{:S(2)}) collective-permute-start(bf16[2,16384]{1,0:T(2,128)(2,1)S(1)} %get-tuple-element.30), channel_id=1, source_target_pairs={{0,6},{1,7},{2,4},{3,5},{4,2},{5,3},{6,0},{7,1},{8,14},{9,15},{10,... | collective-permute-start | bytes 196616 | tf_op jit(solution)/shard_map/ppermute | solution.py:253
  9.8 0.5 %collective-permute-start.2 = (bf16[2,16384]{1,0:T(2,128)(2,1)S(1)}, bf16[2,16384]{1,0:T(2,128)(2,1)S(1)}, u32[]{:S(2)}, u32[]{:S(2)}) collective-permute-start(bf16[2,16384]{1,0:T(2,128)(2,1)S(1)} %get-tuple-element.31), channel_id=1, source_target_pairs={{0,2},{1,3},{2,0},{3,1},{4,6},{5,7},{6,4},{7,5},{8,10},{9,11},{10,... | collective-permute-start | bytes 196616 | tf_op jit(solution)/shard_map/ppermute | solution.py:253
  10.3 0.1 collective-permute-start.3
  10.4 0.0 collective-permute-done.8.got
  10.4 0.1 split1.1
  10.5 2.9 %collective-permute-start.9 = (bf16[2,16384]{1,0:T(2,128)(2,1)S(1)}, bf16[2,16384]{1,0:T(2,128)(2,1)S(1)}, u32[]{:S(2)}, u32[]{:S(2)}) collective-permute-start(bf16[2,16384]{1,0:T(2,128)(2,1)S(1)} %get-tuple-element.37), channel_id=1, source_target_pairs={{0,6},{1,7},{2,4},{3,5},{4,2},{5,3},{6,0},{7,1},{8,14},{9,15},{10,... | collective-permute-start | bytes 196616 | tf_op jit(solution)/shard_map/ppermute | solution.py:253
  13.4 0.5 %collective-permute-start.10 = (bf16[2,16384]{1,0:T(2,128)(2,1)S(1)}, bf16[2,16384]{1,0:T(2,128)(2,1)S(1)}, u32[]{:S(2)}, u32[]{:S(2)}) collective-permute-start(bf16[2,16384]{1,0:T(2,128)(2,1)S(1)} %get-tuple-element.38), channel_id=1, source_target_pairs={{0,2},{1,3},{2,0},{3,1},{4,6},{5,7},{6,4},{7,5},{8,10},{9,11},{10,... | collective-permute-start | bytes 196616 | tf_op jit(solution)/shard_map/ppermute | solution.py:253
  13.9 0.0 collective-permute-done.1.refs_0_
  13.9 0.2 collective-permute-start.11
  14.1 0.0 collective-permute-done.2.refs_1_
  14.1 1.0 %collective-permute-done.3.refs_2_ = bf16[2,16384]{1,0:T(2,128)(2,1)S(1)} collective-permute-done((bf16[2,16384]{1,0:T(2,128)(2,1)S(1)}, bf16[2,16384]{1,0:T(2,128)(2,1)S(1)}, u32[]{:S(2)}, u32[]{:S(2)}) %collective-permute-start.3) | collective-permute-done | bytes 65568 | tf_op jit(solution)/shard_map/ppermute | solution.py:253
  15.2 0.0 copy-done.1
  15.2 0.2 settle0.1
  15.4 2.6 %collective-permute-start.4 = (bf16[2,16384]{1,0:T(2,128)(2,1)S(1)}, bf16[2,16384]{1,0:T(2,128)(2,1)S(1)}, u32[]{:S(2)}, u32[]{:S(2)}) collective-permute-start(bf16[2,16384]{1,0:T(2,128)(2,1)S(1)} %get-tuple-element.34), channel_id=1, source_target_pairs={{0,8},{1,9},{2,10},{3,11},{4,12},{5,13},{6,14},{7,15},{8,0},{9,1},... | collective-permute-start | bytes 196616 | tf_op jit(solution)/shard_map/ppermute | solution.py:253
  18.0 0.0 collective-permute-done.9.refs_0_
  18.0 0.0 collective-permute-done.10.refs_1_
  18.0 0.2 collective-permute-done.11.refs_2_
  18.2 0.2 settle1.1
  18.4 2.7 %collective-permute-start.12 = (bf16[2,16384]{1,0:T(2,128)(2,1)S(1)}, bf16[2,16384]{1,0:T(2,128)(2,1)S(1)}, u32[]{:S(2)}, u32[]{:S(2)}) collective-permute-start(bf16[2,16384]{1,0:T(2,128)(2,1)S(1)} %get-tuple-element.41), channel_id=1, source_target_pairs={{0,8},{1,9},{2,10},{3,11},{4,12},{5,13},{6,14},{7,15},{8,0},{9,1},... | collective-permute-start | bytes 196616 | tf_op jit(solution)/shard_map/ppermute | solution.py:253
  21.0 1.4 %collective-permute-done.4.arrived = bf16[2,16384]{1,0:T(2,128)(2,1)S(1)} collective-permute-done((bf16[2,16384]{1,0:T(2,128)(2,1)S(1)}, bf16[2,16384]{1,0:T(2,128)(2,1)S(1)}, u32[]{:S(2)}, u32[]{:S(2)}) %collective-permute-start.4) | collective-permute-done | bytes 65568 | tf_op jit(solution)/shard_map/ppermute | solution.py:253
  22.5 0.0 copy-done.2
  22.5 0.4 %encode0.1 = (bf16[2,16384]{1,0:T(2,128)(2,1)S(1)}, bf16[2,16384]{1,0:T(2,128)(2,1)S(1)}, f32[2,128]{1,0:T(2,128)S(1)}) custom-call(f32[2,16384]{1,0:T(2,128)S(1)} %get-tuple-element.33.total, bf16[2,16384]{1,0:T(2,128)(2,1)S(1)} %collective-permute-done.4.arrived, f32[1,16384]{1,0:T(1,128)S(1)} %bitcast.3), custom_call_target="tpu_custom_call" | custom-call | bytes 163840 | tf_op jit(solution)/shard_map/encode0/pallas_call | solution.py:228
  22.9 1.3 %collective-permute-start.16 = (bf16[2,16384]{1,0:T(2,128)(2,1)S(1)}, bf16[2,16384]{1,0:T(2,128)(2,1)S(1)}, u32[]{:S(2)}, u32[]{:S(2)}) collective-permute-start(bf16[2,16384]{1,0:T(2,128)(2,1)S(1)} %get-tuple-element.35.refs_0_), channel_id=1, source_target_pairs={{0,1},{2,3},{4,5},{6,7},{8,9},{10,11},{12,13},{14,15},{16,17},{18,... | collective-permute-start | bytes 196616 | tf_op jit(solution)/shard_map/ppermute | solution.py:256
  24.2 1.2 %collective-permute-start.6 = (bf16[2,16384]{1,0:T(2,128)(2,1)S(1)}, bf16[2,16384]{1,0:T(2,128)(2,1)S(1)}, u32[]{:S(2)}, u32[]{:S(2)}) collective-permute-start(bf16[2,16384]{1,0:T(2,128)(2,1)S(1)} %get-tuple-element.35.refs_0_), channel_id=1, source_target_pairs={{0,6},{1,7},{2,4},{3,5},{4,2},{5,3},{6,0},{7,1},{8,14},{9,15},{10,... | collective-permute-start | bytes 196616 | tf_op jit(solution)/shard_map/ppermute | solution.py:253
  25.4 0.2 collective-permute-start.5
  25.7 0.0 collective-permute-done.12.arrived
  25.7 0.5 %encode1.1 = (bf16[2,16384]{1,0:T(2,128)(2,1)S(1)}, bf16[2,16384]{1,0:T(2,128)(2,1)S(1)}, f32[2,128]{1,0:T(2,128)S(1)}) custom-call(f32[2,16384]{1,0:T(2,128)S(1)} %get-tuple-element.40.total, bf16[2,16384]{1,0:T(2,128)(2,1)S(1)} %collective-permute-done.12.arrived, f32[1,16384]{1,0:T(1,128)S(1)} %bitcast.4, bf16[2,16384]{1,0:T(2,128)(2,1)S(1)} %get-tuple-element.35.refs_0_, ...), custom_call_target="tpu_custom_call" | custom-call | bytes 295424 | tf_op jit(solution)/shard_map/encode1/pallas_call | solution.py:228
  26.1 1.8 %collective-permute-start.15 = (bf16[2,16384]{1,0:T(2,128)(2,1)S(1)}, bf16[2,16384]{1,0:T(2,128)(2,1)S(1)}, u32[]{:S(2)}, u32[]{:S(2)}) collective-permute-start(bf16[2,16384]{1,0:T(2,128)(2,1)S(1)} %get-tuple-element.44), channel_id=1, source_target_pairs={{0,6},{1,7},{2,4},{3,5},{4,2},{5,3},{6,0},{7,1},{8,14},{9,15},{10,... | collective-permute-start | bytes 196616 | tf_op jit(solution)/shard_map/ppermute | solution.py:253
  27.9 1.9 %collective-permute-start.14 = (bf16[2,16384]{1,0:T(2,128)(2,1)S(1)}, bf16[2,16384]{1,0:T(2,128)(2,1)S(1)}, u32[]{:S(2)}, u32[]{:S(2)}) collective-permute-start(bf16[2,16384]{1,0:T(2,128)(2,1)S(1)} %get-tuple-element.44), channel_id=1, source_target_pairs={{0,2},{1,3},{2,0},{3,1},{4,6},{5,7},{6,4},{7,5},{8,10},{9,11},{10,... | collective-permute-start | bytes 196616 | tf_op jit(solution)/shard_map/ppermute | solution.py:253
  29.8 0.0 collective-permute-done.16
  29.8 0.0 collective-permute-start.13
  29.8 0.1 collective-permute-done.6
  29.9 0.7 %collective-permute-start.19 = (bf16[2,16384]{1,0:T(2,128)(2,1)S(1)}, bf16[2,16384]{1,0:T(2,128)(2,1)S(1)}, u32[]{:S(2)}, u32[]{:S(2)}) collective-permute-start(bf16[2,16384]{1,0:T(2,128)(2,1)S(1)} %get-tuple-element.35.refs_0_), channel_id=1, source_target_pairs={{1,5},{3,7},{5,1},{7,3},{9,13},{11,15},{13,9},{15,11},{17,21},{19,... | collective-permute-start | bytes 196616 | tf_op jit(solution)/shard_map/ppermute | solution.py:256
  30.6 0.0 collective-permute-done.5
  30.6 0.7 %collective-permute-start.17 = (bf16[2,16384]{1,0:T(2,128)(2,1)S(1)}, bf16[2,16384]{1,0:T(2,128)(2,1)S(1)}, u32[]{:S(2)}, u32[]{:S(2)}) collective-permute-start(bf16[2,16384]{1,0:T(2,128)(2,1)S(1)} %collective-permute-done.16), channel_id=1, source_target_pairs={{1,5},{3,7},{5,1},{7,3},{9,13},{11,15},{13,9},{15,11},{17,21},{19,... | collective-permute-start | bytes 196616 | tf_op jit(solution)/shard_map/ppermute | solution.py:256
  31.2 0.2 pad_maximum_fusion.refs_0_
  31.5 0.4 collective-permute-done.15
  31.9 0.0 collective-permute-start.7
  31.9 0.0 collective-permute-done.19.refs_3_
  31.9 1.3 %collective-permute-start.20 = (bf16[2,16384]{1,0:T(2,128)(2,1)S(1)}, bf16[2,16384]{1,0:T(2,128)(2,1)S(1)}, u32[]{:S(2)}, u32[]{:S(2)}) collective-permute-start(bf16[2,16384]{1,0:T(2,128)(2,1)S(1)} %collective-permute-done.19.refs_3_), channel_id=1, source_target_pairs={{1,0},{3,2},{5,4},{7,6},{9,8},{11,10},{13,12},{15,14},{17,16},{19,... | collective-permute-start | bytes 196616 | tf_op jit(solution)/shard_map/ppermute | solution.py:256
  33.2 0.0 collective-permute-done.17.refs_5_
  33.2 1.3 %collective-permute-start.18 = (bf16[2,16384]{1,0:T(2,128)(2,1)S(1)}, bf16[2,16384]{1,0:T(2,128)(2,1)S(1)}, u32[]{:S(2)}, u32[]{:S(2)}) collective-permute-start(bf16[2,16384]{1,0:T(2,128)(2,1)S(1)} %collective-permute-done.17.refs_5_), channel_id=1, source_target_pairs={{1,0},{3,2},{5,4},{7,6},{9,8},{11,10},{13,12},{15,14},{17,16},{19,... | collective-permute-start | bytes 196616 | tf_op jit(solution)/shard_map/ppermute | solution.py:256
  34.5 0.0 collective-permute-done.14
  34.5 0.3 collective-permute-done.13
  34.7 0.3 pad_maximum_fusion.1.refs_2_
  35.0 0.0 collective-permute-done.20.refs_6_
  35.0 1.8 %collective-permute-done.18.refs_4_ = bf16[2,16384]{1,0:T(2,128)(2,1)S(1)} collective-permute-done((bf16[2,16384]{1,0:T(2,128)(2,1)S(1)}, bf16[2,16384]{1,0:T(2,128)(2,1)S(1)}, u32[]{:S(2)}, u32[]{:S(2)}) %collective-permute-start.18) | collective-permute-done | bytes 65568 | tf_op jit(solution)/shard_map/ppermute | solution.py:256
  36.8 0.0 collective-permute-done.7.refs_1_
  36.8 0.2 collective-permute-start.21
  37.0 0.0 copy-done
  37.0 0.9 %first_dots.1 = (f32[32,128]{1,0:T(8,128)S(1)}, bf16[2,16384]{1,0:T(2,128)(2,1)}, f32[2,128]{1,0:T(2,128)}) custom-call(bf16[6,16384]{1,0:T(8,128)(2,1)S(1)} %pad_maximum_fusion.refs_0_, bf16[6,16384]{1,0:T(8,128)(2,1)S(1)} %collective-permute-done.7.refs_1_, bf16[8,16384]{1,0:T(8,128)(2,1)S(1)} %pad_maximum_fusion.1.refs_2_, ...), custom_call_target="tpu_custom_call" | custom-call | bytes 5177856 | tf_op jit(solution)/shard_map/first_dots/pallas_call | solution.py:228
  37.9 0.5 %collective-permute-done.21.rows = bf16[8,16384]{1,0:T(8,128)(2,1)S(1)} collective-permute-done((bf16[8,16384]{1,0:T(8,128)(2,1)S(1)}, bf16[8,16384]{1,0:T(8,128)(2,1)S(1)}, u32[]{:S(2)}, u32[]{:S(2)}) %collective-permute-start.21) | collective-permute-done | bytes 262176 | tf_op jit(solution)/shard_map/ppermute | solution.py:253
  38.4 1.4 %last_dot.1 = bf16[32,128]{1,0:T(8,128)(2,1)} custom-call(bf16[8,16384]{1,0:T(8,128)(2,1)S(1)} %collective-permute-done.21.rows, f32[32,128]{1,0:T(8,128)S(1)} %get-tuple-element.50.before, bf16[16384,128]{1,0:T(8,128)(2,1)S(1)} %copy-done), custom_call_target="tpu_custom_call" | custom-call | bytes 4464640 | tf_op jit(solution)/shard_map/last_dot/pallas_call | solution.py:228
  (1 shorter events, 0.0 us)
Async XLA Ops:
  3.6 11.5 %copy-start.1 = (bf16[2,16384]{1,0:T(2,128)(2,1)S(1)}, bf16[2,16384]{1,0:T(2,128)(2,1)}, u32[]{:S(2)}) copy-start(bf16[2,16384]{1,0:T(2,128)(2,1)} %old.3) | copy-start | bytes 196612
  3.6 6.8 %collective-permute-start.8 = (bf16[8,16384]{1,0:T(8,128)(2,1)S(1)}, bf16[8,16384]{1,0:T(8,128)(2,1)S(1)}, u32[]{:S(2)}, u32[]{:S(2)}) collective-permute-start(bf16[8,16384]{1,0:T(8,128)(2,1)S(1)} %get-tuple-element.51), channel_id=1, source_target_pairs={{0,1},{1,0},{2,3},{3,2},{4,5},{5,4},{6,7},{7,6},{8,9},{9,8},{10,11... | collective-permute-start | bytes 786440 | tf_op jit(solution)/shard_map/ppermute | solution.py:253
  4.2 18.3 %copy-start.2 = (f32[16384]{0:T(1024)S(1)}, f32[16384]{0:T(1024)}, u32[]{:S(2)}) copy-start(f32[16384]{0:T(1024)} %param.12) | copy-start | bytes 196612
  4.2 32.8 %copy-start = (bf16[16384,128]{1,0:T(8,128)(2,1)S(1)}, bf16[16384,128]{1,0:T(8,128)(2,1)}, u32[]{:S(2)}) copy-start(bf16[16384,128]{1,0:T(8,128)(2,1)} %weight.3) | copy-start | bytes 12582916
  4.2 1.5 %collective-permute-start = (bf16[8,16384]{1,0:T(8,128)(2,1)S(1)}, bf16[8,16384]{1,0:T(8,128)(2,1)S(1)}, u32[]{:S(2)}, u32[]{:S(2)}) collective-permute-start(bf16[8,16384]{1,0:T(8,128)(2,1)S(1)} %get-tuple-element.52), channel_id=1, source_target_pairs={{0,1},{1,0},{2,3},{3,2},{4,5},{5,4},{6,7},{7,6},{8,9},{9,8},{10,11... | collective-permute-start | bytes 786440 | tf_op jit(solution)/shard_map/ppermute | solution.py:253
  5.8 8.1 %collective-permute-start.1 = (bf16[2,16384]{1,0:T(2,128)(2,1)S(1)}, bf16[2,16384]{1,0:T(2,128)(2,1)S(1)}, u32[]{:S(2)}, u32[]{:S(2)}) collective-permute-start(bf16[2,16384]{1,0:T(2,128)(2,1)S(1)} %get-tuple-element.30), channel_id=1, source_target_pairs={{0,6},{1,7},{2,4},{3,5},{4,2},{5,3},{6,0},{7,1},{8,14},{9,15},{10,... | collective-permute-start | bytes 196616 | tf_op jit(solution)/shard_map/ppermute | solution.py:253
  9.8 4.4 %collective-permute-start.2 = (bf16[2,16384]{1,0:T(2,128)(2,1)S(1)}, bf16[2,16384]{1,0:T(2,128)(2,1)S(1)}, u32[]{:S(2)}, u32[]{:S(2)}) collective-permute-start(bf16[2,16384]{1,0:T(2,128)(2,1)S(1)} %get-tuple-element.31), channel_id=1, source_target_pairs={{0,2},{1,3},{2,0},{3,1},{4,6},{5,7},{6,4},{7,5},{8,10},{9,11},{10,... | collective-permute-start | bytes 196616 | tf_op jit(solution)/shard_map/ppermute | solution.py:253
  10.3 4.9 %collective-permute-start.3 = (bf16[2,16384]{1,0:T(2,128)(2,1)S(1)}, bf16[2,16384]{1,0:T(2,128)(2,1)S(1)}, u32[]{:S(2)}, u32[]{:S(2)}) collective-permute-start(bf16[2,16384]{1,0:T(2,128)(2,1)S(1)} %get-tuple-element.32), channel_id=1, source_target_pairs={{0,4},{1,5},{2,6},{3,7},{4,0},{5,1},{6,2},{7,3},{8,12},{9,13},{10,... | collective-permute-start | bytes 196616 | tf_op jit(solution)/shard_map/ppermute | solution.py:253
  10.5 7.5 %collective-permute-start.9 = (bf16[2,16384]{1,0:T(2,128)(2,1)S(1)}, bf16[2,16384]{1,0:T(2,128)(2,1)S(1)}, u32[]{:S(2)}, u32[]{:S(2)}) collective-permute-start(bf16[2,16384]{1,0:T(2,128)(2,1)S(1)} %get-tuple-element.37), channel_id=1, source_target_pairs={{0,6},{1,7},{2,4},{3,5},{4,2},{5,3},{6,0},{7,1},{8,14},{9,15},{10,... | collective-permute-start | bytes 196616 | tf_op jit(solution)/shard_map/ppermute | solution.py:253
  13.4 4.6 %collective-permute-start.10 = (bf16[2,16384]{1,0:T(2,128)(2,1)S(1)}, bf16[2,16384]{1,0:T(2,128)(2,1)S(1)}, u32[]{:S(2)}, u32[]{:S(2)}) collective-permute-start(bf16[2,16384]{1,0:T(2,128)(2,1)S(1)} %get-tuple-element.38), channel_id=1, source_target_pairs={{0,2},{1,3},{2,0},{3,1},{4,6},{5,7},{6,4},{7,5},{8,10},{9,11},{10,... | collective-permute-start | bytes 196616 | tf_op jit(solution)/shard_map/ppermute | solution.py:253
  13.9 4.3 %collective-permute-start.11 = (bf16[2,16384]{1,0:T(2,128)(2,1)S(1)}, bf16[2,16384]{1,0:T(2,128)(2,1)S(1)}, u32[]{:S(2)}, u32[]{:S(2)}) collective-permute-start(bf16[2,16384]{1,0:T(2,128)(2,1)S(1)} %get-tuple-element.39), channel_id=1, source_target_pairs={{0,4},{1,5},{2,6},{3,7},{4,0},{5,1},{6,2},{7,3},{8,12},{9,13},{10,... | collective-permute-start | bytes 196616 | tf_op jit(solution)/shard_map/ppermute | solution.py:253
  15.4 7.1 %collective-permute-start.4 = (bf16[2,16384]{1,0:T(2,128)(2,1)S(1)}, bf16[2,16384]{1,0:T(2,128)(2,1)S(1)}, u32[]{:S(2)}, u32[]{:S(2)}) collective-permute-start(bf16[2,16384]{1,0:T(2,128)(2,1)S(1)} %get-tuple-element.34), channel_id=1, source_target_pairs={{0,8},{1,9},{2,10},{3,11},{4,12},{5,13},{6,14},{7,15},{8,0},{9,1},... | collective-permute-start | bytes 196616 | tf_op jit(solution)/shard_map/ppermute | solution.py:253
  18.4 7.3 %collective-permute-start.12 = (bf16[2,16384]{1,0:T(2,128)(2,1)S(1)}, bf16[2,16384]{1,0:T(2,128)(2,1)S(1)}, u32[]{:S(2)}, u32[]{:S(2)}) collective-permute-start(bf16[2,16384]{1,0:T(2,128)(2,1)S(1)} %get-tuple-element.41), channel_id=1, source_target_pairs={{0,8},{1,9},{2,10},{3,11},{4,12},{5,13},{6,14},{7,15},{8,0},{9,1},... | collective-permute-start | bytes 196616 | tf_op jit(solution)/shard_map/ppermute | solution.py:253
  22.9 6.9 %collective-permute-start.16 = (bf16[2,16384]{1,0:T(2,128)(2,1)S(1)}, bf16[2,16384]{1,0:T(2,128)(2,1)S(1)}, u32[]{:S(2)}, u32[]{:S(2)}) collective-permute-start(bf16[2,16384]{1,0:T(2,128)(2,1)S(1)} %get-tuple-element.35.refs_0_), channel_id=1, source_target_pairs={{0,1},{2,3},{4,5},{6,7},{8,9},{10,11},{12,13},{14,15},{16,17},{18,... | collective-permute-start | bytes 196616 | tf_op jit(solution)/shard_map/ppermute | solution.py:256
  24.2 5.7 %collective-permute-start.6 = (bf16[2,16384]{1,0:T(2,128)(2,1)S(1)}, bf16[2,16384]{1,0:T(2,128)(2,1)S(1)}, u32[]{:S(2)}, u32[]{:S(2)}) collective-permute-start(bf16[2,16384]{1,0:T(2,128)(2,1)S(1)} %get-tuple-element.35.refs_0_), channel_id=1, source_target_pairs={{0,6},{1,7},{2,4},{3,5},{4,2},{5,3},{6,0},{7,1},{8,14},{9,15},{10,... | collective-permute-start | bytes 196616 | tf_op jit(solution)/shard_map/ppermute | solution.py:253
  25.4 5.1 %collective-permute-start.5 = (bf16[2,16384]{1,0:T(2,128)(2,1)S(1)}, bf16[2,16384]{1,0:T(2,128)(2,1)S(1)}, u32[]{:S(2)}, u32[]{:S(2)}) collective-permute-start(bf16[2,16384]{1,0:T(2,128)(2,1)S(1)} %get-tuple-element.35.refs_0_), channel_id=1, source_target_pairs={{0,2},{1,3},{2,0},{3,1},{4,6},{5,7},{6,4},{7,5},{8,10},{9,11},{10,... | collective-permute-start | bytes 196616 | tf_op jit(solution)/shard_map/ppermute | solution.py:253
  26.1 5.7 %collective-permute-start.15 = (bf16[2,16384]{1,0:T(2,128)(2,1)S(1)}, bf16[2,16384]{1,0:T(2,128)(2,1)S(1)}, u32[]{:S(2)}, u32[]{:S(2)}) collective-permute-start(bf16[2,16384]{1,0:T(2,128)(2,1)S(1)} %get-tuple-element.44), channel_id=1, source_target_pairs={{0,6},{1,7},{2,4},{3,5},{4,2},{5,3},{6,0},{7,1},{8,14},{9,15},{10,... | collective-permute-start | bytes 196616 | tf_op jit(solution)/shard_map/ppermute | solution.py:253
  27.9 6.5 %collective-permute-start.14 = (bf16[2,16384]{1,0:T(2,128)(2,1)S(1)}, bf16[2,16384]{1,0:T(2,128)(2,1)S(1)}, u32[]{:S(2)}, u32[]{:S(2)}) collective-permute-start(bf16[2,16384]{1,0:T(2,128)(2,1)S(1)} %get-tuple-element.44), channel_id=1, source_target_pairs={{0,2},{1,3},{2,0},{3,1},{4,6},{5,7},{6,4},{7,5},{8,10},{9,11},{10,... | collective-permute-start | bytes 196616 | tf_op jit(solution)/shard_map/ppermute | solution.py:253
  29.8 4.9 %collective-permute-start.13 = (bf16[2,16384]{1,0:T(2,128)(2,1)S(1)}, bf16[2,16384]{1,0:T(2,128)(2,1)S(1)}, u32[]{:S(2)}, u32[]{:S(2)}) collective-permute-start(bf16[2,16384]{1,0:T(2,128)(2,1)S(1)} %get-tuple-element.44), channel_id=1, source_target_pairs={{0,4},{1,5},{2,6},{3,7},{4,0},{5,1},{6,2},{7,3},{8,12},{9,13},{10,... | collective-permute-start | bytes 196616 | tf_op jit(solution)/shard_map/ppermute | solution.py:253
  29.9 2.0 %collective-permute-start.19 = (bf16[2,16384]{1,0:T(2,128)(2,1)S(1)}, bf16[2,16384]{1,0:T(2,128)(2,1)S(1)}, u32[]{:S(2)}, u32[]{:S(2)}) collective-permute-start(bf16[2,16384]{1,0:T(2,128)(2,1)S(1)} %get-tuple-element.35.refs_0_), channel_id=1, source_target_pairs={{1,5},{3,7},{5,1},{7,3},{9,13},{11,15},{13,9},{15,11},{17,21},{19,... | collective-permute-start | bytes 196616 | tf_op jit(solution)/shard_map/ppermute | solution.py:256
  30.6 2.6 %collective-permute-start.17 = (bf16[2,16384]{1,0:T(2,128)(2,1)S(1)}, bf16[2,16384]{1,0:T(2,128)(2,1)S(1)}, u32[]{:S(2)}, u32[]{:S(2)}) collective-permute-start(bf16[2,16384]{1,0:T(2,128)(2,1)S(1)} %collective-permute-done.16), channel_id=1, source_target_pairs={{1,5},{3,7},{5,1},{7,3},{9,13},{11,15},{13,9},{15,11},{17,21},{19,... | collective-permute-start | bytes 196616 | tf_op jit(solution)/shard_map/ppermute | solution.py:256
  31.9 5.0 %collective-permute-start.7 = (bf16[6,16384]{1,0:T(8,128)(2,1)S(1)}, bf16[6,16384]{1,0:T(8,128)(2,1)S(1)}, u32[]{:S(2)}, u32[]{:S(2)}) collective-permute-start(bf16[6,16384]{1,0:T(8,128)(2,1)S(1)} %pad_maximum_fusion.refs_0_), channel_id=1, source_target_pairs={{0,1},{1,0},{2,3},{3,2},{4,5},{5,4},{6,7},{7,6},{8,9},{9,8},{10,11... | collective-permute-start | bytes 589832 | tf_op jit(solution)/shard_map/ppermute | solution.py:253
  31.9 3.2 %collective-permute-start.20 = (bf16[2,16384]{1,0:T(2,128)(2,1)S(1)}, bf16[2,16384]{1,0:T(2,128)(2,1)S(1)}, u32[]{:S(2)}, u32[]{:S(2)}) collective-permute-start(bf16[2,16384]{1,0:T(2,128)(2,1)S(1)} %collective-permute-done.19.refs_3_), channel_id=1, source_target_pairs={{1,0},{3,2},{5,4},{7,6},{9,8},{11,10},{13,12},{15,14},{17,16},{19,... | collective-permute-start | bytes 196616 | tf_op jit(solution)/shard_map/ppermute | solution.py:256
  33.2 3.7 %collective-permute-start.18 = (bf16[2,16384]{1,0:T(2,128)(2,1)S(1)}, bf16[2,16384]{1,0:T(2,128)(2,1)S(1)}, u32[]{:S(2)}, u32[]{:S(2)}) collective-permute-start(bf16[2,16384]{1,0:T(2,128)(2,1)S(1)} %collective-permute-done.17.refs_5_), channel_id=1, source_target_pairs={{1,0},{3,2},{5,4},{7,6},{9,8},{11,10},{13,12},{15,14},{17,16},{19,... | collective-permute-start | bytes 196616 | tf_op jit(solution)/shard_map/ppermute | solution.py:256
  36.8 1.5 %collective-permute-start.21 = (bf16[8,16384]{1,0:T(8,128)(2,1)S(1)}, bf16[8,16384]{1,0:T(8,128)(2,1)S(1)}, u32[]{:S(2)}, u32[]{:S(2)}) collective-permute-start(bf16[8,16384]{1,0:T(8,128)(2,1)S(1)} %pad_maximum_fusion.1.refs_2_), channel_id=1, source_target_pairs={{0,1},{1,0},{2,3},{3,2},{4,5},{5,4},{6,7},{7,6},{8,9},{9,8},{10,11... | collective-permute-start | bytes 786440 | tf_op jit(solution)/shard_map/ppermute | solution.py:253

commit v18 on v16

--- a/solution.py
+++ b/solution.py
@@ -12,7 +12,7 @@
 EPS = 1e-06
 F32 = jnp.float32
 BF16 = jnp.bfloat16
-PIECES = 16
+PIECES = 4
 STEPS = 8
 VMEM_LIMIT = 24 << 20
 SMALL_LIMIT = 16 << 20
@@ -253,8 +253,10 @@
     gain = norm_gain.reshape(1, D)
     context, weight = attend(n, queries, key_rows, value_rows, out_weight)
     sent = jnp.dot(context[half:], weight, preferred_element_type=F32).astype(BF16)
-    got = [swap(sent[:quarter], 1), swap(sent[quarter:], 1)]
     kept = jnp.dot(context[:half], weight, preferred_element_type=F32)
+    got = [swap(sent[:quarter], 1)]
+    kept, sent = lax.optimization_barrier((kept, sent))
+    got.append(swap(sent[quarter:], 1))
 
     def reduce(which):
         shapes = [((part, D), F32)] + [((part, D), BF16)] * 3

time: 36.7 us -> 36 us (0.981)
  waiting for transfers between devices: 8.32 us -> 7.77 us
    ppermute x18, waiting for transfers between devices: 8.32 us -> 7.77 us  [swap(): return lax.ppermute(x, 'tp', [(i, i ^ distance) for i in range(n)])]
where the time goes in v18:
time: 36 us; the launch traced here: 35.9 us
  starting transfers between devices  19.5 us (54%)
  waiting for transfers between devices  7.77 us (22%)
  Pallas kernels  6.1 us (17%)
  matrix products  1.31 us (4%)
  between operations  0.75 us (2%)
  other arithmetic  0.43 us (1%)
    ppermute x18, starting transfers between devices, swap(): return lax.ppermute(x, 'tp', [(i, i ^ distance) for i in range(n)])  19.5 us
    ppermute x18, waiting for transfers between devices, swap(): return lax.ppermute(x, 'tp', [(i, i ^ distance) for i in range(n)])  7.77 us
    pallas_call x8, Pallas kernels, local_call(): pl.pallas_call(kernel, out_shape=[(space[0] if space else jax.ShapeDtypeS...  3.82 us
    pallas_call x1, Pallas kernels, attend(): pl.pallas_call(functools.partial(attend_kernel, n), out_shape=[jax.ShapeD...  2.28 us
  transfers between devices with their start and end apart: 18, of which 10 were waited for; matrix products, arithmetic and copies ran while one was open for 3% of the time, Pallas kernels for 7%

profile of v18, /device:TPU:0, one launch (start us, length us, event | category | flops | bytes accessed | tf_op | source)
XLA Modules:
  0.0 35.9 jit_solution(1030798388132418009)
XLA Ops:
  0.6 2.3 %attend.1 = (bf16[32,128]{1,0:T(8,128)(2,1)S(1)}, bf16[128,16384]{1,0:T(8,128)(2,1)S(1)}) custom-call(bf16[32,128]{1,0:T(8,128)(2,1)} %queries.1, bf16[32,1024]{1,0:T(8,128)(2,1)} %keys.1, bf16[32,1024]{1,0:T(8,128)(2,1)} %values.1, bf16[128,16384]{1,0:T(8,128)(2,1)} %weight.2), custom_call_target="tpu_custom_call" | custom-call | bytes 4194304 | tf_op jit(solution)/shard_map/attend/pallas_call | solution.py:86
  2.9 0.7 %convolution_convert_fusion = bf16[16,16384]{1,0:T(8,128)(2,1)S(1)} fusion(bf16[128,16384]{1,0:T(8,128)(2,1)S(1)} %get-tuple-element.31, bf16[32,128]{1,0:T(8,128)(2,1)S(1)} %get-tuple-element.30), kind=kOutput, calls=%fused_computation | convolution fusion | flops 67371008 | bytes 4722688 | tf_op jit(solution)/shard_map/dot_general | solution.py:255
  3.6 0.0 copy-start.1
  3.6 0.0 copy-start.2
  3.6 0.0 copy-start
  3.6 0.5 %collective-permute-start = (bf16[8,16384]{1,0:T(8,128)(2,1)S(1)}, bf16[8,16384]{1,0:T(8,128)(2,1)S(1)}, u32[]{:S(2)}, u32[]{:S(2)}) collective-permute-start(bf16[8,16384]{1,0:T(8,128)(2,1)S(1)} %slice.16), channel_id=1, source_target_pairs={{0,1},{1,0},{2,3},{3,2},{4,5},{5,4},{6,7},{7,6},{8,9},{9,8},{10,11... | collective-permute-start | bytes 786440 | tf_op jit(solution)/shard_map/ppermute | solution.py:249
  4.2 0.7 %fusion.1.kept = f32[16,16384]{1,0:T(8,128)S(1)} fusion(bf16[128,16384]{1,0:T(8,128)(2,1)S(1)} %get-tuple-element.31, bf16[32,128]{1,0:T(8,128)(2,1)S(1)} %get-tuple-element.30), kind=kOutput, calls=%fused_computation.4 | convolution fusion | flops 67108864 | bytes 5246976 | tf_op jit(solution)/shard_map/dot_general | solution.py:256
  4.9 0.1 collective-permute-start.8
  5.0 0.4 collective-permute-done.got
  5.3 0.1 split0.1
  5.4 4.0 %collective-permute-start.1 = (bf16[2,16384]{1,0:T(2,128)(2,1)S(1)}, bf16[2,16384]{1,0:T(2,128)(2,1)S(1)}, u32[]{:S(2)}, u32[]{:S(2)}) collective-permute-start(bf16[2,16384]{1,0:T(2,128)(2,1)S(1)} %get-tuple-element.34), channel_id=1, source_target_pairs={{0,6},{1,7},{2,4},{3,5},{4,2},{5,3},{6,0},{7,1},{8,14},{9,15},{10,... | collective-permute-start | bytes 196616 | tf_op jit(solution)/shard_map/ppermute | solution.py:249
  9.4 0.5 %collective-permute-start.2 = (bf16[2,16384]{1,0:T(2,128)(2,1)S(1)}, bf16[2,16384]{1,0:T(2,128)(2,1)S(1)}, u32[]{:S(2)}, u32[]{:S(2)}) collective-permute-start(bf16[2,16384]{1,0:T(2,128)(2,1)S(1)} %get-tuple-element.35), channel_id=1, source_target_pairs={{0,2},{1,3},{2,0},{3,1},{4,6},{5,7},{6,4},{7,5},{8,10},{9,11},{10,... | collective-permute-start | bytes 196616 | tf_op jit(solution)/shard_map/ppermute | solution.py:249
  9.9 0.1 collective-permute-start.3
  10.0 0.0 collective-permute-done.8.got
  10.0 0.1 split1.1
  10.1 2.9 %collective-permute-start.9 = (bf16[2,16384]{1,0:T(2,128)(2,1)S(1)}, bf16[2,16384]{1,0:T(2,128)(2,1)S(1)}, u32[]{:S(2)}, u32[]{:S(2)}) collective-permute-start(bf16[2,16384]{1,0:T(2,128)(2,1)S(1)} %get-tuple-element.42), channel_id=1, source_target_pairs={{0,6},{1,7},{2,4},{3,5},{4,2},{5,3},{6,0},{7,1},{8,14},{9,15},{10,... | collective-permute-start | bytes 196616 | tf_op jit(solution)/shard_map/ppermute | solution.py:249
  13.1 0.5 %collective-permute-start.10 = (bf16[2,16384]{1,0:T(2,128)(2,1)S(1)}, bf16[2,16384]{1,0:T(2,128)(2,1)S(1)}, u32[]{:S(2)}, u32[]{:S(2)}) collective-permute-start(bf16[2,16384]{1,0:T(2,128)(2,1)S(1)} %get-tuple-element.43), channel_id=1, source_target_pairs={{0,2},{1,3},{2,0},{3,1},{4,6},{5,7},{6,4},{7,5},{8,10},{9,11},{10,... | collective-permute-start | bytes 196616 | tf_op jit(solution)/shard_map/ppermute | solution.py:249
  13.6 0.0 collective-permute-done.1.refs_0_
  13.6 0.2 collective-permute-start.11
  13.8 0.0 collective-permute-done.2.refs_1_
  13.8 1.0 %collective-permute-done.3.refs_2_ = bf16[2,16384]{1,0:T(2,128)(2,1)S(1)} collective-permute-done((bf16[2,16384]{1,0:T(2,128)(2,1)S(1)}, bf16[2,16384]{1,0:T(2,128)(2,1)S(1)}, u32[]{:S(2)}, u32[]{:S(2)}) %collective-permute-start.3) | collective-permute-done | bytes 65568 | tf_op jit(solution)/shard_map/ppermute | solution.py:249
  14.8 0.0 copy-done.1
  14.8 0.2 settle0.1
  15.0 2.6 %collective-permute-start.4 = (bf16[2,16384]{1,0:T(2,128)(2,1)S(1)}, bf16[2,16384]{1,0:T(2,128)(2,1)S(1)}, u32[]{:S(2)}, u32[]{:S(2)}) collective-permute-start(bf16[2,16384]{1,0:T(2,128)(2,1)S(1)} %get-tuple-element.38), channel_id=1, source_target_pairs={{0,8},{1,9},{2,10},{3,11},{4,12},{5,13},{6,14},{7,15},{8,0},{9,1},... | collective-permute-start | bytes 196616 | tf_op jit(solution)/shard_map/ppermute | solution.py:249
  17.6 0.0 collective-permute-done.9.refs_0_
  17.6 0.0 collective-permute-done.10.refs_1_
  17.6 0.2 collective-permute-done.11.refs_2_
  17.8 0.2 settle1.1
  18.0 2.7 %collective-permute-start.12 = (bf16[2,16384]{1,0:T(2,128)(2,1)S(1)}, bf16[2,16384]{1,0:T(2,128)(2,1)S(1)}, u32[]{:S(2)}, u32[]{:S(2)}) collective-permute-start(bf16[2,16384]{1,0:T(2,128)(2,1)S(1)} %get-tuple-element.46), channel_id=1, source_target_pairs={{0,8},{1,9},{2,10},{3,11},{4,12},{5,13},{6,14},{7,15},{8,0},{9,1},... | collective-permute-start | bytes 196616 | tf_op jit(solution)/shard_map/ppermute | solution.py:249
  20.7 1.4 %collective-permute-done.4.arrived = bf16[2,16384]{1,0:T(2,128)(2,1)S(1)} collective-permute-done((bf16[2,16384]{1,0:T(2,128)(2,1)S(1)}, bf16[2,16384]{1,0:T(2,128)(2,1)S(1)}, u32[]{:S(2)}, u32[]{:S(2)}) %collective-permute-start.4) | collective-permute-done | bytes 65568 | tf_op jit(solution)/shard_map/ppermute | solution.py:249
  22.1 0.0 copy-done.2
  22.1 0.4 %encode0.1 = (bf16[2,16384]{1,0:T(2,128)(2,1)S(1)}, bf16[2,16384]{1,0:T(2,128)(2,1)S(1)}, f32[2,128]{1,0:T(2,128)S(1)}) custom-call(f32[2,16384]{1,0:T(2,128)S(1)} %get-tuple-element.37.total, bf16[2,16384]{1,0:T(2,128)(2,1)S(1)} %collective-permute-done.4.arrived, f32[1,16384]{1,0:T(1,128)S(1)} %bitcast.3), custom_call_target="tpu_custom_call" | custom-call | bytes 163840 | tf_op jit(solution)/shard_map/encode0/pallas_call | solution.py:224
  22.5 1.2 %collective-permute-start.6 = (bf16[2,16384]{1,0:T(2,128)(2,1)S(1)}, bf16[2,16384]{1,0:T(2,128)(2,1)S(1)}, u32[]{:S(2)}, u32[]{:S(2)}) collective-permute-start(bf16[2,16384]{1,0:T(2,128)(2,1)S(1)} %get-tuple-element.39.refs_0_), channel_id=1, source_target_pairs={{0,6},{1,7},{2,4},{3,5},{4,2},{5,3},{6,0},{7,1},{8,14},{9,15},{10,... | collective-permute-start | bytes 196616 | tf_op jit(solution)/shard_map/ppermute | solution.py:249
  23.8 0.2 collective-permute-start.5
  24.0 0.0 collective-permute-done.12.arrived
  24.0 0.5 %encode1.1 = (bf16[2,16384]{1,0:T(2,128)(2,1)S(1)}, bf16[2,16384]{1,0:T(2,128)(2,1)S(1)}, f32[2,128]{1,0:T(2,128)S(1)}, bf16[4,16384]{1,0:T(4,128)(2,1)S(1)}) custom-call(f32[2,16384]{1,0:T(2,128)S(1)} %get-tuple-element.45.total, bf16[2,16384]{1,0:T(2,128)(2,1)S(1)} %collective-permute-done.12.arrived, f32[1,16384]{1,0:T(1,128)S(1)} %bitcast.4, ...), custom_call_target="tpu_custom_call" | custom-call | bytes 295424 | tf_op jit(solution)/shard_map/encode1/pallas_call | solution.py:224
  24.5 1.8 %collective-permute-start.14 = (bf16[2,16384]{1,0:T(2,128)(2,1)S(1)}, bf16[2,16384]{1,0:T(2,128)(2,1)S(1)}, u32[]{:S(2)}, u32[]{:S(2)}) collective-permute-start(bf16[2,16384]{1,0:T(2,128)(2,1)S(1)} %get-tuple-element.49), channel_id=1, source_target_pairs={{0,6},{1,7},{2,4},{3,5},{4,2},{5,3},{6,0},{7,1},{8,14},{9,15},{10,... | collective-permute-start | bytes 196616 | tf_op jit(solution)/shard_map/ppermute | solution.py:249
  26.3 1.9 %collective-permute-start.13 = (bf16[2,16384]{1,0:T(2,128)(2,1)S(1)}, bf16[2,16384]{1,0:T(2,128)(2,1)S(1)}, u32[]{:S(2)}, u32[]{:S(2)}) collective-permute-start(bf16[2,16384]{1,0:T(2,128)(2,1)S(1)} %get-tuple-element.49), channel_id=1, source_target_pairs={{0,2},{1,3},{2,0},{3,1},{4,6},{5,7},{6,4},{7,5},{8,10},{9,11},{10,... | collective-permute-start | bytes 196616 | tf_op jit(solution)/shard_map/ppermute | solution.py:249
  28.2 0.0 collective-permute-start.16
  28.2 0.0 collective-permute-done.6
  28.2 1.0 %collective-permute-done.5 = bf16[2,16384]{1,0:T(2,128)(2,1)S(1)} collective-permute-done((bf16[2,16384]{1,0:T(2,128)(2,1)S(1)}, bf16[2,16384]{1,0:T(2,128)(2,1)S(1)}, u32[]{:S(2)}, u32[]{:S(2)}) %collective-permute-start.5) | collective-permute-done | bytes 65568 | tf_op jit(solution)/shard_map/ppermute | solution.py:249
  29.2 0.2 pad_maximum_fusion.refs_0_
  29.4 0.1 collective-permute-start.7
  29.5 0.4 %collective-permute-done.14 = bf16[2,16384]{1,0:T(2,128)(2,1)S(1)} collective-permute-done((bf16[2,16384]{1,0:T(2,128)(2,1)S(1)}, bf16[2,16384]{1,0:T(2,128)(2,1)S(1)}, u32[]{:S(2)}, u32[]{:S(2)}) %collective-permute-start.14) | collective-permute-done | bytes 65568 | tf_op jit(solution)/shard_map/ppermute | solution.py:249
  29.9 0.7 %collective-permute-done.13 = bf16[2,16384]{1,0:T(2,128)(2,1)S(1)} collective-permute-done((bf16[2,16384]{1,0:T(2,128)(2,1)S(1)}, bf16[2,16384]{1,0:T(2,128)(2,1)S(1)}, u32[]{:S(2)}, u32[]{:S(2)}) %collective-permute-start.13) | collective-permute-done | bytes 65568 | tf_op jit(solution)/shard_map/ppermute | solution.py:249
  30.6 0.2 pad_maximum_fusion.1.refs_2_
  30.8 0.2 collective-permute-done.7.refs_1_
  31.0 0.1 collective-permute-start.15
  31.1 2.0 %collective-permute-done.16.refs_4_ = bf16[4,16384]{1,0:T(4,128)(2,1)S(1)} collective-permute-done((bf16[4,16384]{1,0:T(4,128)(2,1)S(1)}, bf16[4,16384]{1,0:T(4,128)(2,1)S(1)}, u32[]{:S(2)}, u32[]{:S(2)}) %collective-permute-start.16) | collective-permute-done | bytes 131104 | tf_op jit(solution)/shard_map/ppermute | solution.py:249
  33.1 0.0 collective-permute-start.17
  33.2 0.0 collective-permute-done.15.refs_3_
  33.2 0.0 copy-done
  33.2 0.9 %first_dots.1 = (f32[32,128]{1,0:T(8,128)S(1)}, bf16[2,16384]{1,0:T(2,128)(2,1)}, f32[2,128]{1,0:T(2,128)}) custom-call(bf16[6,16384]{1,0:T(8,128)(2,1)S(1)} %pad_maximum_fusion.refs_0_, bf16[6,16384]{1,0:T(8,128)(2,1)S(1)} %collective-permute-done.7.refs_1_, bf16[6,16384]{1,0:T(8,128)(2,1)S(1)} %pad_maximum_fusion.1.refs_2_, ...), custom_call_target="tpu_custom_call" | custom-call | bytes 5177856 | tf_op jit(solution)/shard_map/first_dots/pallas_call | solution.py:224
  34.1 0.4 %collective-permute-done.17.rows = bf16[4,16384]{1,0:T(4,128)(2,1)S(1)} collective-permute-done((bf16[4,16384]{1,0:T(4,128)(2,1)S(1)}, bf16[4,16384]{1,0:T(4,128)(2,1)S(1)}, u32[]{:S(2)}, u32[]{:S(2)}) %collective-permute-start.17) | collective-permute-done | bytes 131104 | tf_op jit(solution)/shard_map/ppermute | solution.py:249
  34.5 1.4 %last_dot.1 = bf16[32,128]{1,0:T(8,128)(2,1)} custom-call(bf16[4,16384]{1,0:T(4,128)(2,1)S(1)} %collective-permute-done.17.rows, f32[32,128]{1,0:T(8,128)S(1)} %get-tuple-element.56.before, bf16[16384,128]{1,0:T(8,128)(2,1)S(1)} %copy-done), custom_call_target="tpu_custom_call" | custom-call | bytes 4333568 | tf_op jit(solution)/shard_map/last_dot/pallas_call | solution.py:224
  (2 shorter events, 0.0 us)
Async XLA Ops:
  3.6 11.2 %copy-start.1 = (bf16[2,16384]{1,0:T(2,128)(2,1)S(1)}, bf16[2,16384]{1,0:T(2,128)(2,1)}, u32[]{:S(2)}) copy-start(bf16[2,16384]{1,0:T(2,128)(2,1)} %old.3) | copy-start | bytes 196612
  3.6 18.5 %copy-start.2 = (f32[16384]{0:T(1024)S(1)}, f32[16384]{0:T(1024)}, u32[]{:S(2)}) copy-start(f32[16384]{0:T(1024)} %param.12) | copy-start | bytes 196612
  3.6 29.5 %copy-start = (bf16[16384,128]{1,0:T(8,128)(2,1)S(1)}, bf16[16384,128]{1,0:T(8,128)(2,1)}, u32[]{:S(2)}) copy-start(bf16[16384,128]{1,0:T(8,128)(2,1)} %weight.3) | copy-start | bytes 12582916
  3.6 1.7 %collective-permute-start = (bf16[8,16384]{1,0:T(8,128)(2,1)S(1)}, bf16[8,16384]{1,0:T(8,128)(2,1)S(1)}, u32[]{:S(2)}, u32[]{:S(2)}) collective-permute-start(bf16[8,16384]{1,0:T(8,128)(2,1)S(1)} %slice.16), channel_id=1, source_target_pairs={{0,1},{1,0},{2,3},{3,2},{4,5},{5,4},{6,7},{7,6},{8,9},{9,8},{10,11... | collective-permute-start | bytes 786440 | tf_op jit(solution)/shard_map/ppermute | solution.py:249
  4.9 5.2 %collective-permute-start.8 = (bf16[8,16384]{1,0:T(8,128)(2,1)S(1)}, bf16[8,16384]{1,0:T(8,128)(2,1)S(1)}, u32[]{:S(2)}, u32[]{:S(2)}) collective-permute-start(bf16[8,16384]{1,0:T(8,128)(2,1)S(1)} %slice.15), channel_id=1, source_target_pairs={{0,1},{1,0},{2,3},{3,2},{4,5},{5,4},{6,7},{7,6},{8,9},{9,8},{10,11... | collective-permute-start | bytes 786440 | tf_op jit(solution)/shard_map/ppermute | solution.py:249
  5.4 8.1 %collective-permute-start.1 = (bf16[2,16384]{1,0:T(2,128)(2,1)S(1)}, bf16[2,16384]{1,0:T(2,128)(2,1)S(1)}, u32[]{:S(2)}, u32[]{:S(2)}) collective-permute-start(bf16[2,16384]{1,0:T(2,128)(2,1)S(1)} %get-tuple-element.34), channel_id=1, source_target_pairs={{0,6},{1,7},{2,4},{3,5},{4,2},{5,3},{6,0},{7,1},{8,14},{9,15},{10,... | collective-permute-start | bytes 196616 | tf_op jit(solution)/shard_map/ppermute | solution.py:249
  9.4 4.4 %collective-permute-start.2 = (bf16[2,16384]{1,0:T(2,128)(2,1)S(1)}, bf16[2,16384]{1,0:T(2,128)(2,1)S(1)}, u32[]{:S(2)}, u32[]{:S(2)}) collective-permute-start(bf16[2,16384]{1,0:T(2,128)(2,1)S(1)} %get-tuple-element.35), channel_id=1, source_target_pairs={{0,2},{1,3},{2,0},{3,1},{4,6},{5,7},{6,4},{7,5},{8,10},{9,11},{10,... | collective-permute-start | bytes 196616 | tf_op jit(solution)/shard_map/ppermute | solution.py:249
  9.9 4.9 %collective-permute-start.3 = (bf16[2,16384]{1,0:T(2,128)(2,1)S(1)}, bf16[2,16384]{1,0:T(2,128)(2,1)S(1)}, u32[]{:S(2)}, u32[]{:S(2)}) collective-permute-start(bf16[2,16384]{1,0:T(2,128)(2,1)S(1)} %get-tuple-element.36), channel_id=1, source_target_pairs={{0,4},{1,5},{2,6},{3,7},{4,0},{5,1},{6,2},{7,3},{8,12},{9,13},{10,... | collective-permute-start | bytes 196616 | tf_op jit(solution)/shard_map/ppermute | solution.py:249
  10.1 7.5 %collective-permute-start.9 = (bf16[2,16384]{1,0:T(2,128)(2,1)S(1)}, bf16[2,16384]{1,0:T(2,128)(2,1)S(1)}, u32[]{:S(2)}, u32[]{:S(2)}) collective-permute-start(bf16[2,16384]{1,0:T(2,128)(2,1)S(1)} %get-tuple-element.42), channel_id=1, source_target_pairs={{0,6},{1,7},{2,4},{3,5},{4,2},{5,3},{6,0},{7,1},{8,14},{9,15},{10,... | collective-permute-start | bytes 196616 | tf_op jit(solution)/shard_map/ppermute | solution.py:249
  13.1 4.6 %collective-permute-start.10 = (bf16[2,16384]{1,0:T(2,128)(2,1)S(1)}, bf16[2,16384]{1,0:T(2,128)(2,1)S(1)}, u32[]{:S(2)}, u32[]{:S(2)}) collective-permute-start(bf16[2,16384]{1,0:T(2,128)(2,1)S(1)} %get-tuple-element.43), channel_id=1, source_target_pairs={{0,2},{1,3},{2,0},{3,1},{4,6},{5,7},{6,4},{7,5},{8,10},{9,11},{10,... | collective-permute-start | bytes 196616 | tf_op jit(solution)/shard_map/ppermute | solution.py:249
  13.6 4.3 %collective-permute-start.11 = (bf16[2,16384]{1,0:T(2,128)(2,1)S(1)}, bf16[2,16384]{1,0:T(2,128)(2,1)S(1)}, u32[]{:S(2)}, u32[]{:S(2)}) collective-permute-start(bf16[2,16384]{1,0:T(2,128)(2,1)S(1)} %get-tuple-element.44), channel_id=1, source_target_pairs={{0,4},{1,5},{2,6},{3,7},{4,0},{5,1},{6,2},{7,3},{8,12},{9,13},{10,... | collective-permute-start | bytes 196616 | tf_op jit(solution)/shard_map/ppermute | solution.py:249
  15.0 7.1 %collective-permute-start.4 = (bf16[2,16384]{1,0:T(2,128)(2,1)S(1)}, bf16[2,16384]{1,0:T(2,128)(2,1)S(1)}, u32[]{:S(2)}, u32[]{:S(2)}) collective-permute-start(bf16[2,16384]{1,0:T(2,128)(2,1)S(1)} %get-tuple-element.38), channel_id=1, source_target_pairs={{0,8},{1,9},{2,10},{3,11},{4,12},{5,13},{6,14},{7,15},{8,0},{9,1},... | collective-permute-start | bytes 196616 | tf_op jit(solution)/shard_map/ppermute | solution.py:249
  18.0 6.0 %collective-permute-start.12 = (bf16[2,16384]{1,0:T(2,128)(2,1)S(1)}, bf16[2,16384]{1,0:T(2,128)(2,1)S(1)}, u32[]{:S(2)}, u32[]{:S(2)}) collective-permute-start(bf16[2,16384]{1,0:T(2,128)(2,1)S(1)} %get-tuple-element.46), channel_id=1, source_target_pairs={{0,8},{1,9},{2,10},{3,11},{4,12},{5,13},{6,14},{7,15},{8,0},{9,1},... | collective-permute-start | bytes 196616 | tf_op jit(solution)/shard_map/ppermute | solution.py:249
  22.5 5.6 %collective-permute-start.6 = (bf16[2,16384]{1,0:T(2,128)(2,1)S(1)}, bf16[2,16384]{1,0:T(2,128)(2,1)S(1)}, u32[]{:S(2)}, u32[]{:S(2)}) collective-permute-start(bf16[2,16384]{1,0:T(2,128)(2,1)S(1)} %get-tuple-element.39.refs_0_), channel_id=1, source_target_pairs={{0,6},{1,7},{2,4},{3,5},{4,2},{5,3},{6,0},{7,1},{8,14},{9,15},{10,... | collective-permute-start | bytes 196616 | tf_op jit(solution)/shard_map/ppermute | solution.py:249
  23.8 5.4 %collective-permute-start.5 = (bf16[2,16384]{1,0:T(2,128)(2,1)S(1)}, bf16[2,16384]{1,0:T(2,128)(2,1)S(1)}, u32[]{:S(2)}, u32[]{:S(2)}) collective-permute-start(bf16[2,16384]{1,0:T(2,128)(2,1)S(1)} %get-tuple-element.39.refs_0_), channel_id=1, source_target_pairs={{0,2},{1,3},{2,0},{3,1},{4,6},{5,7},{6,4},{7,5},{8,10},{9,11},{10,... | collective-permute-start | bytes 196616 | tf_op jit(solution)/shard_map/ppermute | solution.py:249
  24.5 5.4 %collective-permute-start.14 = (bf16[2,16384]{1,0:T(2,128)(2,1)S(1)}, bf16[2,16384]{1,0:T(2,128)(2,1)S(1)}, u32[]{:S(2)}, u32[]{:S(2)}) collective-permute-start(bf16[2,16384]{1,0:T(2,128)(2,1)S(1)} %get-tuple-element.49), channel_id=1, source_target_pairs={{0,6},{1,7},{2,4},{3,5},{4,2},{5,3},{6,0},{7,1},{8,14},{9,15},{10,... | collective-permute-start | bytes 196616 | tf_op jit(solution)/shard_map/ppermute | solution.py:249
  26.3 4.3 %collective-permute-start.13 = (bf16[2,16384]{1,0:T(2,128)(2,1)S(1)}, bf16[2,16384]{1,0:T(2,128)(2,1)S(1)}, u32[]{:S(2)}, u32[]{:S(2)}) collective-permute-start(bf16[2,16384]{1,0:T(2,128)(2,1)S(1)} %get-tuple-element.49), channel_id=1, source_target_pairs={{0,2},{1,3},{2,0},{3,1},{4,6},{5,7},{6,4},{7,5},{8,10},{9,11},{10,... | collective-permute-start | bytes 196616 | tf_op jit(solution)/shard_map/ppermute | solution.py:249
  28.2 5.0 %collective-permute-start.16 = (bf16[4,16384]{1,0:T(4,128)(2,1)S(1)}, bf16[4,16384]{1,0:T(4,128)(2,1)S(1)}, u32[]{:S(2)}, u32[]{:S(2)}) collective-permute-start(bf16[4,16384]{1,0:T(4,128)(2,1)S(1)} %get-tuple-element.51), channel_id=1, source_target_pairs={{0,4},{1,5},{2,6},{3,7},{4,0},{5,1},{6,2},{7,3},{8,12},{9,13},{10,... | collective-permute-start | bytes 393224 | tf_op jit(solution)/shard_map/ppermute | solution.py:249
  29.4 1.6 %collective-permute-start.7 = (bf16[6,16384]{1,0:T(8,128)(2,1)S(1)}, bf16[6,16384]{1,0:T(8,128)(2,1)S(1)}, u32[]{:S(2)}, u32[]{:S(2)}) collective-permute-start(bf16[6,16384]{1,0:T(8,128)(2,1)S(1)} %pad_maximum_fusion.refs_0_), channel_id=1, source_target_pairs={{0,1},{1,0},{2,3},{3,2},{4,5},{5,4},{6,7},{7,6},{8,9},{9,8},{10,11... | collective-permute-start | bytes 589832 | tf_op jit(solution)/shard_map/ppermute | solution.py:249
  31.0 2.2 %collective-permute-start.15 = (bf16[6,16384]{1,0:T(8,128)(2,1)S(1)}, bf16[6,16384]{1,0:T(8,128)(2,1)S(1)}, u32[]{:S(2)}, u32[]{:S(2)}) collective-permute-start(bf16[6,16384]{1,0:T(8,128)(2,1)S(1)} %pad_maximum_fusion.1.refs_2_), channel_id=1, source_target_pairs={{0,1},{1,0},{2,3},{3,2},{4,5},{5,4},{6,7},{7,6},{8,9},{9,8},{10,11... | collective-permute-start | bytes 589832 | tf_op jit(solution)/shard_map/ppermute | solution.py:249
  33.1 1.3 %collective-permute-start.17 = (bf16[4,16384]{1,0:T(4,128)(2,1)S(1)}, bf16[4,16384]{1,0:T(4,128)(2,1)S(1)}, u32[]{:S(2)}, u32[]{:S(2)}) collective-permute-start(bf16[4,16384]{1,0:T(4,128)(2,1)S(1)} %collective-permute-done.16.refs_4_), channel_id=1, source_target_pairs={{0,1},{1,0},{2,3},{3,2},{4,5},{5,4},{6,7},{7,6},{8,9},{9,8},{10,11... | collective-permute-start | bytes 393224 | tf_op jit(solution)/shard_map/ppermute | solution.py:249

commit v19 on v18

--- a/solution.py
+++ b/solution.py
@@ -292,12 +292,12 @@
     early = [swap(held[0], near), swap(held[0], diagonal), held[0]]
     early = jnp.concatenate(early, axis=0)
     both = swap(joint, far)
-    late = [swap(held[1], near), swap(held[1], diagonal), held[1]]
+    late = [swap(held[1], diagonal), swap(held[1], near), held[1]]
     late = jnp.concatenate(late, axis=0)
     early_other = swap(early, 1)
     late, _ = lax.optimization_barrier((late, early_other))
     both_other, late_other = swap(both, 1), swap(late, 1)
-    orders = [(0, 2), (0, 1), (0, 0)], [(1, 2), (1, 1), (1, 0)], [(0, 3), (1, 3)]
+    orders = [(0, 2), (0, 1), (0, 0)], [(1, 1), (1, 2), (1, 0)], [(0, 3), (1, 3)]
     groups = [(side, order) for order in orders for side in range(2)]
     shape = (tokens, q_weight.shape[1])
     outs = second[1:3]

time: 36 us -> 36 us (level)
  transfers between devices with their start and end apart: 18 -> 18, of which waited for: 10 -> 11; matrix products, arithmetic and copies ran while one was open for 3% -> 3% of each run, Pallas kernels for 7% -> 7%
where the time goes in v19:
time: 36 us; the launch traced here: 35.9 us
  starting transfers between devices  19.4 us (54%)
  waiting for transfers between devices  7.83 us (22%)
  Pallas kernels  6.1 us (17%)
  matrix products  1.31 us (4%)
  between operations  0.76 us (2%)
  other arithmetic  0.43 us (1%)
    ppermute x18, starting transfers between devices, swap(): return lax.ppermute(x, 'tp', [(i, i ^ distance) for i in range(n)])  19.4 us
    ppermute x18, waiting for transfers between devices, swap(): return lax.ppermute(x, 'tp', [(i, i ^ distance) for i in range(n)])  7.83 us
    pallas_call x8, Pallas kernels, local_call(): pl.pallas_call(kernel, out_shape=[(space[0] if space else jax.ShapeDtypeS...  3.81 us
    pallas_call x1, Pallas kernels, attend(): pl.pallas_call(functools.partial(attend_kernel, n), out_shape=[jax.ShapeD...  2.28 us
  transfers between devices with their start and end apart: 18, of which 11 were waited for; matrix products, arithmetic and copies ran while one was open for 3% of the time, Pallas kernels for 7%

profile of v19, /device:TPU:0, one launch (start us, length us, event | category | flops | bytes accessed | tf_op | source)
XLA Modules:
  0.0 35.9 jit_solution(12797125635294905055)
XLA Ops:
  0.6 2.3 %attend.1 = (bf16[32,128]{1,0:T(8,128)(2,1)S(1)}, bf16[128,16384]{1,0:T(8,128)(2,1)S(1)}) custom-call(bf16[32,128]{1,0:T(8,128)(2,1)} %queries.1, bf16[32,1024]{1,0:T(8,128)(2,1)} %keys.1, bf16[32,1024]{1,0:T(8,128)(2,1)} %values.1, bf16[128,16384]{1,0:T(8,128)(2,1)} %weight.2), custom_call_target="tpu_custom_call" | custom-call | bytes 4194304 | tf_op jit(solution)/shard_map/attend/pallas_call | solution.py:86
  2.9 0.7 %convolution_convert_fusion = bf16[16,16384]{1,0:T(8,128)(2,1)S(1)} fusion(bf16[128,16384]{1,0:T(8,128)(2,1)S(1)} %get-tuple-element.31, bf16[32,128]{1,0:T(8,128)(2,1)S(1)} %get-tuple-element.30), kind=kOutput, calls=%fused_computation | convolution fusion | flops 67371008 | bytes 4722688 | tf_op jit(solution)/shard_map/dot_general | solution.py:255
  3.6 0.0 copy-start.1
  3.6 0.0 copy-start.2
  3.6 0.0 copy-start
  3.6 0.5 %collective-permute-start = (bf16[8,16384]{1,0:T(8,128)(2,1)S(1)}, bf16[8,16384]{1,0:T(8,128)(2,1)S(1)}, u32[]{:S(2)}, u32[]{:S(2)}) collective-permute-start(bf16[8,16384]{1,0:T(8,128)(2,1)S(1)} %slice.16), channel_id=1, source_target_pairs={{0,1},{1,0},{2,3},{3,2},{4,5},{5,4},{6,7},{7,6},{8,9},{9,8},{10,11... | collective-permute-start | bytes 786440 | tf_op jit(solution)/shard_map/ppermute | solution.py:249
  4.2 0.7 %fusion.1.kept = f32[16,16384]{1,0:T(8,128)S(1)} fusion(bf16[128,16384]{1,0:T(8,128)(2,1)S(1)} %get-tuple-element.31, bf16[32,128]{1,0:T(8,128)(2,1)S(1)} %get-tuple-element.30), kind=kOutput, calls=%fused_computation.4 | convolution fusion | flops 67108864 | bytes 5246976 | tf_op jit(solution)/shard_map/dot_general | solution.py:256
  4.9 0.1 collective-permute-start.8
  5.0 0.4 collective-permute-done.got
  5.3 0.1 split0.1
  5.4 4.0 %collective-permute-start.1 = (bf16[2,16384]{1,0:T(2,128)(2,1)S(1)}, bf16[2,16384]{1,0:T(2,128)(2,1)S(1)}, u32[]{:S(2)}, u32[]{:S(2)}) collective-permute-start(bf16[2,16384]{1,0:T(2,128)(2,1)S(1)} %get-tuple-element.34), channel_id=1, source_target_pairs={{0,6},{1,7},{2,4},{3,5},{4,2},{5,3},{6,0},{7,1},{8,14},{9,15},{10,... | collective-permute-start | bytes 196616 | tf_op jit(solution)/shard_map/ppermute | solution.py:249
  9.4 0.5 %collective-permute-start.2 = (bf16[2,16384]{1,0:T(2,128)(2,1)S(1)}, bf16[2,16384]{1,0:T(2,128)(2,1)S(1)}, u32[]{:S(2)}, u32[]{:S(2)}) collective-permute-start(bf16[2,16384]{1,0:T(2,128)(2,1)S(1)} %get-tuple-element.35), channel_id=1, source_target_pairs={{0,2},{1,3},{2,0},{3,1},{4,6},{5,7},{6,4},{7,5},{8,10},{9,11},{10,... | collective-permute-start | bytes 196616 | tf_op jit(solution)/shard_map/ppermute | solution.py:249
  9.9 0.1 collective-permute-start.3
  10.0 0.0 collective-permute-done.8.got
  10.0 0.1 split1.1
  10.1 2.9 %collective-permute-start.9 = (bf16[2,16384]{1,0:T(2,128)(2,1)S(1)}, bf16[2,16384]{1,0:T(2,128)(2,1)S(1)}, u32[]{:S(2)}, u32[]{:S(2)}) collective-permute-start(bf16[2,16384]{1,0:T(2,128)(2,1)S(1)} %get-tuple-element.42), channel_id=1, source_target_pairs={{0,6},{1,7},{2,4},{3,5},{4,2},{5,3},{6,0},{7,1},{8,14},{9,15},{10,... | collective-permute-start | bytes 196616 | tf_op jit(solution)/shard_map/ppermute | solution.py:249
  13.1 0.5 %collective-permute-start.10 = (bf16[2,16384]{1,0:T(2,128)(2,1)S(1)}, bf16[2,16384]{1,0:T(2,128)(2,1)S(1)}, u32[]{:S(2)}, u32[]{:S(2)}) collective-permute-start(bf16[2,16384]{1,0:T(2,128)(2,1)S(1)} %get-tuple-element.43), channel_id=1, source_target_pairs={{0,2},{1,3},{2,0},{3,1},{4,6},{5,7},{6,4},{7,5},{8,10},{9,11},{10,... | collective-permute-start | bytes 196616 | tf_op jit(solution)/shard_map/ppermute | solution.py:249
  13.6 0.0 collective-permute-done.1.refs_0_
  13.6 0.2 collective-permute-start.11
  13.8 0.0 collective-permute-done.2.refs_1_
  13.8 1.0 %collective-permute-done.3.refs_2_ = bf16[2,16384]{1,0:T(2,128)(2,1)S(1)} collective-permute-done((bf16[2,16384]{1,0:T(2,128)(2,1)S(1)}, bf16[2,16384]{1,0:T(2,128)(2,1)S(1)}, u32[]{:S(2)}, u32[]{:S(2)}) %collective-permute-start.3) | collective-permute-done | bytes 65568 | tf_op jit(solution)/shard_map/ppermute | solution.py:249
  14.8 0.0 copy-done.1
  14.8 0.2 settle0.1
  15.0 2.6 %collective-permute-start.4 = (bf16[2,16384]{1,0:T(2,128)(2,1)S(1)}, bf16[2,16384]{1,0:T(2,128)(2,1)S(1)}, u32[]{:S(2)}, u32[]{:S(2)}) collective-permute-start(bf16[2,16384]{1,0:T(2,128)(2,1)S(1)} %get-tuple-element.38), channel_id=1, source_target_pairs={{0,8},{1,9},{2,10},{3,11},{4,12},{5,13},{6,14},{7,15},{8,0},{9,1},... | collective-permute-start | bytes 196616 | tf_op jit(solution)/shard_map/ppermute | solution.py:249
  17.6 0.0 collective-permute-done.9.refs_0_
  17.6 0.0 collective-permute-done.10.refs_1_
  17.6 0.2 collective-permute-done.11.refs_2_
  17.8 0.2 settle1.1
  18.0 2.7 %collective-permute-start.12 = (bf16[2,16384]{1,0:T(2,128)(2,1)S(1)}, bf16[2,16384]{1,0:T(2,128)(2,1)S(1)}, u32[]{:S(2)}, u32[]{:S(2)}) collective-permute-start(bf16[2,16384]{1,0:T(2,128)(2,1)S(1)} %get-tuple-element.46), channel_id=1, source_target_pairs={{0,8},{1,9},{2,10},{3,11},{4,12},{5,13},{6,14},{7,15},{8,0},{9,1},... | collective-permute-start | bytes 196616 | tf_op jit(solution)/shard_map/ppermute | solution.py:249
  20.7 1.4 %collective-permute-done.4.arrived = bf16[2,16384]{1,0:T(2,128)(2,1)S(1)} collective-permute-done((bf16[2,16384]{1,0:T(2,128)(2,1)S(1)}, bf16[2,16384]{1,0:T(2,128)(2,1)S(1)}, u32[]{:S(2)}, u32[]{:S(2)}) %collective-permute-start.4) | collective-permute-done | bytes 65568 | tf_op jit(solution)/shard_map/ppermute | solution.py:249
  22.1 0.0 copy-done.2
  22.1 0.4 %encode0.1 = (bf16[2,16384]{1,0:T(2,128)(2,1)S(1)}, bf16[2,16384]{1,0:T(2,128)(2,1)S(1)}, f32[2,128]{1,0:T(2,128)S(1)}) custom-call(f32[2,16384]{1,0:T(2,128)S(1)} %get-tuple-element.37.total, bf16[2,16384]{1,0:T(2,128)(2,1)S(1)} %collective-permute-done.4.arrived, f32[1,16384]{1,0:T(1,128)S(1)} %bitcast.3), custom_call_target="tpu_custom_call" | custom-call | bytes 163840 | tf_op jit(solution)/shard_map/encode0/pallas_call | solution.py:224
  22.5 1.2 %collective-permute-start.6 = (bf16[2,16384]{1,0:T(2,128)(2,1)S(1)}, bf16[2,16384]{1,0:T(2,128)(2,1)S(1)}, u32[]{:S(2)}, u32[]{:S(2)}) collective-permute-start(bf16[2,16384]{1,0:T(2,128)(2,1)S(1)} %get-tuple-element.39.refs_0_), channel_id=1, source_target_pairs={{0,6},{1,7},{2,4},{3,5},{4,2},{5,3},{6,0},{7,1},{8,14},{9,15},{10,... | collective-permute-start | bytes 196616 | tf_op jit(solution)/shard_map/ppermute | solution.py:249
  23.8 0.2 collective-permute-start.5
  24.0 0.0 collective-permute-done.12.arrived
  24.0 0.5 %encode1.1 = (bf16[2,16384]{1,0:T(2,128)(2,1)S(1)}, bf16[2,16384]{1,0:T(2,128)(2,1)S(1)}, f32[2,128]{1,0:T(2,128)S(1)}, bf16[4,16384]{1,0:T(4,128)(2,1)S(1)}) custom-call(f32[2,16384]{1,0:T(2,128)S(1)} %get-tuple-element.45.total, bf16[2,16384]{1,0:T(2,128)(2,1)S(1)} %collective-permute-done.12.arrived, f32[1,16384]{1,0:T(1,128)S(1)} %bitcast.4, ...), custom_call_target="tpu_custom_call" | custom-call | bytes 295424 | tf_op jit(solution)/shard_map/encode1/pallas_call | solution.py:224
  24.5 2.0 %collective-permute-start.14 = (bf16[2,16384]{1,0:T(2,128)(2,1)S(1)}, bf16[2,16384]{1,0:T(2,128)(2,1)S(1)}, u32[]{:S(2)}, u32[]{:S(2)}) collective-permute-start(bf16[2,16384]{1,0:T(2,128)(2,1)S(1)} %get-tuple-element.49), channel_id=1, source_target_pairs={{0,2},{1,3},{2,0},{3,1},{4,6},{5,7},{6,4},{7,5},{8,10},{9,11},{10,... | collective-permute-start | bytes 196616 | tf_op jit(solution)/shard_map/ppermute | solution.py:249
  26.5 1.7 %collective-permute-start.13 = (bf16[2,16384]{1,0:T(2,128)(2,1)S(1)}, bf16[2,16384]{1,0:T(2,128)(2,1)S(1)}, u32[]{:S(2)}, u32[]{:S(2)}) collective-permute-start(bf16[2,16384]{1,0:T(2,128)(2,1)S(1)} %get-tuple-element.49), channel_id=1, source_target_pairs={{0,6},{1,7},{2,4},{3,5},{4,2},{5,3},{6,0},{7,1},{8,14},{9,15},{10,... | collective-permute-start | bytes 196616 | tf_op jit(solution)/shard_map/ppermute | solution.py:249
  28.2 0.0 collective-permute-start.16
  28.2 0.3 collective-permute-done.6
  28.5 0.5 %collective-permute-done.5 = bf16[2,16384]{1,0:T(2,128)(2,1)S(1)} collective-permute-done((bf16[2,16384]{1,0:T(2,128)(2,1)S(1)}, bf16[2,16384]{1,0:T(2,128)(2,1)S(1)}, u32[]{:S(2)}, u32[]{:S(2)}) %collective-permute-start.5) | collective-permute-done | bytes 65568 | tf_op jit(solution)/shard_map/ppermute | solution.py:249
  29.0 0.2 pad_maximum_fusion.refs_0_
  29.2 0.1 collective-permute-start.7
  29.3 0.4 %collective-permute-done.14 = bf16[2,16384]{1,0:T(2,128)(2,1)S(1)} collective-permute-done((bf16[2,16384]{1,0:T(2,128)(2,1)S(1)}, bf16[2,16384]{1,0:T(2,128)(2,1)S(1)}, u32[]{:S(2)}, u32[]{:S(2)}) %collective-permute-start.14) | collective-permute-done | bytes 65568 | tf_op jit(solution)/shard_map/ppermute | solution.py:249
  29.7 2.0 %collective-permute-done.13 = bf16[2,16384]{1,0:T(2,128)(2,1)S(1)} collective-permute-done((bf16[2,16384]{1,0:T(2,128)(2,1)S(1)}, bf16[2,16384]{1,0:T(2,128)(2,1)S(1)}, u32[]{:S(2)}, u32[]{:S(2)}) %collective-permute-start.13) | collective-permute-done | bytes 65568 | tf_op jit(solution)/shard_map/ppermute | solution.py:249
  31.7 0.2 pad_maximum_fusion.1.refs_2_
  31.9 0.0 collective-permute-done.7.refs_1_
  31.9 0.1 collective-permute-start.15
  32.0 1.2 %collective-permute-done.16.refs_4_ = bf16[4,16384]{1,0:T(4,128)(2,1)S(1)} collective-permute-done((bf16[4,16384]{1,0:T(4,128)(2,1)S(1)}, bf16[4,16384]{1,0:T(4,128)(2,1)S(1)}, u32[]{:S(2)}, u32[]{:S(2)}) %collective-permute-start.16) | collective-permute-done | bytes 131104 | tf_op jit(solution)/shard_map/ppermute | solution.py:249
  33.1 0.0 collective-permute-start.17
  33.1 0.4 %collective-permute-done.15.refs_3_ = bf16[6,16384]{1,0:T(8,128)(2,1)S(1)} collective-permute-done((bf16[6,16384]{1,0:T(8,128)(2,1)S(1)}, bf16[6,16384]{1,0:T(8,128)(2,1)S(1)}, u32[]{:S(2)}, u32[]{:S(2)}) %collective-permute-start.15) | collective-permute-done | bytes 196640 | tf_op jit(solution)/shard_map/ppermute | solution.py:249
  33.5 0.0 copy-done
  33.5 0.9 %first_dots.1 = (f32[32,128]{1,0:T(8,128)S(1)}, bf16[2,16384]{1,0:T(2,128)(2,1)}, f32[2,128]{1,0:T(2,128)}) custom-call(bf16[6,16384]{1,0:T(8,128)(2,1)S(1)} %pad_maximum_fusion.refs_0_, bf16[6,16384]{1,0:T(8,128)(2,1)S(1)} %collective-permute-done.7.refs_1_, bf16[6,16384]{1,0:T(8,128)(2,1)S(1)} %pad_maximum_fusion.1.refs_2_, ...), custom_call_target="tpu_custom_call" | custom-call | bytes 5177856 | tf_op jit(solution)/shard_map/first_dots/pallas_call | solution.py:224
  34.4 0.1 collective-permute-done.17.rows
  34.5 1.4 %last_dot.1 = bf16[32,128]{1,0:T(8,128)(2,1)} custom-call(bf16[4,16384]{1,0:T(4,128)(2,1)S(1)} %collective-permute-done.17.rows, f32[32,128]{1,0:T(8,128)S(1)} %get-tuple-element.56.before, bf16[16384,128]{1,0:T(8,128)(2,1)S(1)} %copy-done), custom_call_target="tpu_custom_call" | custom-call | bytes 4333568 | tf_op jit(solution)/shard_map/last_dot/pallas_call | solution.py:224
  (2 shorter events, 0.0 us)
Async XLA Ops:
  3.6 11.2 %copy-start.1 = (bf16[2,16384]{1,0:T(2,128)(2,1)S(1)}, bf16[2,16384]{1,0:T(2,128)(2,1)}, u32[]{:S(2)}) copy-start(bf16[2,16384]{1,0:T(2,128)(2,1)} %old.3) | copy-start | bytes 196612
  3.6 18.5 %copy-start.2 = (f32[16384]{0:T(1024)S(1)}, f32[16384]{0:T(1024)}, u32[]{:S(2)}) copy-start(f32[16384]{0:T(1024)} %param.12) | copy-start | bytes 196612
  3.6 29.9 %copy-start = (bf16[16384,128]{1,0:T(8,128)(2,1)S(1)}, bf16[16384,128]{1,0:T(8,128)(2,1)}, u32[]{:S(2)}) copy-start(bf16[16384,128]{1,0:T(8,128)(2,1)} %weight.3) | copy-start | bytes 12582916
  3.6 1.7 %collective-permute-start = (bf16[8,16384]{1,0:T(8,128)(2,1)S(1)}, bf16[8,16384]{1,0:T(8,128)(2,1)S(1)}, u32[]{:S(2)}, u32[]{:S(2)}) collective-permute-start(bf16[8,16384]{1,0:T(8,128)(2,1)S(1)} %slice.16), channel_id=1, source_target_pairs={{0,1},{1,0},{2,3},{3,2},{4,5},{5,4},{6,7},{7,6},{8,9},{9,8},{10,11... | collective-permute-start | bytes 786440 | tf_op jit(solution)/shard_map/ppermute | solution.py:249
  4.9 5.2 %collective-permute-start.8 = (bf16[8,16384]{1,0:T(8,128)(2,1)S(1)}, bf16[8,16384]{1,0:T(8,128)(2,1)S(1)}, u32[]{:S(2)}, u32[]{:S(2)}) collective-permute-start(bf16[8,16384]{1,0:T(8,128)(2,1)S(1)} %slice.15), channel_id=1, source_target_pairs={{0,1},{1,0},{2,3},{3,2},{4,5},{5,4},{6,7},{7,6},{8,9},{9,8},{10,11... | collective-permute-start | bytes 786440 | tf_op jit(solution)/shard_map/ppermute | solution.py:249
  5.4 8.1 %collective-permute-start.1 = (bf16[2,16384]{1,0:T(2,128)(2,1)S(1)}, bf16[2,16384]{1,0:T(2,128)(2,1)S(1)}, u32[]{:S(2)}, u32[]{:S(2)}) collective-permute-start(bf16[2,16384]{1,0:T(2,128)(2,1)S(1)} %get-tuple-element.34), channel_id=1, source_target_pairs={{0,6},{1,7},{2,4},{3,5},{4,2},{5,3},{6,0},{7,1},{8,14},{9,15},{10,... | collective-permute-start | bytes 196616 | tf_op jit(solution)/shard_map/ppermute | solution.py:249
  9.4 4.4 %collective-permute-start.2 = (bf16[2,16384]{1,0:T(2,128)(2,1)S(1)}, bf16[2,16384]{1,0:T(2,128)(2,1)S(1)}, u32[]{:S(2)}, u32[]{:S(2)}) collective-permute-start(bf16[2,16384]{1,0:T(2,128)(2,1)S(1)} %get-tuple-element.35), channel_id=1, source_target_pairs={{0,2},{1,3},{2,0},{3,1},{4,6},{5,7},{6,4},{7,5},{8,10},{9,11},{10,... | collective-permute-start | bytes 196616 | tf_op jit(solution)/shard_map/ppermute | solution.py:249
  9.9 4.9 %collective-permute-start.3 = (bf16[2,16384]{1,0:T(2,128)(2,1)S(1)}, bf16[2,16384]{1,0:T(2,128)(2,1)S(1)}, u32[]{:S(2)}, u32[]{:S(2)}) collective-permute-start(bf16[2,16384]{1,0:T(2,128)(2,1)S(1)} %get-tuple-element.36), channel_id=1, source_target_pairs={{0,4},{1,5},{2,6},{3,7},{4,0},{5,1},{6,2},{7,3},{8,12},{9,13},{10,... | collective-permute-start | bytes 196616 | tf_op jit(solution)/shard_map/ppermute | solution.py:249
  10.1 7.5 %collective-permute-start.9 = (bf16[2,16384]{1,0:T(2,128)(2,1)S(1)}, bf16[2,16384]{1,0:T(2,128)(2,1)S(1)}, u32[]{:S(2)}, u32[]{:S(2)}) collective-permute-start(bf16[2,16384]{1,0:T(2,128)(2,1)S(1)} %get-tuple-element.42), channel_id=1, source_target_pairs={{0,6},{1,7},{2,4},{3,5},{4,2},{5,3},{6,0},{7,1},{8,14},{9,15},{10,... | collective-permute-start | bytes 196616 | tf_op jit(solution)/shard_map/ppermute | solution.py:249
  13.1 4.6 %collective-permute-start.10 = (bf16[2,16384]{1,0:T(2,128)(2,1)S(1)}, bf16[2,16384]{1,0:T(2,128)(2,1)S(1)}, u32[]{:S(2)}, u32[]{:S(2)}) collective-permute-start(bf16[2,16384]{1,0:T(2,128)(2,1)S(1)} %get-tuple-element.43), channel_id=1, source_target_pairs={{0,2},{1,3},{2,0},{3,1},{4,6},{5,7},{6,4},{7,5},{8,10},{9,11},{10,... | collective-permute-start | bytes 196616 | tf_op jit(solution)/shard_map/ppermute | solution.py:249
  13.6 4.3 %collective-permute-start.11 = (bf16[2,16384]{1,0:T(2,128)(2,1)S(1)}, bf16[2,16384]{1,0:T(2,128)(2,1)S(1)}, u32[]{:S(2)}, u32[]{:S(2)}) collective-permute-start(bf16[2,16384]{1,0:T(2,128)(2,1)S(1)} %get-tuple-element.44), channel_id=1, source_target_pairs={{0,4},{1,5},{2,6},{3,7},{4,0},{5,1},{6,2},{7,3},{8,12},{9,13},{10,... | collective-permute-start | bytes 196616 | tf_op jit(solution)/shard_map/ppermute | solution.py:249
  15.0 7.1 %collective-permute-start.4 = (bf16[2,16384]{1,0:T(2,128)(2,1)S(1)}, bf16[2,16384]{1,0:T(2,128)(2,1)S(1)}, u32[]{:S(2)}, u32[]{:S(2)}) collective-permute-start(bf16[2,16384]{1,0:T(2,128)(2,1)S(1)} %get-tuple-element.38), channel_id=1, source_target_pairs={{0,8},{1,9},{2,10},{3,11},{4,12},{5,13},{6,14},{7,15},{8,0},{9,1},... | collective-permute-start | bytes 196616 | tf_op jit(solution)/shard_map/ppermute | solution.py:249
  18.0 6.0 %collective-permute-start.12 = (bf16[2,16384]{1,0:T(2,128)(2,1)S(1)}, bf16[2,16384]{1,0:T(2,128)(2,1)S(1)}, u32[]{:S(2)}, u32[]{:S(2)}) collective-permute-start(bf16[2,16384]{1,0:T(2,128)(2,1)S(1)} %get-tuple-element.46), channel_id=1, source_target_pairs={{0,8},{1,9},{2,10},{3,11},{4,12},{5,13},{6,14},{7,15},{8,0},{9,1},... | collective-permute-start | bytes 196616 | tf_op jit(solution)/shard_map/ppermute | solution.py:249
  22.5 5.9 %collective-permute-start.6 = (bf16[2,16384]{1,0:T(2,128)(2,1)S(1)}, bf16[2,16384]{1,0:T(2,128)(2,1)S(1)}, u32[]{:S(2)}, u32[]{:S(2)}) collective-permute-start(bf16[2,16384]{1,0:T(2,128)(2,1)S(1)} %get-tuple-element.39.refs_0_), channel_id=1, source_target_pairs={{0,6},{1,7},{2,4},{3,5},{4,2},{5,3},{6,0},{7,1},{8,14},{9,15},{10,... | collective-permute-start | bytes 196616 | tf_op jit(solution)/shard_map/ppermute | solution.py:249
  23.8 5.2 %collective-permute-start.5 = (bf16[2,16384]{1,0:T(2,128)(2,1)S(1)}, bf16[2,16384]{1,0:T(2,128)(2,1)S(1)}, u32[]{:S(2)}, u32[]{:S(2)}) collective-permute-start(bf16[2,16384]{1,0:T(2,128)(2,1)S(1)} %get-tuple-element.39.refs_0_), channel_id=1, source_target_pairs={{0,2},{1,3},{2,0},{3,1},{4,6},{5,7},{6,4},{7,5},{8,10},{9,11},{10,... | collective-permute-start | bytes 196616 | tf_op jit(solution)/shard_map/ppermute | solution.py:249
  24.5 5.2 %collective-permute-start.14 = (bf16[2,16384]{1,0:T(2,128)(2,1)S(1)}, bf16[2,16384]{1,0:T(2,128)(2,1)S(1)}, u32[]{:S(2)}, u32[]{:S(2)}) collective-permute-start(bf16[2,16384]{1,0:T(2,128)(2,1)S(1)} %get-tuple-element.49), channel_id=1, source_target_pairs={{0,2},{1,3},{2,0},{3,1},{4,6},{5,7},{6,4},{7,5},{8,10},{9,11},{10,... | collective-permute-start | bytes 196616 | tf_op jit(solution)/shard_map/ppermute | solution.py:249
  26.5 5.2 %collective-permute-start.13 = (bf16[2,16384]{1,0:T(2,128)(2,1)S(1)}, bf16[2,16384]{1,0:T(2,128)(2,1)S(1)}, u32[]{:S(2)}, u32[]{:S(2)}) collective-permute-start(bf16[2,16384]{1,0:T(2,128)(2,1)S(1)} %get-tuple-element.49), channel_id=1, source_target_pairs={{0,6},{1,7},{2,4},{3,5},{4,2},{5,3},{6,0},{7,1},{8,14},{9,15},{10,... | collective-permute-start | bytes 196616 | tf_op jit(solution)/shard_map/ppermute | solution.py:249
  28.2 5.0 %collective-permute-start.16 = (bf16[4,16384]{1,0:T(4,128)(2,1)S(1)}, bf16[4,16384]{1,0:T(4,128)(2,1)S(1)}, u32[]{:S(2)}, u32[]{:S(2)}) collective-permute-start(bf16[4,16384]{1,0:T(4,128)(2,1)S(1)} %get-tuple-element.51), channel_id=1, source_target_pairs={{0,4},{1,5},{2,6},{3,7},{4,0},{5,1},{6,2},{7,3},{8,12},{9,13},{10,... | collective-permute-start | bytes 393224 | tf_op jit(solution)/shard_map/ppermute | solution.py:249
  29.2 2.7 %collective-permute-start.7 = (bf16[6,16384]{1,0:T(8,128)(2,1)S(1)}, bf16[6,16384]{1,0:T(8,128)(2,1)S(1)}, u32[]{:S(2)}, u32[]{:S(2)}) collective-permute-start(bf16[6,16384]{1,0:T(8,128)(2,1)S(1)} %pad_maximum_fusion.refs_0_), channel_id=1, source_target_pairs={{0,1},{1,0},{2,3},{3,2},{4,5},{5,4},{6,7},{7,6},{8,9},{9,8},{10,11... | collective-permute-start | bytes 589832 | tf_op jit(solution)/shard_map/ppermute | solution.py:249
  31.9 1.6 %collective-permute-start.15 = (bf16[6,16384]{1,0:T(8,128)(2,1)S(1)}, bf16[6,16384]{1,0:T(8,128)(2,1)S(1)}, u32[]{:S(2)}, u32[]{:S(2)}) collective-permute-start(bf16[6,16384]{1,0:T(8,128)(2,1)S(1)} %pad_maximum_fusion.1.refs_2_), channel_id=1, source_target_pairs={{0,1},{1,0},{2,3},{3,2},{4,5},{5,4},{6,7},{7,6},{8,9},{9,8},{10,11... | collective-permute-start | bytes 589832 | tf_op jit(solution)/shard_map/ppermute | solution.py:249
  33.1 1.3 %collective-permute-start.17 = (bf16[4,16384]{1,0:T(4,128)(2,1)S(1)}, bf16[4,16384]{1,0:T(4,128)(2,1)S(1)}, u32[]{:S(2)}, u32[]{:S(2)}) collective-permute-start(bf16[4,16384]{1,0:T(4,128)(2,1)S(1)} %collective-permute-done.16.refs_4_), channel_id=1, source_target_pairs={{0,1},{1,0},{2,3},{3,2},{4,5},{5,4},{6,7},{7,6},{8,9},{9,8},{10,11... | collective-permute-start | bytes 393224 | tf_op jit(solution)/shard_map/ppermute | solution.py:249

commit v20 on v18

--- a/solution.py
+++ b/solution.py
@@ -12,7 +12,7 @@
 EPS = 1e-06
 F32 = jnp.float32
 BF16 = jnp.bfloat16
-PIECES = 4
+PIECES = 2
 STEPS = 8
 VMEM_LIMIT = 24 << 20
 SMALL_LIMIT = 16 << 20
@@ -288,7 +288,7 @@
     second = local_call(encode_kernel, shapes, "encode1", *sums[1], gain, *first, scratch=scratch)
     held = [widen(first[0]), widen(second[0])]
     joint = second[3] if len(levels) == 1 else jnp.concatenate(held, axis=0)
-    diagonal, near, far = square
+    diagonal, far, near = square
     early = [swap(held[0], near), swap(held[0], diagonal), held[0]]
     early = jnp.concatenate(early, axis=0)
     both = swap(joint, far)
@@ -297,7 +297,7 @@
     early_other = swap(early, 1)
     late, _ = lax.optimization_barrier((late, early_other))
     both_other, late_other = swap(both, 1), swap(late, 1)
-    orders = [(0, 2), (0, 1), (0, 0)], [(1, 2), (1, 1), (1, 0)], [(0, 3), (1, 3)]
+    orders = [(0, 3), (0, 1), (0, 0)], [(1, 3), (1, 1), (1, 0)], [(0, 2), (1, 2)]
     groups = [(side, order) for order in orders for side in range(2)]
     shape = (tokens, q_weight.shape[1])
     outs = second[1:3]

time: 36 us -> 36.5 us (1.014)
  transfers between devices with their start and end apart: 18 -> 18, of which waited for: 10 -> 9; matrix products, arithmetic and copies ran while one was open for 3% -> 3% of each run, Pallas kernels for 7% -> 7%
where the time goes in v20:
time: 36.5 us; the launch traced here: 36.3 us
  starting transfers between devices  19.3 us (53%)
  waiting for transfers between devices  8.01 us (22%)
  Pallas kernels  6.38 us (17%)
  matrix products  1.31 us (4%)
  between operations  0.76 us (2%)
  other arithmetic  0.43 us (1%)
    ppermute x18, starting transfers between devices, swap(): return lax.ppermute(x, 'tp', [(i, i ^ distance) for i in range(n)])  19.3 us
    ppermute x18, waiting for transfers between devices, swap(): return lax.ppermute(x, 'tp', [(i, i ^ distance) for i in range(n)])  8.01 us
    pallas_call x8, Pallas kernels, local_call(): pl.pallas_call(kernel, out_shape=[(space[0] if space else jax.ShapeDtypeS...  3.81 us
    pallas_call x1, Pallas kernels, attend(): pl.pallas_call(functools.partial(attend_kernel, n), out_shape=[jax.ShapeD...  2.56 us
  transfers between devices with their start and end apart: 18, of which 9 were waited for; matrix products, arithmetic and copies ran while one was open for 3% of the time, Pallas kernels for 7%

profile of v20, /device:TPU:0, one launch (start us, length us, event | category | flops | bytes accessed | tf_op | source)
XLA Modules:
  0.0 36.3 jit_solution(5372609305070900241)
XLA Ops:
  0.6 2.6 %attend.1 = (bf16[32,128]{1,0:T(8,128)(2,1)S(1)}, bf16[128,16384]{1,0:T(8,128)(2,1)S(1)}) custom-call(bf16[32,128]{1,0:T(8,128)(2,1)} %queries.1, bf16[32,1024]{1,0:T(8,128)(2,1)} %keys.1, bf16[32,1024]{1,0:T(8,128)(2,1)} %values.1, bf16[128,16384]{1,0:T(8,128)(2,1)} %weight.2), custom_call_target="tpu_custom_call" | custom-call | bytes 4194304 | tf_op jit(solution)/shard_map/attend/pallas_call | solution.py:86
  3.2 0.7 %convolution_convert_fusion = bf16[16,16384]{1,0:T(8,128)(2,1)S(1)} fusion(bf16[128,16384]{1,0:T(8,128)(2,1)S(1)} %get-tuple-element.31, bf16[32,128]{1,0:T(8,128)(2,1)S(1)} %get-tuple-element.30), kind=kOutput, calls=%fused_computation | convolution fusion | flops 67371008 | bytes 4722688 | tf_op jit(solution)/shard_map/dot_general | solution.py:255
  3.9 0.0 copy-start.1
  3.9 0.0 copy-start.2
  3.9 0.0 copy-start
  3.9 0.5 %collective-permute-start = (bf16[8,16384]{1,0:T(8,128)(2,1)S(1)}, bf16[8,16384]{1,0:T(8,128)(2,1)S(1)}, u32[]{:S(2)}, u32[]{:S(2)}) collective-permute-start(bf16[8,16384]{1,0:T(8,128)(2,1)S(1)} %slice.16), channel_id=1, source_target_pairs={{0,1},{1,0},{2,3},{3,2},{4,5},{5,4},{6,7},{7,6},{8,9},{9,8},{10,11... | collective-permute-start | bytes 786440 | tf_op jit(solution)/shard_map/ppermute | solution.py:249
  4.4 0.7 %fusion.1.kept = f32[16,16384]{1,0:T(8,128)S(1)} fusion(bf16[128,16384]{1,0:T(8,128)(2,1)S(1)} %get-tuple-element.31, bf16[32,128]{1,0:T(8,128)(2,1)S(1)} %get-tuple-element.30), kind=kOutput, calls=%fused_computation.4 | convolution fusion | flops 67108864 | bytes 5246976 | tf_op jit(solution)/shard_map/dot_general | solution.py:256
  5.1 0.1 collective-permute-start.8
  5.3 0.4 collective-permute-done.got
  5.6 0.1 split0.1
  5.7 4.0 %collective-permute-start.1 = (bf16[2,16384]{1,0:T(2,128)(2,1)S(1)}, bf16[2,16384]{1,0:T(2,128)(2,1)S(1)}, u32[]{:S(2)}, u32[]{:S(2)}) collective-permute-start(bf16[2,16384]{1,0:T(2,128)(2,1)S(1)} %get-tuple-element.34), channel_id=1, source_target_pairs={{0,6},{1,7},{2,4},{3,5},{4,2},{5,3},{6,0},{7,1},{8,14},{9,15},{10,... | collective-permute-start | bytes 196616 | tf_op jit(solution)/shard_map/ppermute | solution.py:249
  9.7 0.5 %collective-permute-start.2 = (bf16[2,16384]{1,0:T(2,128)(2,1)S(1)}, bf16[2,16384]{1,0:T(2,128)(2,1)S(1)}, u32[]{:S(2)}, u32[]{:S(2)}) collective-permute-start(bf16[2,16384]{1,0:T(2,128)(2,1)S(1)} %get-tuple-element.35), channel_id=1, source_target_pairs={{0,2},{1,3},{2,0},{3,1},{4,6},{5,7},{6,4},{7,5},{8,10},{9,11},{10,... | collective-permute-start | bytes 196616 | tf_op jit(solution)/shard_map/ppermute | solution.py:249
  10.2 0.1 collective-permute-start.3
  10.3 0.0 collective-permute-done.8.got
  10.3 0.1 split1.1
  10.4 2.9 %collective-permute-start.9 = (bf16[2,16384]{1,0:T(2,128)(2,1)S(1)}, bf16[2,16384]{1,0:T(2,128)(2,1)S(1)}, u32[]{:S(2)}, u32[]{:S(2)}) collective-permute-start(bf16[2,16384]{1,0:T(2,128)(2,1)S(1)} %get-tuple-element.42), channel_id=1, source_target_pairs={{0,6},{1,7},{2,4},{3,5},{4,2},{5,3},{6,0},{7,1},{8,14},{9,15},{10,... | collective-permute-start | bytes 196616 | tf_op jit(solution)/shard_map/ppermute | solution.py:249
  13.3 0.5 %collective-permute-start.10 = (bf16[2,16384]{1,0:T(2,128)(2,1)S(1)}, bf16[2,16384]{1,0:T(2,128)(2,1)S(1)}, u32[]{:S(2)}, u32[]{:S(2)}) collective-permute-start(bf16[2,16384]{1,0:T(2,128)(2,1)S(1)} %get-tuple-element.43), channel_id=1, source_target_pairs={{0,2},{1,3},{2,0},{3,1},{4,6},{5,7},{6,4},{7,5},{8,10},{9,11},{10,... | collective-permute-start | bytes 196616 | tf_op jit(solution)/shard_map/ppermute | solution.py:249
  13.8 0.0 collective-permute-done.1.refs_0_
  13.8 0.1 collective-permute-start.11
  14.0 0.0 collective-permute-done.2.refs_1_
  14.0 1.2 %collective-permute-done.3.refs_2_ = bf16[2,16384]{1,0:T(2,128)(2,1)S(1)} collective-permute-done((bf16[2,16384]{1,0:T(2,128)(2,1)S(1)}, bf16[2,16384]{1,0:T(2,128)(2,1)S(1)}, u32[]{:S(2)}, u32[]{:S(2)}) %collective-permute-start.3) | collective-permute-done | bytes 65568 | tf_op jit(solution)/shard_map/ppermute | solution.py:249
  15.1 0.0 copy-done.1
  15.1 0.2 settle0.1
  15.3 2.6 %collective-permute-start.4 = (bf16[2,16384]{1,0:T(2,128)(2,1)S(1)}, bf16[2,16384]{1,0:T(2,128)(2,1)S(1)}, u32[]{:S(2)}, u32[]{:S(2)}) collective-permute-start(bf16[2,16384]{1,0:T(2,128)(2,1)S(1)} %get-tuple-element.38), channel_id=1, source_target_pairs={{0,8},{1,9},{2,10},{3,11},{4,12},{5,13},{6,14},{7,15},{8,0},{9,1},... | collective-permute-start | bytes 196616 | tf_op jit(solution)/shard_map/ppermute | solution.py:249
  17.9 0.0 collective-permute-done.9.refs_0_
  17.9 0.0 collective-permute-done.10.refs_1_
  17.9 0.2 collective-permute-done.11.refs_2_
  18.1 0.2 settle1.1
  18.3 2.6 %collective-permute-start.12 = (bf16[2,16384]{1,0:T(2,128)(2,1)S(1)}, bf16[2,16384]{1,0:T(2,128)(2,1)S(1)}, u32[]{:S(2)}, u32[]{:S(2)}) collective-permute-start(bf16[2,16384]{1,0:T(2,128)(2,1)S(1)} %get-tuple-element.46), channel_id=1, source_target_pairs={{0,8},{1,9},{2,10},{3,11},{4,12},{5,13},{6,14},{7,15},{8,0},{9,1},... | collective-permute-start | bytes 196616 | tf_op jit(solution)/shard_map/ppermute | solution.py:249
  21.0 1.6 %collective-permute-done.4.arrived = bf16[2,16384]{1,0:T(2,128)(2,1)S(1)} collective-permute-done((bf16[2,16384]{1,0:T(2,128)(2,1)S(1)}, bf16[2,16384]{1,0:T(2,128)(2,1)S(1)}, u32[]{:S(2)}, u32[]{:S(2)}) %collective-permute-start.4) | collective-permute-done | bytes 65568 | tf_op jit(solution)/shard_map/ppermute | solution.py:249
  22.5 0.0 copy-done.2
  22.5 0.4 %encode0.1 = (bf16[2,16384]{1,0:T(2,128)(2,1)S(1)}, bf16[2,16384]{1,0:T(2,128)(2,1)S(1)}, f32[2,128]{1,0:T(2,128)S(1)}) custom-call(f32[2,16384]{1,0:T(2,128)S(1)} %get-tuple-element.37.total, bf16[2,16384]{1,0:T(2,128)(2,1)S(1)} %collective-permute-done.4.arrived, f32[1,16384]{1,0:T(1,128)S(1)} %bitcast.3), custom_call_target="tpu_custom_call" | custom-call | bytes 163840 | tf_op jit(solution)/shard_map/encode0/pallas_call | solution.py:224
  22.9 1.2 %collective-permute-start.6 = (bf16[2,16384]{1,0:T(2,128)(2,1)S(1)}, bf16[2,16384]{1,0:T(2,128)(2,1)S(1)}, u32[]{:S(2)}, u32[]{:S(2)}) collective-permute-start(bf16[2,16384]{1,0:T(2,128)(2,1)S(1)} %get-tuple-element.39.refs_0_), channel_id=1, source_target_pairs={{0,6},{1,7},{2,4},{3,5},{4,2},{5,3},{6,0},{7,1},{8,14},{9,15},{10,... | collective-permute-start | bytes 196616 | tf_op jit(solution)/shard_map/ppermute | solution.py:249
  24.1 0.4 %collective-permute-start.5 = (bf16[2,16384]{1,0:T(2,128)(2,1)S(1)}, bf16[2,16384]{1,0:T(2,128)(2,1)S(1)}, u32[]{:S(2)}, u32[]{:S(2)}) collective-permute-start(bf16[2,16384]{1,0:T(2,128)(2,1)S(1)} %get-tuple-element.39.refs_0_), channel_id=1, source_target_pairs={{0,4},{1,5},{2,6},{3,7},{4,0},{5,1},{6,2},{7,3},{8,12},{9,13},{10,... | collective-permute-start | bytes 196616 | tf_op jit(solution)/shard_map/ppermute | solution.py:249
  24.5 0.0 collective-permute-done.12.arrived
  24.5 0.5 %encode1.1 = (bf16[2,16384]{1,0:T(2,128)(2,1)S(1)}, bf16[2,16384]{1,0:T(2,128)(2,1)S(1)}, f32[2,128]{1,0:T(2,128)S(1)}, bf16[4,16384]{1,0:T(4,128)(2,1)S(1)}) custom-call(f32[2,16384]{1,0:T(2,128)S(1)} %get-tuple-element.45.total, bf16[2,16384]{1,0:T(2,128)(2,1)S(1)} %collective-permute-done.12.arrived, f32[1,16384]{1,0:T(1,128)S(1)} %bitcast.4, ...), custom_call_target="tpu_custom_call" | custom-call | bytes 295424 | tf_op jit(solution)/shard_map/encode1/pallas_call | solution.py:224
  25.1 1.5 %collective-permute-start.14 = (bf16[2,16384]{1,0:T(2,128)(2,1)S(1)}, bf16[2,16384]{1,0:T(2,128)(2,1)S(1)}, u32[]{:S(2)}, u32[]{:S(2)}) collective-permute-start(bf16[2,16384]{1,0:T(2,128)(2,1)S(1)} %get-tuple-element.49), channel_id=1, source_target_pairs={{0,6},{1,7},{2,4},{3,5},{4,2},{5,3},{6,0},{7,1},{8,14},{9,15},{10,... | collective-permute-start | bytes 196616 | tf_op jit(solution)/shard_map/ppermute | solution.py:249
  26.5 2.0 %collective-permute-start.13 = (bf16[2,16384]{1,0:T(2,128)(2,1)S(1)}, bf16[2,16384]{1,0:T(2,128)(2,1)S(1)}, u32[]{:S(2)}, u32[]{:S(2)}) collective-permute-start(bf16[2,16384]{1,0:T(2,128)(2,1)S(1)} %get-tuple-element.49), channel_id=1, source_target_pairs={{0,4},{1,5},{2,6},{3,7},{4,0},{5,1},{6,2},{7,3},{8,12},{9,13},{10,... | collective-permute-start | bytes 196616 | tf_op jit(solution)/shard_map/ppermute | solution.py:249
  28.6 0.1 collective-permute-start.16
  28.6 0.2 collective-permute-done.6
  28.8 0.0 collective-permute-done.5
  28.8 0.2 pad_maximum_fusion.refs_0_
  29.0 0.1 collective-permute-start.7
  29.1 1.2 %collective-permute-done.14 = bf16[2,16384]{1,0:T(2,128)(2,1)S(1)} collective-permute-done((bf16[2,16384]{1,0:T(2,128)(2,1)S(1)}, bf16[2,16384]{1,0:T(2,128)(2,1)S(1)}, u32[]{:S(2)}, u32[]{:S(2)}) %collective-permute-start.14) | collective-permute-done | bytes 65568 | tf_op jit(solution)/shard_map/ppermute | solution.py:249
  30.3 1.2 %collective-permute-done.13 = bf16[2,16384]{1,0:T(2,128)(2,1)S(1)} collective-permute-done((bf16[2,16384]{1,0:T(2,128)(2,1)S(1)}, bf16[2,16384]{1,0:T(2,128)(2,1)S(1)}, u32[]{:S(2)}, u32[]{:S(2)}) %collective-permute-start.13) | collective-permute-done | bytes 65568 | tf_op jit(solution)/shard_map/ppermute | solution.py:249
  31.5 0.2 pad_maximum_fusion.1.refs_2_
  31.7 0.0 collective-permute-done.7.refs_1_
  31.7 0.1 collective-permute-start.15
  31.8 1.7 %collective-permute-done.16.refs_4_ = bf16[4,16384]{1,0:T(4,128)(2,1)S(1)} collective-permute-done((bf16[4,16384]{1,0:T(4,128)(2,1)S(1)}, bf16[4,16384]{1,0:T(4,128)(2,1)S(1)}, u32[]{:S(2)}, u32[]{:S(2)}) %collective-permute-start.16) | collective-permute-done | bytes 131104 | tf_op jit(solution)/shard_map/ppermute | solution.py:249
  33.5 0.0 collective-permute-start.17
  33.5 0.0 collective-permute-done.15.refs_3_
  33.5 0.0 copy-done
  33.5 0.9 %first_dots.1 = (f32[32,128]{1,0:T(8,128)S(1)}, bf16[2,16384]{1,0:T(2,128)(2,1)}, f32[2,128]{1,0:T(2,128)}) custom-call(bf16[6,16384]{1,0:T(8,128)(2,1)S(1)} %pad_maximum_fusion.refs_0_, bf16[6,16384]{1,0:T(8,128)(2,1)S(1)} %collective-permute-done.7.refs_1_, bf16[6,16384]{1,0:T(8,128)(2,1)S(1)} %pad_maximum_fusion.1.refs_2_, ...), custom_call_target="tpu_custom_call" | custom-call | bytes 5177856 | tf_op jit(solution)/shard_map/first_dots/pallas_call | solution.py:224
  34.5 0.4 %collective-permute-done.17.rows = bf16[4,16384]{1,0:T(4,128)(2,1)S(1)} collective-permute-done((bf16[4,16384]{1,0:T(4,128)(2,1)S(1)}, bf16[4,16384]{1,0:T(4,128)(2,1)S(1)}, u32[]{:S(2)}, u32[]{:S(2)}) %collective-permute-start.17) | collective-permute-done | bytes 131104 | tf_op jit(solution)/shard_map/ppermute | solution.py:249
  34.9 1.4 %last_dot.1 = bf16[32,128]{1,0:T(8,128)(2,1)} custom-call(bf16[4,16384]{1,0:T(4,128)(2,1)S(1)} %collective-permute-done.17.rows, f32[32,128]{1,0:T(8,128)S(1)} %get-tuple-element.56.before, bf16[16384,128]{1,0:T(8,128)(2,1)S(1)} %copy-done), custom_call_target="tpu_custom_call" | custom-call | bytes 4333568 | tf_op jit(solution)/shard_map/last_dot/pallas_call | solution.py:224
  (2 shorter events, 0.0 us)
Async XLA Ops:
  3.9 11.3 %copy-start.1 = (bf16[2,16384]{1,0:T(2,128)(2,1)S(1)}, bf16[2,16384]{1,0:T(2,128)(2,1)}, u32[]{:S(2)}) copy-start(bf16[2,16384]{1,0:T(2,128)(2,1)} %old.3) | copy-start | bytes 196612
  3.9 18.6 %copy-start.2 = (f32[16384]{0:T(1024)S(1)}, f32[16384]{0:T(1024)}, u32[]{:S(2)}) copy-start(f32[16384]{0:T(1024)} %param.12) | copy-start | bytes 196612
  3.9 29.6 %copy-start = (bf16[16384,128]{1,0:T(8,128)(2,1)S(1)}, bf16[16384,128]{1,0:T(8,128)(2,1)}, u32[]{:S(2)}) copy-start(bf16[16384,128]{1,0:T(8,128)(2,1)} %weight.3) | copy-start | bytes 12582916
  3.9 1.7 %collective-permute-start = (bf16[8,16384]{1,0:T(8,128)(2,1)S(1)}, bf16[8,16384]{1,0:T(8,128)(2,1)S(1)}, u32[]{:S(2)}, u32[]{:S(2)}) collective-permute-start(bf16[8,16384]{1,0:T(8,128)(2,1)S(1)} %slice.16), channel_id=1, source_target_pairs={{0,1},{1,0},{2,3},{3,2},{4,5},{5,4},{6,7},{7,6},{8,9},{9,8},{10,11... | collective-permute-start | bytes 786440 | tf_op jit(solution)/shard_map/ppermute | solution.py:249
  5.1 5.2 %collective-permute-start.8 = (bf16[8,16384]{1,0:T(8,128)(2,1)S(1)}, bf16[8,16384]{1,0:T(8,128)(2,1)S(1)}, u32[]{:S(2)}, u32[]{:S(2)}) collective-permute-start(bf16[8,16384]{1,0:T(8,128)(2,1)S(1)} %slice.15), channel_id=1, source_target_pairs={{0,1},{1,0},{2,3},{3,2},{4,5},{5,4},{6,7},{7,6},{8,9},{9,8},{10,11... | collective-permute-start | bytes 786440 | tf_op jit(solution)/shard_map/ppermute | solution.py:249
  5.7 8.1 %collective-permute-start.1 = (bf16[2,16384]{1,0:T(2,128)(2,1)S(1)}, bf16[2,16384]{1,0:T(2,128)(2,1)S(1)}, u32[]{:S(2)}, u32[]{:S(2)}) collective-permute-start(bf16[2,16384]{1,0:T(2,128)(2,1)S(1)} %get-tuple-element.34), channel_id=1, source_target_pairs={{0,6},{1,7},{2,4},{3,5},{4,2},{5,3},{6,0},{7,1},{8,14},{9,15},{10,... | collective-permute-start | bytes 196616 | tf_op jit(solution)/shard_map/ppermute | solution.py:249
  9.7 4.3 %collective-permute-start.2 = (bf16[2,16384]{1,0:T(2,128)(2,1)S(1)}, bf16[2,16384]{1,0:T(2,128)(2,1)S(1)}, u32[]{:S(2)}, u32[]{:S(2)}) collective-permute-start(bf16[2,16384]{1,0:T(2,128)(2,1)S(1)} %get-tuple-element.35), channel_id=1, source_target_pairs={{0,2},{1,3},{2,0},{3,1},{4,6},{5,7},{6,4},{7,5},{8,10},{9,11},{10,... | collective-permute-start | bytes 196616 | tf_op jit(solution)/shard_map/ppermute | solution.py:249
  10.2 5.0 %collective-permute-start.3 = (bf16[2,16384]{1,0:T(2,128)(2,1)S(1)}, bf16[2,16384]{1,0:T(2,128)(2,1)S(1)}, u32[]{:S(2)}, u32[]{:S(2)}) collective-permute-start(bf16[2,16384]{1,0:T(2,128)(2,1)S(1)} %get-tuple-element.36), channel_id=1, source_target_pairs={{0,4},{1,5},{2,6},{3,7},{4,0},{5,1},{6,2},{7,3},{8,12},{9,13},{10,... | collective-permute-start | bytes 196616 | tf_op jit(solution)/shard_map/ppermute | solution.py:249
  10.4 7.5 %collective-permute-start.9 = (bf16[2,16384]{1,0:T(2,128)(2,1)S(1)}, bf16[2,16384]{1,0:T(2,128)(2,1)S(1)}, u32[]{:S(2)}, u32[]{:S(2)}) collective-permute-start(bf16[2,16384]{1,0:T(2,128)(2,1)S(1)} %get-tuple-element.42), channel_id=1, source_target_pairs={{0,6},{1,7},{2,4},{3,5},{4,2},{5,3},{6,0},{7,1},{8,14},{9,15},{10,... | collective-permute-start | bytes 196616 | tf_op jit(solution)/shard_map/ppermute | solution.py:249
  13.3 4.6 %collective-permute-start.10 = (bf16[2,16384]{1,0:T(2,128)(2,1)S(1)}, bf16[2,16384]{1,0:T(2,128)(2,1)S(1)}, u32[]{:S(2)}, u32[]{:S(2)}) collective-permute-start(bf16[2,16384]{1,0:T(2,128)(2,1)S(1)} %get-tuple-element.43), channel_id=1, source_target_pairs={{0,2},{1,3},{2,0},{3,1},{4,6},{5,7},{6,4},{7,5},{8,10},{9,11},{10,... | collective-permute-start | bytes 196616 | tf_op jit(solution)/shard_map/ppermute | solution.py:249
  13.8 4.3 %collective-permute-start.11 = (bf16[2,16384]{1,0:T(2,128)(2,1)S(1)}, bf16[2,16384]{1,0:T(2,128)(2,1)S(1)}, u32[]{:S(2)}, u32[]{:S(2)}) collective-permute-start(bf16[2,16384]{1,0:T(2,128)(2,1)S(1)} %get-tuple-element.44), channel_id=1, source_target_pairs={{0,4},{1,5},{2,6},{3,7},{4,0},{5,1},{6,2},{7,3},{8,12},{9,13},{10,... | collective-permute-start | bytes 196616 | tf_op jit(solution)/shard_map/ppermute | solution.py:249
  15.3 7.2 %collective-permute-start.4 = (bf16[2,16384]{1,0:T(2,128)(2,1)S(1)}, bf16[2,16384]{1,0:T(2,128)(2,1)S(1)}, u32[]{:S(2)}, u32[]{:S(2)}) collective-permute-start(bf16[2,16384]{1,0:T(2,128)(2,1)S(1)} %get-tuple-element.38), channel_id=1, source_target_pairs={{0,8},{1,9},{2,10},{3,11},{4,12},{5,13},{6,14},{7,15},{8,0},{9,1},... | collective-permute-start | bytes 196616 | tf_op jit(solution)/shard_map/ppermute | solution.py:249
  18.3 6.2 %collective-permute-start.12 = (bf16[2,16384]{1,0:T(2,128)(2,1)S(1)}, bf16[2,16384]{1,0:T(2,128)(2,1)S(1)}, u32[]{:S(2)}, u32[]{:S(2)}) collective-permute-start(bf16[2,16384]{1,0:T(2,128)(2,1)S(1)} %get-tuple-element.46), channel_id=1, source_target_pairs={{0,8},{1,9},{2,10},{3,11},{4,12},{5,13},{6,14},{7,15},{8,0},{9,1},... | collective-permute-start | bytes 196616 | tf_op jit(solution)/shard_map/ppermute | solution.py:249
  22.9 5.9 %collective-permute-start.6 = (bf16[2,16384]{1,0:T(2,128)(2,1)S(1)}, bf16[2,16384]{1,0:T(2,128)(2,1)S(1)}, u32[]{:S(2)}, u32[]{:S(2)}) collective-permute-start(bf16[2,16384]{1,0:T(2,128)(2,1)S(1)} %get-tuple-element.39.refs_0_), channel_id=1, source_target_pairs={{0,6},{1,7},{2,4},{3,5},{4,2},{5,3},{6,0},{7,1},{8,14},{9,15},{10,... | collective-permute-start | bytes 196616 | tf_op jit(solution)/shard_map/ppermute | solution.py:249
  24.1 4.7 %collective-permute-start.5 = (bf16[2,16384]{1,0:T(2,128)(2,1)S(1)}, bf16[2,16384]{1,0:T(2,128)(2,1)S(1)}, u32[]{:S(2)}, u32[]{:S(2)}) collective-permute-start(bf16[2,16384]{1,0:T(2,128)(2,1)S(1)} %get-tuple-element.39.refs_0_), channel_id=1, source_target_pairs={{0,4},{1,5},{2,6},{3,7},{4,0},{5,1},{6,2},{7,3},{8,12},{9,13},{10,... | collective-permute-start | bytes 196616 | tf_op jit(solution)/shard_map/ppermute | solution.py:249
  25.1 5.2 %collective-permute-start.14 = (bf16[2,16384]{1,0:T(2,128)(2,1)S(1)}, bf16[2,16384]{1,0:T(2,128)(2,1)S(1)}, u32[]{:S(2)}, u32[]{:S(2)}) collective-permute-start(bf16[2,16384]{1,0:T(2,128)(2,1)S(1)} %get-tuple-element.49), channel_id=1, source_target_pairs={{0,6},{1,7},{2,4},{3,5},{4,2},{5,3},{6,0},{7,1},{8,14},{9,15},{10,... | collective-permute-start | bytes 196616 | tf_op jit(solution)/shard_map/ppermute | solution.py:249
  26.5 5.0 %collective-permute-start.13 = (bf16[2,16384]{1,0:T(2,128)(2,1)S(1)}, bf16[2,16384]{1,0:T(2,128)(2,1)S(1)}, u32[]{:S(2)}, u32[]{:S(2)}) collective-permute-start(bf16[2,16384]{1,0:T(2,128)(2,1)S(1)} %get-tuple-element.49), channel_id=1, source_target_pairs={{0,4},{1,5},{2,6},{3,7},{4,0},{5,1},{6,2},{7,3},{8,12},{9,13},{10,... | collective-permute-start | bytes 196616 | tf_op jit(solution)/shard_map/ppermute | solution.py:249
  28.6 5.0 %collective-permute-start.16 = (bf16[4,16384]{1,0:T(4,128)(2,1)S(1)}, bf16[4,16384]{1,0:T(4,128)(2,1)S(1)}, u32[]{:S(2)}, u32[]{:S(2)}) collective-permute-start(bf16[4,16384]{1,0:T(4,128)(2,1)S(1)} %get-tuple-element.51), channel_id=1, source_target_pairs={{0,2},{1,3},{2,0},{3,1},{4,6},{5,7},{6,4},{7,5},{8,10},{9,11},{10,... | collective-permute-start | bytes 393224 | tf_op jit(solution)/shard_map/ppermute | solution.py:249
  29.0 2.7 %collective-permute-start.7 = (bf16[6,16384]{1,0:T(8,128)(2,1)S(1)}, bf16[6,16384]{1,0:T(8,128)(2,1)S(1)}, u32[]{:S(2)}, u32[]{:S(2)}) collective-permute-start(bf16[6,16384]{1,0:T(8,128)(2,1)S(1)} %pad_maximum_fusion.refs_0_), channel_id=1, source_target_pairs={{0,1},{1,0},{2,3},{3,2},{4,5},{5,4},{6,7},{7,6},{8,9},{9,8},{10,11... | collective-permute-start | bytes 589832 | tf_op jit(solution)/shard_map/ppermute | solution.py:249
  31.7 1.8 %collective-permute-start.15 = (bf16[6,16384]{1,0:T(8,128)(2,1)S(1)}, bf16[6,16384]{1,0:T(8,128)(2,1)S(1)}, u32[]{:S(2)}, u32[]{:S(2)}) collective-permute-start(bf16[6,16384]{1,0:T(8,128)(2,1)S(1)} %pad_maximum_fusion.1.refs_2_), channel_id=1, source_target_pairs={{0,1},{1,0},{2,3},{3,2},{4,5},{5,4},{6,7},{7,6},{8,9},{9,8},{10,11... | collective-permute-start | bytes 589832 | tf_op jit(solution)/shard_map/ppermute | solution.py:249
  33.5 1.3 %collective-permute-start.17 = (bf16[4,16384]{1,0:T(4,128)(2,1)S(1)}, bf16[4,16384]{1,0:T(4,128)(2,1)S(1)}, u32[]{:S(2)}, u32[]{:S(2)}) collective-permute-start(bf16[4,16384]{1,0:T(4,128)(2,1)S(1)} %collective-permute-done.16.refs_4_), channel_id=1, source_target_pairs={{0,1},{1,0},{2,3},{3,2},{4,5},{5,4},{6,7},{7,6},{8,9},{9,8},{10,11... | collective-permute-start | bytes 393224 | tf_op jit(solution)/shard_map/ppermute | solution.py:249
